TPU v7x, 128 devices: a whole 4x4x4 slice. The times are simulated.
128 devices in a mesh: gx: 4 (over y), yz: 32 (over x, z, core).
Axes of the slice: x: 4, y: 4, z: 4, core: 2. Of those that a mesh axis runs over, the one named last changes fastest.
Arguments:
- adjoint_seed: float32 [216, 16, 128, 128], P(None, 'gx', 'yz'), may hold values from -6 to 6
- elem_scale: float32 [16, 128, 128], P('gx', 'yz'), may hold values from 1 to 3
- face_coef: float32 [3, 16, 128, 128], P(None, 'gx', 'yz'), may hold values from 0.25 to 1
- fine_block: float32 [216, 216], replicated, may hold values from -0.4375 to 0.4375
- fine_smoother: float32 [216, 216], replicated, may hold values from -0.0546875 to 0.0546875
- mid_block: float32 [64, 64], replicated, may hold values from -0.75 to 0.75
- coarse_block: float32 [8, 8], replicated, may hold values from -4 to 4
- prolong_mid: float32 [216, 64], replicated, may hold values from -0.75 to 0.75
- prolong_low: float32 [64, 8], replicated, may hold values from -2 to 2
- noise_map: float32 [216, 216], replicated, may hold values from -0.4375 to 0.4375
- increments: float32 [16, 128, 128], P('gx', 'yz'), may hold values from -3 to 3
Outputs:
- adjoint_solution: float32 [216, 16, 128, 128], P(None, 'gx', 'yz')
- adjoint_prev: float32 [216, 16, 128, 128], P(None, 'gx', 'yz')
All inputs are finite; a program needn't handle non-finite values.
Results may differ from a plain program's by a relative error of at most 0.0001.
Values sent between devices are 32-bit elements; how exact they have to be, the bound alone decides.
No kernel may reach another device: no remote copies, remote signals or barrier semaphores. Data moves between devices by JAX's collectives and lax.ppermute only.
A program may use at most 128 MiB of HBM per device.

v0:
```python
import jax
import jax.numpy as jnp
from jax import lax
from jax.sharding import PartitionSpec as P

NF = 6
NM = 4
NC = 2
SWEEPS = 2
COARSE_SWEEPS = 6


precise = lax.Precision.HIGHEST
upwind = 0.9
downwind = 0.3


def with_halo(cells, sides, width):
    for axis, dim in sides:
        count = lax.axis_size(axis)
        ends = count - 1
        head = lax.slice_in_dim(cells, 0, width, axis=dim)
        tail = lax.slice_in_dim(cells, cells.shape[dim] - width, cells.shape[dim], axis=dim)
        cells = jnp.concatenate(
            [
                lax.ppermute(tail, axis, [(i, (i + 1) % count) for i in range(ends)]),
                cells,
                lax.ppermute(head, axis, [((i + 1) % count, i) for i in range(ends)]),
            ],
            axis=dim,
        )
    return cells


def transpose_apply(matrix, values):
    flattened = values.reshape((values.shape[0], -1))
    result = jnp.einsum("ji,jm->im", matrix, flattened, precision=precise)
    return result.reshape((matrix.shape[1],) + values.shape[1:])


def forward_apply(matrix, values):
    flattened = values.reshape((values.shape[0], -1))
    result = jnp.einsum("ij,jm->im", matrix, flattened, precision=precise)
    return result.reshape((matrix.shape[0],) + values.shape[1:])


def face_neighbours(nodal, order_nodes, direction, across):
    element_dim = 2 + direction
    upper_layer = jnp.take(nodal, order_nodes - 1, axis=direction)
    lower_layer = jnp.take(nodal, 0, axis=direction)
    length = upper_layer.shape[element_dim]
    first_slab = lax.slice_in_dim(lower_layer, 0, 1, axis=element_dim)
    last_slab = lax.slice_in_dim(upper_layer, length - 1, length, axis=element_dim)
    if direction == 0 and across != "none":
        traces = jnp.concatenate([first_slab, last_slab], axis=element_dim)
        padded = with_halo(traces, (("gx", 2),), 1)
        lower_edge = lax.slice_in_dim(padded, 0, 1, axis=element_dim)
        upper_edge = lax.slice_in_dim(padded, 3, 4, axis=element_dim)
    elif direction == 1 and across == "both":
        traces = jnp.concatenate([first_slab, last_slab], axis=element_dim)
        padded = with_halo(traces, (("yz", 3),), 1)
        lower_edge = lax.slice_in_dim(padded, 0, 1, axis=element_dim)
        upper_edge = lax.slice_in_dim(padded, 3, 4, axis=element_dim)
    else:
        lower_edge = jnp.zeros_like(last_slab)
        upper_edge = jnp.zeros_like(first_slab)
    from_lower = jnp.concatenate(
        [lower_edge, lax.slice_in_dim(upper_layer, 0, length - 1, axis=element_dim)],
        axis=element_dim,
    )
    from_upper = jnp.concatenate(
        [lax.slice_in_dim(lower_layer, 1, length, axis=element_dim), upper_edge], axis=element_dim
    )
    return (from_lower, from_upper)


def assemble(values, matrix, scales, coefficients, order_nodes, neighbours):
    nodal_shape = (order_nodes, order_nodes, order_nodes) + values.shape[1:]
    result = (scales * (4.0 * values + transpose_apply(matrix, values))).reshape(nodal_shape)
    for direction in range(3):
        from_lower, from_upper = neighbours[direction]
        lower_spot = tuple((0 if place == direction else slice(None) for place in range(3)))
        upper_spot = tuple(
            (order_nodes - 1 if place == direction else slice(None) for place in range(3))
        )
        result = result.at[lower_spot].add(-(coefficients[direction] * (upwind * from_lower)))
        result = result.at[upper_spot].add(-(coefficients[direction] * (downwind * from_upper)))
    return result.reshape(values.shape)


def adjoint_op(values, matrix, scales, coefficients, order_nodes, across):
    nodal = values.reshape((order_nodes, order_nodes, order_nodes) + values.shape[1:])
    neighbours = [face_neighbours(nodal, order_nodes, direction, across) for direction in range(3)]
    return assemble(values, matrix, scales, coefficients, order_nodes, neighbours)


def fine_sweep(current, target, matrix, smoother, scales, coefficients):
    scaled = (target - adjoint_op(current, matrix, scales, coefficients, NF, "both")) / scales
    return current + 0.25 * scaled + transpose_apply(smoother, scaled)


def point_sweep(current, target, matrix, scales, coefficients, order_nodes, across):
    return (
        current
        + 0.2
        * (target - adjoint_op(current, matrix, scales, coefficients, order_nodes, across))
        / scales
    )


def coarse_solve(target, matrix, scales, coefficients, across):
    coarse = jnp.zeros_like(target)
    for sweep_index in range(COARSE_SWEEPS):
        coarse = point_sweep(coarse, target, matrix, scales, coefficients, NC, across)
    return coarse


def body(
    adjoint_seed,
    elem_scale,
    face_coef,
    fine_block,
    fine_smoother,
    mid_block,
    coarse_block,
    prolong_mid,
    prolong_low,
    noise_map,
    increments,
):
    fine_field = jnp.zeros_like(adjoint_seed)
    for sweep_index in range(SWEEPS):
        fine_field = fine_sweep(
            fine_field, adjoint_seed, fine_block, fine_smoother, elem_scale, face_coef
        )
    rest_mid = transpose_apply(
        prolong_mid,
        adjoint_seed - adjoint_op(fine_field, fine_block, elem_scale, face_coef, NF, "both"),
    )
    middle = jnp.zeros_like(rest_mid)
    for sweep_index in range(SWEEPS):
        middle = point_sweep(middle, rest_mid, mid_block, elem_scale, face_coef, NM, "both")
    rest_low = transpose_apply(
        prolong_low, rest_mid - adjoint_op(middle, mid_block, elem_scale, face_coef, NM, "both")
    )
    coarse = coarse_solve(rest_low, coarse_block, elem_scale, face_coef, "both")
    middle = middle + forward_apply(prolong_low, coarse)
    for sweep_index in range(SWEEPS):
        middle = point_sweep(middle, rest_mid, mid_block, elem_scale, face_coef, NM, "both")
    fine_field = fine_field + forward_apply(prolong_mid, middle)
    for sweep_index in range(SWEEPS):
        fine_field = fine_sweep(
            fine_field, adjoint_seed, fine_block, fine_smoother, elem_scale, face_coef
        )
    adjoint_prev = fine_field + increments * transpose_apply(noise_map, fine_field)
    return (fine_field, adjoint_prev)


def solution(mesh):
    return jax.shard_map(
        body,
        mesh=mesh,
        in_specs=(
            P(None, "gx", "yz", None),
            P("gx", "yz", None),
            P(None, "gx", "yz", None),
            P(),
            P(),
            P(),
            P(),
            P(),
            P(),
            P(),
            P("gx", "yz", None),
        ),
        out_specs=(P(None, "gx", "yz", None), P(None, "gx", "yz", None)),
        check_vma=False,
    )
```

profile of v0, /device:TPU:14, one launch (start us, length us, event | category | flops | bytes accessed | tf_op | source)
XLA Modules:
  0.0 561.0 jit_solution(3117068383370328758)
XLA Ops:
  0.7 3.6 collective-permute-start
  8.6 5.8 %collective-permute-start.3 = (f32[6,6,4,1,128]{4,2,0,1,3:T(4,128)S(1)}, f32[6,6,4,1,128]{4,2,0,1,3:T(4,128)S(1)}, u32[]{:S(2)}, u32[]{:S(2)}) collective-permute-start(f32[6,6,4,1,128]{4,2,0,1,3:T(4,128)S(1)} %slice.4095), channel_id=1, source_target_pairs={{1,0},{2,1},{3,2},{4,3},{5,4},{6,5},{7,6},{8,7},{9,8},{10,9},{11,1... | collective-permute-start | bytes 221192 | tf_op jit(solution)/shard_map/ppermute | solution.py:28
  14.4 3.5 collective-permute-start.24
  26.5 3.1 collective-permute-done.25
  31.6 5.1 collective-permute-done.26
  40.0 3.2 collective-permute-start.12
  48.1 3.4 collective-permute-done.13
  53.6 5.2 collective-permute-done.14
  78.5 2.9 reshape.5657
  81.3 3.2 convolution_bitcast_fusion.9
  94.6 3.0 convolution_bitcast_fusion.8
  97.6 3.3 reshape.5660
  103.4 3.2 collective-permute-start.4
  112.6 6.0 %collective-permute-start.7 = (f32[6,6,4,1,128]{4,2,0,1,3:T(4,128)S(1)}, f32[6,6,4,1,128]{4,2,0,1,3:T(4,128)S(1)}, u32[]{:S(2)}, u32[]{:S(2)}) collective-permute-start(f32[6,6,4,1,128]{4,2,0,1,3:T(4,128)S(1)} %slice.4772), channel_id=1, source_target_pairs={{1,0},{2,1},{3,2},{4,3},{5,4},{6,5},{7,6},{8,7},{9,8},{10,9},{11,1... | collective-permute-start | bytes 221192 | tf_op jit(solution)/shard_map/ppermute | solution.py:28
  125.1 2.9 reshape.5667
  128.0 3.2 convolution_bitcast_fusion.7
  133.6 3.3 add_add_fusion.2
  142.0 3.0 convolution_bitcast_fusion.6
  144.9 3.3 reshape.5670
  150.7 3.6 collective-permute-start.8
  160.4 5.8 %collective-permute-start.11 = (f32[6,6,4,1,128]{4,2,0,1,3:T(4,128)S(1)}, f32[6,6,4,1,128]{4,2,0,1,3:T(4,128)S(1)}, u32[]{:S(2)}, u32[]{:S(2)}) collective-permute-start(f32[6,6,4,1,128]{4,2,0,1,3:T(4,128)S(1)} %slice.4794), channel_id=1, source_target_pairs={{1,0},{2,1},{3,2},{4,3},{5,4},{6,5},{7,6},{8,7},{9,8},{10,9},{11,1... | collective-permute-start | bytes 221192 | tf_op jit(solution)/shard_map/ppermute | solution.py:28
  172.7 2.9 reshape.5677
  189.3 3.2 collective-permute-start.16
  194.5 2.8 collective-permute-start.17
  199.2 5.8 %collective-permute-start.19 = (f32[4,4,4,1,128]{4,3,2,0,1:T(1,128)S(1)}, f32[4,4,4,1,128]{4,3,2,0,1:T(1,128)S(1)}, u32[]{:S(2)}, u32[]{:S(2)}) collective-permute-start(f32[4,4,4,1,128]{4,3,2,0,1:T(1,128)S(1)} %slice.4822), channel_id=1, source_target_pairs={{1,0},{2,1},{3,2},{4,3},{5,4},{6,5},{7,6},{8,7},{9,8},{10,9},{11,1... | collective-permute-start | bytes 98312 | tf_op jit(solution)/shard_map/ppermute | solution.py:28
  218.3 3.2 collective-permute-start.20
  226.3 5.9 %collective-permute-start.23 = (f32[4,4,4,1,128]{4,3,2,0,1:T(1,128)S(1)}, f32[4,4,4,1,128]{4,3,2,0,1:T(1,128)S(1)}, u32[]{:S(2)}, u32[]{:S(2)}) collective-permute-start(f32[4,4,4,1,128]{4,3,2,0,1:T(1,128)S(1)} %slice.4844), channel_id=1, source_target_pairs={{1,0},{2,1},{3,2},{4,3},{5,4},{6,5},{7,6},{8,7},{9,8},{10,9},{11,1... | collective-permute-start | bytes 98312 | tf_op jit(solution)/shard_map/ppermute | solution.py:28
  247.1 3.2 collective-permute-start.28
  256.4 5.8 %collective-permute-start.31 = (f32[2,2,4,1,128]{4,2,0,1,3:T(4,128)S(1)}, f32[2,2,4,1,128]{4,2,0,1,3:T(4,128)S(1)}, u32[]{:S(2)}, u32[]{:S(2)}) collective-permute-start(f32[2,2,4,1,128]{4,2,0,1,3:T(4,128)S(1)} %slice.4872), channel_id=1, source_target_pairs={{1,0},{2,1},{3,2},{4,3},{5,4},{6,5},{7,6},{8,7},{9,8},{10,9},{11,1... | collective-permute-start | bytes 24584 | tf_op jit(solution)/shard_map/ppermute | solution.py:28
  276.0 3.2 collective-permute-start.32
  285.4 5.8 %collective-permute-start.35 = (f32[2,2,4,1,128]{4,2,0,1,3:T(4,128)S(1)}, f32[2,2,4,1,128]{4,2,0,1,3:T(4,128)S(1)}, u32[]{:S(2)}, u32[]{:S(2)}) collective-permute-start(f32[2,2,4,1,128]{4,2,0,1,3:T(4,128)S(1)} %slice.4894), channel_id=1, source_target_pairs={{1,0},{2,1},{3,2},{4,3},{5,4},{6,5},{7,6},{8,7},{9,8},{10,9},{11,1... | collective-permute-start | bytes 24584 | tf_op jit(solution)/shard_map/ppermute | solution.py:28
  302.2 3.2 collective-permute-start.36
  313.8 5.8 %collective-permute-start.39 = (f32[2,2,4,1,128]{4,3,2,0,1:T(1,128)S(1)}, f32[2,2,4,1,128]{4,3,2,0,1:T(1,128)S(1)}, u32[]{:S(2)}, u32[]{:S(2)}) collective-permute-start(f32[2,2,4,1,128]{4,3,2,0,1:T(1,128)S(1)} %slice.4916), channel_id=1, source_target_pairs={{1,0},{2,1},{3,2},{4,3},{5,4},{6,5},{7,6},{8,7},{9,8},{10,9},{11,1... | collective-permute-start | bytes 24584 | tf_op jit(solution)/shard_map/ppermute | solution.py:28
  332.9 3.2 collective-permute-start.40
  343.7 5.8 %collective-permute-start.43 = (f32[2,2,4,1,128]{4,3,2,0,1:T(1,128)S(1)}, f32[2,2,4,1,128]{4,3,2,0,1:T(1,128)S(1)}, u32[]{:S(2)}, u32[]{:S(2)}) collective-permute-start(f32[2,2,4,1,128]{4,3,2,0,1:T(1,128)S(1)} %slice.4938), channel_id=1, source_target_pairs={{1,0},{2,1},{3,2},{4,3},{5,4},{6,5},{7,6},{8,7},{9,8},{10,9},{11,1... | collective-permute-start | bytes 24584 | tf_op jit(solution)/shard_map/ppermute | solution.py:28
  362.9 3.2 collective-permute-start.44
  372.3 5.8 %collective-permute-start.47 = (f32[2,2,4,1,128]{4,2,0,1,3:T(4,128)S(1)}, f32[2,2,4,1,128]{4,2,0,1,3:T(4,128)S(1)}, u32[]{:S(2)}, u32[]{:S(2)}) collective-permute-start(f32[2,2,4,1,128]{4,2,0,1,3:T(4,128)S(1)} %slice.4960), channel_id=1, source_target_pairs={{1,0},{2,1},{3,2},{4,3},{5,4},{6,5},{7,6},{8,7},{9,8},{10,9},{11,1... | collective-permute-start | bytes 24584 | tf_op jit(solution)/shard_map/ppermute | solution.py:28
  394.4 3.2 collective-permute-start.48
  402.4 5.8 %collective-permute-start.51 = (f32[4,4,4,1,128]{4,2,0,1,3:T(4,128)S(1)}, f32[4,4,4,1,128]{4,2,0,1,3:T(4,128)S(1)}, u32[]{:S(2)}, u32[]{:S(2)}) collective-permute-start(f32[4,4,4,1,128]{4,2,0,1,3:T(4,128)S(1)} %slice.4982), channel_id=1, source_target_pairs={{1,0},{2,1},{3,2},{4,3},{5,4},{6,5},{7,6},{8,7},{9,8},{10,9},{11,1... | collective-permute-start | bytes 98312 | tf_op jit(solution)/shard_map/ppermute | solution.py:28
  414.2 2.8 convolution_bitcast_fusion.12
  420.8 3.2 collective-permute-start.52
  429.1 5.5 collective-permute-start.55
  438.8 4.0 convolution_bitcast_fusion.5
  442.9 3.3 reshape.5719
  446.2 3.6 add.1075
  449.8 3.0 reshape.5720
  455.9 3.0 convolution_bitcast_fusion.4
  458.8 3.4 reshape.5721
  464.6 3.2 collective-permute-start.56
  473.9 6.2 %collective-permute-start.59 = (f32[6,6,4,1,128]{4,2,0,1,3:T(4,128)S(1)}, f32[6,6,4,1,128]{4,2,0,1,3:T(4,128)S(1)}, u32[]{:S(2)}, u32[]{:S(2)}) collective-permute-start(f32[6,6,4,1,128]{4,2,0,1,3:T(4,128)S(1)} %slice.5026), channel_id=1, source_target_pairs={{1,0},{2,1},{3,2},{4,3},{5,4},{6,5},{7,6},{8,7},{9,8},{10,9},{11,1... | collective-permute-start | bytes 221192 | tf_op jit(solution)/shard_map/ppermute | solution.py:28
  486.3 2.9 reshape.5728
  489.2 3.2 convolution_bitcast_fusion.3
  494.9 3.3 add_add_fusion.1
  503.8 3.0 convolution_bitcast_fusion.2
  506.8 3.3 reshape.5731
  512.5 3.4 collective-permute-start.60
  522.0 5.8 %collective-permute-start.63 = (f32[6,6,4,1,128]{4,2,0,1,3:T(4,128)S(1)}, f32[6,6,4,1,128]{4,2,0,1,3:T(4,128)S(1)}, u32[]{:S(2)}, u32[]{:S(2)}) collective-permute-start(f32[6,6,4,1,128]{4,2,0,1,3:T(4,128)S(1)} %slice.5048), channel_id=1, source_target_pairs={{1,0},{2,1},{3,2},{4,3},{5,4},{6,5},{7,6},{8,7},{9,8},{10,9},{11,1... | collective-permute-start | bytes 221192 | tf_op jit(solution)/shard_map/ppermute | solution.py:28
  534.2 2.9 reshape.5738
  537.1 4.4 convolution_bitcast_fusion.1
  541.5 3.3 reshape.5739
  544.9 4.4 add_add_fusion
  551.3 3.0 convolution_bitcast_fusion
  554.3 3.5 reshape.5741
  557.8 3.0 multiply_add_fusion
  (654 shorter events, 309.6 us)
Async XLA Ops:
  0.7 63.0 %collective-permute-start = (f32[6,6,1,4,128]{4,3,0,1,2:T(4,128)S(1)}, f32[6,6,1,4,128]{4,3,0,1,2:T(4,128)S(1)}, u32[]{:S(2)}, u32[]{:S(2)}) collective-permute-start(f32[6,6,1,4,128]{4,3,0,1,2:T(4,128)S(1)} %slice.4091), channel_id=1, source_target_pairs={{0,32},{32,64},{64,96},{1,33},{33,65},{65,97},{2,34},{34,66},{66,9... | collective-permute-start | bytes 221192 | tf_op jit(solution)/shard_map/ppermute | solution.py:26
  4.3 61.1 %collective-permute-start.1 = (f32[6,6,1,4,128]{4,3,0,1,2:T(4,128)S(1)}, f32[6,6,1,4,128]{4,3,0,1,2:T(4,128)S(1)}, u32[]{:S(2)}, u32[]{:S(2)}) collective-permute-start(f32[6,6,1,4,128]{4,3,0,1,2:T(4,128)S(1)} %slice.4091), channel_id=1, source_target_pairs={{32,0},{64,32},{96,64},{33,1},{65,33},{97,65},{34,2},{66,34},{98,6... | collective-permute-start | bytes 221192 | tf_op jit(solution)/shard_map/ppermute | solution.py:28
  6.7 61.5 %collective-permute-start.2 = (f32[6,6,4,1,128]{4,2,0,1,3:T(4,128)S(1)}, f32[6,6,4,1,128]{4,2,0,1,3:T(4,128)S(1)}, u32[]{:S(2)}, u32[]{:S(2)}) collective-permute-start(f32[6,6,4,1,128]{4,2,0,1,3:T(4,128)S(1)} %slice.4095), channel_id=1, source_target_pairs={{0,1},{1,2},{2,3},{3,4},{4,5},{5,6},{6,7},{7,8},{8,9},{9,10},{10,1... | collective-permute-start | bytes 221192 | tf_op jit(solution)/shard_map/ppermute | solution.py:26
  8.6 60.5 %collective-permute-start.3 = (f32[6,6,4,1,128]{4,2,0,1,3:T(4,128)S(1)}, f32[6,6,4,1,128]{4,2,0,1,3:T(4,128)S(1)}, u32[]{:S(2)}, u32[]{:S(2)}) collective-permute-start(f32[6,6,4,1,128]{4,2,0,1,3:T(4,128)S(1)} %slice.4095), channel_id=1, source_target_pairs={{1,0},{2,1},{3,2},{4,3},{5,4},{6,5},{7,6},{8,7},{9,8},{10,9},{11,1... | collective-permute-start | bytes 221192 | tf_op jit(solution)/shard_map/ppermute | solution.py:28
  14.4 9.7 %collective-permute-start.24 = (f32[2,2,1,4,128]{4,1,3,0,2:T(2,128)S(1)}, f32[2,2,1,4,128]{4,1,3,0,2:T(2,128)S(1)}, u32[]{:S(2)}, u32[]{:S(2)}) collective-permute-start(f32[2,2,1,4,128]{4,1,3,0,2:T(2,128)S(1)} %slice.4174), channel_id=1, source_target_pairs={{0,32},{32,64},{64,96},{1,33},{33,65},{65,97},{2,34},{34,66},{66,9... | collective-permute-start | bytes 24584 | tf_op jit(solution)/shard_map/ppermute | solution.py:26
  24.1 5.5 collective-permute-start.25
  29.6 7.1 %collective-permute-start.26 = (f32[2,2,4,1,128]{4,2,0,1,3:T(4,128)S(1)}, f32[2,2,4,1,128]{4,2,0,1,3:T(4,128)S(1)}, u32[]{:S(2)}, u32[]{:S(2)}) collective-permute-start(f32[2,2,4,1,128]{4,2,0,1,3:T(4,128)S(1)} %slice.4177), channel_id=1, source_target_pairs={{0,1},{1,2},{2,3},{3,4},{4,5},{5,6},{6,7},{7,8},{8,9},{9,10},{10,1... | collective-permute-start | bytes 24584 | tf_op jit(solution)/shard_map/ppermute | solution.py:26
  36.7 3.3 collective-permute-start.27
  40.0 5.8 %collective-permute-start.12 = (f32[4,4,1,4,128]{4,1,3,0,2:T(4,128)S(1)}, f32[4,4,1,4,128]{4,1,3,0,2:T(4,128)S(1)}, u32[]{:S(2)}, u32[]{:S(2)}) collective-permute-start(f32[4,4,1,4,128]{4,1,3,0,2:T(4,128)S(1)} %slice.4134), channel_id=1, source_target_pairs={{0,32},{32,64},{64,96},{1,33},{33,65},{65,97},{2,34},{34,66},{66,9... | collective-permute-start | bytes 98312 | tf_op jit(solution)/shard_map/ppermute | solution.py:26
  45.8 5.8 %collective-permute-start.13 = (f32[4,4,1,4,128]{4,1,3,0,2:T(4,128)S(1)}, f32[4,4,1,4,128]{4,1,3,0,2:T(4,128)S(1)}, u32[]{:S(2)}, u32[]{:S(2)}) collective-permute-start(f32[4,4,1,4,128]{4,1,3,0,2:T(4,128)S(1)} %slice.4134), channel_id=1, source_target_pairs={{32,0},{64,32},{96,64},{33,1},{65,33},{97,65},{34,2},{66,34},{98,6... | collective-permute-start | bytes 98312 | tf_op jit(solution)/shard_map/ppermute | solution.py:28
  51.6 7.3 %collective-permute-start.14 = (f32[4,4,4,1,128]{4,2,0,1,3:T(4,128)S(1)}, f32[4,4,4,1,128]{4,2,0,1,3:T(4,128)S(1)}, u32[]{:S(2)}, u32[]{:S(2)}) collective-permute-start(f32[4,4,4,1,128]{4,2,0,1,3:T(4,128)S(1)} %slice.4137), channel_id=1, source_target_pairs={{0,1},{1,2},{2,3},{3,4},{4,5},{5,6},{6,7},{7,8},{8,9},{9,10},{10,1... | collective-permute-start | bytes 98312 | tf_op jit(solution)/shard_map/ppermute | solution.py:26
  58.9 3.5 collective-permute-start.15
  103.4 15.5 %collective-permute-start.4 = (f32[6,6,1,4,128]{4,3,2,0,1:T(4,128)S(1)}, f32[6,6,1,4,128]{4,3,2,0,1:T(4,128)S(1)}, u32[]{:S(2)}, u32[]{:S(2)}) collective-permute-start(f32[6,6,1,4,128]{4,3,2,0,1:T(4,128)S(1)} %copy-done.63), channel_id=1, source_target_pairs={{0,32},{32,64},{64,96},{1,33},{33,65},{65,97},{2,34},{34,66},{66,9... | collective-permute-start | bytes 221192 | tf_op jit(solution)/shard_map/ppermute | solution.py:26
  107.9 11.0 %collective-permute-start.5 = (f32[6,6,1,4,128]{4,3,0,1,2:T(4,128)S(1)}, f32[6,6,1,4,128]{4,3,0,1,2:T(4,128)S(1)}, u32[]{:S(2)}, u32[]{:S(2)}) collective-permute-start(f32[6,6,1,4,128]{4,3,0,1,2:T(4,128)S(1)} %slice.4764), channel_id=1, source_target_pairs={{32,0},{64,32},{96,64},{33,1},{65,33},{97,65},{34,2},{66,34},{98,6... | collective-permute-start | bytes 221192 | tf_op jit(solution)/shard_map/ppermute | solution.py:28
  110.6 8.6 %collective-permute-start.6 = (f32[6,6,4,1,128]{4,3,2,0,1:T(1,128)S(1)}, f32[6,6,4,1,128]{4,3,2,0,1:T(1,128)S(1)}, u32[]{:S(2)}, u32[]{:S(2)}) collective-permute-start(f32[6,6,4,1,128]{4,3,2,0,1:T(1,128)S(1)} %slice.4767), channel_id=1, source_target_pairs={{0,1},{1,2},{2,3},{3,4},{4,5},{5,6},{6,7},{7,8},{8,9},{9,10},{10,1... | collective-permute-start | bytes 221192 | tf_op jit(solution)/shard_map/ppermute | solution.py:26
  112.6 7.7 %collective-permute-start.7 = (f32[6,6,4,1,128]{4,2,0,1,3:T(4,128)S(1)}, f32[6,6,4,1,128]{4,2,0,1,3:T(4,128)S(1)}, u32[]{:S(2)}, u32[]{:S(2)}) collective-permute-start(f32[6,6,4,1,128]{4,2,0,1,3:T(4,128)S(1)} %slice.4772), channel_id=1, source_target_pairs={{1,0},{2,1},{3,2},{4,3},{5,4},{6,5},{7,6},{8,7},{9,8},{10,9},{11,1... | collective-permute-start | bytes 221192 | tf_op jit(solution)/shard_map/ppermute | solution.py:28
  150.7 15.7 %collective-permute-start.8 = (f32[6,6,1,4,128]{4,3,2,0,1:T(4,128)S(1)}, f32[6,6,1,4,128]{4,3,2,0,1:T(4,128)S(1)}, u32[]{:S(2)}, u32[]{:S(2)}) collective-permute-start(f32[6,6,1,4,128]{4,3,2,0,1:T(4,128)S(1)} %copy-done.64), channel_id=1, source_target_pairs={{0,32},{32,64},{64,96},{1,33},{33,65},{65,97},{2,34},{34,66},{66,9... | collective-permute-start | bytes 221192 | tf_op jit(solution)/shard_map/ppermute | solution.py:26
  155.7 10.8 %collective-permute-start.9 = (f32[6,6,1,4,128]{4,3,0,1,2:T(4,128)S(1)}, f32[6,6,1,4,128]{4,3,0,1,2:T(4,128)S(1)}, u32[]{:S(2)}, u32[]{:S(2)}) collective-permute-start(f32[6,6,1,4,128]{4,3,0,1,2:T(4,128)S(1)} %slice.4786), channel_id=1, source_target_pairs={{32,0},{64,32},{96,64},{33,1},{65,33},{97,65},{34,2},{66,34},{98,6... | collective-permute-start | bytes 221192 | tf_op jit(solution)/shard_map/ppermute | solution.py:28
  158.3 8.4 %collective-permute-start.10 = (f32[6,6,4,1,128]{4,3,2,0,1:T(1,128)S(1)}, f32[6,6,4,1,128]{4,3,2,0,1:T(1,128)S(1)}, u32[]{:S(2)}, u32[]{:S(2)}) collective-permute-start(f32[6,6,4,1,128]{4,3,2,0,1:T(1,128)S(1)} %slice.4789), channel_id=1, source_target_pairs={{0,1},{1,2},{2,3},{3,4},{4,5},{5,6},{6,7},{7,8},{8,9},{9,10},{10,1... | collective-permute-start | bytes 221192 | tf_op jit(solution)/shard_map/ppermute | solution.py:26
  160.4 7.7 %collective-permute-start.11 = (f32[6,6,4,1,128]{4,2,0,1,3:T(4,128)S(1)}, f32[6,6,4,1,128]{4,2,0,1,3:T(4,128)S(1)}, u32[]{:S(2)}, u32[]{:S(2)}) collective-permute-start(f32[6,6,4,1,128]{4,2,0,1,3:T(4,128)S(1)} %slice.4794), channel_id=1, source_target_pairs={{1,0},{2,1},{3,2},{4,3},{5,4},{6,5},{7,6},{8,7},{9,8},{10,9},{11,1... | collective-permute-start | bytes 221192 | tf_op jit(solution)/shard_map/ppermute | solution.py:28
  189.3 15.8 %collective-permute-start.16 = (f32[4,4,1,4,128]{4,3,0,1,2:T(4,128)}, f32[4,4,1,4,128]{4,3,0,1,2:T(4,128)S(1)}, u32[]{:S(2)}, u32[]{:S(2)}) collective-permute-start(f32[4,4,1,4,128]{4,3,0,1,2:T(4,128)} %slice_bitcast_fusion.87), channel_id=1, source_target_pairs={{0,32},{32,64},{64,96},{1,33},{33,65},{65,97},{2,34},{34,66},{66,9... | collective-permute-start | bytes 98312 | tf_op jit(solution)/shard_map/ppermute | solution.py:26
  194.5 10.7 %collective-permute-start.17 = (f32[4,4,1,4,128]{4,3,2,0,1:T(4,128)S(1)}, f32[4,4,1,4,128]{4,3,2,0,1:T(4,128)S(1)}, u32[]{:S(2)}, u32[]{:S(2)}) collective-permute-start(f32[4,4,1,4,128]{4,3,2,0,1:T(4,128)S(1)} %slice.4814), channel_id=1, source_target_pairs={{32,0},{64,32},{96,64},{33,1},{65,33},{97,65},{34,2},{66,34},{98,6... | collective-permute-start | bytes 98312 | tf_op jit(solution)/shard_map/ppermute | solution.py:28
  197.3 8.1 %collective-permute-start.18 = (f32[4,4,4,1,128]{4,2,0,1,3:T(4,128)S(1)}, f32[4,4,4,1,128]{4,2,0,1,3:T(4,128)S(1)}, u32[]{:S(2)}, u32[]{:S(2)}) collective-permute-start(f32[4,4,4,1,128]{4,2,0,1,3:T(4,128)S(1)} %bitcast.907), channel_id=1, source_target_pairs={{0,1},{1,2},{2,3},{3,4},{4,5},{5,6},{6,7},{7,8},{8,9},{9,10},{10,1... | collective-permute-start | bytes 98312 | tf_op jit(solution)/shard_map/ppermute | solution.py:26
  199.2 7.3 %collective-permute-start.19 = (f32[4,4,4,1,128]{4,3,2,0,1:T(1,128)S(1)}, f32[4,4,4,1,128]{4,3,2,0,1:T(1,128)S(1)}, u32[]{:S(2)}, u32[]{:S(2)}) collective-permute-start(f32[4,4,4,1,128]{4,3,2,0,1:T(1,128)S(1)} %slice.4822), channel_id=1, source_target_pairs={{1,0},{2,1},{3,2},{4,3},{5,4},{6,5},{7,6},{8,7},{9,8},{10,9},{11,1... | collective-permute-start | bytes 98312 | tf_op jit(solution)/shard_map/ppermute | solution.py:28
  218.3 14.0 %collective-permute-start.20 = (f32[4,4,1,4,128]{4,3,2,0,1:T(4,128)S(1)}, f32[4,4,1,4,128]{4,3,2,0,1:T(4,128)S(1)}, u32[]{:S(2)}, u32[]{:S(2)}) collective-permute-start(f32[4,4,1,4,128]{4,3,2,0,1:T(4,128)S(1)} %slice.4831), channel_id=1, source_target_pairs={{0,32},{32,64},{64,96},{1,33},{33,65},{65,97},{2,34},{34,66},{66,9... | collective-permute-start | bytes 98312 | tf_op jit(solution)/shard_map/ppermute | solution.py:26
  221.7 10.8 %collective-permute-start.21 = (f32[4,4,1,4,128]{4,3,2,0,1:T(4,128)S(1)}, f32[4,4,1,4,128]{4,3,2,0,1:T(4,128)S(1)}, u32[]{:S(2)}, u32[]{:S(2)}) collective-permute-start(f32[4,4,1,4,128]{4,3,2,0,1:T(4,128)S(1)} %slice.4836), channel_id=1, source_target_pairs={{32,0},{64,32},{96,64},{33,1},{65,33},{97,65},{34,2},{66,34},{98,6... | collective-permute-start | bytes 98312 | tf_op jit(solution)/shard_map/ppermute | solution.py:28
  224.3 8.2 %collective-permute-start.22 = (f32[4,4,4,1,128]{4,2,0,1,3:T(4,128)S(1)}, f32[4,4,4,1,128]{4,2,0,1,3:T(4,128)S(1)}, u32[]{:S(2)}, u32[]{:S(2)}) collective-permute-start(f32[4,4,4,1,128]{4,2,0,1,3:T(4,128)S(1)} %bitcast.906), channel_id=1, source_target_pairs={{0,1},{1,2},{2,3},{3,4},{4,5},{5,6},{6,7},{7,8},{8,9},{9,10},{10,1... | collective-permute-start | bytes 98312 | tf_op jit(solution)/shard_map/ppermute | solution.py:26
  226.3 7.3 %collective-permute-start.23 = (f32[4,4,4,1,128]{4,3,2,0,1:T(1,128)S(1)}, f32[4,4,4,1,128]{4,3,2,0,1:T(1,128)S(1)}, u32[]{:S(2)}, u32[]{:S(2)}) collective-permute-start(f32[4,4,4,1,128]{4,3,2,0,1:T(1,128)S(1)} %slice.4844), channel_id=1, source_target_pairs={{1,0},{2,1},{3,2},{4,3},{5,4},{6,5},{7,6},{8,7},{9,8},{10,9},{11,1... | collective-permute-start | bytes 98312 | tf_op jit(solution)/shard_map/ppermute | solution.py:28
  247.1 16.0 %collective-permute-start.28 = (f32[2,2,1,4,128]{4,3,2,0,1:T(4,128)}, f32[2,2,1,4,128]{4,3,2,0,1:T(4,128)S(1)}, u32[]{:S(2)}, u32[]{:S(2)}) collective-permute-start(f32[2,2,1,4,128]{4,3,2,0,1:T(4,128)} %slice.4859), channel_id=1, source_target_pairs={{0,32},{32,64},{64,96},{1,33},{33,65},{65,97},{2,34},{34,66},{66,9... | collective-permute-start | bytes 24584 | tf_op jit(solution)/shard_map/ppermute | solution.py:26
  251.1 12.8 %collective-permute-start.29 = (f32[2,2,1,4,128]{4,3,0,1,2:T(4,128)S(1)}, f32[2,2,1,4,128]{4,3,0,1,2:T(4,128)S(1)}, u32[]{:S(2)}, u32[]{:S(2)}) collective-permute-start(f32[2,2,1,4,128]{4,3,0,1,2:T(4,128)S(1)} %slice.4864), channel_id=1, source_target_pairs={{32,0},{64,32},{96,64},{33,1},{65,33},{97,65},{34,2},{66,34},{98,6... | collective-permute-start | bytes 24584 | tf_op jit(solution)/shard_map/ppermute | solution.py:28
  253.7 10.2 %collective-permute-start.30 = (f32[2,2,4,1,128]{4,3,2,0,1:T(1,128)}, f32[2,2,4,1,128]{4,3,2,0,1:T(1,128)S(1)}, u32[]{:S(2)}, u32[]{:S(2)}) collective-permute-start(f32[2,2,4,1,128]{4,3,2,0,1:T(1,128)} %slice.4867), channel_id=1, source_target_pairs={{0,1},{1,2},{2,3},{3,4},{4,5},{5,6},{6,7},{7,8},{8,9},{9,10},{10,1... | collective-permute-start | bytes 24584 | tf_op jit(solution)/shard_map/ppermute | solution.py:26
  256.4 7.5 %collective-permute-start.31 = (f32[2,2,4,1,128]{4,2,0,1,3:T(4,128)S(1)}, f32[2,2,4,1,128]{4,2,0,1,3:T(4,128)S(1)}, u32[]{:S(2)}, u32[]{:S(2)}) collective-permute-start(f32[2,2,4,1,128]{4,2,0,1,3:T(4,128)S(1)} %slice.4872), channel_id=1, source_target_pairs={{1,0},{2,1},{3,2},{4,3},{5,4},{6,5},{7,6},{8,7},{9,8},{10,9},{11,1... | collective-permute-start | bytes 24584 | tf_op jit(solution)/shard_map/ppermute | solution.py:28
  276.0 16.0 %collective-permute-start.32 = (f32[2,2,1,4,128]{4,3,2,0,1:T(4,128)}, f32[2,2,1,4,128]{4,3,2,0,1:T(4,128)S(1)}, u32[]{:S(2)}, u32[]{:S(2)}) collective-permute-start(f32[2,2,1,4,128]{4,3,2,0,1:T(4,128)} %slice.4881), channel_id=1, source_target_pairs={{0,32},{32,64},{64,96},{1,33},{33,65},{65,97},{2,34},{34,66},{66,9... | collective-permute-start | bytes 24584 | tf_op jit(solution)/shard_map/ppermute | solution.py:26
  280.0 12.8 %collective-permute-start.33 = (f32[2,2,1,4,128]{4,3,0,1,2:T(4,128)S(1)}, f32[2,2,1,4,128]{4,3,0,1,2:T(4,128)S(1)}, u32[]{:S(2)}, u32[]{:S(2)}) collective-permute-start(f32[2,2,1,4,128]{4,3,0,1,2:T(4,128)S(1)} %slice.4886), channel_id=1, source_target_pairs={{32,0},{64,32},{96,64},{33,1},{65,33},{97,65},{34,2},{66,34},{98,6... | collective-permute-start | bytes 24584 | tf_op jit(solution)/shard_map/ppermute | solution.py:28
  282.7 10.2 %collective-permute-start.34 = (f32[2,2,4,1,128]{4,3,2,0,1:T(1,128)}, f32[2,2,4,1,128]{4,3,2,0,1:T(1,128)S(1)}, u32[]{:S(2)}, u32[]{:S(2)}) collective-permute-start(f32[2,2,4,1,128]{4,3,2,0,1:T(1,128)} %slice.4889), channel_id=1, source_target_pairs={{0,1},{1,2},{2,3},{3,4},{4,5},{5,6},{6,7},{7,8},{8,9},{9,10},{10,1... | collective-permute-start | bytes 24584 | tf_op jit(solution)/shard_map/ppermute | solution.py:26
  285.4 8.3 %collective-permute-start.35 = (f32[2,2,4,1,128]{4,2,0,1,3:T(4,128)S(1)}, f32[2,2,4,1,128]{4,2,0,1,3:T(4,128)S(1)}, u32[]{:S(2)}, u32[]{:S(2)}) collective-permute-start(f32[2,2,4,1,128]{4,2,0,1,3:T(4,128)S(1)} %slice.4894), channel_id=1, source_target_pairs={{1,0},{2,1},{3,2},{4,3},{5,4},{6,5},{7,6},{8,7},{9,8},{10,9},{11,1... | collective-permute-start | bytes 24584 | tf_op jit(solution)/shard_map/ppermute | solution.py:28
  302.2 17.4 %collective-permute-start.36 = (f32[2,2,1,4,128]{4,3,2,1,0:T(4,128)S(1)}, f32[2,2,1,4,128]{4,3,2,1,0:T(4,128)S(1)}, u32[]{:S(2)}, u32[]{:S(2)}) collective-permute-start(f32[2,2,1,4,128]{4,3,2,1,0:T(4,128)S(1)} %slice.4903), channel_id=1, source_target_pairs={{0,32},{32,64},{64,96},{1,33},{33,65},{65,97},{2,34},{34,66},{66,9... | collective-permute-start | bytes 24584 | tf_op jit(solution)/shard_map/ppermute | solution.py:26
  309.2 10.3 %collective-permute-start.37 = (f32[2,2,1,4,128]{4,3,1,0,2:T(4,128)S(1)}, f32[2,2,1,4,128]{4,3,1,0,2:T(4,128)S(1)}, u32[]{:S(2)}, u32[]{:S(2)}) collective-permute-start(f32[2,2,1,4,128]{4,3,1,0,2:T(4,128)S(1)} %slice.4908), channel_id=1, source_target_pairs={{32,0},{64,32},{96,64},{33,1},{65,33},{97,65},{34,2},{66,34},{98,6... | collective-permute-start | bytes 24584 | tf_op jit(solution)/shard_map/ppermute | solution.py:28
  311.9 7.8 %collective-permute-start.38 = (f32[2,2,4,1,128]{4,2,0,1,3:T(4,128)S(1)}, f32[2,2,4,1,128]{4,2,0,1,3:T(4,128)S(1)}, u32[]{:S(2)}, u32[]{:S(2)}) collective-permute-start(f32[2,2,4,1,128]{4,2,0,1,3:T(4,128)S(1)} %bitcast.931), channel_id=1, source_target_pairs={{0,1},{1,2},{2,3},{3,4},{4,5},{5,6},{6,7},{7,8},{8,9},{9,10},{10,1... | collective-permute-start | bytes 24584 | tf_op jit(solution)/shard_map/ppermute | solution.py:26
  313.8 7.1 %collective-permute-start.39 = (f32[2,2,4,1,128]{4,3,2,0,1:T(1,128)S(1)}, f32[2,2,4,1,128]{4,3,2,0,1:T(1,128)S(1)}, u32[]{:S(2)}, u32[]{:S(2)}) collective-permute-start(f32[2,2,4,1,128]{4,3,2,0,1:T(1,128)S(1)} %slice.4916), channel_id=1, source_target_pairs={{1,0},{2,1},{3,2},{4,3},{5,4},{6,5},{7,6},{8,7},{9,8},{10,9},{11,1... | collective-permute-start | bytes 24584 | tf_op jit(solution)/shard_map/ppermute | solution.py:28
  332.9 17.4 %collective-permute-start.40 = (f32[2,2,1,4,128]{4,3,2,1,0:T(4,128)S(1)}, f32[2,2,1,4,128]{4,3,2,1,0:T(4,128)S(1)}, u32[]{:S(2)}, u32[]{:S(2)}) collective-permute-start(f32[2,2,1,4,128]{4,3,2,1,0:T(4,128)S(1)} %slice.4925), channel_id=1, source_target_pairs={{0,32},{32,64},{64,96},{1,33},{33,65},{65,97},{2,34},{34,66},{66,9... | collective-permute-start | bytes 24584 | tf_op jit(solution)/shard_map/ppermute | solution.py:26
  339.2 11.2 %collective-permute-start.41 = (f32[2,2,1,4,128]{4,3,1,0,2:T(4,128)S(1)}, f32[2,2,1,4,128]{4,3,1,0,2:T(4,128)S(1)}, u32[]{:S(2)}, u32[]{:S(2)}) collective-permute-start(f32[2,2,1,4,128]{4,3,1,0,2:T(4,128)S(1)} %slice.4930), channel_id=1, source_target_pairs={{32,0},{64,32},{96,64},{33,1},{65,33},{97,65},{34,2},{66,34},{98,6... | collective-permute-start | bytes 24584 | tf_op jit(solution)/shard_map/ppermute | solution.py:28
  341.8 9.4 %collective-permute-start.42 = (f32[2,2,4,1,128]{4,3,2,0,1:T(1,128)S(1)}, f32[2,2,4,1,128]{4,3,2,0,1:T(1,128)S(1)}, u32[]{:S(2)}, u32[]{:S(2)}) collective-permute-start(f32[2,2,4,1,128]{4,3,2,0,1:T(1,128)S(1)} %slice.4933), channel_id=1, source_target_pairs={{0,1},{1,2},{2,3},{3,4},{4,5},{5,6},{6,7},{7,8},{8,9},{9,10},{10,1... | collective-permute-start | bytes 24584 | tf_op jit(solution)/shard_map/ppermute | solution.py:26
  343.7 8.2 %collective-permute-start.43 = (f32[2,2,4,1,128]{4,3,2,0,1:T(1,128)S(1)}, f32[2,2,4,1,128]{4,3,2,0,1:T(1,128)S(1)}, u32[]{:S(2)}, u32[]{:S(2)}) collective-permute-start(f32[2,2,4,1,128]{4,3,2,0,1:T(1,128)S(1)} %slice.4938), channel_id=1, source_target_pairs={{1,0},{2,1},{3,2},{4,3},{5,4},{6,5},{7,6},{8,7},{9,8},{10,9},{11,1... | collective-permute-start | bytes 24584 | tf_op jit(solution)/shard_map/ppermute | solution.py:28
  362.9 16.0 %collective-permute-start.44 = (f32[2,2,1,4,128]{4,3,2,1,0:T(4,128)}, f32[2,2,1,4,128]{4,3,2,1,0:T(4,128)S(1)}, u32[]{:S(2)}, u32[]{:S(2)}) collective-permute-start(f32[2,2,1,4,128]{4,3,2,1,0:T(4,128)} %slice.4947), channel_id=1, source_target_pairs={{0,32},{32,64},{64,96},{1,33},{33,65},{65,97},{2,34},{34,66},{66,9... | collective-permute-start | bytes 24584 | tf_op jit(solution)/shard_map/ppermute | solution.py:26
  367.7 11.9 %collective-permute-start.45 = (f32[2,2,1,4,128]{4,3,1,0,2:T(4,128)S(1)}, f32[2,2,1,4,128]{4,3,1,0,2:T(4,128)S(1)}, u32[]{:S(2)}, u32[]{:S(2)}) collective-permute-start(f32[2,2,1,4,128]{4,3,1,0,2:T(4,128)S(1)} %slice.4952), channel_id=1, source_target_pairs={{32,0},{64,32},{96,64},{33,1},{65,33},{97,65},{34,2},{66,34},{98,6... | collective-permute-start | bytes 24584 | tf_op jit(solution)/shard_map/ppermute | solution.py:28
  370.4 9.4 %collective-permute-start.46 = (f32[2,2,4,1,128]{4,3,2,0,1:T(1,128)S(1)}, f32[2,2,4,1,128]{4,3,2,0,1:T(1,128)S(1)}, u32[]{:S(2)}, u32[]{:S(2)}) collective-permute-start(f32[2,2,4,1,128]{4,3,2,0,1:T(1,128)S(1)} %slice.4955), channel_id=1, source_target_pairs={{0,1},{1,2},{2,3},{3,4},{4,5},{5,6},{6,7},{7,8},{8,9},{9,10},{10,1... | collective-permute-start | bytes 24584 | tf_op jit(solution)/shard_map/ppermute | solution.py:26
  372.3 7.5 %collective-permute-start.47 = (f32[2,2,4,1,128]{4,2,0,1,3:T(4,128)S(1)}, f32[2,2,4,1,128]{4,2,0,1,3:T(4,128)S(1)}, u32[]{:S(2)}, u32[]{:S(2)}) collective-permute-start(f32[2,2,4,1,128]{4,2,0,1,3:T(4,128)S(1)} %slice.4960), channel_id=1, source_target_pairs={{1,0},{2,1},{3,2},{4,3},{5,4},{6,5},{7,6},{8,7},{9,8},{10,9},{11,1... | collective-permute-start | bytes 24584 | tf_op jit(solution)/shard_map/ppermute | solution.py:28
  394.4 13.9 %collective-permute-start.48 = (f32[4,4,1,4,128]{4,3,2,0,1:T(4,128)S(1)}, f32[4,4,1,4,128]{4,3,2,0,1:T(4,128)S(1)}, u32[]{:S(2)}, u32[]{:S(2)}) collective-permute-start(f32[4,4,1,4,128]{4,3,2,0,1:T(4,128)S(1)} %slice.4969), channel_id=1, source_target_pairs={{0,32},{32,64},{64,96},{1,33},{33,65},{65,97},{2,34},{34,66},{66,9... | collective-permute-start | bytes 98312 | tf_op jit(solution)/shard_map/ppermute | solution.py:26
  397.8 10.6 %collective-permute-start.49 = (f32[4,4,1,4,128]{4,3,0,1,2:T(4,128)S(1)}, f32[4,4,1,4,128]{4,3,0,1,2:T(4,128)S(1)}, u32[]{:S(2)}, u32[]{:S(2)}) collective-permute-start(f32[4,4,1,4,128]{4,3,0,1,2:T(4,128)S(1)} %slice.4974), channel_id=1, source_target_pairs={{32,0},{64,32},{96,64},{33,1},{65,33},{97,65},{34,2},{66,34},{98,6... | collective-permute-start | bytes 98312 | tf_op jit(solution)/shard_map/ppermute | solution.py:28
  400.4 8.2 %collective-permute-start.50 = (f32[4,4,4,1,128]{4,3,2,0,1:T(1,128)S(1)}, f32[4,4,4,1,128]{4,3,2,0,1:T(1,128)S(1)}, u32[]{:S(2)}, u32[]{:S(2)}) collective-permute-start(f32[4,4,4,1,128]{4,3,2,0,1:T(1,128)S(1)} %slice.4977), channel_id=1, source_target_pairs={{0,1},{1,2},{2,3},{3,4},{4,5},{5,6},{6,7},{7,8},{8,9},{9,10},{10,1... | collective-permute-start | bytes 98312 | tf_op jit(solution)/shard_map/ppermute | solution.py:26
  402.4 7.3 %collective-permute-start.51 = (f32[4,4,4,1,128]{4,2,0,1,3:T(4,128)S(1)}, f32[4,4,4,1,128]{4,2,0,1,3:T(4,128)S(1)}, u32[]{:S(2)}, u32[]{:S(2)}) collective-permute-start(f32[4,4,4,1,128]{4,2,0,1,3:T(4,128)S(1)} %slice.4982), channel_id=1, source_target_pairs={{1,0},{2,1},{3,2},{4,3},{5,4},{6,5},{7,6},{8,7},{9,8},{10,9},{11,1... | collective-permute-start | bytes 98312 | tf_op jit(solution)/shard_map/ppermute | solution.py:28
  420.8 13.9 %collective-permute-start.52 = (f32[4,4,1,4,128]{4,3,2,0,1:T(4,128)S(1)}, f32[4,4,1,4,128]{4,3,2,0,1:T(4,128)S(1)}, u32[]{:S(2)}, u32[]{:S(2)}) collective-permute-start(f32[4,4,1,4,128]{4,3,2,0,1:T(4,128)S(1)} %slice.4991), channel_id=1, source_target_pairs={{0,32},{32,64},{64,96},{1,33},{33,65},{65,97},{2,34},{34,66},{66,9... | collective-permute-start | bytes 98312 | tf_op jit(solution)/shard_map/ppermute | solution.py:26
  424.2 10.6 %collective-permute-start.53 = (f32[4,4,1,4,128]{4,3,0,1,2:T(4,128)S(1)}, f32[4,4,1,4,128]{4,3,0,1,2:T(4,128)S(1)}, u32[]{:S(2)}, u32[]{:S(2)}) collective-permute-start(f32[4,4,1,4,128]{4,3,0,1,2:T(4,128)S(1)} %slice.4996), channel_id=1, source_target_pairs={{32,0},{64,32},{96,64},{33,1},{65,33},{97,65},{34,2},{66,34},{98,6... | collective-permute-start | bytes 98312 | tf_op jit(solution)/shard_map/ppermute | solution.py:28
  426.8 8.1 %collective-permute-start.54 = (f32[4,4,4,1,128]{4,3,2,0,1:T(1,128)S(1)}, f32[4,4,4,1,128]{4,3,2,0,1:T(1,128)S(1)}, u32[]{:S(2)}, u32[]{:S(2)}) collective-permute-start(f32[4,4,4,1,128]{4,3,2,0,1:T(1,128)S(1)} %slice.4999), channel_id=1, source_target_pairs={{0,1},{1,2},{2,3},{3,4},{4,5},{5,6},{6,7},{7,8},{8,9},{9,10},{10,1... | collective-permute-start | bytes 98312 | tf_op jit(solution)/shard_map/ppermute | solution.py:26
  429.1 7.1 %collective-permute-start.55 = (f32[4,4,4,1,128]{4,2,0,1,3:T(4,128)S(1)}, f32[4,4,4,1,128]{4,2,0,1,3:T(4,128)S(1)}, u32[]{:S(2)}, u32[]{:S(2)}) collective-permute-start(f32[4,4,4,1,128]{4,2,0,1,3:T(4,128)S(1)} %slice.5004), channel_id=1, source_target_pairs={{1,0},{2,1},{3,2},{4,3},{5,4},{6,5},{7,6},{8,7},{9,8},{10,9},{11,1... | collective-permute-start | bytes 98312 | tf_op jit(solution)/shard_map/ppermute | solution.py:28
  464.6 15.6 %collective-permute-start.56 = (f32[6,6,1,4,128]{4,3,2,0,1:T(4,128)S(1)}, f32[6,6,1,4,128]{4,3,2,0,1:T(4,128)S(1)}, u32[]{:S(2)}, u32[]{:S(2)}) collective-permute-start(f32[6,6,1,4,128]{4,3,2,0,1:T(4,128)S(1)} %slice.5013), channel_id=1, source_target_pairs={{0,32},{32,64},{64,96},{1,33},{33,65},{65,97},{2,34},{34,66},{66,9... | collective-permute-start | bytes 221192 | tf_op jit(solution)/shard_map/ppermute | solution.py:26
  469.2 11.2 %collective-permute-start.57 = (f32[6,6,1,4,128]{4,3,0,1,2:T(4,128)S(1)}, f32[6,6,1,4,128]{4,3,0,1,2:T(4,128)S(1)}, u32[]{:S(2)}, u32[]{:S(2)}) collective-permute-start(f32[6,6,1,4,128]{4,3,0,1,2:T(4,128)S(1)} %slice.5018), channel_id=1, source_target_pairs={{32,0},{64,32},{96,64},{33,1},{65,33},{97,65},{34,2},{66,34},{98,6... | collective-permute-start | bytes 221192 | tf_op jit(solution)/shard_map/ppermute | solution.py:28
  471.8 8.8 %collective-permute-start.58 = (f32[6,6,4,1,128]{4,3,2,0,1:T(1,128)S(1)}, f32[6,6,4,1,128]{4,3,2,0,1:T(1,128)S(1)}, u32[]{:S(2)}, u32[]{:S(2)}) collective-permute-start(f32[6,6,4,1,128]{4,3,2,0,1:T(1,128)S(1)} %slice.5021), channel_id=1, source_target_pairs={{0,1},{1,2},{2,3},{3,4},{4,5},{5,6},{6,7},{7,8},{8,9},{9,10},{10,1... | collective-permute-start | bytes 221192 | tf_op jit(solution)/shard_map/ppermute | solution.py:26
  473.9 7.7 %collective-permute-start.59 = (f32[6,6,4,1,128]{4,2,0,1,3:T(4,128)S(1)}, f32[6,6,4,1,128]{4,2,0,1,3:T(4,128)S(1)}, u32[]{:S(2)}, u32[]{:S(2)}) collective-permute-start(f32[6,6,4,1,128]{4,2,0,1,3:T(4,128)S(1)} %slice.5026), channel_id=1, source_target_pairs={{1,0},{2,1},{3,2},{4,3},{5,4},{6,5},{7,6},{8,7},{9,8},{10,9},{11,1... | collective-permute-start | bytes 221192 | tf_op jit(solution)/shard_map/ppermute | solution.py:28
  512.5 15.4 %collective-permute-start.60 = (f32[6,6,1,4,128]{4,3,2,0,1:T(4,128)}, f32[6,6,1,4,128]{4,3,2,0,1:T(4,128)S(1)}, u32[]{:S(2)}, u32[]{:S(2)}) collective-permute-start(f32[6,6,1,4,128]{4,3,2,0,1:T(4,128)} %slice.5035), channel_id=1, source_target_pairs={{0,32},{32,64},{64,96},{1,33},{33,65},{65,97},{2,34},{34,66},{66,9... | collective-permute-start | bytes 221192 | tf_op jit(solution)/shard_map/ppermute | solution.py:26
  517.3 10.8 %collective-permute-start.61 = (f32[6,6,1,4,128]{4,3,0,1,2:T(4,128)S(1)}, f32[6,6,1,4,128]{4,3,0,1,2:T(4,128)S(1)}, u32[]{:S(2)}, u32[]{:S(2)}) collective-permute-start(f32[6,6,1,4,128]{4,3,0,1,2:T(4,128)S(1)} %slice.5040), channel_id=1, source_target_pairs={{32,0},{64,32},{96,64},{33,1},{65,33},{97,65},{34,2},{66,34},{98,6... | collective-permute-start | bytes 221192 | tf_op jit(solution)/shard_map/ppermute | solution.py:28
  519.9 8.4 %collective-permute-start.62 = (f32[6,6,4,1,128]{4,3,2,0,1:T(1,128)S(1)}, f32[6,6,4,1,128]{4,3,2,0,1:T(1,128)S(1)}, u32[]{:S(2)}, u32[]{:S(2)}) collective-permute-start(f32[6,6,4,1,128]{4,3,2,0,1:T(1,128)S(1)} %slice.5043), channel_id=1, source_target_pairs={{0,1},{1,2},{2,3},{3,4},{4,5},{5,6},{6,7},{7,8},{8,9},{9,10},{10,1... | collective-permute-start | bytes 221192 | tf_op jit(solution)/shard_map/ppermute | solution.py:26
  522.0 7.7 %collective-permute-start.63 = (f32[6,6,4,1,128]{4,2,0,1,3:T(4,128)S(1)}, f32[6,6,4,1,128]{4,2,0,1,3:T(4,128)S(1)}, u32[]{:S(2)}, u32[]{:S(2)}) collective-permute-start(f32[6,6,4,1,128]{4,2,0,1,3:T(4,128)S(1)} %slice.5048), channel_id=1, source_target_pairs={{1,0},{2,1},{3,2},{4,3},{5,4},{6,5},{7,6},{8,7},{9,8},{10,9},{11,1... | collective-permute-start | bytes 221192 | tf_op jit(solution)/shard_map/ppermute | solution.py:28
  (69 other events, 1389.4 us)
where the time goes:
time: 571 us; the launch traced here: 561 us
  starting transfers between devices  209 us (37%)
  local copies, waits for them, and re-layouts  167 us (29%)
  other arithmetic  97.3 us (17%)
  matrix products  54.6 us (10%)
  waiting for transfers between devices  29.2 us (5%)
    ppermute x32, starting transfers between devices, with_halo(): lax.ppermute(head, axis, [((i + 1) % count, i) for i in range(ends)])  126 us
    ppermute x32, starting transfers between devices, with_halo(): lax.ppermute(tail, axis, [(i, (i + 1) % count) for i in range(ends)])  83.6 us
    dot_general x20, matrix products, transpose_apply(): result = jnp.einsum('ji,jm->im', matrix, flattened, precision=precise)  47.9 us
    reshape x20, local copies, waits for them, and re-layouts, transpose_apply(): return result.reshape((matrix.shape[1],) + values.shape[1:])  44.1 us
    reshape x10, local copies, waits for them, and re-layouts, transpose_apply(): flattened = values.reshape((values.shape[0], -1))  25.1 us
    scatter-add x47, other arithmetic, assemble(): result.at[lower_spot]  17.8 us
    ppermute x32, waiting for transfers between devices, with_halo(): lax.ppermute(head, axis, [((i + 1) % count, i) for i in range(ends)])  16.9 us
    reshape x11, local copies, waits for them, and re-layouts, assemble(): return result.reshape(values.shape)  15.2 us
  transfers between devices with their start and end apart: 64, of which 16 were waited for; matrix products, arithmetic and copies ran while one was open for 8% of the time, Pallas kernels for 0%

commit v1 on v0

v1 whole, which is shorter than its diff:
```python
import numpy as np
import jax
import jax.numpy as jnp
from jax import lax
from jax.sharding import PartitionSpec as P
from jax.experimental import pallas as pl
from jax.experimental.pallas import tpu as pltpu

NF = 6
QF = 216
SF = 240
QM = 64
QC = 8
COLS = 16
LANES = COLS * 128
F32 = jnp.float32
BF16 = jnp.bfloat16


def fine_slots():
    slots = []
    for i in range(6):
        slots += [(i, 0, k) for k in range(6)] + [None] * 2
        slots += [(i, 5, k) for k in range(6)] + [None] * 2
        slots += [(i, j, 0) for j in range(1, 5)] + [(i, j, 5) for j in range(1, 5)]
        slots += [(i, j, k) for j in range(1, 5) for k in range(1, 5)]
    return slots


def slot_matrix():
    to_slot = np.zeros((SF, QF), np.float32)
    for slot, node in enumerate(fine_slots()):
        if node is not None:
            to_slot[slot, (node[0] * 6 + node[1]) * 6 + node[2]] = 1.0
    return to_slot


def call(kernel, outs, scratch=(), smem=()):
    def run(*operands):
        specs = [
            pl.BlockSpec(memory_space=pltpu.SMEM if n in smem else pltpu.VMEM)
            for n in range(len(operands))
        ]
        return pl.pallas_call(
            kernel,
            out_shape=tuple(jax.ShapeDtypeStruct(s, d) for s, d in outs),
            in_specs=specs,
            out_specs=tuple(pl.BlockSpec(memory_space=pltpu.VMEM) for _ in outs),
            scratch_shapes=list(scratch),
            compiler_params=pltpu.CompilerParams(vmem_limit_bytes=32 * 1024 * 1024),
        )(*operands)

    return run


def dot(a, b):
    return lax.dot_general(a, b, (((1,), (0,)), ((), ())), preferred_element_type=F32)


def dot_nt(a, b):
    return lax.dot_general(a, b, (((1,), (1,)), ((), ())), preferred_element_type=F32)


def halves(values):
    high = values.astype(BF16)
    return high, (values - high.astype(F32)).astype(BF16)


def lane_roll(values, shift):
    return jnp.concatenate(
        [
            pltpu.roll(values[:, c * 128 : (c + 1) * 128], shift % 128, 1)
            for c in range(values.shape[1] // 128)
        ],
        axis=1,
    )


def sub_roll(values, shift):
    return pltpu.roll(values, shift % values.shape[0], 0)


def sublane(shape):
    return lax.broadcasted_iota(jnp.int32, shape, 0)


def x_from_lower(edge, values):
    return jnp.concatenate([edge, values[:, :1536]], axis=1)


def x_from_upper(values, edge):
    return jnp.concatenate([values[:, 512:], edge], axis=1)


def y_from_lower(edge, values):
    parts = []
    for x in range(4):
        parts += [edge[:, x * 128 : x * 128 + 128], values[:, x * 512 : x * 512 + 384]]
    return jnp.concatenate(parts, axis=1)


def y_from_upper(values, edge):
    parts = []
    for x in range(4):
        parts += [values[:, x * 512 + 128 : x * 512 + 512], edge[:, x * 128 : x * 128 + 128]]
    return jnp.concatenate(parts, axis=1)


def y_column(values, y):
    return jnp.concatenate(
        [values[:, x * 512 + y * 128 : x * 512 + y * 128 + 128] for x in range(4)], axis=1
    )


def even(idx_ref, axis):
    return idx_ref[axis] % 2 == 0


def prep_kernel(to_slot, fine, smooth, noise, mid, pmid, plow, kf, sf, nf, pmt, pm, km, plt):
    slot = to_slot[...]

    def eye(n, width=None):
        shape = (n, width or n)
        row = lax.broadcasted_iota(jnp.int32, shape, 0)
        col = lax.broadcasted_iota(jnp.int32, shape, 1)
        return row, col

    def one_hot(n):
        row, col = eye(n)
        return jnp.where(row == col, 1.0, 0.0).astype(BF16)

    def wide(out, rows, high, low):
        gap = jnp.zeros((rows, 16), BF16)
        out[:, 0:256] = jnp.concatenate([high, gap], axis=1)
        out[:, 256:512] = jnp.concatenate([high, gap], axis=1)
        out[:, 512:768] = jnp.concatenate([low, gap], axis=1)

    def narrow(out, high, low):
        row, col = eye(64, 128)
        twice = jnp.where((row == col) | (row == col - 64), 1.0, 0.0).astype(BF16)
        once = jnp.where(row == col, 1.0, 0.0).astype(BF16)
        out[:, 0:128] = dot(high, twice).astype(BF16)
        out[:, 128:256] = dot(low, once).astype(BF16)

    for source, out in ((fine, kf), (smooth, sf)):
        parts = [
            dot_nt(dot_nt(slot, part).astype(BF16), slot).astype(BF16)
            for part in halves(source[...])
        ]
        wide(out, SF, *parts)
    turn = one_hot(QF)
    wide(
        nf,
        QF,
        *[
            dot_nt(dot_nt(turn, part).astype(BF16), slot).astype(BF16)
            for part in halves(noise[...])
        ],
    )
    turn = one_hot(QM)
    high, low = halves(pmid[...])
    wide(
        pmt,
        QM,
        *[dot_nt(dot_nt(turn, part).astype(BF16), slot).astype(BF16) for part in (high, low)],
    )
    narrow(pm, *[dot(slot, part).astype(BF16) for part in (high, low)])
    narrow(km, *[dot_nt(turn, part).astype(BF16) for part in halves(mid[...])])
    row, col = eye(16, 8)
    turn = jnp.where(row == col, 1.0, 0.0).astype(BF16)
    narrow(plt, *[dot_nt(turn, part).astype(BF16) for part in halves(plow[...])])


def split_fine(values, x_ref, lanes):
    high, low = halves(values)
    x_ref[0:SF, lanes] = high
    x_ref[256 : 256 + SF, lanes] = low


def clear_fine(x_ref):
    x_ref[SF:256, :] = jnp.zeros((256 - SF, LANES), BF16)
    x_ref[256 + SF : 512, :] = jnp.zeros((256 - SF, LANES), BF16)


def fine_product(w_ref, x_ref, lanes):
    return dot(w_ref[:, 0:512], x_ref[:, lanes]) + dot(w_ref[:, 512:768], x_ref[0:256, lanes])


def mid_product(w_ref, values, x_ref):
    high, low = halves(values)
    x_ref[0:64, :] = high
    x_ref[64:128, :] = low
    x_ref[128:192, :] = high
    x_ref[192:256, :] = jnp.zeros((64, LANES), BF16)
    return dot(w_ref[...], x_ref[...])


def chunk(n):
    return slice(n * 512, n * 512 + 512)


def fine_sends(u_ref, idx, s1, s2, s3, s4):
    x_even, y_even = even(idx, 0), even(idx, 1)
    upper, lower = u_ref[200:240, 1536:2048], u_ref[0:40, 0:512]
    s1[...] = jnp.where(x_even, upper, lower)
    s2[...] = jnp.where(x_even, lower, upper)
    for i in range(6):
        upper = y_column(u_ref[40 * i + 8 : 40 * i + 16, :], 3)
        lower = y_column(u_ref[40 * i : 40 * i + 8, :], 0)
        s3[8 * i : 8 * i + 8, :] = jnp.where(y_even, upper, lower)
        s4[8 * i : 8 * i + 8, :] = jnp.where(y_even, lower, upper)


def fine_defect(u_ref, g_ref, csr, idx, r1, r2, r3, r4, kf, x_ref, t_ref):
    for n in range(4):
        u = u_ref[:, chunk(n)]
        split_fine(u, x_ref, chunk(n))
        t_ref[:, chunk(n)] = g_ref[:, chunk(n)] - 4.0 * u - fine_product(kf, x_ref, chunk(n))
    x_even, y_even = even(idx, 0), even(idx, 1)
    below = jnp.where(x_even, r2[...], r1[...])
    above = jnp.where(x_even, r1[...], r2[...])
    t_ref[0:40, :] += csr[0:1, :] * x_from_lower(below, u_ref[200:240, :])
    t_ref[200:240, :] += csr[1:2, :] * x_from_upper(u_ref[0:40, :], above)
    row = sublane((8, LANES))
    for i in range(6):
        base = 40 * i
        first, last, sides = (u_ref[base + 8 * n : base + 8 * n + 8, :] for n in range(3))
        edge = slice(8 * i, 8 * i + 8)
        below = jnp.where(y_even, r4[edge, :], r3[edge, :])
        above = jnp.where(y_even, r3[edge, :], r4[edge, :])
        t0 = csr[2:3, :] * y_from_lower(below, last)
        t1 = csr[3:4, :] * y_from_upper(first, above)
        for n, tile, extra in ((0, first, t0), (1, last, t1)):
            lower = csr[4:5, :] * sub_roll(lane_roll(tile, 1), 3)
            upper = csr[5:6, :] * sub_roll(lane_roll(tile, -1), 5)
            t_ref[base + 8 * n : base + 8 * n + 8, :] += (
                extra + jnp.where(row == 0, lower, 0.0) + jnp.where(row == 5, upper, 0.0)
            )
        lower = csr[4:5, :] * sub_roll(lane_roll(sides, 1), 4)
        upper = csr[5:6, :] * sub_roll(lane_roll(sides, -1), 4)
        t_ref[base + 16 : base + 24, :] += jnp.where(row < 4, lower, upper)


def fine_update(u_ref, out_ref, sf, x_ref, t_ref):
    for n in range(4):
        t = t_ref[:, chunk(n)]
        split_fine(t, x_ref, chunk(n))
        out_ref[:, chunk(n)] = u_ref[:, chunk(n)] + 0.25 * t + fine_product(sf, x_ref, chunk(n))


def first_kernel(seed, scale, coef, to_slot, sf, idx, g, u1, cs, csr, s1, s2, s3, s4, x_ref):
    over = 1.0 / scale[...]
    cs[...] = jnp.concatenate([coef[16 * d : 16 * d + 16, :] * over for d in range(3)], axis=0)
    csr[...] = jnp.zeros((8, LANES), F32)
    lane = lax.broadcasted_iota(jnp.int32, (1, 128), 1)
    for c in range(COLS):
        x, y = c // 4, c % 4
        lanes = slice(c * 128, c * 128 + 128)
        for d in range(3):
            value = cs[16 * d + c : 16 * d + c + 1, :]
            low, high = 0.9 * value, 0.3 * value
            if d == 0 and x == 0:
                low = jnp.where(idx[0] == 0, 0.0, low)
            if d == 0 and x == 3:
                high = jnp.where(idx[0] == idx[2] - 1, 0.0, high)
            if d == 1 and y == 0:
                low = jnp.where(idx[1] == 0, 0.0, low)
            if d == 1 and y == 3:
                high = jnp.where(idx[1] == idx[3] - 1, 0.0, high)
            if d == 2:
                low = jnp.where(lane == 0, 0.0, low)
                high = jnp.where(lane == 127, 0.0, high)
            csr[2 * d : 2 * d + 1, lanes] = low
            csr[2 * d + 1 : 2 * d + 2, lanes] = high
    clear_fine(x_ref)
    x_ref[QF:SF, :] = jnp.zeros((SF - QF, LANES), BF16)
    x_ref[256 + QF : 256 + SF, :] = jnp.zeros((SF - QF, LANES), BF16)
    slot = to_slot[...]
    for c in range(COLS):
        lanes = slice(c * 128, c * 128 + 128)
        values = seed[pl.ds(c, QF, stride=COLS), :] * over[c : c + 1, :]
        high, low = halves(values)
        rest = (values - high.astype(F32) - low.astype(F32)).astype(BF16)
        g[:, lanes] = dot(slot, high) + dot(slot, low) + dot(slot, rest)
    for n in range(4):
        values = g[:, chunk(n)]
        split_fine(values, x_ref, chunk(n))
        u1[:, chunk(n)] = 0.25 * values + fine_product(sf, x_ref, chunk(n))
    fine_sends(u1, idx, s1, s2, s3, s4)


def sweep_kernel(u, g, csr, idx, r1, r2, r3, r4, kf, sf, out, s1, s2, s3, s4, x_ref, t_ref):
    clear_fine(x_ref)
    fine_defect(u, g, csr, idx, r1, r2, r3, r4, kf, x_ref, t_ref)
    fine_update(u, out, sf, x_ref, t_ref)
    fine_sends(out, idx, s1, s2, s3, s4)


def restrict_kernel(u, g, csr, idx, r1, r2, r3, r4, kf, pmt, gm, m1, s1, s2, s3, s4, x_ref, t_ref):
    clear_fine(x_ref)
    fine_defect(u, g, csr, idx, r1, r2, r3, r4, kf, x_ref, t_ref)
    for n in range(4):
        split_fine(t_ref[:, chunk(n)], x_ref, chunk(n))
        value = fine_product(pmt, x_ref, chunk(n))
        gm[:, chunk(n)] = value
        m1[:, chunk(n)] = 0.2 * value
    mid_sends(m1, idx, s1, s2, s3, s4)


def last_kernel(u, g, csr, idx, r1, r2, r3, r4, kf, sf, nf, from_slot, inc, out, prev, x_ref, t_ref, w_ref):
    clear_fine(x_ref)
    fine_defect(u, g, csr, idx, r1, r2, r3, r4, kf, x_ref, t_ref)
    fine_update(u, w_ref, sf, x_ref, t_ref)
    slot = from_slot[...]
    for n in range(4):
        values = w_ref[:, chunk(n)]
        split_fine(values, x_ref, chunk(n))
        high, low = halves(values)
        rest = (values - high.astype(F32) - low.astype(F32)).astype(BF16)
        natural = dot(slot, high) + dot(slot, low) + dot(slot, rest)
        noise = fine_product(nf, x_ref, chunk(n))
        for y in range(4):
            c = 4 * n + y
            lanes = slice(y * 128, y * 128 + 128)
            out[pl.ds(c, QF, stride=COLS), :] = natural[:, lanes]
            prev[pl.ds(c, QF, stride=COLS), :] = (
                natural[:, lanes] + inc[c : c + 1, :] * noise[:, lanes]
            )


def mid_sends(m_ref, idx, s1, s2, s3, s4):
    x_even, y_even = even(idx, 0), even(idx, 1)
    upper, lower = m_ref[48:64, 1536:2048], m_ref[0:16, 0:512]
    s1[...] = jnp.where(x_even, upper, lower)
    s2[...] = jnp.where(x_even, lower, upper)
    for i in range(4):
        upper = y_column(m_ref[16 * i + 8 : 16 * i + 16, :], 3)
        lower = y_column(m_ref[16 * i : 16 * i + 8, :], 0)
        s3[8 * i : 8 * i + 8, :] = jnp.where(y_even, upper, lower)
        s4[8 * i : 8 * i + 8, :] = jnp.where(y_even, lower, upper)


def mid_edges(idx, r1, r2, r3, r4):
    x_even, y_even = even(idx, 0), even(idx, 1)
    return (
        jnp.where(x_even, r2[...], r1[...]),
        jnp.where(x_even, r1[...], r2[...]),
        jnp.where(y_even, r4[...], r3[...]),
        jnp.where(y_even, r3[...], r4[...]),
    )


def mid_defect(m_ref, g_ref, csr, edges, km, x_ref, t_ref):
    below_x, above_x, below_y, above_y = edges
    m = m_ref[...]
    t_ref[...] = g_ref[...] - 4.0 * m - mid_product(km, m, x_ref)
    t_ref[0:16, :] += csr[0:1, :] * x_from_lower(below_x, m_ref[48:64, :])
    t_ref[48:64, :] += csr[1:2, :] * x_from_upper(m_ref[0:16, :], above_x)
    row = sublane((8, LANES))
    for i in range(4):
        base = 16 * i
        first, last = m_ref[base : base + 8, :], m_ref[base + 8 : base + 16, :]
        edge = slice(8 * i, 8 * i + 8)
        extra0 = csr[2:3, :] * sub_roll(y_from_lower(below_y[edge, :], last), 4)
        extra1 = csr[3:4, :] * sub_roll(y_from_upper(first, above_y[edge, :]), 4)
        for n, tile, extra in (
            (0, first, jnp.where(row < 4, extra0, 0.0)),
            (1, last, jnp.where(row >= 4, extra1, 0.0)),
        ):
            lower = csr[4:5, :] * sub_roll(lane_roll(tile, 1), 5)
            upper = csr[5:6, :] * sub_roll(lane_roll(tile, -1), 3)
            t_ref[base + 8 * n : base + 8 * n + 8, :] += (
                extra + jnp.where(row % 4 == 0, lower, 0.0) + jnp.where(row % 4 == 3, upper, 0.0)
            )


def mid_kernel(m, g, csr, idx, r1, r2, r3, r4, km, out, s1, s2, s3, s4, x_ref, t_ref):
    mid_defect(m, g, csr, mid_edges(idx, r1, r2, r3, r4), km, x_ref, t_ref)
    out[...] = m[...] + 0.2 * t_ref[...]
    mid_sends(out, idx, s1, s2, s3, s4)


def low_kernel(m, g, csr, cs, idx, r1, r2, r3, r4, km, plt, pay, x_ref, t_ref):
    mid_defect(m, g, csr, mid_edges(idx, r1, r2, r3, r4), km, x_ref, t_ref)
    value = mid_product(plt, t_ref[...], x_ref)
    for c in range(COLS):
        pay[pl.ds(c, QC, stride=COLS), :] = value[0:8, c * 128 : c * 128 + 128]
    pay[QC * COLS : (QC + 3) * COLS, :] = cs[...]


def lift_kernel(m, csr, idx, r1, r2, r3, r4, km, pm, g, u, out, s1, s2, s3, s4, x_ref, t_ref):
    mid_defect(m, g, csr, mid_edges(idx, r1, r2, r3, r4), km, x_ref, t_ref)
    t_ref[...] = m[...] + 0.2 * t_ref[...]
    high, low = halves(t_ref[...])
    x_ref[0:64, :] = high
    x_ref[64:128, :] = low
    x_ref[128:192, :] = high
    for n in range(4):
        out[:, chunk(n)] = u[:, chunk(n)] + dot(pm[...], x_ref[:, chunk(n)])
    fine_sends(out, idx, s1, s2, s3, s4)


WX = 12
WROWS = WX * 16


def place(window, fields, blocks, idx):
    own, r1, r2, y3, y4 = blocks
    x_even, y_even = even(idx, 0), even(idx, 1)
    count = own.shape[0]
    zero = jnp.zeros((4, 128), F32)
    for d in range(fields):
        for x in range(4):
            rows = pl.ds(d * COLS + x * 4, 4)
            first = (own[rows, :], r1[rows, :], r2[rows, :])
            side = []
            for ref in (y3, y4):
                side.append(
                    tuple(ref[pl.ds(n * count + d * COLS + x * 4, 4), :] for n in range(3))
                )
            below = tuple(jnp.where(y_even, b, a) for a, b in zip(*side))
            above = tuple(jnp.where(y_even, a, b) for a, b in zip(*side))
            for offset, (mine, one, two) in ((0, below), (4, first), (8, above)):
                left = jnp.where(x_even, two, one)
                right = jnp.where(x_even, one, two)
                for plane, value in ((x, left), (4 + x, mine), (8 + x, right)):
                    window[d, pl.ds(plane * 16 + offset, 4), :] = value
            for plane in (x, 4 + x, 8 + x):
                window[d, pl.ds(plane * 16 + 12, 4), :] = zero


def coarse_sweep(c_ref, out_ref, g_ref, coef, kc, first, last):
    def step(plane, carry):
        here = pl.ds(pl.multiple_of(plane * 16, 16), 16)
        before = pl.ds(pl.multiple_of(plane * 16 - 16, 16), 16)
        after = pl.ds(pl.multiple_of(plane * 16 + 16, 16), 16)
        c = [c_ref[d, here, :] for d in range(QC)]
        weights = [coef[n, here, :] for n in range(6)]
        for d in range(QC):
            t = g_ref[d, here, :] - 4.0 * c[d]
            for j in range(QC):
                t = t - kc[j, d] * c[j]
            if d & 4:
                t = t + weights[1] * c_ref[d - 4, after, :]
            else:
                t = t + weights[0] * c_ref[d + 4, before, :]
            if d & 2:
                t = t + weights[3] * sub_roll(c[d - 2], -1)
            else:
                t = t + weights[2] * sub_roll(c[d + 2], 1)
            if d & 1:
                t = t + weights[5] * pltpu.roll(c[d - 1], 127, 1)
            else:
                t = t + weights[4] * pltpu.roll(c[d + 1], 1, 1)
            out_ref[d, here, :] = c[d] + 0.2 * t
        return carry

    lax.fori_loop(first, last, step, 0)


def coarse_kernel(own, r1, r2, y3, y4, kc, idx, g, coef, pay, window, one, two):
    place(window, QC + 3, (own, r1, r2, y3, y4), idx)
    g[...] = window[0:QC]
    lane = lax.broadcasted_iota(jnp.int32, (WROWS, 128), 1)
    row = lax.broadcasted_iota(jnp.int32, (WROWS, 128), 0)
    plane, y = row // 16, row % 16 - 4
    csx, csy, csz = (window[QC + d] for d in range(3))
    coef[0] = jnp.where((plane == 4) & (idx[0] == 0), 0.0, 0.9 * csx)
    coef[1] = jnp.where((plane == 7) & (idx[0] == idx[2] - 1), 0.0, 0.3 * csx)
    coef[2] = jnp.where((y == 0) & (idx[1] == 0), 0.0, 0.9 * csy)
    coef[3] = jnp.where((y == 3) & (idx[1] == idx[3] - 1), 0.0, 0.3 * csy)
    coef[4] = jnp.where(lane == 0, 0.0, 0.9 * csz)
    coef[5] = jnp.where(lane == 127, 0.0, 0.3 * csz)
    one[...] = 0.2 * g[...]
    coarse_sweep(one, two, g, coef, kc, 1, 11)
    coarse_sweep(two, one, g, coef, kc, 2, 10)
    coarse_sweep(one, two, g, coef, kc, 3, 9)
    coarse_sweep(two, one, g, coef, kc, 4, 8)
    for d in range(QC):
        for x in range(4):
            pay[pl.ds(d * COLS + x * 4, 4), :] = one[d, pl.ds((4 + x) * 16 + 4, 4), :]


def correct_kernel(
    own, r1, r2, y3, y4, kc, idx, g, coef, plow, m, gm, csr, q1, q2, q3, q4, km,
    out, s1, s2, s3, s4, window, one, x_ref, t_ref, m_ref, spread,
):
    place(window, QC, (own, r1, r2, y3, y4), idx)
    coarse_sweep(window, one, g, coef, kc, 3, 9)
    for d in range(QC):
        spread[d] = jnp.broadcast_to(plow[:, d : d + 1], (QM, 128))

    def lifted(x, y, rows):
        total = None
        for d in range(QC):
            part = spread[d, rows, :] * one[d, pl.ds((4 + x) * 16 + 4 + y, 1), :]
            total = part if total is None else total + part
        return total

    whole = slice(0, QM)
    for c in range(COLS):
        lanes = slice(c * 128, c * 128 + 128)
        m_ref[:, lanes] = m[:, lanes] + lifted(c // 4, c % 4, whole)
    below_x, above_x, below_y, above_y = mid_edges(idx, q1, q2, q3, q4)
    below_x = below_x + jnp.concatenate([lifted(-1, y, slice(48, 64)) for y in range(4)], axis=1)
    above_x = above_x + jnp.concatenate([lifted(4, y, slice(0, 16)) for y in range(4)], axis=1)
    below_rows, above_rows = [], []
    for i in range(4):
        last, first = slice(16 * i + 8, 16 * i + 16), slice(16 * i, 16 * i + 8)
        below_rows.append(jnp.concatenate([lifted(x, -1, last) for x in range(4)], axis=1))
        above_rows.append(jnp.concatenate([lifted(x, 4, first) for x in range(4)], axis=1))
    below_y = below_y + jnp.concatenate(below_rows, axis=0)
    above_y = above_y + jnp.concatenate(above_rows, axis=0)
    mid_defect(m_ref, gm, csr, (below_x, above_x, below_y, above_y), km, x_ref, t_ref)
    out[...] = m_ref[...] + 0.2 * t_ref[...]
    mid_sends(out, idx, s1, s2, s3, s4)


def swap(values, axis, odd):
    count = lax.axis_size(axis)
    pairs = [(i, (((i + odd) ^ 1) - odd) % count) for i in range(count)]
    return lax.ppermute(values, axis, pairs)


def exchange(sends):
    s1, s2, s3, s4 = sends
    return swap(s1, "gx", 0), swap(s2, "gx", 1), swap(s3, "yz", 0), swap(s4, "yz", 1)


def exchange_blocks(own):
    r1, r2 = swap(own, "gx", 0), swap(own, "gx", 1)
    three = jnp.concatenate([own, r1, r2], axis=0)
    return own, r1, r2, swap(three, "yz", 0), swap(three, "yz", 1)


def body(seed, scale, coef, fine, smooth, mid, coarse, pmid, plow, noise, inc):
    idx = jnp.stack(
        [
            lax.axis_index("gx"),
            lax.axis_index("yz"),
            jnp.int32(lax.axis_size("gx")),
            jnp.int32(lax.axis_size("yz")),
        ]
    ).astype(jnp.int32)
    rows = seed.reshape(QF * COLS, 128)
    scale = scale.reshape(COLS, 128)
    coef = coef.reshape(3 * COLS, 128)
    inc = inc.reshape(COLS, 128)
    slots = slot_matrix()
    to_slot, from_slot = jnp.asarray(slots, BF16), jnp.asarray(slots.T, BF16)

    kf, sf, nf, pmt, pm, km, plt = call(
        prep_kernel,
        [
            ((SF, 768), BF16),
            ((SF, 768), BF16),
            ((QF, 768), BF16),
            ((QM, 768), BF16),
            ((SF, 256), BF16),
            ((QM, 256), BF16),
            ((16, 256), BF16),
        ],
    )(to_slot, fine, smooth, noise, mid, pmid, plow)

    fine_field = ((SF, LANES), F32)
    fine_faces = [((40, 512), F32)] * 2 + [((48, 512), F32)] * 2
    mid_field = ((QM, LANES), F32)
    mid_faces = [((16, 512), F32)] * 2 + [((32, 512), F32)] * 2
    xf, tf = pltpu.VMEM((512, LANES), BF16), pltpu.VMEM((SF, LANES), F32)
    xm, tm = pltpu.VMEM((256, LANES), BF16), pltpu.VMEM((QM, LANES), F32)

    g, u, cs, csr, *sends = call(
        first_kernel,
        [fine_field, fine_field, ((3 * COLS, 128), F32), ((8, LANES), F32)] + fine_faces,
        [xf],
        (5,),
    )(rows, scale, coef, to_slot, sf, idx)

    sweep = call(sweep_kernel, [fine_field] + fine_faces, [xf, tf], (3,))
    u, *sends = sweep(u, g, csr, idx, *exchange(sends), kf, sf)
    gm, m, *sends = call(restrict_kernel, [mid_field, mid_field] + mid_faces, [xf, tf], (3,))(
        u, g, csr, idx, *exchange(sends), kf, pmt
    )
    m, *sends = call(mid_kernel, [mid_field] + mid_faces, [xm, tm], (3,))(
        m, gm, csr, idx, *exchange(sends), km
    )
    edges = exchange(sends)
    (pay,) = call(low_kernel, [(((QC + 3) * COLS, 128), F32)], [xm, tm], (4,))(
        m, gm, csr, cs, idx, *edges, km, plt
    )
    window = ((QC, WROWS, 128), F32)
    gw, coefw, pay = call(
        coarse_kernel,
        [window, ((6, WROWS, 128), F32), ((QC * COLS, 128), F32)],
        [
            pltpu.VMEM((QC + 3, WROWS, 128), F32),
            pltpu.VMEM((QC, WROWS, 128), F32),
            pltpu.VMEM((QC, WROWS, 128), F32),
        ],
        (5, 6),
    )(*exchange_blocks(pay), coarse, idx)
    m, *sends = call(
        correct_kernel,
        [mid_field] + mid_faces,
        [
            pltpu.VMEM((QC, WROWS, 128), F32),
            pltpu.VMEM((QC, WROWS, 128), F32),
            xm,
            tm,
            pltpu.VMEM((QM, LANES), F32),
            pltpu.VMEM((QC, QM, 128), F32),
        ],
        (5, 6),
    )(*exchange_blocks(pay), coarse, idx, gw, coefw, plow, m, gm, csr, *edges, km)
    u, *sends = call(lift_kernel, [fine_field] + fine_faces, [xm, tm], (2,))(
        m, csr, idx, *exchange(sends), km, pm, gm, u
    )
    u, *sends = sweep(u, g, csr, idx, *exchange(sends), kf, sf)
    out, prev = call(
        last_kernel,
        [((QF * COLS, 128), F32)] * 2,
        [xf, tf, pltpu.VMEM((SF, LANES), F32)],
        (3,),
    )(u, g, csr, idx, *exchange(sends), kf, sf, nf, from_slot, inc)
    shape = seed.shape
    return out.reshape(shape), prev.reshape(shape)


def solution(mesh):
    cell, field = P("gx", "yz", None), P(None, "gx", "yz", None)
    return jax.shard_map(
        body,
        mesh=mesh,
        in_specs=(field, cell, field) + (P(),) * 7 + (cell,),
        out_specs=(field, field),
        check_vma=False,
    )
```

time: 571 us -> 131 us (0.23)
  the two profiles are of different devices: /device:TPU:14 before, /device:TPU:0 now
where the time goes in v1:
time: 131 us
  waiting for transfers between devices  50.5 us (39%)
  starting transfers between devices  39.3 us (30%)
  Pallas kernels  31 us (24%)
  local copies, waits for them, and re-layouts  9.12 us (7%)
    ppermute x36, waiting for transfers between devices, swap(): return lax.ppermute(values, axis, pairs)  50.5 us
    ppermute x36, starting transfers between devices, swap(): return lax.ppermute(values, axis, pairs)  39.3 us
    pallas_call x11, Pallas kernels, run(): pl.pallas_call(kernel, out_shape=tuple((jax.ShapeDtypeStruct(s, d) for s,...  31 us
    unnamed x26, local copies, waits for them, and re-layouts  9.11 us
  transfers between devices with their start and end apart: 36, of which 20 were waited for; matrix products, arithmetic and copies ran while one was open for 0% of the time, Pallas kernels for 0%

profile of v1, /device:TPU:0, one launch (start us, length us, event | category | flops | bytes accessed | tf_op | source)
XLA Modules:
  0.0 130.9 jit_solution(12633240149925012894)
XLA Ops:
  0.6 0.8 copy.16.plow
  1.4 0.9 copy.15.pmid
  2.4 0.9 copy-done.1
  3.3 0.9 copy-done.2
  4.3 0.9 copy-done.3
  5.2 0.9 copy-done.4
  6.1 0.8 copy-done.6
  6.9 1.1 shard_map.140
  8.0 1.5 %copy-done = f32[216,4,4,128]{3,2,1,0:T(4,128)S(1)} copy-done((f32[216,4,4,128]{3,2,1,0:T(4,128)S(1)}, f32[216,4,4,128]{3,2,1,0:T(4,128)}, u32[]{:S(2)}) %copy-start) | copy-done | bytes 1769496
  9.5 0.7 copy-done.7
  10.2 0.7 copy-done.9
  10.9 3.5 %shard_map.141 = (f32[240,2048]{1,0:T(8,128)S(1)}, f32[240,2048]{1,0:T(8,128)S(1)}, f32[48,128]{1,0:T(8,128)S(1)}, f32[8,2048]{1,0:T(8,128)S(1)}, f32[40,512]{1,...) custom-call(f32[3456,128]{1,0:T(8,128)S(1)} %bitcast.8, ...), custom_call_target="tpu_custom_call" | custom-call | tf_op jit(solution)/shard_map/pallas_call | solution.py:44
  14.5 6.4 %collective-permute-start.3 = (f32[48,512]{1,0:T(8,128)S(1)}, f32[48,512]{1,0:T(8,128)S(1)}, u32[]{:S(2)}, u32[]{:S(2)}) collective-permute-start(f32[48,512]{1,0:T(8,128)S(1)} %get-tuple-element.60), channel_id=1, source_target_pairs={{0,31},{1,2},{2,1},{3,4},{4,3},{5,6},{6,5},{7,8},{8,7},{9,10},{10,... | collective-permute-start | bytes 294920 | tf_op jit(solution)/shard_map/ppermute | solution.py:522
  20.9 1.6 %collective-permute-start = (f32[40,512]{1,0:T(8,128)S(1)}, f32[40,512]{1,0:T(8,128)S(1)}, u32[]{:S(2)}, u32[]{:S(2)}) collective-permute-start(f32[40,512]{1,0:T(8,128)S(1)} %get-tuple-element.57), channel_id=1, source_target_pairs={{0,32},{32,0},{64,96},{96,64},{1,33},{33,1},{65,97},{97,65},{2,34}... | collective-permute-start | bytes 245768 | tf_op jit(solution)/shard_map/ppermute | solution.py:522
  22.5 2.2 %collective-permute-start.1 = (f32[40,512]{1,0:T(8,128)S(1)}, f32[40,512]{1,0:T(8,128)S(1)}, u32[]{:S(2)}, u32[]{:S(2)}) collective-permute-start(f32[40,512]{1,0:T(8,128)S(1)} %get-tuple-element.58), channel_id=1, source_target_pairs={{0,96},{32,64},{64,32},{96,0},{1,97},{33,65},{65,33},{97,1},{2,98}... | collective-permute-start | bytes 245768 | tf_op jit(solution)/shard_map/ppermute | solution.py:522
  24.7 0.7 collective-permute-done.r1
  25.4 2.8 %collective-permute-done.1.r2 = f32[40,512]{1,0:T(8,128)S(1)} collective-permute-done((f32[40,512]{1,0:T(8,128)S(1)}, f32[40,512]{1,0:T(8,128)S(1)}, u32[]{:S(2)}, u32[]{:S(2)}) %collective-permute-start.1) | collective-permute-done | bytes 81952 | tf_op jit(solution)/shard_map/ppermute | solution.py:522
  28.2 3.3 %shard_map.142 = (f32[240,2048]{1,0:T(8,128)S(1)}, f32[40,512]{1,0:T(8,128)S(1)}, f32[40,512]{1,0:T(8,128)S(1)}, f32[48,512]{1,0:T(8,128)S(1)}, f32[48,512]{1,0:T(8,128)S(1)}) custom-call(f32[240,2048]{1,0:T(8,128)S(1)} %get-tuple-element.54.u, f32[240,2048]{1,0:T(8,128)S(1)} %get-tuple-element.55.g, f32[8,2048]{1,0:T(8,128)S(1)} %get-tuple-element.56.csr, ...), custom_call_target="tpu_custom_call" | custom-call | tf_op jit(solution)/shard_map/pallas_call | solution.py:44
  31.6 0.5 collective-permute-start.7
  32.1 1.3 collective-permute-start.4
  33.3 2.2 %collective-permute-start.5 = (f32[40,512]{1,0:T(8,128)S(1)}, f32[40,512]{1,0:T(8,128)S(1)}, u32[]{:S(2)}, u32[]{:S(2)}) collective-permute-start(f32[40,512]{1,0:T(8,128)S(1)} %get-tuple-element.64), channel_id=1, source_target_pairs={{0,96},{32,64},{64,32},{96,0},{1,97},{33,65},{65,33},{97,1},{2,98}... | collective-permute-start | bytes 245768 | tf_op jit(solution)/shard_map/ppermute | solution.py:522
  35.5 1.0 collective-permute-done.4.r1
  36.5 2.5 %collective-permute-done.5.r2 = f32[40,512]{1,0:T(8,128)S(1)} collective-permute-done((f32[40,512]{1,0:T(8,128)S(1)}, f32[40,512]{1,0:T(8,128)S(1)}, u32[]{:S(2)}, u32[]{:S(2)}) %collective-permute-start.5) | collective-permute-done | bytes 81952 | tf_op jit(solution)/shard_map/ppermute | solution.py:522
  39.0 2.8 %shard_map.143 = (f32[64,2048]{1,0:T(8,128)S(1)}, f32[64,2048]{1,0:T(8,128)S(1)}, f32[16,512]{1,0:T(8,128)S(1)}, f32[16,512]{1,0:T(8,128)S(1)}, f32[32,512]{1,0:T(8,128)S(1)}, /*index=5*/f32[32,512]{1,0:T(8,128)S(1)}) custom-call(f32[240,2048]{1,0:T(8,128)S(1)} %get-tuple-element.62.u, f32[240,2048]{1,0:T(8,128)S(1)} %get-tuple-element.55.g, ...), custom_call_target="tpu_custom_call" | custom-call | tf_op jit(solution)/shard_map/pallas_call | solution.py:44
  41.9 2.3 %collective-permute-start.11 = (f32[32,512]{1,0:T(8,128)S(1)}, f32[32,512]{1,0:T(8,128)S(1)}, u32[]{:S(2)}, u32[]{:S(2)}) collective-permute-start(f32[32,512]{1,0:T(8,128)S(1)} %get-tuple-element.73), channel_id=1, source_target_pairs={{0,31},{1,2},{2,1},{3,4},{4,3},{5,6},{6,5},{7,8},{8,7},{9,10},{10,... | collective-permute-start | bytes 196616 | tf_op jit(solution)/shard_map/ppermute | solution.py:522
  44.2 0.5 collective-permute-start.8
  44.8 2.2 %collective-permute-start.9 = (f32[16,512]{1,0:T(8,128)S(1)}, f32[16,512]{1,0:T(8,128)S(1)}, u32[]{:S(2)}, u32[]{:S(2)}) collective-permute-start(f32[16,512]{1,0:T(8,128)S(1)} %get-tuple-element.71), channel_id=1, source_target_pairs={{0,96},{32,64},{64,32},{96,0},{1,97},{33,65},{65,33},{97,1},{2,98}... | collective-permute-start | bytes 98312 | tf_op jit(solution)/shard_map/ppermute | solution.py:522
  47.0 1.2 collective-permute-done.8.r1
  48.2 1.8 %collective-permute-done.9.r2 = f32[16,512]{1,0:T(8,128)S(1)} collective-permute-done((f32[16,512]{1,0:T(8,128)S(1)}, f32[16,512]{1,0:T(8,128)S(1)}, u32[]{:S(2)}, u32[]{:S(2)}) %collective-permute-start.9) | collective-permute-done | bytes 32800 | tf_op jit(solution)/shard_map/ppermute | solution.py:522
  49.9 1.2 shard_map.144
  51.2 1.4 %collective-permute-start.15 = (f32[32,512]{1,0:T(8,128)S(1)}, f32[32,512]{1,0:T(8,128)S(1)}, u32[]{:S(2)}, u32[]{:S(2)}) collective-permute-start(f32[32,512]{1,0:T(8,128)S(1)} %get-tuple-element.80), channel_id=1, source_target_pairs={{0,31},{1,2},{2,1},{3,4},{4,3},{5,6},{6,5},{7,8},{8,7},{9,10},{10,... | collective-permute-start | bytes 196616 | tf_op jit(solution)/shard_map/ppermute | solution.py:522
  52.6 0.5 collective-permute-start.12
  53.1 2.2 %collective-permute-start.13 = (f32[16,512]{1,0:T(8,128)S(1)}, f32[16,512]{1,0:T(8,128)S(1)}, u32[]{:S(2)}, u32[]{:S(2)}) collective-permute-start(f32[16,512]{1,0:T(8,128)S(1)} %get-tuple-element.78), channel_id=1, source_target_pairs={{0,96},{32,64},{64,32},{96,0},{1,97},{33,65},{65,33},{97,1},{2,98}... | collective-permute-start | bytes 98312 | tf_op jit(solution)/shard_map/ppermute | solution.py:522
  55.3 1.2 collective-permute-done.12.r1.q1
  56.5 1.8 %collective-permute-done.13.r2.q2 = f32[16,512]{1,0:T(8,128)S(1)} collective-permute-done((f32[16,512]{1,0:T(8,128)S(1)}, f32[16,512]{1,0:T(8,128)S(1)}, u32[]{:S(2)}, u32[]{:S(2)}) %collective-permute-start.13) | collective-permute-done | bytes 32800 | tf_op jit(solution)/shard_map/ppermute | solution.py:522
  58.3 1.3 shard_map.145.own
  59.5 2.2 %collective-permute-start.17 = (f32[176,128]{1,0:T(8,128)S(1)}, f32[176,128]{1,0:T(8,128)S(1)}, u32[]{:S(2)}, u32[]{:S(2)}) collective-permute-start(f32[176,128]{1,0:T(8,128)S(1)} %shard_map.145.own), channel_id=1, source_target_pairs={{0,96},{32,64},{64,32},{96,0},{1,97},{33,65},{65,33},{97,1},{2,98}... | collective-permute-start | bytes 270344 | tf_op jit(solution)/shard_map/ppermute | solution.py:522
  61.7 3.6 %collective-permute-done.17.r2 = f32[176,128]{1,0:T(8,128)S(1)} collective-permute-done((f32[176,128]{1,0:T(8,128)S(1)}, f32[176,128]{1,0:T(8,128)S(1)}, u32[]{:S(2)}, u32[]{:S(2)}) %collective-permute-start.17) | collective-permute-done | bytes 90144 | tf_op jit(solution)/shard_map/ppermute | solution.py:522
  65.3 1.0 collective-permute-done.16.r1
  66.3 0.8 collective-permute-start.19
  67.1 8.5 %collective-permute-done.19.y4 = f32[528,128]{1,0:T(8,128)S(1)} collective-permute-done((f32[528,128]{1,0:T(8,128)S(1)}, f32[528,128]{1,0:T(8,128)S(1)}, u32[]{:S(2)}, u32[]{:S(2)}) %collective-permute-start.19) | collective-permute-done | bytes 270368 | tf_op jit(solution)/shard_map/ppermute | solution.py:522
  75.6 3.5 %shard_map.146 = (f32[8,192,128]{2,1,0:T(8,128)S(1)}, f32[6,192,128]{2,1,0:T(8,128)S(1)}, f32[128,128]{1,0:T(8,128)S(1)}) custom-call(f32[176,128]{1,0:T(8,128)S(1)} %shard_map.145.own, f32[176,128]{1,0:T(8,128)S(1)} %collective-permute-done.16.r1, f32[176,128]{1,0:T(8,128)S(1)} %collective-permute-done.17.r2, f32[528,128]{1,0:T(8,128)S(1)} %collective-permute-done.18.y3, ...), custom_call_target="tpu_custom_call" | custom-call | tf_op jit(solution)/shard_map/pallas_call | solution.py:44
  79.0 1.3 collective-permute-start.21
  80.3 4.3 %collective-permute-done.20.r1 = f32[128,128]{1,0:T(8,128)S(1)} collective-permute-done((f32[128,128]{1,0:T(8,128)S(1)}, f32[128,128]{1,0:T(8,128)S(1)}, u32[]{:S(2)}, u32[]{:S(2)}) %collective-permute-start.20) | collective-permute-done | bytes 65568 | tf_op jit(solution)/shard_map/ppermute | solution.py:522
  84.6 0.1 collective-permute-start.23
  84.8 8.3 %collective-permute-done.23.y4 = f32[384,128]{1,0:T(8,128)S(1)} collective-permute-done((f32[384,128]{1,0:T(8,128)S(1)}, f32[384,128]{1,0:T(8,128)S(1)}, u32[]{:S(2)}, u32[]{:S(2)}) %collective-permute-start.23) | collective-permute-done | bytes 196640 | tf_op jit(solution)/shard_map/ppermute | solution.py:522
  93.1 2.3 %shard_map.147 = (f32[64,2048]{1,0:T(8,128)S(1)}, f32[16,512]{1,0:T(8,128)S(1)}, f32[16,512]{1,0:T(8,128)S(1)}, f32[32,512]{1,0:T(8,128)S(1)}, f32[32,512]{1,0:T(8,128)S(1)}) custom-call(f32[128,128]{1,0:T(8,128)S(1)} %get-tuple-element.82.own, f32[128,128]{1,0:T(8,128)S(1)} %collective-permute-done.20.r1, f32[128,128]{1,0:T(8,128)S(1)} %collective-permute-done.21.r2, ...), custom_call_target="tpu_custom_call" | custom-call | tf_op jit(solution)/shard_map/pallas_call | solution.py:44
  95.7 2.1 %collective-permute-start.25 = (f32[16,512]{1,0:T(8,128)S(1)}, f32[16,512]{1,0:T(8,128)S(1)}, u32[]{:S(2)}, u32[]{:S(2)}) collective-permute-start(f32[16,512]{1,0:T(8,128)S(1)} %get-tuple-element.87), channel_id=1, source_target_pairs={{0,96},{32,64},{64,32},{96,0},{1,97},{33,65},{65,33},{97,1},{2,98}... | collective-permute-start | bytes 98312 | tf_op jit(solution)/shard_map/ppermute | solution.py:522
  97.8 1.8 %collective-permute-done.24.r1 = f32[16,512]{1,0:T(8,128)S(1)} collective-permute-done((f32[16,512]{1,0:T(8,128)S(1)}, f32[16,512]{1,0:T(8,128)S(1)}, u32[]{:S(2)}, u32[]{:S(2)}) %collective-permute-start.24) | collective-permute-done | bytes 32800 | tf_op jit(solution)/shard_map/ppermute | solution.py:522
  99.6 1.3 collective-permute-done.25.r2
  100.9 1.7 %collective-permute-done.27.r4 = f32[32,512]{1,0:T(8,128)S(1)} collective-permute-done((f32[32,512]{1,0:T(8,128)S(1)}, f32[32,512]{1,0:T(8,128)S(1)}, u32[]{:S(2)}, u32[]{:S(2)}) %collective-permute-start.27) | collective-permute-done | bytes 65568 | tf_op jit(solution)/shard_map/ppermute | solution.py:522
  102.6 1.5 %shard_map.148 = (f32[240,2048]{1,0:T(8,128)S(1)}, f32[40,512]{1,0:T(8,128)S(1)}, f32[40,512]{1,0:T(8,128)S(1)}, f32[48,512]{1,0:T(8,128)S(1)}, f32[48,512]{1,0:T(8,128)S(1)}) custom-call(f32[64,2048]{1,0:T(8,128)S(1)} %get-tuple-element.85.m, f32[8,2048]{1,0:T(8,128)S(1)} %get-tuple-element.56.csr, s32[4]{0:T(128)S(1)} %pad_add_fusion.idx, ...), custom_call_target="tpu_custom_call" | custom-call | tf_op jit(solution)/shard_map/pallas_call | solution.py:44
  104.3 2.1 %collective-permute-start.31 = (f32[48,512]{1,0:T(8,128)S(1)}, f32[48,512]{1,0:T(8,128)S(1)}, u32[]{:S(2)}, u32[]{:S(2)}) collective-permute-start(f32[48,512]{1,0:T(8,128)S(1)} %get-tuple-element.95), channel_id=1, source_target_pairs={{0,31},{1,2},{2,1},{3,4},{4,3},{5,6},{6,5},{7,8},{8,7},{9,10},{10,... | collective-permute-start | bytes 294920 | tf_op jit(solution)/shard_map/ppermute | solution.py:522
  106.4 0.5 collective-permute-start.28
  107.0 2.0 %collective-permute-start.29 = (f32[40,512]{1,0:T(8,128)S(1)}, f32[40,512]{1,0:T(8,128)S(1)}, u32[]{:S(2)}, u32[]{:S(2)}) collective-permute-start(f32[40,512]{1,0:T(8,128)S(1)} %get-tuple-element.93), channel_id=1, source_target_pairs={{0,96},{32,64},{64,32},{96,0},{1,97},{33,65},{65,33},{97,1},{2,98}... | collective-permute-start | bytes 245768 | tf_op jit(solution)/shard_map/ppermute | solution.py:522
  109.0 1.9 %collective-permute-done.28.r1 = f32[40,512]{1,0:T(8,128)S(1)} collective-permute-done((f32[40,512]{1,0:T(8,128)S(1)}, f32[40,512]{1,0:T(8,128)S(1)}, u32[]{:S(2)}, u32[]{:S(2)}) %collective-permute-start.28) | collective-permute-done | bytes 81952 | tf_op jit(solution)/shard_map/ppermute | solution.py:522
  110.9 1.8 %collective-permute-done.29.r2 = f32[40,512]{1,0:T(8,128)S(1)} collective-permute-done((f32[40,512]{1,0:T(8,128)S(1)}, f32[40,512]{1,0:T(8,128)S(1)}, u32[]{:S(2)}, u32[]{:S(2)}) %collective-permute-start.29) | collective-permute-done | bytes 81952 | tf_op jit(solution)/shard_map/ppermute | solution.py:522
  112.6 3.3 %shard_map.149 = (f32[240,2048]{1,0:T(8,128)S(1)}, f32[40,512]{1,0:T(8,128)S(1)}, f32[40,512]{1,0:T(8,128)S(1)}, f32[48,512]{1,0:T(8,128)S(1)}, f32[48,512]{1,0:T(8,128)S(1)}) custom-call(f32[240,2048]{1,0:T(8,128)S(1)} %get-tuple-element.91.u, f32[240,2048]{1,0:T(8,128)S(1)} %get-tuple-element.55.g, f32[8,2048]{1,0:T(8,128)S(1)} %get-tuple-element.56.csr, ...), custom_call_target="tpu_custom_call" | custom-call | tf_op jit(solution)/shard_map/pallas_call | solution.py:44
  116.0 1.4 %collective-permute-start.35 = (f32[48,512]{1,0:T(8,128)S(1)}, f32[48,512]{1,0:T(8,128)S(1)}, u32[]{:S(2)}, u32[]{:S(2)}) collective-permute-start(f32[48,512]{1,0:T(8,128)S(1)} %get-tuple-element.100), channel_id=1, source_target_pairs={{0,31},{1,2},{2,1},{3,4},{4,3},{5,6},{6,5},{7,8},{8,7},{9,10},{10,... | collective-permute-start | bytes 294920 | tf_op jit(solution)/shard_map/ppermute | solution.py:522
  117.4 0.5 collective-permute-start.32
  118.0 2.0 %collective-permute-start.33 = (f32[40,512]{1,0:T(8,128)S(1)}, f32[40,512]{1,0:T(8,128)S(1)}, u32[]{:S(2)}, u32[]{:S(2)}) collective-permute-start(f32[40,512]{1,0:T(8,128)S(1)} %get-tuple-element.98), channel_id=1, source_target_pairs={{0,96},{32,64},{64,32},{96,0},{1,97},{33,65},{65,33},{97,1},{2,98}... | collective-permute-start | bytes 245768 | tf_op jit(solution)/shard_map/ppermute | solution.py:522
  120.0 1.9 %collective-permute-done.32.r1 = f32[40,512]{1,0:T(8,128)S(1)} collective-permute-done((f32[40,512]{1,0:T(8,128)S(1)}, f32[40,512]{1,0:T(8,128)S(1)}, u32[]{:S(2)}, u32[]{:S(2)}) %collective-permute-start.32) | collective-permute-done | bytes 81952 | tf_op jit(solution)/shard_map/ppermute | solution.py:522
  121.9 1.7 %collective-permute-done.33.r2 = f32[40,512]{1,0:T(8,128)S(1)} collective-permute-done((f32[40,512]{1,0:T(8,128)S(1)}, f32[40,512]{1,0:T(8,128)S(1)}, u32[]{:S(2)}, u32[]{:S(2)}) %collective-permute-start.33) | collective-permute-done | bytes 81952 | tf_op jit(solution)/shard_map/ppermute | solution.py:522
  123.6 7.3 %shard_map.150 = (f32[3456,128]{1,0:T(8,128)}, f32[3456,128]{1,0:T(8,128)}) custom-call(f32[240,2048]{1,0:T(8,128)S(1)} %get-tuple-element.96.u, f32[240,2048]{1,0:T(8,128)S(1)} %get-tuple-element.55.g, f32[8,2048]{1,0:T(8,128)S(1)} %get-tuple-element.56.csr, s32[4]{0:T(128)S(1)} %pad_add_fusion.idx, f32[40,512]{1,0:T(8,128)S(1)} %collective-permute-done.32.r1, ...), custom_call_target="tpu_custom_call" | custom-call | tf_op jit(solution)/shard_map/pallas_call | solution.py:44
  (48 shorter events, 1.1 us)
Async XLA Ops:
  2.4 0.9 copy-start.1
  3.3 0.9 copy-start.2
  4.3 0.9 copy-start.3
  5.2 0.9 copy-start.4
  6.1 0.8 copy-start.6
  8.0 1.5 %copy-start = (f32[216,4,4,128]{3,2,1,0:T(4,128)S(1)}, f32[216,4,4,128]{3,2,1,0:T(4,128)}, u32[]{:S(2)}) copy-start(f32[216,4,4,128]{3,2,1,0:T(4,128)} %param.13) | copy-start | bytes 5308420
  9.5 0.7 copy-start.7
  10.2 0.7 copy-start.9
  14.4 13.7 %collective-permute-start.2 = (f32[48,512]{1,0:T(8,128)S(1)}, f32[48,512]{1,0:T(8,128)S(1)}, u32[]{:S(2)}, u32[]{:S(2)}) collective-permute-start(f32[48,512]{1,0:T(8,128)S(1)} %get-tuple-element.59), channel_id=1, source_target_pairs={{0,1},{1,0},{2,3},{3,2},{4,5},{5,4},{6,7},{7,6},{8,9},{9,8},{10,11... | collective-permute-start | bytes 294920 | tf_op jit(solution)/shard_map/ppermute | solution.py:522
  14.5 13.7 %collective-permute-start.3 = (f32[48,512]{1,0:T(8,128)S(1)}, f32[48,512]{1,0:T(8,128)S(1)}, u32[]{:S(2)}, u32[]{:S(2)}) collective-permute-start(f32[48,512]{1,0:T(8,128)S(1)} %get-tuple-element.60), channel_id=1, source_target_pairs={{0,31},{1,2},{2,1},{3,4},{4,3},{5,6},{6,5},{7,8},{8,7},{9,10},{10,... | collective-permute-start | bytes 294920 | tf_op jit(solution)/shard_map/ppermute | solution.py:522
  20.9 4.4 %collective-permute-start = (f32[40,512]{1,0:T(8,128)S(1)}, f32[40,512]{1,0:T(8,128)S(1)}, u32[]{:S(2)}, u32[]{:S(2)}) collective-permute-start(f32[40,512]{1,0:T(8,128)S(1)} %get-tuple-element.57), channel_id=1, source_target_pairs={{0,32},{32,0},{64,96},{96,64},{1,33},{33,1},{65,97},{97,65},{2,34}... | collective-permute-start | bytes 245768 | tf_op jit(solution)/shard_map/ppermute | solution.py:522
  22.5 5.7 %collective-permute-start.1 = (f32[40,512]{1,0:T(8,128)S(1)}, f32[40,512]{1,0:T(8,128)S(1)}, u32[]{:S(2)}, u32[]{:S(2)}) collective-permute-start(f32[40,512]{1,0:T(8,128)S(1)} %get-tuple-element.58), channel_id=1, source_target_pairs={{0,96},{32,64},{64,32},{96,0},{1,97},{33,65},{65,33},{97,1},{2,98}... | collective-permute-start | bytes 245768 | tf_op jit(solution)/shard_map/ppermute | solution.py:522
  31.5 7.5 %collective-permute-start.6 = (f32[48,512]{1,0:T(8,128)S(1)}, f32[48,512]{1,0:T(8,128)S(1)}, u32[]{:S(2)}, u32[]{:S(2)}) collective-permute-start(f32[48,512]{1,0:T(8,128)S(1)} %get-tuple-element.65), channel_id=1, source_target_pairs={{0,1},{1,0},{2,3},{3,2},{4,5},{5,4},{6,7},{7,6},{8,9},{9,8},{10,11... | collective-permute-start | bytes 294920 | tf_op jit(solution)/shard_map/ppermute | solution.py:522
  31.6 7.4 %collective-permute-start.7 = (f32[48,512]{1,0:T(8,128)S(1)}, f32[48,512]{1,0:T(8,128)S(1)}, u32[]{:S(2)}, u32[]{:S(2)}) collective-permute-start(f32[48,512]{1,0:T(8,128)S(1)} %get-tuple-element.66), channel_id=1, source_target_pairs={{0,31},{1,2},{2,1},{3,4},{4,3},{5,6},{6,5},{7,8},{8,7},{9,10},{10,... | collective-permute-start | bytes 294920 | tf_op jit(solution)/shard_map/ppermute | solution.py:522
  32.1 4.4 %collective-permute-start.4 = (f32[40,512]{1,0:T(8,128)S(1)}, f32[40,512]{1,0:T(8,128)S(1)}, u32[]{:S(2)}, u32[]{:S(2)}) collective-permute-start(f32[40,512]{1,0:T(8,128)S(1)} %get-tuple-element.63), channel_id=1, source_target_pairs={{0,32},{32,0},{64,96},{96,64},{1,33},{33,1},{65,97},{97,65},{2,34}... | collective-permute-start | bytes 245768 | tf_op jit(solution)/shard_map/ppermute | solution.py:522
  33.3 5.7 %collective-permute-start.5 = (f32[40,512]{1,0:T(8,128)S(1)}, f32[40,512]{1,0:T(8,128)S(1)}, u32[]{:S(2)}, u32[]{:S(2)}) collective-permute-start(f32[40,512]{1,0:T(8,128)S(1)} %get-tuple-element.64), channel_id=1, source_target_pairs={{0,96},{32,64},{64,32},{96,0},{1,97},{33,65},{65,33},{97,1},{2,98}... | collective-permute-start | bytes 245768 | tf_op jit(solution)/shard_map/ppermute | solution.py:522
  41.8 33.7 %copy-start.8 = (f32[8,8]{1,0:T(8,128)S(1)}, f32[8,8]{1,0:T(8,128)}, u32[]{:S(2)}) copy-start(f32[8,8]{1,0:T(8,128)} %kc.3) | copy-start | bytes 772
  41.9 8.1 %collective-permute-start.10 = (f32[32,512]{1,0:T(8,128)S(1)}, f32[32,512]{1,0:T(8,128)S(1)}, u32[]{:S(2)}, u32[]{:S(2)}) collective-permute-start(f32[32,512]{1,0:T(8,128)S(1)} %get-tuple-element.72), channel_id=1, source_target_pairs={{0,1},{1,0},{2,3},{3,2},{4,5},{5,4},{6,7},{7,6},{8,9},{9,8},{10,11... | collective-permute-start | bytes 196616 | tf_op jit(solution)/shard_map/ppermute | solution.py:522
  41.9 8.0 %collective-permute-start.11 = (f32[32,512]{1,0:T(8,128)S(1)}, f32[32,512]{1,0:T(8,128)S(1)}, u32[]{:S(2)}, u32[]{:S(2)}) collective-permute-start(f32[32,512]{1,0:T(8,128)S(1)} %get-tuple-element.73), channel_id=1, source_target_pairs={{0,31},{1,2},{2,1},{3,4},{4,3},{5,6},{6,5},{7,8},{8,7},{9,10},{10,... | collective-permute-start | bytes 196616 | tf_op jit(solution)/shard_map/ppermute | solution.py:522
  44.2 3.9 %collective-permute-start.8 = (f32[16,512]{1,0:T(8,128)S(1)}, f32[16,512]{1,0:T(8,128)S(1)}, u32[]{:S(2)}, u32[]{:S(2)}) collective-permute-start(f32[16,512]{1,0:T(8,128)S(1)} %get-tuple-element.70), channel_id=1, source_target_pairs={{0,32},{32,0},{64,96},{96,64},{1,33},{33,1},{65,97},{97,65},{2,34}... | collective-permute-start | bytes 98312 | tf_op jit(solution)/shard_map/ppermute | solution.py:522
  44.8 5.1 %collective-permute-start.9 = (f32[16,512]{1,0:T(8,128)S(1)}, f32[16,512]{1,0:T(8,128)S(1)}, u32[]{:S(2)}, u32[]{:S(2)}) collective-permute-start(f32[16,512]{1,0:T(8,128)S(1)} %get-tuple-element.71), channel_id=1, source_target_pairs={{0,96},{32,64},{64,32},{96,0},{1,97},{33,65},{65,33},{97,1},{2,98}... | collective-permute-start | bytes 98312 | tf_op jit(solution)/shard_map/ppermute | solution.py:522
  51.1 7.2 %collective-permute-start.14 = (f32[32,512]{1,0:T(8,128)S(1)}, f32[32,512]{1,0:T(8,128)S(1)}, u32[]{:S(2)}, u32[]{:S(2)}) collective-permute-start(f32[32,512]{1,0:T(8,128)S(1)} %get-tuple-element.79), channel_id=1, source_target_pairs={{0,1},{1,0},{2,3},{3,2},{4,5},{5,4},{6,7},{7,6},{8,9},{9,8},{10,11... | collective-permute-start | bytes 196616 | tf_op jit(solution)/shard_map/ppermute | solution.py:522
  51.2 7.1 %collective-permute-start.15 = (f32[32,512]{1,0:T(8,128)S(1)}, f32[32,512]{1,0:T(8,128)S(1)}, u32[]{:S(2)}, u32[]{:S(2)}) collective-permute-start(f32[32,512]{1,0:T(8,128)S(1)} %get-tuple-element.80), channel_id=1, source_target_pairs={{0,31},{1,2},{2,1},{3,4},{4,3},{5,6},{6,5},{7,8},{8,7},{9,10},{10,... | collective-permute-start | bytes 196616 | tf_op jit(solution)/shard_map/ppermute | solution.py:522
  52.6 3.9 %collective-permute-start.12 = (f32[16,512]{1,0:T(8,128)S(1)}, f32[16,512]{1,0:T(8,128)S(1)}, u32[]{:S(2)}, u32[]{:S(2)}) collective-permute-start(f32[16,512]{1,0:T(8,128)S(1)} %get-tuple-element.77), channel_id=1, source_target_pairs={{0,32},{32,0},{64,96},{96,64},{1,33},{33,1},{65,97},{97,65},{2,34}... | collective-permute-start | bytes 98312 | tf_op jit(solution)/shard_map/ppermute | solution.py:522
  53.1 5.1 %collective-permute-start.13 = (f32[16,512]{1,0:T(8,128)S(1)}, f32[16,512]{1,0:T(8,128)S(1)}, u32[]{:S(2)}, u32[]{:S(2)}) collective-permute-start(f32[16,512]{1,0:T(8,128)S(1)} %get-tuple-element.78), channel_id=1, source_target_pairs={{0,96},{32,64},{64,32},{96,0},{1,97},{33,65},{65,33},{97,1},{2,98}... | collective-permute-start | bytes 98312 | tf_op jit(solution)/shard_map/ppermute | solution.py:522
  59.5 5.8 %collective-permute-start.17 = (f32[176,128]{1,0:T(8,128)S(1)}, f32[176,128]{1,0:T(8,128)S(1)}, u32[]{:S(2)}, u32[]{:S(2)}) collective-permute-start(f32[176,128]{1,0:T(8,128)S(1)} %shard_map.145.own), channel_id=1, source_target_pairs={{0,96},{32,64},{64,32},{96,0},{1,97},{33,65},{65,33},{97,1},{2,98}... | collective-permute-start | bytes 270344 | tf_op jit(solution)/shard_map/ppermute | solution.py:522
  61.7 4.5 %collective-permute-start.16 = (f32[176,128]{1,0:T(8,128)S(1)}, f32[176,128]{1,0:T(8,128)S(1)}, u32[]{:S(2)}, u32[]{:S(2)}) collective-permute-start(f32[176,128]{1,0:T(8,128)S(1)} %shard_map.145.own), channel_id=1, source_target_pairs={{0,32},{32,0},{64,96},{96,64},{1,33},{33,1},{65,97},{97,65},{2,34}... | collective-permute-start | bytes 270344 | tf_op jit(solution)/shard_map/ppermute | solution.py:522
  66.3 9.3 %collective-permute-start.19 = (f32[528,128]{1,0:T(8,128)S(1)}, f32[528,128]{1,0:T(8,128)S(1)}, u32[]{:S(2)}, u32[]{:S(2)}) collective-permute-start(f32[528,128]{1,0:T(8,128)S(1)} %pad_maximum_fusion), channel_id=1, source_target_pairs={{0,31},{1,2},{2,1},{3,4},{4,3},{5,6},{6,5},{7,8},{8,7},{9,10},{10,... | collective-permute-start | bytes 811016 | tf_op jit(solution)/shard_map/ppermute | solution.py:522
  67.1 8.5 %collective-permute-start.18 = (f32[528,128]{1,0:T(8,128)S(1)}, f32[528,128]{1,0:T(8,128)S(1)}, u32[]{:S(2)}, u32[]{:S(2)}) collective-permute-start(f32[528,128]{1,0:T(8,128)S(1)} %pad_maximum_fusion), channel_id=1, source_target_pairs={{0,1},{1,0},{2,3},{3,2},{4,5},{5,4},{6,7},{7,6},{8,9},{9,8},{10,11... | collective-permute-start | bytes 811016 | tf_op jit(solution)/shard_map/ppermute | solution.py:522
  79.0 5.6 %collective-permute-start.21 = (f32[128,128]{1,0:T(8,128)S(1)}, f32[128,128]{1,0:T(8,128)S(1)}, u32[]{:S(2)}, u32[]{:S(2)}) collective-permute-start(f32[128,128]{1,0:T(8,128)S(1)} %get-tuple-element.82.own), channel_id=1, source_target_pairs={{0,96},{32,64},{64,32},{96,0},{1,97},{33,65},{65,33},{97,1},{2,98}... | collective-permute-start | bytes 196616 | tf_op jit(solution)/shard_map/ppermute | solution.py:522
  80.3 4.3 %collective-permute-start.20 = (f32[128,128]{1,0:T(8,128)S(1)}, f32[128,128]{1,0:T(8,128)S(1)}, u32[]{:S(2)}, u32[]{:S(2)}) collective-permute-start(f32[128,128]{1,0:T(8,128)S(1)} %get-tuple-element.82.own), channel_id=1, source_target_pairs={{0,32},{32,0},{64,96},{96,64},{1,33},{33,1},{65,97},{97,65},{2,34}... | collective-permute-start | bytes 196616 | tf_op jit(solution)/shard_map/ppermute | solution.py:522
  84.6 8.5 %collective-permute-start.23 = (f32[384,128]{1,0:T(8,128)S(1)}, f32[384,128]{1,0:T(8,128)S(1)}, u32[]{:S(2)}, u32[]{:S(2)}) collective-permute-start(f32[384,128]{1,0:T(8,128)S(1)} %constant_dynamic-update-slice_fusion), channel_id=1, source_target_pairs={{0,31},{1,2},{2,1},{3,4},{4,3},{5,6},{6,5},{7,8},{8,7},{9,10},{10,... | collective-permute-start | bytes 589832 | tf_op jit(solution)/shard_map/ppermute | solution.py:522
  84.7 8.4 %collective-permute-start.22 = (f32[384,128]{1,0:T(8,128)S(1)}, f32[384,128]{1,0:T(8,128)S(1)}, u32[]{:S(2)}, u32[]{:S(2)}) collective-permute-start(f32[384,128]{1,0:T(8,128)S(1)} %constant_dynamic-update-slice_fusion), channel_id=1, source_target_pairs={{0,1},{1,0},{2,3},{3,2},{4,5},{5,4},{6,7},{7,6},{8,9},{9,8},{10,11... | collective-permute-start | bytes 589832 | tf_op jit(solution)/shard_map/ppermute | solution.py:522
  95.5 5.5 %collective-permute-start.26 = (f32[32,512]{1,0:T(8,128)S(1)}, f32[32,512]{1,0:T(8,128)S(1)}, u32[]{:S(2)}, u32[]{:S(2)}) collective-permute-start(f32[32,512]{1,0:T(8,128)S(1)} %get-tuple-element.88), channel_id=1, source_target_pairs={{0,1},{1,0},{2,3},{3,2},{4,5},{5,4},{6,7},{7,6},{8,9},{9,8},{10,11... | collective-permute-start | bytes 196616 | tf_op jit(solution)/shard_map/ppermute | solution.py:522
  95.5 7.1 %collective-permute-start.27 = (f32[32,512]{1,0:T(8,128)S(1)}, f32[32,512]{1,0:T(8,128)S(1)}, u32[]{:S(2)}, u32[]{:S(2)}) collective-permute-start(f32[32,512]{1,0:T(8,128)S(1)} %get-tuple-element.89), channel_id=1, source_target_pairs={{0,31},{1,2},{2,1},{3,4},{4,3},{5,6},{6,5},{7,8},{8,7},{9,10},{10,... | collective-permute-start | bytes 196616 | tf_op jit(solution)/shard_map/ppermute | solution.py:522
  95.6 4.0 %collective-permute-start.24 = (f32[16,512]{1,0:T(8,128)S(1)}, f32[16,512]{1,0:T(8,128)S(1)}, u32[]{:S(2)}, u32[]{:S(2)}) collective-permute-start(f32[16,512]{1,0:T(8,128)S(1)} %get-tuple-element.86), channel_id=1, source_target_pairs={{0,32},{32,0},{64,96},{96,64},{1,33},{33,1},{65,97},{97,65},{2,34}... | collective-permute-start | bytes 98312 | tf_op jit(solution)/shard_map/ppermute | solution.py:522
  95.7 5.2 %collective-permute-start.25 = (f32[16,512]{1,0:T(8,128)S(1)}, f32[16,512]{1,0:T(8,128)S(1)}, u32[]{:S(2)}, u32[]{:S(2)}) collective-permute-start(f32[16,512]{1,0:T(8,128)S(1)} %get-tuple-element.87), channel_id=1, source_target_pairs={{0,96},{32,64},{64,32},{96,0},{1,97},{33,65},{65,33},{97,1},{2,98}... | collective-permute-start | bytes 98312 | tf_op jit(solution)/shard_map/ppermute | solution.py:522
  104.2 8.4 %collective-permute-start.30 = (f32[48,512]{1,0:T(8,128)S(1)}, f32[48,512]{1,0:T(8,128)S(1)}, u32[]{:S(2)}, u32[]{:S(2)}) collective-permute-start(f32[48,512]{1,0:T(8,128)S(1)} %get-tuple-element.94), channel_id=1, source_target_pairs={{0,1},{1,0},{2,3},{3,2},{4,5},{5,4},{6,7},{7,6},{8,9},{9,8},{10,11... | collective-permute-start | bytes 294920 | tf_op jit(solution)/shard_map/ppermute | solution.py:522
  104.3 8.3 %collective-permute-start.31 = (f32[48,512]{1,0:T(8,128)S(1)}, f32[48,512]{1,0:T(8,128)S(1)}, u32[]{:S(2)}, u32[]{:S(2)}) collective-permute-start(f32[48,512]{1,0:T(8,128)S(1)} %get-tuple-element.95), channel_id=1, source_target_pairs={{0,31},{1,2},{2,1},{3,4},{4,3},{5,6},{6,5},{7,8},{8,7},{9,10},{10,... | collective-permute-start | bytes 294920 | tf_op jit(solution)/shard_map/ppermute | solution.py:522
  106.4 4.4 %collective-permute-start.28 = (f32[40,512]{1,0:T(8,128)S(1)}, f32[40,512]{1,0:T(8,128)S(1)}, u32[]{:S(2)}, u32[]{:S(2)}) collective-permute-start(f32[40,512]{1,0:T(8,128)S(1)} %get-tuple-element.92), channel_id=1, source_target_pairs={{0,32},{32,0},{64,96},{96,64},{1,33},{33,1},{65,97},{97,65},{2,34}... | collective-permute-start | bytes 245768 | tf_op jit(solution)/shard_map/ppermute | solution.py:522
  107.0 5.7 %collective-permute-start.29 = (f32[40,512]{1,0:T(8,128)S(1)}, f32[40,512]{1,0:T(8,128)S(1)}, u32[]{:S(2)}, u32[]{:S(2)}) collective-permute-start(f32[40,512]{1,0:T(8,128)S(1)} %get-tuple-element.93), channel_id=1, source_target_pairs={{0,96},{32,64},{64,32},{96,0},{1,97},{33,65},{65,33},{97,1},{2,98}... | collective-permute-start | bytes 245768 | tf_op jit(solution)/shard_map/ppermute | solution.py:522
  112.6 11.0 %copy-start.5 = (bf16[216,240]{1,0:T(8,128)(2,1)S(1)}, bf16[216,240]{1,0:T(8,128)(2,1)}, u32[]{:S(2)}) copy-start(bf16[216,240]{1,0:T(8,128)(2,1)} %constant.18.clone.from_slot) | copy-start | bytes 311044
  112.6 11.0 %copy-start.10 = (f32[4,4,128]{2,1,0:T(4,128)S(1)}, f32[4,4,128]{2,1,0:T(4,128)}, u32[]{:S(2)}) copy-start(f32[4,4,128]{2,1,0:T(4,128)} %param.23) | copy-start | bytes 24580
  115.9 7.7 %collective-permute-start.34 = (f32[48,512]{1,0:T(8,128)S(1)}, f32[48,512]{1,0:T(8,128)S(1)}, u32[]{:S(2)}, u32[]{:S(2)}) collective-permute-start(f32[48,512]{1,0:T(8,128)S(1)} %get-tuple-element.99), channel_id=1, source_target_pairs={{0,1},{1,0},{2,3},{3,2},{4,5},{5,4},{6,7},{7,6},{8,9},{9,8},{10,11... | collective-permute-start | bytes 294920 | tf_op jit(solution)/shard_map/ppermute | solution.py:522
  116.0 7.6 %collective-permute-start.35 = (f32[48,512]{1,0:T(8,128)S(1)}, f32[48,512]{1,0:T(8,128)S(1)}, u32[]{:S(2)}, u32[]{:S(2)}) collective-permute-start(f32[48,512]{1,0:T(8,128)S(1)} %get-tuple-element.100), channel_id=1, source_target_pairs={{0,31},{1,2},{2,1},{3,4},{4,3},{5,6},{6,5},{7,8},{8,7},{9,10},{10,... | collective-permute-start | bytes 294920 | tf_op jit(solution)/shard_map/ppermute | solution.py:522
  117.4 4.4 %collective-permute-start.32 = (f32[40,512]{1,0:T(8,128)S(1)}, f32[40,512]{1,0:T(8,128)S(1)}, u32[]{:S(2)}, u32[]{:S(2)}) collective-permute-start(f32[40,512]{1,0:T(8,128)S(1)} %get-tuple-element.97), channel_id=1, source_target_pairs={{0,32},{32,0},{64,96},{96,64},{1,33},{33,1},{65,97},{97,65},{2,34}... | collective-permute-start | bytes 245768 | tf_op jit(solution)/shard_map/ppermute | solution.py:522
  118.0 5.7 %collective-permute-start.33 = (f32[40,512]{1,0:T(8,128)S(1)}, f32[40,512]{1,0:T(8,128)S(1)}, u32[]{:S(2)}, u32[]{:S(2)}) collective-permute-start(f32[40,512]{1,0:T(8,128)S(1)} %get-tuple-element.98), channel_id=1, source_target_pairs={{0,96},{32,64},{64,32},{96,0},{1,97},{33,65},{65,33},{97,1},{2,98}... | collective-permute-start | bytes 245768 | tf_op jit(solution)/shard_map/ppermute | solution.py:522

commit v2 on v1

v2 whole, which is shorter than its diff:
```python
import numpy as np
import jax
import jax.numpy as jnp
from jax import lax
from jax.sharding import PartitionSpec as P
from jax.experimental import pallas as pl
from jax.experimental.pallas import tpu as pltpu

NF = 6
QF = 216
SF = 240
QM = 64
QC = 8
COLS = 16
LANES = COLS * 128
F32 = jnp.float32
BF16 = jnp.bfloat16


def fine_slots():
    slots = []
    for i in range(6):
        slots += [(i, 0, k) for k in range(6)] + [None] * 2
        slots += [(i, 5, k) for k in range(6)] + [None] * 2
        slots += [(i, j, 0) for j in range(1, 5)] + [(i, j, 5) for j in range(1, 5)]
        slots += [(i, j, k) for j in range(1, 5) for k in range(1, 5)]
    return slots


def slot_matrix():
    to_slot = np.zeros((SF, QF), np.float32)
    for slot, node in enumerate(fine_slots()):
        if node is not None:
            to_slot[slot, (node[0] * 6 + node[1]) * 6 + node[2]] = 1.0
    return to_slot


def call(kernel, outs, scratch=(), smem=(), hbm=(), cost=None):
    def run(*operands):
        specs = [
            pl.BlockSpec(
                memory_space=pltpu.SMEM if n in smem else pltpu.HBM if n in hbm else pltpu.VMEM
            )
            for n in range(len(operands))
        ]
        operands = [
            pltpu.with_memory_space_constraint(value, pltpu.HBM) if n in hbm else value
            for n, value in enumerate(operands)
        ]
        return pl.pallas_call(
            kernel,
            out_shape=tuple(jax.ShapeDtypeStruct(s, d) for s, d in outs),
            in_specs=specs,
            out_specs=tuple(pl.BlockSpec(memory_space=pltpu.VMEM) for _ in outs),
            scratch_shapes=list(scratch),
            compiler_params=pltpu.CompilerParams(vmem_limit_bytes=20 * 1024 * 1024),
            cost_estimate=cost,
        )(*operands)

    return run


def dot(a, b):
    return lax.dot_general(a, b, (((1,), (0,)), ((), ())), preferred_element_type=F32)


def dot_nt(a, b):
    return lax.dot_general(a, b, (((1,), (1,)), ((), ())), preferred_element_type=F32)


def halves(values):
    high = values.astype(BF16)
    return high, (values - high.astype(F32)).astype(BF16)


def lane_roll(values, shift):
    return jnp.concatenate(
        [
            pltpu.roll(values[:, c * 128 : (c + 1) * 128], shift % 128, 1)
            for c in range(values.shape[1] // 128)
        ],
        axis=1,
    )


def sub_roll(values, shift):
    return pltpu.roll(values, shift % values.shape[0], 0)


def sublane(shape):
    return lax.broadcasted_iota(jnp.int32, shape, 0)


def y_from_lower(values):
    parts, edge = [], jnp.zeros((values.shape[0], 128), F32)
    for x in range(4):
        parts += [edge, values[:, x * 512 : x * 512 + 384]]
    return jnp.concatenate(parts, axis=1)


def y_from_upper(values):
    parts, edge = [], jnp.zeros((values.shape[0], 128), F32)
    for x in range(4):
        parts += [values[:, x * 512 + 128 : x * 512 + 512], edge]
    return jnp.concatenate(parts, axis=1)


def y_column(values, y):
    return jnp.concatenate(
        [values[:, x * 512 + y * 128 : x * 512 + y * 128 + 128] for x in range(4)], axis=1
    )


def even(idx_ref, axis):
    return idx_ref[axis] % 2 == 0


def prepare(slot, fine, smooth, noise, mid, pmid_t, plow_t, kf, sf, nf, pmt, pm, km, plt, spread):
    def grid(rows, columns):
        return tuple(lax.broadcasted_iota(jnp.int32, (rows, columns), n) for n in range(2))

    def one_hot(n):
        row, col = grid(n, n)
        return jnp.where(row == col, 1.0, 0.0).astype(BF16)

    def wide(out, rows, high, low):
        gap = jnp.zeros((rows, 16), BF16)
        out[:, 0:256] = jnp.concatenate([high, gap], axis=1)
        out[:, 256:512] = jnp.concatenate([high, gap], axis=1)
        out[:, 512:768] = jnp.concatenate([low, gap], axis=1)

    def narrow(out, high, low):
        row, col = grid(64, 128)
        twice = jnp.where((row == col) | (row == col - 64), 1.0, 0.0).astype(BF16)
        once = jnp.where(row == col, 1.0, 0.0).astype(BF16)
        out[:, 0:128] = dot(high, twice).astype(BF16)
        out[:, 128:256] = dot(low, once).astype(BF16)

    def moved(left, part, right):
        return dot_nt(dot_nt(left, part).astype(BF16), right).astype(BF16)

    wide(sf, SF, *[moved(slot, part, slot) for part in halves(smooth)])
    wide(kf, SF, *[moved(slot, part, slot) for part in halves(fine)])
    turn = one_hot(QF)
    wide(nf, QF, *[moved(turn, part, slot) for part in halves(noise)])
    high, low = halves(pmid_t)
    wide(pmt, QM, *[dot_nt(part, slot).astype(BF16) for part in (high, low)])
    narrow(pm, *[dot_nt(slot, part).astype(BF16) for part in (high, low)])
    turn = one_hot(QM)
    narrow(km, *[dot_nt(turn, part).astype(BF16) for part in halves(mid)])
    high, low = halves(plow_t)
    rest = (plow_t - high.astype(F32) - low.astype(F32)).astype(BF16)
    gap = jnp.zeros((8, QM), BF16)
    narrow(plt, *[jnp.concatenate([part, gap], axis=0) for part in (high, low)])
    columns = dot_nt(turn, high) + dot_nt(turn, low) + dot_nt(turn, rest)
    for d in range(QC):
        spread[d] = jnp.broadcast_to(columns[:, d : d + 1], (QM, 128))


def split_fine(values, x_ref, lanes):
    high, low = halves(values)
    x_ref[0:SF, lanes] = high
    x_ref[256 : 256 + SF, lanes] = low


def clear_fine(x_ref):
    x_ref[SF:256, :] = jnp.zeros((256 - SF, LANES), BF16)
    x_ref[256 + SF : 512, :] = jnp.zeros((256 - SF, LANES), BF16)


def fine_product(w_ref, x_ref, lanes):
    return dot(w_ref[:, 0:512], x_ref[:, lanes]) + dot(w_ref[:, 512:768], x_ref[0:256, lanes])


def mid_product(w_ref, values, x_ref):
    high, low = halves(values)
    x_ref[0:64, :] = high
    x_ref[64:128, :] = low
    x_ref[128:192, :] = high
    x_ref[192:256, :] = jnp.zeros((64, LANES), BF16)
    return dot(w_ref[...], x_ref[...])


def chunk(n):
    return slice(n * 512, n * 512 + 512)


def fine_sends(u_ref, idx, s1, s2, s3, s4):
    x_even, y_even = even(idx, 0), even(idx, 1)
    upper, lower = u_ref[200:240, 1536:2048], u_ref[0:40, 0:512]
    s1[0:40, :] = jnp.where(x_even, upper, lower)
    s2[0:40, :] = jnp.where(x_even, lower, upper)
    for i in range(6):
        upper = y_column(u_ref[40 * i + 8 : 40 * i + 16, :], 3)
        lower = y_column(u_ref[40 * i : 40 * i + 8, :], 0)
        s3[8 * i : 8 * i + 8, :] = jnp.where(y_even, upper, lower)
        s4[8 * i : 8 * i + 8, :] = jnp.where(y_even, lower, upper)


def fine_local_kernel(u_ref, g_ref, csr, kf, t_ref, x_ref):
    clear_fine(x_ref)
    for n in range(4):
        u = u_ref[:, chunk(n)]
        split_fine(u, x_ref, chunk(n))
        t_ref[:, chunk(n)] = g_ref[:, chunk(n)] - 4.0 * u - fine_product(kf, x_ref, chunk(n))
    t_ref[0:40, 512:2048] += csr[0:1, 512:2048] * u_ref[200:240, 0:1536]
    t_ref[200:240, 0:1536] += csr[1:2, 0:1536] * u_ref[0:40, 512:2048]
    row = sublane((8, LANES))
    for i in range(6):
        base = 40 * i
        first, last, sides = (u_ref[base + 8 * n : base + 8 * n + 8, :] for n in range(3))
        t0 = csr[2:3, :] * y_from_lower(last)
        t1 = csr[3:4, :] * y_from_upper(first)
        for n, tile, extra in ((0, first, t0), (1, last, t1)):
            lower = csr[4:5, :] * sub_roll(lane_roll(tile, 1), 3)
            upper = csr[5:6, :] * sub_roll(lane_roll(tile, -1), 5)
            t_ref[base + 8 * n : base + 8 * n + 8, :] += (
                extra + jnp.where(row == 0, lower, 0.0) + jnp.where(row == 5, upper, 0.0)
            )
        lower = csr[4:5, :] * sub_roll(lane_roll(sides, 1), 4)
        upper = csr[5:6, :] * sub_roll(lane_roll(sides, -1), 4)
        t_ref[base + 16 : base + 24, :] += jnp.where(row < 4, lower, upper)


def fine_edges(n, t_in, csr, idx, r1, r2, r3, r4, t_ref):
    x_even, y_even = even(idx, 0), even(idx, 1)
    lanes = chunk(n)
    t_ref[:, lanes] = t_in[:, lanes]
    if n == 0:
        below = jnp.where(x_even, r2[0:40, :], r1[0:40, :])
        t_ref[0:40, lanes] += csr[0:1, lanes] * below
    if n == 3:
        above = jnp.where(x_even, r1[0:40, :], r2[0:40, :])
        t_ref[200:240, lanes] += csr[1:2, lanes] * above
    edge = slice(n * 128, n * 128 + 128)
    first, last = (slice(n * 512 + y * 128, n * 512 + y * 128 + 128) for y in (0, 3))
    for i in range(6):
        rows = slice(8 * i, 8 * i + 8)
        below = jnp.where(y_even, r4[rows, edge], r3[rows, edge])
        above = jnp.where(y_even, r3[rows, edge], r4[rows, edge])
        t_ref[40 * i : 40 * i + 8, first] += csr[2:3, first] * below
        t_ref[40 * i + 8 : 40 * i + 16, last] += csr[3:4, last] * above


def fine_update(u_ref, t_in, csr, idx, received, out_ref, sf, x_ref, t_ref):
    clear_fine(x_ref)
    for n in range(4):
        fine_edges(n, t_in, csr, idx, *received, t_ref)
        t = t_ref[:, chunk(n)]
        split_fine(t, x_ref, chunk(n))
        out_ref[:, chunk(n)] = u_ref[:, chunk(n)] + 0.25 * t + fine_product(sf, x_ref, chunk(n))


def first_kernel(
    seed_in, scale_in, coef_in, slot_in, smooth_in, fine_in, noise_in, mid_in, pmid_in, plow_in, idx,
    g, u1, csx, csr, s1, s2, s3, s4, kf, sf, nf, pmt, pm, km, plt, spread,
    x_ref, seed, scale, coef, slot, smooth, fine, noise, mid, pmid, plow, done,
):
    copies = {}
    for n, (name, source, target) in enumerate(
        (
            ("slot", slot_in, slot),
            ("smooth", smooth_in, smooth),
            ("fine", fine_in, fine),
            ("noise", noise_in, noise),
            ("pmid", pmid_in, pmid),
            ("plow", plow_in, plow),
            ("mid", mid_in, mid),
            ("scale", scale_in, scale),
            ("coef", coef_in, coef),
            ("seed", seed_in, seed),
        )
    ):
        copies[name] = pltpu.make_async_copy(source, target, done.at[n])
        copies[name].start()
    clear_fine(x_ref)
    x_ref[QF:SF, :] = jnp.zeros((SF - QF, LANES), BF16)
    x_ref[256 + QF : 256 + SF, :] = jnp.zeros((SF - QF, LANES), BF16)
    csr[...] = jnp.zeros((8, LANES), F32)
    csx[...] = jnp.zeros((16, 512), F32)
    for name in ("slot", "smooth", "fine", "noise", "pmid", "plow", "mid"):
        copies[name].wait()
    matrices = (ref[...] for ref in (slot, fine, smooth, noise, mid, pmid, plow))
    prepare(*matrices, kf, sf, nf, pmt, pm, km, plt, spread)
    copies["scale"].wait()
    copies["coef"].wait()
    over = 1.0 / scale[...]
    lane = lax.broadcasted_iota(jnp.int32, (1, 128), 1)
    for c in range(COLS):
        x, y = c // 4, c % 4
        lanes = slice(c * 128, c * 128 + 128)
        for d in range(3):
            value = coef[16 * d + c : 16 * d + c + 1, :] * over[c : c + 1, :]
            csx[4 * x + d : 4 * x + d + 1, y * 128 : y * 128 + 128] = value
            low, high = 0.9 * value, 0.3 * value
            if d == 0 and x == 0:
                low = jnp.where(idx[0] == 0, 0.0, low)
            if d == 0 and x == 3:
                high = jnp.where(idx[0] == idx[2] - 1, 0.0, high)
            if d == 1 and y == 0:
                low = jnp.where(idx[1] == 0, 0.0, low)
            if d == 1 and y == 3:
                high = jnp.where(idx[1] == idx[3] - 1, 0.0, high)
            if d == 2:
                low = jnp.where(lane == 0, 0.0, low)
                high = jnp.where(lane == 127, 0.0, high)
            csr[2 * d : 2 * d + 1, lanes] = low
            csr[2 * d + 1 : 2 * d + 2, lanes] = high
    copies["seed"].wait()
    for c in range(COLS):
        lanes = slice(c * 128, c * 128 + 128)
        values = seed[pl.ds(c, QF, stride=COLS), :] * over[c : c + 1, :]
        high, low = halves(values)
        rest = (values - high.astype(F32) - low.astype(F32)).astype(BF16)
        g[:, lanes] = dot(slot[...], high) + dot(slot[...], low) + dot(slot[...], rest)
    for n in range(4):
        values = g[:, chunk(n)]
        split_fine(values, x_ref, chunk(n))
        u1[:, chunk(n)] = 0.25 * values + fine_product(sf, x_ref, chunk(n))
    fine_sends(u1, idx, s1, s2, s3, s4)
    x_even = even(idx, 0)
    far, near = csx[4:16, :], csx[0:12, :]
    gap = jnp.zeros((4, 512), F32)
    s1[40:56, :] = jnp.concatenate([jnp.where(x_even, far, near), gap], axis=0)
    s2[40:56, :] = jnp.concatenate([jnp.where(x_even, near, far), gap], axis=0)


def spread_kernel(u, t_in, csr, idx, r1, r2, r3, r4, sf, csx, out, s1, s2, s3, s4, x_ref, t_ref):
    fine_update(u, t_in, csr, idx, (r1, r2, r3, r4), out, sf, x_ref, t_ref)
    fine_sends(out, idx, s1, s2, s3, s4)
    x_even, y_even = even(idx, 0), even(idx, 1)
    left = jnp.where(x_even, r2[40:56, :], r1[40:56, :])
    right = jnp.where(x_even, r1[40:56, :], r2[40:56, :])
    planes = jnp.concatenate([left[0:12], csx[...], right[0:12]], axis=0)
    gap = jnp.zeros((40, 128), F32)
    far, near = planes[:, 128:512], planes[:, 0:384]
    s3[48:88, :] = jnp.concatenate([jnp.where(y_even, far, near), gap], axis=1)
    s4[48:88, :] = jnp.concatenate([jnp.where(y_even, near, far), gap], axis=1)


def coefficient_kernel(idx, csx, r1, r2, r3, r4, coef):
    x_even, y_even = even(idx, 0), even(idx, 1)
    left = jnp.where(x_even, r2[40:56, :], r1[40:56, :])
    right = jnp.where(x_even, r1[40:56, :], r2[40:56, :])
    planes = jnp.concatenate([left[0:12], csx[...], right[0:12]], axis=0)
    below = jnp.where(y_even, r4[48:88, :], r3[48:88, :])
    above = jnp.where(y_even, r3[48:88, :], r4[48:88, :])
    first_x, last_x = idx[0] == 0, idx[0] == idx[2] - 1
    first_y, last_y = idx[1] == 0, idx[1] == idx[3] - 1
    lane = lax.broadcasted_iota(jnp.int32, (1, 128), 1)
    coef[...] = jnp.zeros((6, WROWS, 128), F32)
    for plane in range(WX):
        for y in range(-3, 7):
            source, at = (below, y + 3) if y < 0 else (planes, y) if y < 4 else (above, y - 4)
            row = slice(plane * 16 + 4 + y, plane * 16 + 5 + y)
            for d in range(3):
                value = source[4 * plane + d : 4 * plane + d + 1, at * 128 : at * 128 + 128]
                low, high = 0.9 * value, 0.3 * value
                if d == 0 and plane == 3:
                    low = jnp.where(first_x, 0.0, low)
                if d == 0 and plane == 6:
                    high = jnp.where(last_x, 0.0, high)
                if d == 1 and y == 0:
                    low = jnp.where(first_y, 0.0, low)
                if d == 1 and y == 3:
                    high = jnp.where(last_y, 0.0, high)
                if d == 2:
                    low = jnp.where(lane == 0, 0.0, low)
                    high = jnp.where(lane == 127, 0.0, high)
                coef[2 * d, row, :] = low
                coef[2 * d + 1, row, :] = high


def sweep_kernel(u, t_in, csr, idx, r1, r2, r3, r4, sf, out, s1, s2, s3, s4, x_ref, t_ref):
    fine_update(u, t_in, csr, idx, (r1, r2, r3, r4), out, sf, x_ref, t_ref)
    fine_sends(out, idx, s1, s2, s3, s4)


def restrict_kernel(t_in, csr, idx, r1, r2, r3, r4, pmt, gm, m1, s1, s2, s3, s4, x_ref, t_ref):
    clear_fine(x_ref)
    for n in range(4):
        fine_edges(n, t_in, csr, idx, r1, r2, r3, r4, t_ref)
        split_fine(t_ref[:, chunk(n)], x_ref, chunk(n))
        value = fine_product(pmt, x_ref, chunk(n))
        gm[:, chunk(n)] = value
        m1[:, chunk(n)] = 0.2 * value
    mid_sends(m1, idx, s1, s2, s3, s4)


def last_kernel(
    u, t_in, csr, idx, r1, r2, r3, r4, sf, nf, from_slot, inc, out, prev, x_ref, t_ref, w_ref
):
    fine_update(u, t_in, csr, idx, (r1, r2, r3, r4), w_ref, sf, x_ref, t_ref)
    slot = from_slot[...]
    for n in range(4):
        values = w_ref[:, chunk(n)]
        split_fine(values, x_ref, chunk(n))
        high, low = halves(values)
        rest = (values - high.astype(F32) - low.astype(F32)).astype(BF16)
        natural = dot(slot, high) + dot(slot, low) + dot(slot, rest)
        noise = fine_product(nf, x_ref, chunk(n))
        for y in range(4):
            c = 4 * n + y
            lanes = slice(y * 128, y * 128 + 128)
            out[pl.ds(c, QF, stride=COLS), :] = natural[:, lanes]
            prev[pl.ds(c, QF, stride=COLS), :] = (
                natural[:, lanes] + inc[c : c + 1, :] * noise[:, lanes]
            )


def mid_sends(m_ref, idx, s1, s2, s3, s4):
    x_even, y_even = even(idx, 0), even(idx, 1)
    upper, lower = m_ref[48:64, 1536:2048], m_ref[0:16, 0:512]
    s1[...] = jnp.where(x_even, upper, lower)
    s2[...] = jnp.where(x_even, lower, upper)
    for i in range(4):
        upper = y_column(m_ref[16 * i + 8 : 16 * i + 16, :], 3)
        lower = y_column(m_ref[16 * i : 16 * i + 8, :], 0)
        s3[8 * i : 8 * i + 8, :] = jnp.where(y_even, upper, lower)
        s4[8 * i : 8 * i + 8, :] = jnp.where(y_even, lower, upper)


def mid_edges(idx, r1, r2, r3, r4):
    x_even, y_even = even(idx, 0), even(idx, 1)
    return (
        jnp.where(x_even, r2[...], r1[...]),
        jnp.where(x_even, r1[...], r2[...]),
        jnp.where(y_even, r4[...], r3[...]),
        jnp.where(y_even, r3[...], r4[...]),
    )


def mid_local(m_ref, g_ref, csr, km, t_ref, x_ref):
    m = m_ref[...]
    t_ref[...] = g_ref[...] - 4.0 * m - mid_product(km, m, x_ref)
    t_ref[0:16, 512:2048] += csr[0:1, 512:2048] * m_ref[48:64, 0:1536]
    t_ref[48:64, 0:1536] += csr[1:2, 0:1536] * m_ref[0:16, 512:2048]
    row = sublane((8, LANES))
    for i in range(4):
        base = 16 * i
        first, last = m_ref[base : base + 8, :], m_ref[base + 8 : base + 16, :]
        extra0 = csr[2:3, :] * sub_roll(y_from_lower(last), 4)
        extra1 = csr[3:4, :] * sub_roll(y_from_upper(first), 4)
        for n, tile, extra in (
            (0, first, jnp.where(row < 4, extra0, 0.0)),
            (1, last, jnp.where(row >= 4, extra1, 0.0)),
        ):
            lower = csr[4:5, :] * sub_roll(lane_roll(tile, 1), 5)
            upper = csr[5:6, :] * sub_roll(lane_roll(tile, -1), 3)
            t_ref[base + 8 * n : base + 8 * n + 8, :] += (
                extra + jnp.where(row % 4 == 0, lower, 0.0) + jnp.where(row % 4 == 3, upper, 0.0)
            )


def mid_edge_terms(csr, edges, t_ref):
    below_x, above_x, below_y, above_y = edges
    t_ref[0:16, 0:512] += csr[0:1, 0:512] * below_x
    t_ref[48:64, 1536:2048] += csr[1:2, 1536:2048] * above_x
    row = sublane((8, 128))
    for i in range(4):
        rows = slice(8 * i, 8 * i + 8)
        for x in range(4):
            edge = slice(x * 128, x * 128 + 128)
            first, last = (slice(x * 512 + y * 128, x * 512 + y * 128 + 128) for y in (0, 3))
            below = csr[2:3, first] * sub_roll(below_y[rows, edge], 4)
            above = csr[3:4, last] * sub_roll(above_y[rows, edge], 4)
            t_ref[16 * i : 16 * i + 8, first] += jnp.where(row < 4, below, 0.0)
            t_ref[16 * i + 8 : 16 * i + 16, last] += jnp.where(row >= 4, above, 0.0)


def mid_local_kernel(m_ref, g_ref, csr, km, t_ref, x_ref):
    mid_local(m_ref, g_ref, csr, km, t_ref, x_ref)


def mid_kernel(m, t_in, csr, idx, r1, r2, r3, r4, out, s1, s2, s3, s4, t_ref):
    t_ref[...] = t_in[...]
    mid_edge_terms(csr, mid_edges(idx, r1, r2, r3, r4), t_ref)
    out[...] = m[...] + 0.2 * t_ref[...]
    mid_sends(out, idx, s1, s2, s3, s4)


def block_sends(pay, idx, s1, s2):
    x_even = even(idx, 0)
    far, near = pay[32:128, :], pay[0:96, :]
    s1[...] = jnp.where(x_even, far, near)
    s2[...] = jnp.where(x_even, near, far)


def row_kernel(idx, own, r1, r2, s3, s4):
    x_even, y_even = even(idx, 0), even(idx, 1)
    for plane in range(WX):
        tiles = []
        for y in range(4):
            if 3 <= plane < 7:
                at = QC * (4 * (plane - 3) + y)
                tiles.append(own[at : at + QC, :])
            else:
                at = QC * (4 * (plane % 7) + y)
                one, two = r1[at : at + QC, :], r2[at : at + QC, :]
                tiles.append(jnp.where(x_even == (plane < 3), two, one))
        for y in range(3):
            rows = slice(QC * (3 * plane + y), QC * (3 * plane + y) + QC)
            s3[rows, :] = jnp.where(y_even, tiles[y + 1], tiles[y])
            s4[rows, :] = jnp.where(y_even, tiles[y], tiles[y + 1])


def low_kernel(t_in, csr, idx, r1, r2, r3, r4, plt, pay, s1, s2, x_ref, t_ref):
    t_ref[...] = t_in[...]
    mid_edge_terms(csr, mid_edges(idx, r1, r2, r3, r4), t_ref)
    value = mid_product(plt, t_ref[...], x_ref)
    for c in range(COLS):
        pay[QC * c : QC * c + QC, :] = value[0:8, c * 128 : c * 128 + 128]
    block_sends(pay, idx, s1, s2)


def lift_kernel(m, t_in, csr, idx, r1, r2, r3, r4, pm, u, out, s1, s2, s3, s4, x_ref, t_ref):
    t_ref[...] = t_in[...]
    mid_edge_terms(csr, mid_edges(idx, r1, r2, r3, r4), t_ref)
    high, low = halves(m[...] + 0.2 * t_ref[...])
    x_ref[0:64, :] = high
    x_ref[64:128, :] = low
    x_ref[128:192, :] = high
    x_ref[192:256, :] = jnp.zeros((64, LANES), BF16)
    for n in range(4):
        out[:, chunk(n)] = u[:, chunk(n)] + dot(pm[...], x_ref[:, chunk(n)])
    fine_sends(out, idx, s1, s2, s3, s4)


WX = 10
WROWS = WX * 16


def place(window, own, r1, r2, r3, r4, idx):
    x_even, y_even = even(idx, 0), even(idx, 1)
    window[...] = jnp.zeros((QC * WROWS, 128), F32)

    def put(plane, y, tile):
        window[pl.ds(plane * 16 + 4 + y, QC, stride=WROWS), :] = tile

    for y in range(4):
        for x in range(4):
            c = 4 * x + y
            put(3 + x, y, own[QC * c : QC * c + QC, :])
        for x in range(3):
            rows = slice(QC * (4 * x + y), QC * (4 * x + y) + QC)
            put(x, y, jnp.where(x_even, r2[rows, :], r1[rows, :]))
            put(7 + x, y, jnp.where(x_even, r1[rows, :], r2[rows, :]))
    for plane in range(WX):
        for y in range(3):
            rows = slice(QC * (3 * plane + y), QC * (3 * plane + y) + QC)
            put(plane, y - 3, jnp.where(y_even, r4[rows, :], r3[rows, :]))
            put(plane, y + 4, jnp.where(y_even, r3[rows, :], r4[rows, :]))


def coarse_sweep(c_ref, out_ref, g_ref, coef, kc, first, last):
    def rows(d, plane):
        return pl.ds(pl.multiple_of(d * WROWS + plane * 16, 16), 16)

    def step(plane, carry):
        c = [c_ref[rows(d, plane), :] for d in range(QC)]
        weights = [coef[n, pl.ds(pl.multiple_of(plane * 16, 16), 16), :] for n in range(6)]
        for d in range(QC):
            t = g_ref[rows(d, plane), :] - 4.0 * c[d]
            for j in range(QC):
                t = t - kc[j, d] * c[j]
            if d & 4:
                t = t + weights[1] * c_ref[rows(d - 4, plane + 1), :]
            else:
                t = t + weights[0] * c_ref[rows(d + 4, plane - 1), :]
            if d & 2:
                t = t + weights[3] * sub_roll(c[d - 2], -1)
            else:
                t = t + weights[2] * sub_roll(c[d + 2], 1)
            if d & 1:
                t = t + weights[5] * pltpu.roll(c[d - 1], 127, 1)
            else:
                t = t + weights[4] * pltpu.roll(c[d + 1], 1, 1)
            out_ref[rows(d, plane), :] = c[d] + 0.2 * t
        return carry

    lax.fori_loop(first, last, step, 0)


def coarse_kernel(own, r1, r2, r3, r4, kc, idx, coef, g, pay, s1, s2, one, two):
    place(g, own, r1, r2, r3, r4, idx)
    one[...] = 0.2 * g[...]
    coarse_sweep(one, two, g, coef, kc, 1, 9)
    coarse_sweep(two, one, g, coef, kc, 2, 8)
    coarse_sweep(one, two, g, coef, kc, 3, 7)
    for c in range(COLS):
        row = (3 + c // 4) * 16 + 4 + c % 4
        pay[QC * c : QC * c + QC, :] = two[pl.ds(row, QC, stride=WROWS), :]
    block_sends(pay, idx, s1, s2)


def correct_kernel(
    own, r1, r2, r3, r4, kc, idx, g, coef, spread, m, gm, csr, q1, q2, q3, q4, km,
    out, s1, s2, s3, s4, one, two, x_ref, t_ref, m_ref,
):
    place(one, own, r1, r2, r3, r4, idx)
    coarse_sweep(one, two, g, coef, kc, 1, 9)
    coarse_sweep(two, one, g, coef, kc, 2, 8)

    def lifted(x, y, rows):
        total = None
        for d in range(QC):
            row = d * WROWS + (3 + x) * 16 + 4 + y
            part = spread[d, rows, :] * one[row : row + 1, :]
            total = part if total is None else total + part
        return total

    whole = slice(0, QM)
    for c in range(COLS):
        lanes = slice(c * 128, c * 128 + 128)
        m_ref[:, lanes] = m[:, lanes] + lifted(c // 4, c % 4, whole)
    below_x, above_x, below_y, above_y = mid_edges(idx, q1, q2, q3, q4)
    below_x = below_x + jnp.concatenate([lifted(-1, y, slice(48, 64)) for y in range(4)], axis=1)
    above_x = above_x + jnp.concatenate([lifted(4, y, slice(0, 16)) for y in range(4)], axis=1)
    below_rows, above_rows = [], []
    for i in range(4):
        last, first = slice(16 * i + 8, 16 * i + 16), slice(16 * i, 16 * i + 8)
        below_rows.append(jnp.concatenate([lifted(x, -1, last) for x in range(4)], axis=1))
        above_rows.append(jnp.concatenate([lifted(x, 4, first) for x in range(4)], axis=1))
    below_y = below_y + jnp.concatenate(below_rows, axis=0)
    above_y = above_y + jnp.concatenate(above_rows, axis=0)
    mid_local(m_ref, gm, csr, km, t_ref, x_ref)
    mid_edge_terms(csr, (below_x, above_x, below_y, above_y), t_ref)
    out[...] = m_ref[...] + 0.2 * t_ref[...]
    mid_sends(out, idx, s1, s2, s3, s4)


def swap(values, axis, odd):
    count = lax.axis_size(axis)
    pairs = [(i, (((i + odd) ^ 1) - odd) % count) for i in range(count)]
    return lax.ppermute(values, axis, pairs)


def exchange(sends):
    s1, s2, s3, s4 = sends
    return swap(s1, "gx", 0), swap(s2, "gx", 1), swap(s3, "yz", 0), swap(s4, "yz", 1)


def exchange_blocks(idx, own, s1, s2):
    r1, r2 = swap(s1, "gx", 0), swap(s2, "gx", 1)
    s3, s4 = call(row_kernel, [((QC * 3 * WX, 128), F32)] * 2, (), (0,))(idx, own, r1, r2)
    return own, r1, r2, swap(s3, "yz", 0), swap(s4, "yz", 1)


def body(seed, scale, coef, fine, smooth, mid, coarse, pmid, plow, noise, inc):
    idx = jnp.stack(
        [
            lax.axis_index("gx"),
            lax.axis_index("yz"),
            jnp.int32(lax.axis_size("gx")),
            jnp.int32(lax.axis_size("yz")),
        ]
    ).astype(jnp.int32)
    slots = slot_matrix()
    to_slot, from_slot = jnp.asarray(slots, BF16), jnp.asarray(slots.T, BF16)

    fine_field = ((SF, LANES), F32)
    fine_faces = [((40, 512), F32)] * 2 + [((48, 512), F32)] * 2
    mid_field = ((QM, LANES), F32)
    mid_faces = [((16, 512), F32)] * 2 + [((32, 512), F32)] * 2
    xf, tf = pltpu.VMEM((512, LANES), BF16), pltpu.VMEM((SF, LANES), F32)
    xm, tm = pltpu.VMEM((256, LANES), BF16), pltpu.VMEM((QM, LANES), F32)
    window = ((QC * WROWS, 128), F32)
    windows = [pltpu.VMEM((QC * WROWS, 128), F32)] * 2
    blocks = [((QC * COLS, 128), F32)] + [((QC * 12, 128), F32)] * 2

    operands = (
        seed.reshape(QF * COLS, 128),
        scale.reshape(COLS, 128),
        coef.reshape(3 * COLS, 128),
        to_slot,
        smooth,
        fine,
        noise,
        mid,
        pmid.T,
        plow.T,
    )
    g, u, csx, csr, s1, s2, s3, s4, kf, sf, nf, pmt, pm, km, plt, spread = call(
        first_kernel,
        [fine_field, fine_field, ((16, 512), F32), ((8, LANES), F32)]
        + [((56, 512), F32)] * 2
        + [((48, 512), F32)] * 2
        + [
            ((SF, 768), BF16),
            ((SF, 768), BF16),
            ((QF, 768), BF16),
            ((QM, 768), BF16),
            ((SF, 256), BF16),
            ((QM, 256), BF16),
            ((16, 256), BF16),
            ((QC, QM, 128), F32),
        ],
        [xf]
        + [pltpu.VMEM(operand.shape, operand.dtype) for operand in operands]
        + [pltpu.SemaphoreType.DMA((len(operands),))],
        (10,),
        range(10),
    )(*operands, idx)

    def fine_local(u):
        (t,) = call(fine_local_kernel, [fine_field], [xf])(u, g, csr, kf)
        return t

    def mid_local_part(m):
        (t,) = call(mid_local_kernel, [mid_field], [xm])(m, gm, csr, km)
        return t

    first = exchange((s1, s2, s3, s4))
    u, *sends = call(
        spread_kernel,
        [fine_field] + fine_faces[:2] + [((88, 512), F32)] * 2,
        [xf, tf],
        (3,),
    )(u, fine_local(u), csr, idx, *first, sf, csx)
    edges = exchange(sends)
    (coefw,) = call(coefficient_kernel, [((6, WROWS, 128), F32)], (), (0,))(
        idx, csx, first[0], first[1], edges[2], edges[3]
    )
    gm, m, *sends = call(restrict_kernel, [mid_field, mid_field] + mid_faces, [xf, tf], (2,))(
        fine_local(u), csr, idx, *edges, pmt
    )
    edges = exchange(sends)
    m, *sends = call(mid_kernel, [mid_field] + mid_faces, [tm], (3,))(
        m, mid_local_part(m), csr, idx, *edges
    )
    edges = exchange(sends)
    pay = call(low_kernel, blocks, [xm, tm], (2,))(mid_local_part(m), csr, idx, *edges, plt)
    gw, *pay = call(coarse_kernel, [window] + blocks, windows, (5, 6))(
        *exchange_blocks(idx, *pay), coarse, idx, coefw
    )
    m, *sends = call(
        correct_kernel,
        [mid_field] + mid_faces,
        windows + [xm, tm, pltpu.VMEM((QM, LANES), F32)],
        (5, 6),
    )(*exchange_blocks(idx, *pay), coarse, idx, gw, coefw, spread, m, gm, csr, *edges, km)
    edges = exchange(sends)
    u, *sends = call(lift_kernel, [fine_field] + fine_faces, [xm, tm], (3,))(
        m, mid_local_part(m), csr, idx, *edges, pm, u
    )
    edges = exchange(sends)
    u, *sends = call(sweep_kernel, [fine_field] + fine_faces, [xf, tf], (3,))(
        u, fine_local(u), csr, idx, *edges, sf
    )
    edges = exchange(sends)
    out, prev = call(
        last_kernel,
        [((QF * COLS, 128), F32)] * 2,
        [xf, tf, pltpu.VMEM((SF, LANES), F32)],
        (3,),
    )(u, fine_local(u), csr, idx, *edges, sf, nf, from_slot, inc.reshape(COLS, 128))
    shape = seed.shape
    return out.reshape(shape), prev.reshape(shape)


def solution(mesh):
    cell, field = P("gx", "yz", None), P(None, "gx", "yz", None)
    return jax.shard_map(
        body,
        mesh=mesh,
        in_specs=(field, cell, field) + (P(),) * 7 + (cell,),
        out_specs=(field, field),
        check_vma=False,
    )
```

time: 131 us -> 117 us (0.89)
  local copies, waits for them, and re-layouts: 9.12 us -> 0.01 us
  waiting for transfers between devices: 50.5 us -> 46 us
  starting transfers between devices: 39.3 us -> 35 us
  Pallas kernels: 31 us -> 34.4 us
    unnamed x26 -> x6, local copies, waits for them, and re-layouts: 9.11 us -> 0.01 us
    ppermute x36, waiting for transfers between devices: 50.5 us -> 46 us  [swap(): return lax.ppermute(values, axis, pairs)]
    ppermute x36, starting transfers between devices: 39.3 us -> 35 us  [swap(): return lax.ppermute(values, axis, pairs)]
    pallas_call x11 -> x20, Pallas kernels: 31 us -> 34.4 us  [run(): pl.pallas_call(kernel, out_shape=tuple((jax.ShapeDtypeStruct(s, d) for s,...]
  transfers between devices with their start and end apart: 36 -> 36, of which waited for: 20 -> 21; matrix products, arithmetic and copies ran while one was open for 0% -> 0% of each run, Pallas kernels for 0% -> 7%
where the time goes in v2:
time: 117 us; the launch traced here: 116 us
  waiting for transfers between devices  46 us (39%)
  starting transfers between devices  35 us (30%)
  Pallas kernels  34.4 us (29%)
    ppermute x36, waiting for transfers between devices, swap(): return lax.ppermute(values, axis, pairs)  46 us
    ppermute x36, starting transfers between devices, swap(): return lax.ppermute(values, axis, pairs)  35 us
    pallas_call x20, Pallas kernels, run(): pl.pallas_call(kernel, out_shape=tuple((jax.ShapeDtypeStruct(s, d) for s,...  34.4 us
  transfers between devices with their start and end apart: 36, of which 21 were waited for; matrix products, arithmetic and copies ran while one was open for 0% of the time, Pallas kernels for 7%

profile of v2, /device:TPU:0, one launch (start us, length us, event | category | flops | bytes accessed | tf_op | source)
XLA Modules:
  0.0 116.5 jit_solution(12223062923458883814)
XLA Ops:
  0.7 6.0 %shard_map.140 = (f32[240,2048]{1,0:T(8,128)S(1)}, f32[240,2048]{1,0:T(8,128)S(1)}, f32[16,512]{1,0:T(8,128)S(1)}, f32[8,2048]{1,0:T(8,128)S(1)}, f32[56,512]{1,...) custom-call(f32[3456,128]{1,0:T(8,128)} %bitcast.11, ...), custom_call_target="tpu_custom_call" | custom-call | tf_op jit(solution)/shard_map/pallas_call | solution.py:50
  6.7 1.7 %collective-permute-start = (f32[56,512]{1,0:T(8,128)S(1)}, f32[56,512]{1,0:T(8,128)S(1)}, u32[]{:S(2)}, u32[]{:S(2)}) collective-permute-start(f32[56,512]{1,0:T(8,128)S(1)} %get-tuple-element.66), channel_id=1, source_target_pairs={{0,32},{32,0},{64,96},{96,64},{1,33},{33,1},{65,97},{97,65},{2,34}... | collective-permute-start | bytes 344072 | tf_op jit(solution)/shard_map/ppermute | solution.py:635
  8.5 2.2 %collective-permute-start.1 = (f32[56,512]{1,0:T(8,128)S(1)}, f32[56,512]{1,0:T(8,128)S(1)}, u32[]{:S(2)}, u32[]{:S(2)}) collective-permute-start(f32[56,512]{1,0:T(8,128)S(1)} %get-tuple-element.67), channel_id=1, source_target_pairs={{0,96},{32,64},{64,32},{96,0},{1,97},{33,65},{65,33},{97,1},{2,98}... | collective-permute-start | bytes 344072 | tf_op jit(solution)/shard_map/ppermute | solution.py:635
  10.7 6.3 %collective-permute-start.3 = (f32[48,512]{1,0:T(8,128)S(1)}, f32[48,512]{1,0:T(8,128)S(1)}, u32[]{:S(2)}, u32[]{:S(2)}) collective-permute-start(f32[48,512]{1,0:T(8,128)S(1)} %get-tuple-element.69), channel_id=1, source_target_pairs={{0,31},{1,2},{2,1},{3,4},{4,3},{5,6},{6,5},{7,8},{8,7},{9,10},{10,... | collective-permute-start | bytes 294920 | tf_op jit(solution)/shard_map/ppermute | solution.py:635
  17.0 1.6 %shard_map.141.t_in = f32[240,2048]{1,0:T(8,128)S(1)} custom-call(f32[240,2048]{1,0:T(8,128)S(1)} %get-tuple-element.62.u_ref.u, f32[240,2048]{1,0:T(8,128)S(1)} %get-tuple-element.63.g_ref, f32[8,2048]{1,0:T(8,128)S(1)} %get-tuple-element.64.csr, bf16[240,768]{1,0:T(8,128)(2,1)S(1)} %get-tuple-element.65.kf), custom_call_target="tpu_custom_call" | custom-call | tf_op jit(solution)/shard_map/pallas_call | solution.py:50
  18.6 0.7 collective-permute-done.3.r4
  19.3 1.8 %shard_map.142 = (f32[240,2048]{1,0:T(8,128)S(1)}, f32[40,512]{1,0:T(8,128)S(1)}, f32[40,512]{1,0:T(8,128)S(1)}, f32[88,512]{1,0:T(8,128)S(1)}, f32[88,512]{1,0:T(8,128)S(1)}) custom-call(f32[240,2048]{1,0:T(8,128)S(1)} %get-tuple-element.62.u_ref.u, f32[240,2048]{1,0:T(8,128)S(1)} %shard_map.141.t_in, f32[8,2048]{1,0:T(8,128)S(1)} %get-tuple-element.64.csr, ...), custom_call_target="tpu_custom_call" | custom-call | tf_op jit(solution)/shard_map/pallas_call | solution.py:50
  21.2 5.1 %collective-permute-start.7 = (f32[88,512]{1,0:T(8,128)S(1)}, f32[88,512]{1,0:T(8,128)S(1)}, u32[]{:S(2)}, u32[]{:S(2)}) collective-permute-start(f32[88,512]{1,0:T(8,128)S(1)} %get-tuple-element.76), channel_id=1, source_target_pairs={{0,31},{1,2},{2,1},{3,4},{4,3},{5,6},{6,5},{7,8},{8,7},{9,10},{10,... | collective-permute-start | bytes 540680 | tf_op jit(solution)/shard_map/ppermute | solution.py:635
  26.3 0.7 collective-permute-start.4
  27.0 0.6 collective-permute-start.5
  27.6 1.5 %shard_map.143.t_in = f32[240,2048]{1,0:T(8,128)S(1)} custom-call(f32[240,2048]{1,0:T(8,128)S(1)} %get-tuple-element.72.u_ref.u, f32[240,2048]{1,0:T(8,128)S(1)} %get-tuple-element.63.g_ref, f32[8,2048]{1,0:T(8,128)S(1)} %get-tuple-element.64.csr, bf16[240,768]{1,0:T(8,128)(2,1)S(1)} %get-tuple-element.65.kf), custom_call_target="tpu_custom_call" | custom-call | tf_op jit(solution)/shard_map/pallas_call | solution.py:50
  29.2 1.6 %collective-permute-done.4.r1 = f32[40,512]{1,0:T(8,128)S(1)} collective-permute-done((f32[40,512]{1,0:T(8,128)S(1)}, f32[40,512]{1,0:T(8,128)S(1)}, u32[]{:S(2)}, u32[]{:S(2)}) %collective-permute-start.4) | collective-permute-done | bytes 81952 | tf_op jit(solution)/shard_map/ppermute | solution.py:635
  30.8 1.9 %collective-permute-done.5.r2 = f32[40,512]{1,0:T(8,128)S(1)} collective-permute-done((f32[40,512]{1,0:T(8,128)S(1)}, f32[40,512]{1,0:T(8,128)S(1)}, u32[]{:S(2)}, u32[]{:S(2)}) %collective-permute-start.5) | collective-permute-done | bytes 81952 | tf_op jit(solution)/shard_map/ppermute | solution.py:635
  32.7 1.3 %shard_map.144 = (f32[64,2048]{1,0:T(8,128)S(1)}, f32[64,2048]{1,0:T(8,128)S(1)}, f32[16,512]{1,0:T(8,128)S(1)}, f32[16,512]{1,0:T(8,128)S(1)}, f32[32,512]{1,0:T(8,128)S(1)}, /*index=5*/f32[32,512]{1,0:T(8,128)S(1)}) custom-call(f32[240,2048]{1,0:T(8,128)S(1)} %shard_map.143.t_in, f32[8,2048]{1,0:T(8,128)S(1)} %get-tuple-element.64.csr, ...), custom_call_target="tpu_custom_call" | custom-call | tf_op jit(solution)/shard_map/pallas_call | solution.py:50
  34.1 2.0 %collective-permute-start.11 = (f32[32,512]{1,0:T(8,128)S(1)}, f32[32,512]{1,0:T(8,128)S(1)}, u32[]{:S(2)}, u32[]{:S(2)}) collective-permute-start(f32[32,512]{1,0:T(8,128)S(1)} %get-tuple-element.84), channel_id=1, source_target_pairs={{0,31},{1,2},{2,1},{3,4},{4,3},{5,6},{6,5},{7,8},{8,7},{9,10},{10,... | collective-permute-start | bytes 196616 | tf_op jit(solution)/shard_map/ppermute | solution.py:635
  36.0 0.7 collective-permute-start.8
  36.7 0.6 collective-permute-start.9
  37.3 0.5 shard_map.145.t_in
  37.8 2.1 %collective-permute-done.8.r1 = f32[16,512]{1,0:T(8,128)S(1)} collective-permute-done((f32[16,512]{1,0:T(8,128)S(1)}, f32[16,512]{1,0:T(8,128)S(1)}, u32[]{:S(2)}, u32[]{:S(2)}) %collective-permute-start.8) | collective-permute-done | bytes 32800 | tf_op jit(solution)/shard_map/ppermute | solution.py:635
  40.0 1.9 %collective-permute-done.9.r2 = f32[16,512]{1,0:T(8,128)S(1)} collective-permute-done((f32[16,512]{1,0:T(8,128)S(1)}, f32[16,512]{1,0:T(8,128)S(1)}, u32[]{:S(2)}, u32[]{:S(2)}) %collective-permute-start.9) | collective-permute-done | bytes 32800 | tf_op jit(solution)/shard_map/ppermute | solution.py:635
  41.8 0.7 shard_map.146
  42.6 1.4 %collective-permute-start.15 = (f32[32,512]{1,0:T(8,128)S(1)}, f32[32,512]{1,0:T(8,128)S(1)}, u32[]{:S(2)}, u32[]{:S(2)}) collective-permute-start(f32[32,512]{1,0:T(8,128)S(1)} %get-tuple-element.89), channel_id=1, source_target_pairs={{0,31},{1,2},{2,1},{3,4},{4,3},{5,6},{6,5},{7,8},{8,7},{9,10},{10,... | collective-permute-start | bytes 196616 | tf_op jit(solution)/shard_map/ppermute | solution.py:635
  44.1 0.5 collective-permute-start.12
  44.6 0.9 collective-permute-start.13
  45.5 0.5 shard_map.147.t_in
  46.0 2.0 %collective-permute-done.12.r1.q1 = f32[16,512]{1,0:T(8,128)S(1)} collective-permute-done((f32[16,512]{1,0:T(8,128)S(1)}, f32[16,512]{1,0:T(8,128)S(1)}, u32[]{:S(2)}, u32[]{:S(2)}) %collective-permute-start.12) | collective-permute-done | bytes 32800 | tf_op jit(solution)/shard_map/ppermute | solution.py:635
  48.0 1.7 %collective-permute-done.13.r2.q2 = f32[16,512]{1,0:T(8,128)S(1)} collective-permute-done((f32[16,512]{1,0:T(8,128)S(1)}, f32[16,512]{1,0:T(8,128)S(1)}, u32[]{:S(2)}, u32[]{:S(2)}) %collective-permute-start.13) | collective-permute-done | bytes 32800 | tf_op jit(solution)/shard_map/ppermute | solution.py:635
  49.7 0.8 shard_map.148
  50.9 0.9 collective-permute-start.17
  51.8 2.9 %collective-permute-done.16.r1 = f32[96,128]{1,0:T(8,128)S(1)} collective-permute-done((f32[96,128]{1,0:T(8,128)S(1)}, f32[96,128]{1,0:T(8,128)S(1)}, u32[]{:S(2)}, u32[]{:S(2)}) %collective-permute-start.16) | collective-permute-done | bytes 49184 | tf_op jit(solution)/shard_map/ppermute | solution.py:635
  54.7 1.5 %collective-permute-done.17.r2 = f32[96,128]{1,0:T(8,128)S(1)} collective-permute-done((f32[96,128]{1,0:T(8,128)S(1)}, f32[96,128]{1,0:T(8,128)S(1)}, u32[]{:S(2)}, u32[]{:S(2)}) %collective-permute-start.17) | collective-permute-done | bytes 49184 | tf_op jit(solution)/shard_map/ppermute | solution.py:635
  56.2 0.6 shard_map.149
  56.8 0.9 collective-permute-start.19
  57.8 0.7 shard_map.150.coef
  58.5 6.1 %collective-permute-done.19.r4 = f32[240,128]{1,0:T(8,128)S(1)} collective-permute-done((f32[240,128]{1,0:T(8,128)S(1)}, f32[240,128]{1,0:T(8,128)S(1)}, u32[]{:S(2)}, u32[]{:S(2)}) %collective-permute-start.19) | collective-permute-done | bytes 122912 | tf_op jit(solution)/shard_map/ppermute | solution.py:635
  64.5 2.6 %shard_map.151 = (f32[1280,128]{1,0:T(8,128)S(1)}, f32[128,128]{1,0:T(8,128)S(1)}, f32[96,128]{1,0:T(8,128)S(1)}, f32[96,128]{1,0:T(8,128)S(1)}) custom-call(f32[128,128]{1,0:T(8,128)S(1)} %get-tuple-element.91.own, f32[96,128]{1,0:T(8,128)S(1)} %collective-permute-done.16.r1, f32[96,128]{1,0:T(8,128)S(1)} %collective-permute-done.17.r2, ...), custom_call_target="tpu_custom_call" | custom-call | tf_op jit(solution)/shard_map/pallas_call | solution.py:50
  67.2 0.6 collective-permute-start.20
  67.8 0.9 collective-permute-start.21
  68.7 2.7 %collective-permute-done.20.r1 = f32[96,128]{1,0:T(8,128)S(1)} collective-permute-done((f32[96,128]{1,0:T(8,128)S(1)}, f32[96,128]{1,0:T(8,128)S(1)}, u32[]{:S(2)}, u32[]{:S(2)}) %collective-permute-start.20) | collective-permute-done | bytes 49184 | tf_op jit(solution)/shard_map/ppermute | solution.py:635
  71.3 1.7 %collective-permute-done.21.r2 = f32[96,128]{1,0:T(8,128)S(1)} collective-permute-done((f32[96,128]{1,0:T(8,128)S(1)}, f32[96,128]{1,0:T(8,128)S(1)}, u32[]{:S(2)}, u32[]{:S(2)}) %collective-permute-start.21) | collective-permute-done | bytes 49184 | tf_op jit(solution)/shard_map/ppermute | solution.py:635
  73.1 0.6 shard_map.152
  73.8 1.2 %collective-permute-done.22.r3 = f32[240,128]{1,0:T(8,128)S(1)} collective-permute-done((f32[240,128]{1,0:T(8,128)S(1)}, f32[240,128]{1,0:T(8,128)S(1)}, u32[]{:S(2)}, u32[]{:S(2)}) %collective-permute-start.22) | collective-permute-done | bytes 122912 | tf_op jit(solution)/shard_map/ppermute | solution.py:635
  75.1 6.4 %collective-permute-done.23.r4 = f32[240,128]{1,0:T(8,128)S(1)} collective-permute-done((f32[240,128]{1,0:T(8,128)S(1)}, f32[240,128]{1,0:T(8,128)S(1)}, u32[]{:S(2)}, u32[]{:S(2)}) %collective-permute-start.23) | collective-permute-done | bytes 122912 | tf_op jit(solution)/shard_map/ppermute | solution.py:635
  81.5 3.2 %shard_map.153 = (f32[64,2048]{1,0:T(8,128)S(1)}, f32[16,512]{1,0:T(8,128)S(1)}, f32[16,512]{1,0:T(8,128)S(1)}, f32[32,512]{1,0:T(8,128)S(1)}, f32[32,512]{1,0:T(8,128)S(1)}) custom-call(f32[128,128]{1,0:T(8,128)S(1)} %get-tuple-element.96.own, f32[96,128]{1,0:T(8,128)S(1)} %collective-permute-done.20.r1, f32[96,128]{1,0:T(8,128)S(1)} %collective-permute-done.21.r2, ...), custom_call_target="tpu_custom_call" | custom-call | tf_op jit(solution)/shard_map/pallas_call | solution.py:50
  85.3 0.9 collective-permute-start.25
  86.2 0.5 shard_map.154.t_in
  86.7 2.2 %collective-permute-done.24.r1 = f32[16,512]{1,0:T(8,128)S(1)} collective-permute-done((f32[16,512]{1,0:T(8,128)S(1)}, f32[16,512]{1,0:T(8,128)S(1)}, u32[]{:S(2)}, u32[]{:S(2)}) %collective-permute-start.24) | collective-permute-done | bytes 32800 | tf_op jit(solution)/shard_map/ppermute | solution.py:635
  88.9 1.5 %collective-permute-done.25.r2 = f32[16,512]{1,0:T(8,128)S(1)} collective-permute-done((f32[16,512]{1,0:T(8,128)S(1)}, f32[16,512]{1,0:T(8,128)S(1)}, u32[]{:S(2)}, u32[]{:S(2)}) %collective-permute-start.25) | collective-permute-done | bytes 32800 | tf_op jit(solution)/shard_map/ppermute | solution.py:635
  90.4 1.5 %collective-permute-done.27.r4 = f32[32,512]{1,0:T(8,128)S(1)} collective-permute-done((f32[32,512]{1,0:T(8,128)S(1)}, f32[32,512]{1,0:T(8,128)S(1)}, u32[]{:S(2)}, u32[]{:S(2)}) %collective-permute-start.27) | collective-permute-done | bytes 65568 | tf_op jit(solution)/shard_map/ppermute | solution.py:635
  91.9 1.0 shard_map.155
  93.0 2.1 %collective-permute-start.31 = (f32[48,512]{1,0:T(8,128)S(1)}, f32[48,512]{1,0:T(8,128)S(1)}, u32[]{:S(2)}, u32[]{:S(2)}) collective-permute-start(f32[48,512]{1,0:T(8,128)S(1)} %get-tuple-element.113), channel_id=1, source_target_pairs={{0,31},{1,2},{2,1},{3,4},{4,3},{5,6},{6,5},{7,8},{8,7},{9,10},{10,... | collective-permute-start | bytes 294920 | tf_op jit(solution)/shard_map/ppermute | solution.py:635
  95.1 0.5 collective-permute-start.28
  95.7 0.9 collective-permute-start.29
  96.6 1.5 %shard_map.156.t_in = f32[240,2048]{1,0:T(8,128)S(1)} custom-call(f32[240,2048]{1,0:T(8,128)S(1)} %get-tuple-element.109.u_ref.u, f32[240,2048]{1,0:T(8,128)S(1)} %get-tuple-element.63.g_ref, f32[8,2048]{1,0:T(8,128)S(1)} %get-tuple-element.64.csr, bf16[240,768]{1,0:T(8,128)(2,1)S(1)} %get-tuple-element.65.kf), custom_call_target="tpu_custom_call" | custom-call | tf_op jit(solution)/shard_map/pallas_call | solution.py:50
  98.1 1.5 %collective-permute-done.28.r1 = f32[40,512]{1,0:T(8,128)S(1)} collective-permute-done((f32[40,512]{1,0:T(8,128)S(1)}, f32[40,512]{1,0:T(8,128)S(1)}, u32[]{:S(2)}, u32[]{:S(2)}) %collective-permute-start.28) | collective-permute-done | bytes 81952 | tf_op jit(solution)/shard_map/ppermute | solution.py:635
  99.6 1.7 %collective-permute-done.29.r2 = f32[40,512]{1,0:T(8,128)S(1)} collective-permute-done((f32[40,512]{1,0:T(8,128)S(1)}, f32[40,512]{1,0:T(8,128)S(1)}, u32[]{:S(2)}, u32[]{:S(2)}) %collective-permute-start.29) | collective-permute-done | bytes 81952 | tf_op jit(solution)/shard_map/ppermute | solution.py:635
  101.3 1.7 %shard_map.157 = (f32[240,2048]{1,0:T(8,128)S(1)}, f32[40,512]{1,0:T(8,128)S(1)}, f32[40,512]{1,0:T(8,128)S(1)}, f32[48,512]{1,0:T(8,128)S(1)}, f32[48,512]{1,0:T(8,128)S(1)}) custom-call(f32[240,2048]{1,0:T(8,128)S(1)} %get-tuple-element.109.u_ref.u, f32[240,2048]{1,0:T(8,128)S(1)} %shard_map.156.t_in, f32[8,2048]{1,0:T(8,128)S(1)} %get-tuple-element.64.csr, ...), custom_call_target="tpu_custom_call" | custom-call | tf_op jit(solution)/shard_map/pallas_call | solution.py:50
  103.2 1.4 %collective-permute-start.35 = (f32[48,512]{1,0:T(8,128)S(1)}, f32[48,512]{1,0:T(8,128)S(1)}, u32[]{:S(2)}, u32[]{:S(2)}) collective-permute-start(f32[48,512]{1,0:T(8,128)S(1)} %get-tuple-element.118), channel_id=1, source_target_pairs={{0,31},{1,2},{2,1},{3,4},{4,3},{5,6},{6,5},{7,8},{8,7},{9,10},{10,... | collective-permute-start | bytes 294920 | tf_op jit(solution)/shard_map/ppermute | solution.py:635
  104.6 0.5 collective-permute-start.32
  105.1 0.9 collective-permute-start.33
  106.0 1.5 %shard_map.158.t_in = f32[240,2048]{1,0:T(8,128)S(1)} custom-call(f32[240,2048]{1,0:T(8,128)S(1)} %get-tuple-element.114.u_ref.u, f32[240,2048]{1,0:T(8,128)S(1)} %get-tuple-element.63.g_ref, f32[8,2048]{1,0:T(8,128)S(1)} %get-tuple-element.64.csr, bf16[240,768]{1,0:T(8,128)(2,1)S(1)} %get-tuple-element.65.kf), custom_call_target="tpu_custom_call" | custom-call | tf_op jit(solution)/shard_map/pallas_call | solution.py:50
  107.6 1.5 %collective-permute-done.32.r1 = f32[40,512]{1,0:T(8,128)S(1)} collective-permute-done((f32[40,512]{1,0:T(8,128)S(1)}, f32[40,512]{1,0:T(8,128)S(1)}, u32[]{:S(2)}, u32[]{:S(2)}) %collective-permute-start.32) | collective-permute-done | bytes 81952 | tf_op jit(solution)/shard_map/ppermute | solution.py:635
  109.0 1.7 %collective-permute-done.33.r2 = f32[40,512]{1,0:T(8,128)S(1)} collective-permute-done((f32[40,512]{1,0:T(8,128)S(1)}, f32[40,512]{1,0:T(8,128)S(1)}, u32[]{:S(2)}, u32[]{:S(2)}) %collective-permute-start.33) | collective-permute-done | bytes 81952 | tf_op jit(solution)/shard_map/ppermute | solution.py:635
  110.8 5.7 %shard_map.159 = (f32[3456,128]{1,0:T(8,128)}, f32[3456,128]{1,0:T(8,128)}) custom-call(f32[240,2048]{1,0:T(8,128)S(1)} %get-tuple-element.114.u_ref.u, f32[240,2048]{1,0:T(8,128)S(1)} %shard_map.158.t_in, f32[8,2048]{1,0:T(8,128)S(1)} %get-tuple-element.64.csr, s32[4]{0:T(128)S(1)} %pad_add_fusion.idx, f32[40,512]{1,0:T(8,128)S(1)} %collective-permute-done.32.r1, ...), custom_call_target="tpu_custom_call" | custom-call | tf_op jit(solution)/shard_map/pallas_call | solution.py:50
  (35 shorter events, 1.7 us)
Async XLA Ops:
  6.7 12.6 %collective-permute-start = (f32[56,512]{1,0:T(8,128)S(1)}, f32[56,512]{1,0:T(8,128)S(1)}, u32[]{:S(2)}, u32[]{:S(2)}) collective-permute-start(f32[56,512]{1,0:T(8,128)S(1)} %get-tuple-element.66), channel_id=1, source_target_pairs={{0,32},{32,0},{64,96},{96,64},{1,33},{33,1},{65,97},{97,65},{2,34}... | collective-permute-start | bytes 344072 | tf_op jit(solution)/shard_map/ppermute | solution.py:635
  8.5 10.8 %collective-permute-start.1 = (f32[56,512]{1,0:T(8,128)S(1)}, f32[56,512]{1,0:T(8,128)S(1)}, u32[]{:S(2)}, u32[]{:S(2)}) collective-permute-start(f32[56,512]{1,0:T(8,128)S(1)} %get-tuple-element.67), channel_id=1, source_target_pairs={{0,96},{32,64},{64,32},{96,0},{1,97},{33,65},{65,33},{97,1},{2,98}... | collective-permute-start | bytes 344072 | tf_op jit(solution)/shard_map/ppermute | solution.py:635
  10.7 7.9 %collective-permute-start.2 = (f32[48,512]{1,0:T(8,128)S(1)}, f32[48,512]{1,0:T(8,128)S(1)}, u32[]{:S(2)}, u32[]{:S(2)}) collective-permute-start(f32[48,512]{1,0:T(8,128)S(1)} %get-tuple-element.68), channel_id=1, source_target_pairs={{0,1},{1,0},{2,3},{3,2},{4,5},{5,4},{6,7},{7,6},{8,9},{9,8},{10,11... | collective-permute-start | bytes 294920 | tf_op jit(solution)/shard_map/ppermute | solution.py:635
  10.7 8.6 %collective-permute-start.3 = (f32[48,512]{1,0:T(8,128)S(1)}, f32[48,512]{1,0:T(8,128)S(1)}, u32[]{:S(2)}, u32[]{:S(2)}) collective-permute-start(f32[48,512]{1,0:T(8,128)S(1)} %get-tuple-element.69), channel_id=1, source_target_pairs={{0,31},{1,2},{2,1},{3,4},{4,3},{5,6},{6,5},{7,8},{8,7},{9,10},{10,... | collective-permute-start | bytes 294920 | tf_op jit(solution)/shard_map/ppermute | solution.py:635
  21.1 11.6 %collective-permute-start.6 = (f32[88,512]{1,0:T(8,128)S(1)}, f32[88,512]{1,0:T(8,128)S(1)}, u32[]{:S(2)}, u32[]{:S(2)}) collective-permute-start(f32[88,512]{1,0:T(8,128)S(1)} %get-tuple-element.75), channel_id=1, source_target_pairs={{0,1},{1,0},{2,3},{3,2},{4,5},{5,4},{6,7},{7,6},{8,9},{9,8},{10,11... | collective-permute-start | bytes 540680 | tf_op jit(solution)/shard_map/ppermute | solution.py:635
  21.2 11.5 %collective-permute-start.7 = (f32[88,512]{1,0:T(8,128)S(1)}, f32[88,512]{1,0:T(8,128)S(1)}, u32[]{:S(2)}, u32[]{:S(2)}) collective-permute-start(f32[88,512]{1,0:T(8,128)S(1)} %get-tuple-element.76), channel_id=1, source_target_pairs={{0,31},{1,2},{2,1},{3,4},{4,3},{5,6},{6,5},{7,8},{8,7},{9,10},{10,... | collective-permute-start | bytes 540680 | tf_op jit(solution)/shard_map/ppermute | solution.py:635
  26.3 4.4 %collective-permute-start.4 = (f32[40,512]{1,0:T(8,128)S(1)}, f32[40,512]{1,0:T(8,128)S(1)}, u32[]{:S(2)}, u32[]{:S(2)}) collective-permute-start(f32[40,512]{1,0:T(8,128)S(1)} %get-tuple-element.73), channel_id=1, source_target_pairs={{0,32},{32,0},{64,96},{96,64},{1,33},{33,1},{65,97},{97,65},{2,34}... | collective-permute-start | bytes 245768 | tf_op jit(solution)/shard_map/ppermute | solution.py:635
  27.0 5.7 %collective-permute-start.5 = (f32[40,512]{1,0:T(8,128)S(1)}, f32[40,512]{1,0:T(8,128)S(1)}, u32[]{:S(2)}, u32[]{:S(2)}) collective-permute-start(f32[40,512]{1,0:T(8,128)S(1)} %get-tuple-element.74), channel_id=1, source_target_pairs={{0,96},{32,64},{64,32},{96,0},{1,97},{33,65},{65,33},{97,1},{2,98}... | collective-permute-start | bytes 245768 | tf_op jit(solution)/shard_map/ppermute | solution.py:635
  34.0 7.9 %collective-permute-start.10 = (f32[32,512]{1,0:T(8,128)S(1)}, f32[32,512]{1,0:T(8,128)S(1)}, u32[]{:S(2)}, u32[]{:S(2)}) collective-permute-start(f32[32,512]{1,0:T(8,128)S(1)} %get-tuple-element.83), channel_id=1, source_target_pairs={{0,1},{1,0},{2,3},{3,2},{4,5},{5,4},{6,7},{7,6},{8,9},{9,8},{10,11... | collective-permute-start | bytes 196616 | tf_op jit(solution)/shard_map/ppermute | solution.py:635
  34.1 7.8 %collective-permute-start.11 = (f32[32,512]{1,0:T(8,128)S(1)}, f32[32,512]{1,0:T(8,128)S(1)}, u32[]{:S(2)}, u32[]{:S(2)}) collective-permute-start(f32[32,512]{1,0:T(8,128)S(1)} %get-tuple-element.84), channel_id=1, source_target_pairs={{0,31},{1,2},{2,1},{3,4},{4,3},{5,6},{6,5},{7,8},{8,7},{9,10},{10,... | collective-permute-start | bytes 196616 | tf_op jit(solution)/shard_map/ppermute | solution.py:635
  36.0 3.9 %collective-permute-start.8 = (f32[16,512]{1,0:T(8,128)S(1)}, f32[16,512]{1,0:T(8,128)S(1)}, u32[]{:S(2)}, u32[]{:S(2)}) collective-permute-start(f32[16,512]{1,0:T(8,128)S(1)} %get-tuple-element.81), channel_id=1, source_target_pairs={{0,32},{32,0},{64,96},{96,64},{1,33},{33,1},{65,97},{97,65},{2,34}... | collective-permute-start | bytes 98312 | tf_op jit(solution)/shard_map/ppermute | solution.py:635
  36.7 5.1 %collective-permute-start.9 = (f32[16,512]{1,0:T(8,128)S(1)}, f32[16,512]{1,0:T(8,128)S(1)}, u32[]{:S(2)}, u32[]{:S(2)}) collective-permute-start(f32[16,512]{1,0:T(8,128)S(1)} %get-tuple-element.82), channel_id=1, source_target_pairs={{0,96},{32,64},{64,32},{96,0},{1,97},{33,65},{65,33},{97,1},{2,98}... | collective-permute-start | bytes 98312 | tf_op jit(solution)/shard_map/ppermute | solution.py:635
  42.5 22.0 %copy-start.1 = (f32[8,8]{1,0:T(8,128)S(1)}, f32[8,8]{1,0:T(8,128)}, u32[]{:S(2)}) copy-start(f32[8,8]{1,0:T(8,128)} %kc.3) | copy-start | bytes 772
  42.5 7.2 %collective-permute-start.14 = (f32[32,512]{1,0:T(8,128)S(1)}, f32[32,512]{1,0:T(8,128)S(1)}, u32[]{:S(2)}, u32[]{:S(2)}) collective-permute-start(f32[32,512]{1,0:T(8,128)S(1)} %get-tuple-element.88), channel_id=1, source_target_pairs={{0,1},{1,0},{2,3},{3,2},{4,5},{5,4},{6,7},{7,6},{8,9},{9,8},{10,11... | collective-permute-start | bytes 196616 | tf_op jit(solution)/shard_map/ppermute | solution.py:635
  42.6 7.1 %collective-permute-start.15 = (f32[32,512]{1,0:T(8,128)S(1)}, f32[32,512]{1,0:T(8,128)S(1)}, u32[]{:S(2)}, u32[]{:S(2)}) collective-permute-start(f32[32,512]{1,0:T(8,128)S(1)} %get-tuple-element.89), channel_id=1, source_target_pairs={{0,31},{1,2},{2,1},{3,4},{4,3},{5,6},{6,5},{7,8},{8,7},{9,10},{10,... | collective-permute-start | bytes 196616 | tf_op jit(solution)/shard_map/ppermute | solution.py:635
  44.1 3.9 %collective-permute-start.12 = (f32[16,512]{1,0:T(8,128)S(1)}, f32[16,512]{1,0:T(8,128)S(1)}, u32[]{:S(2)}, u32[]{:S(2)}) collective-permute-start(f32[16,512]{1,0:T(8,128)S(1)} %get-tuple-element.86), channel_id=1, source_target_pairs={{0,32},{32,0},{64,96},{96,64},{1,33},{33,1},{65,97},{97,65},{2,34}... | collective-permute-start | bytes 98312 | tf_op jit(solution)/shard_map/ppermute | solution.py:635
  44.6 5.1 %collective-permute-start.13 = (f32[16,512]{1,0:T(8,128)S(1)}, f32[16,512]{1,0:T(8,128)S(1)}, u32[]{:S(2)}, u32[]{:S(2)}) collective-permute-start(f32[16,512]{1,0:T(8,128)S(1)} %get-tuple-element.87), channel_id=1, source_target_pairs={{0,96},{32,64},{64,32},{96,0},{1,97},{33,65},{65,33},{97,1},{2,98}... | collective-permute-start | bytes 98312 | tf_op jit(solution)/shard_map/ppermute | solution.py:635
  50.5 4.1 %collective-permute-start.16 = (f32[96,128]{1,0:T(8,128)S(1)}, f32[96,128]{1,0:T(8,128)S(1)}, u32[]{:S(2)}, u32[]{:S(2)}) collective-permute-start(f32[96,128]{1,0:T(8,128)S(1)} %get-tuple-element.92), channel_id=1, source_target_pairs={{0,32},{32,0},{64,96},{96,64},{1,33},{33,1},{65,97},{97,65},{2,34}... | collective-permute-start | bytes 147464 | tf_op jit(solution)/shard_map/ppermute | solution.py:635
  50.9 5.3 %collective-permute-start.17 = (f32[96,128]{1,0:T(8,128)S(1)}, f32[96,128]{1,0:T(8,128)S(1)}, u32[]{:S(2)}, u32[]{:S(2)}) collective-permute-start(f32[96,128]{1,0:T(8,128)S(1)} %get-tuple-element.93), channel_id=1, source_target_pairs={{0,96},{32,64},{64,32},{96,0},{1,97},{33,65},{65,33},{97,1},{2,98}... | collective-permute-start | bytes 147464 | tf_op jit(solution)/shard_map/ppermute | solution.py:635
  56.7 1.7 %collective-permute-start.18 = (f32[240,128]{1,0:T(8,128)S(1)}, f32[240,128]{1,0:T(8,128)S(1)}, u32[]{:S(2)}, u32[]{:S(2)}) collective-permute-start(f32[240,128]{1,0:T(8,128)S(1)} %get-tuple-element.94), channel_id=1, source_target_pairs={{0,1},{1,0},{2,3},{3,2},{4,5},{5,4},{6,7},{7,6},{8,9},{9,8},{10,11... | collective-permute-start | bytes 368648 | tf_op jit(solution)/shard_map/ppermute | solution.py:635
  56.8 7.7 %collective-permute-start.19 = (f32[240,128]{1,0:T(8,128)S(1)}, f32[240,128]{1,0:T(8,128)S(1)}, u32[]{:S(2)}, u32[]{:S(2)}) collective-permute-start(f32[240,128]{1,0:T(8,128)S(1)} %get-tuple-element.95), channel_id=1, source_target_pairs={{0,31},{1,2},{2,1},{3,4},{4,3},{5,6},{6,5},{7,8},{8,7},{9,10},{10,... | collective-permute-start | bytes 368648 | tf_op jit(solution)/shard_map/ppermute | solution.py:635
  67.2 4.2 %collective-permute-start.20 = (f32[96,128]{1,0:T(8,128)S(1)}, f32[96,128]{1,0:T(8,128)S(1)}, u32[]{:S(2)}, u32[]{:S(2)}) collective-permute-start(f32[96,128]{1,0:T(8,128)S(1)} %get-tuple-element.97), channel_id=1, source_target_pairs={{0,32},{32,0},{64,96},{96,64},{1,33},{33,1},{65,97},{97,65},{2,34}... | collective-permute-start | bytes 147464 | tf_op jit(solution)/shard_map/ppermute | solution.py:635
  67.8 5.3 %collective-permute-start.21 = (f32[96,128]{1,0:T(8,128)S(1)}, f32[96,128]{1,0:T(8,128)S(1)}, u32[]{:S(2)}, u32[]{:S(2)}) collective-permute-start(f32[96,128]{1,0:T(8,128)S(1)} %get-tuple-element.98), channel_id=1, source_target_pairs={{0,96},{32,64},{64,32},{96,0},{1,97},{33,65},{65,33},{97,1},{2,98}... | collective-permute-start | bytes 147464 | tf_op jit(solution)/shard_map/ppermute | solution.py:635
  73.7 1.4 %collective-permute-start.22 = (f32[240,128]{1,0:T(8,128)S(1)}, f32[240,128]{1,0:T(8,128)S(1)}, u32[]{:S(2)}, u32[]{:S(2)}) collective-permute-start(f32[240,128]{1,0:T(8,128)S(1)} %get-tuple-element.99), channel_id=1, source_target_pairs={{0,1},{1,0},{2,3},{3,2},{4,5},{5,4},{6,7},{7,6},{8,9},{9,8},{10,11... | collective-permute-start | bytes 368648 | tf_op jit(solution)/shard_map/ppermute | solution.py:635
  73.8 7.7 %collective-permute-start.23 = (f32[240,128]{1,0:T(8,128)S(1)}, f32[240,128]{1,0:T(8,128)S(1)}, u32[]{:S(2)}, u32[]{:S(2)}) collective-permute-start(f32[240,128]{1,0:T(8,128)S(1)} %get-tuple-element.100), channel_id=1, source_target_pairs={{0,31},{1,2},{2,1},{3,4},{4,3},{5,6},{6,5},{7,8},{8,7},{9,10},{10,... | collective-permute-start | bytes 368648 | tf_op jit(solution)/shard_map/ppermute | solution.py:635
  84.7 5.7 %collective-permute-start.26 = (f32[32,512]{1,0:T(8,128)S(1)}, f32[32,512]{1,0:T(8,128)S(1)}, u32[]{:S(2)}, u32[]{:S(2)}) collective-permute-start(f32[32,512]{1,0:T(8,128)S(1)} %get-tuple-element.106), channel_id=1, source_target_pairs={{0,1},{1,0},{2,3},{3,2},{4,5},{5,4},{6,7},{7,6},{8,9},{9,8},{10,11... | collective-permute-start | bytes 196616 | tf_op jit(solution)/shard_map/ppermute | solution.py:635
  84.8 7.1 %collective-permute-start.27 = (f32[32,512]{1,0:T(8,128)S(1)}, f32[32,512]{1,0:T(8,128)S(1)}, u32[]{:S(2)}, u32[]{:S(2)}) collective-permute-start(f32[32,512]{1,0:T(8,128)S(1)} %get-tuple-element.107), channel_id=1, source_target_pairs={{0,31},{1,2},{2,1},{3,4},{4,3},{5,6},{6,5},{7,8},{8,7},{9,10},{10,... | collective-permute-start | bytes 196616 | tf_op jit(solution)/shard_map/ppermute | solution.py:635
  84.9 4.0 %collective-permute-start.24 = (f32[16,512]{1,0:T(8,128)S(1)}, f32[16,512]{1,0:T(8,128)S(1)}, u32[]{:S(2)}, u32[]{:S(2)}) collective-permute-start(f32[16,512]{1,0:T(8,128)S(1)} %get-tuple-element.104), channel_id=1, source_target_pairs={{0,32},{32,0},{64,96},{96,64},{1,33},{33,1},{65,97},{97,65},{2,34}... | collective-permute-start | bytes 98312 | tf_op jit(solution)/shard_map/ppermute | solution.py:635
  85.3 5.1 %collective-permute-start.25 = (f32[16,512]{1,0:T(8,128)S(1)}, f32[16,512]{1,0:T(8,128)S(1)}, u32[]{:S(2)}, u32[]{:S(2)}) collective-permute-start(f32[16,512]{1,0:T(8,128)S(1)} %get-tuple-element.105), channel_id=1, source_target_pairs={{0,96},{32,64},{64,32},{96,0},{1,97},{33,65},{65,33},{97,1},{2,98}... | collective-permute-start | bytes 98312 | tf_op jit(solution)/shard_map/ppermute | solution.py:635
  92.9 8.4 %collective-permute-start.30 = (f32[48,512]{1,0:T(8,128)S(1)}, f32[48,512]{1,0:T(8,128)S(1)}, u32[]{:S(2)}, u32[]{:S(2)}) collective-permute-start(f32[48,512]{1,0:T(8,128)S(1)} %get-tuple-element.112), channel_id=1, source_target_pairs={{0,1},{1,0},{2,3},{3,2},{4,5},{5,4},{6,7},{7,6},{8,9},{9,8},{10,11... | collective-permute-start | bytes 294920 | tf_op jit(solution)/shard_map/ppermute | solution.py:635
  93.0 8.3 %collective-permute-start.31 = (f32[48,512]{1,0:T(8,128)S(1)}, f32[48,512]{1,0:T(8,128)S(1)}, u32[]{:S(2)}, u32[]{:S(2)}) collective-permute-start(f32[48,512]{1,0:T(8,128)S(1)} %get-tuple-element.113), channel_id=1, source_target_pairs={{0,31},{1,2},{2,1},{3,4},{4,3},{5,6},{6,5},{7,8},{8,7},{9,10},{10,... | collective-permute-start | bytes 294920 | tf_op jit(solution)/shard_map/ppermute | solution.py:635
  95.1 4.4 %collective-permute-start.28 = (f32[40,512]{1,0:T(8,128)S(1)}, f32[40,512]{1,0:T(8,128)S(1)}, u32[]{:S(2)}, u32[]{:S(2)}) collective-permute-start(f32[40,512]{1,0:T(8,128)S(1)} %get-tuple-element.110), channel_id=1, source_target_pairs={{0,32},{32,0},{64,96},{96,64},{1,33},{33,1},{65,97},{97,65},{2,34}... | collective-permute-start | bytes 245768 | tf_op jit(solution)/shard_map/ppermute | solution.py:635
  95.7 5.7 %collective-permute-start.29 = (f32[40,512]{1,0:T(8,128)S(1)}, f32[40,512]{1,0:T(8,128)S(1)}, u32[]{:S(2)}, u32[]{:S(2)}) collective-permute-start(f32[40,512]{1,0:T(8,128)S(1)} %get-tuple-element.111), channel_id=1, source_target_pairs={{0,96},{32,64},{64,32},{96,0},{1,97},{33,65},{65,33},{97,1},{2,98}... | collective-permute-start | bytes 245768 | tf_op jit(solution)/shard_map/ppermute | solution.py:635
  103.1 7.7 %collective-permute-start.34 = (f32[48,512]{1,0:T(8,128)S(1)}, f32[48,512]{1,0:T(8,128)S(1)}, u32[]{:S(2)}, u32[]{:S(2)}) collective-permute-start(f32[48,512]{1,0:T(8,128)S(1)} %get-tuple-element.117), channel_id=1, source_target_pairs={{0,1},{1,0},{2,3},{3,2},{4,5},{5,4},{6,7},{7,6},{8,9},{9,8},{10,11... | collective-permute-start | bytes 294920 | tf_op jit(solution)/shard_map/ppermute | solution.py:635
  103.2 7.6 %collective-permute-start.35 = (f32[48,512]{1,0:T(8,128)S(1)}, f32[48,512]{1,0:T(8,128)S(1)}, u32[]{:S(2)}, u32[]{:S(2)}) collective-permute-start(f32[48,512]{1,0:T(8,128)S(1)} %get-tuple-element.118), channel_id=1, source_target_pairs={{0,31},{1,2},{2,1},{3,4},{4,3},{5,6},{6,5},{7,8},{8,7},{9,10},{10,... | collective-permute-start | bytes 294920 | tf_op jit(solution)/shard_map/ppermute | solution.py:635
  104.6 4.4 %collective-permute-start.32 = (f32[40,512]{1,0:T(8,128)S(1)}, f32[40,512]{1,0:T(8,128)S(1)}, u32[]{:S(2)}, u32[]{:S(2)}) collective-permute-start(f32[40,512]{1,0:T(8,128)S(1)} %get-tuple-element.115), channel_id=1, source_target_pairs={{0,32},{32,0},{64,96},{96,64},{1,33},{33,1},{65,97},{97,65},{2,34}... | collective-permute-start | bytes 245768 | tf_op jit(solution)/shard_map/ppermute | solution.py:635
  105.1 5.7 %collective-permute-start.33 = (f32[40,512]{1,0:T(8,128)S(1)}, f32[40,512]{1,0:T(8,128)S(1)}, u32[]{:S(2)}, u32[]{:S(2)}) collective-permute-start(f32[40,512]{1,0:T(8,128)S(1)} %get-tuple-element.116), channel_id=1, source_target_pairs={{0,96},{32,64},{64,32},{96,0},{1,97},{33,65},{65,33},{97,1},{2,98}... | collective-permute-start | bytes 245768 | tf_op jit(solution)/shard_map/ppermute | solution.py:635
  106.0 4.8 %copy-start = (bf16[216,240]{1,0:T(8,128)(2,1)S(1)}, bf16[216,240]{1,0:T(8,128)(2,1)}, u32[]{:S(2)}) copy-start(bf16[216,240]{1,0:T(8,128)(2,1)} %constant.18.clone.from_slot) | copy-start | bytes 311044
  106.0 4.8 %copy-start.2 = (f32[4,4,128]{2,1,0:T(4,128)S(1)}, f32[4,4,128]{2,1,0:T(4,128)}, u32[]{:S(2)}) copy-start(f32[4,4,128]{2,1,0:T(4,128)} %param.23) | copy-start | bytes 24580

commit v3 on v2

--- a/solution.py
+++ b/solution.py
@@ -629,21 +629,37 @@
     mid_sends(out, idx, s1, s2, s3, s4)
 
 
-def swap(values, axis, odd):
-    count = lax.axis_size(axis)
-    pairs = [(i, (((i + odd) ^ 1) - odd) % count) for i in range(count)]
-    return lax.ppermute(values, axis, pairs)
+def partners(step):
+    nx, ny = lax.axis_size("gx"), lax.axis_size("yz")
+    pairs = []
+    for a in range(nx):
+        for b in range(ny):
+            to = (a, b)
+            if step < 2:
+                at = ((a + step) ^ 1) - step
+                to = (at, b) if 0 <= at < nx else (a, b ^ 1)
+            else:
+                at = ((b + step - 2) ^ 1) - (step - 2)
+                to = (a, at) if 0 <= at < ny else (a ^ 1, b)
+            pairs.append((a * ny + b, to[0] * ny + to[1]))
+    return pairs
+
+
+def swap(values, step):
+    return lax.ppermute(values, ("gx", "yz"), partners(step))
 
 
 def exchange(sends):
     s1, s2, s3, s4 = sends
-    return swap(s1, "gx", 0), swap(s2, "gx", 1), swap(s3, "yz", 0), swap(s4, "yz", 1)
+    r2, r1, r4, r3 = swap(s2, 1), swap(s1, 0), swap(s4, 3), swap(s3, 2)
+    return r1, r2, r3, r4
 
 
 def exchange_blocks(idx, own, s1, s2):
-    r1, r2 = swap(s1, "gx", 0), swap(s2, "gx", 1)
+    r2, r1 = swap(s2, 1), swap(s1, 0)
     s3, s4 = call(row_kernel, [((QC * 3 * WX, 128), F32)] * 2, (), (0,))(idx, own, r1, r2)
-    return own, r1, r2, swap(s3, "yz", 0), swap(s4, "yz", 1)
+    r4, r3 = swap(s4, 3), swap(s3, 2)
+    return own, r1, r2, r3, r4
 
 
 def body(seed, scale, coef, fine, smooth, mid, coarse, pmid, plow, noise, inc):

time: 117 us -> 98 us (0.84)
  the two profiles are of different devices: /device:TPU:0 before, /device:TPU:14 now
where the time goes in v3:
time: 98 us; the launch traced here: 97.9 us
  waiting for transfers between devices  34.9 us (36%)
  Pallas kernels  34.4 us (35%)
  starting transfers between devices  27.6 us (28%)
    ppermute x36, waiting for transfers between devices, swap(): return lax.ppermute(values, ('gx', 'yz'), partners(step))  34.9 us
    pallas_call x20, Pallas kernels, run(): pl.pallas_call(kernel, out_shape=tuple((jax.ShapeDtypeStruct(s, d) for s,...  34.4 us
    ppermute x36, starting transfers between devices, swap(): return lax.ppermute(values, ('gx', 'yz'), partners(step))  27.6 us
  transfers between devices with their start and end apart: 36, of which 20 were waited for; matrix products, arithmetic and copies ran while one was open for 0% of the time, Pallas kernels for 9%

profile of v3, /device:TPU:14, one launch (start us, length us, event | category | flops | bytes accessed | tf_op | source)
XLA Modules:
  0.0 97.9 jit_solution(790650811358719721)
XLA Ops:
  0.7 6.0 %shard_map.140 = (f32[240,2048]{1,0:T(8,128)S(1)}, f32[240,2048]{1,0:T(8,128)S(1)}, f32[16,512]{1,0:T(8,128)S(1)}, f32[8,2048]{1,0:T(8,128)S(1)}, f32[56,512]{1,...) custom-call(f32[3456,128]{1,0:T(8,128)} %bitcast.11, ...), custom_call_target="tpu_custom_call" | custom-call | tf_op jit(solution)/shard_map/pallas_call | solution.py:50
  6.7 0.5 collective-permute-start
  7.3 2.4 %collective-permute-start.1 = (f32[56,512]{1,0:T(8,128)S(1)}, f32[56,512]{1,0:T(8,128)S(1)}, u32[]{:S(2)}, u32[]{:S(2)}) collective-permute-start(f32[56,512]{1,0:T(8,128)S(1)} %get-tuple-element.67), channel_id=1, source_target_pairs={{0,1},{1,0},{2,3},{3,2},{4,5},{5,4},{6,7},{7,6},{8,9},{9,8},{10,11... | collective-permute-start | bytes 344072 | tf_op jit(solution)/shard_map/ppermute | solution.py:649
  9.7 4.4 %collective-permute-start.3 = (f32[48,512]{1,0:T(8,128)S(1)}, f32[48,512]{1,0:T(8,128)S(1)}, u32[]{:S(2)}, u32[]{:S(2)}) collective-permute-start(f32[48,512]{1,0:T(8,128)S(1)} %get-tuple-element.69), channel_id=1, source_target_pairs={{0,32},{1,2},{2,1},{3,4},{4,3},{5,6},{6,5},{7,8},{8,7},{9,10},{10,... | collective-permute-start | bytes 294920 | tf_op jit(solution)/shard_map/ppermute | solution.py:649
  14.1 1.6 %shard_map.141.t_in = f32[240,2048]{1,0:T(8,128)S(1)} custom-call(f32[240,2048]{1,0:T(8,128)S(1)} %get-tuple-element.62.u_ref.u, f32[240,2048]{1,0:T(8,128)S(1)} %get-tuple-element.63.g_ref, f32[8,2048]{1,0:T(8,128)S(1)} %get-tuple-element.64.csr, bf16[240,768]{1,0:T(8,128)(2,1)S(1)} %get-tuple-element.65.kf), custom_call_target="tpu_custom_call" | custom-call | tf_op jit(solution)/shard_map/pallas_call | solution.py:50
  15.7 0.7 collective-permute-done.3.r4
  16.4 1.8 %shard_map.142 = (f32[240,2048]{1,0:T(8,128)S(1)}, f32[40,512]{1,0:T(8,128)S(1)}, f32[40,512]{1,0:T(8,128)S(1)}, f32[88,512]{1,0:T(8,128)S(1)}, f32[88,512]{1,0:T(8,128)S(1)}) custom-call(f32[240,2048]{1,0:T(8,128)S(1)} %get-tuple-element.62.u_ref.u, f32[240,2048]{1,0:T(8,128)S(1)} %shard_map.141.t_in, f32[8,2048]{1,0:T(8,128)S(1)} %get-tuple-element.64.csr, ...), custom_call_target="tpu_custom_call" | custom-call | tf_op jit(solution)/shard_map/pallas_call | solution.py:50
  18.3 3.9 %collective-permute-start.7 = (f32[88,512]{1,0:T(8,128)S(1)}, f32[88,512]{1,0:T(8,128)S(1)}, u32[]{:S(2)}, u32[]{:S(2)}) collective-permute-start(f32[88,512]{1,0:T(8,128)S(1)} %get-tuple-element.76), channel_id=1, source_target_pairs={{0,32},{1,2},{2,1},{3,4},{4,3},{5,6},{6,5},{7,8},{8,7},{9,10},{10,... | collective-permute-start | bytes 540680 | tf_op jit(solution)/shard_map/ppermute | solution.py:649
  22.2 0.7 collective-permute-start.5
  23.0 1.5 %shard_map.143.t_in = f32[240,2048]{1,0:T(8,128)S(1)} custom-call(f32[240,2048]{1,0:T(8,128)S(1)} %get-tuple-element.72.u_ref.u, f32[240,2048]{1,0:T(8,128)S(1)} %get-tuple-element.63.g_ref, f32[8,2048]{1,0:T(8,128)S(1)} %get-tuple-element.64.csr, bf16[240,768]{1,0:T(8,128)(2,1)S(1)} %get-tuple-element.65.kf), custom_call_target="tpu_custom_call" | custom-call | tf_op jit(solution)/shard_map/pallas_call | solution.py:50
  24.5 2.1 %collective-permute-done.4.r1 = f32[40,512]{1,0:T(8,128)S(1)} collective-permute-done((f32[40,512]{1,0:T(8,128)S(1)}, f32[40,512]{1,0:T(8,128)S(1)}, u32[]{:S(2)}, u32[]{:S(2)}) %collective-permute-start.4) | collective-permute-done | bytes 81952 | tf_op jit(solution)/shard_map/ppermute | solution.py:649
  26.7 1.3 %shard_map.144 = (f32[64,2048]{1,0:T(8,128)S(1)}, f32[64,2048]{1,0:T(8,128)S(1)}, f32[16,512]{1,0:T(8,128)S(1)}, f32[16,512]{1,0:T(8,128)S(1)}, f32[32,512]{1,0:T(8,128)S(1)}, /*index=5*/f32[32,512]{1,0:T(8,128)S(1)}) custom-call(f32[240,2048]{1,0:T(8,128)S(1)} %shard_map.143.t_in, f32[8,2048]{1,0:T(8,128)S(1)} %get-tuple-element.64.csr, ...), custom_call_target="tpu_custom_call" | custom-call | tf_op jit(solution)/shard_map/pallas_call | solution.py:50
  28.1 2.7 %collective-permute-start.11 = (f32[32,512]{1,0:T(8,128)S(1)}, f32[32,512]{1,0:T(8,128)S(1)}, u32[]{:S(2)}, u32[]{:S(2)}) collective-permute-start(f32[32,512]{1,0:T(8,128)S(1)} %get-tuple-element.84), channel_id=1, source_target_pairs={{0,32},{1,2},{2,1},{3,4},{4,3},{5,6},{6,5},{7,8},{8,7},{9,10},{10,... | collective-permute-start | bytes 196616 | tf_op jit(solution)/shard_map/ppermute | solution.py:649
  30.7 0.7 collective-permute-start.9
  31.5 0.5 shard_map.145.t_in
  32.0 2.7 %collective-permute-done.8.r1 = f32[16,512]{1,0:T(8,128)S(1)} collective-permute-done((f32[16,512]{1,0:T(8,128)S(1)}, f32[16,512]{1,0:T(8,128)S(1)}, u32[]{:S(2)}, u32[]{:S(2)}) %collective-permute-start.8) | collective-permute-done | bytes 32800 | tf_op jit(solution)/shard_map/ppermute | solution.py:649
  34.6 0.7 shard_map.146
  35.4 1.9 %collective-permute-start.15 = (f32[32,512]{1,0:T(8,128)S(1)}, f32[32,512]{1,0:T(8,128)S(1)}, u32[]{:S(2)}, u32[]{:S(2)}) collective-permute-start(f32[32,512]{1,0:T(8,128)S(1)} %get-tuple-element.89), channel_id=1, source_target_pairs={{0,32},{1,2},{2,1},{3,4},{4,3},{5,6},{6,5},{7,8},{8,7},{9,10},{10,... | collective-permute-start | bytes 196616 | tf_op jit(solution)/shard_map/ppermute | solution.py:649
  37.4 0.7 collective-permute-start.13
  38.1 0.5 shard_map.147.t_in
  38.6 2.6 %collective-permute-done.12.r1.q1 = f32[16,512]{1,0:T(8,128)S(1)} collective-permute-done((f32[16,512]{1,0:T(8,128)S(1)}, f32[16,512]{1,0:T(8,128)S(1)}, u32[]{:S(2)}, u32[]{:S(2)}) %collective-permute-start.12) | collective-permute-done | bytes 32800 | tf_op jit(solution)/shard_map/ppermute | solution.py:649
  41.3 0.8 shard_map.148
  42.2 0.8 collective-permute-start.17
  43.0 3.3 %collective-permute-done.16.r1 = f32[96,128]{1,0:T(8,128)S(1)} collective-permute-done((f32[96,128]{1,0:T(8,128)S(1)}, f32[96,128]{1,0:T(8,128)S(1)}, u32[]{:S(2)}, u32[]{:S(2)}) %collective-permute-start.16) | collective-permute-done | bytes 49184 | tf_op jit(solution)/shard_map/ppermute | solution.py:649
  46.2 0.1 collective-permute-done.17.r2
  46.3 0.6 shard_map.149
  46.9 0.1 collective-permute-start.18
  47.0 1.3 %collective-permute-start.19 = (f32[240,128]{1,0:T(8,128)S(1)}, f32[240,128]{1,0:T(8,128)S(1)}, u32[]{:S(2)}, u32[]{:S(2)}) collective-permute-start(f32[240,128]{1,0:T(8,128)S(1)} %get-tuple-element.95), channel_id=1, source_target_pairs={{0,32},{1,2},{2,1},{3,4},{4,3},{5,6},{6,5},{7,8},{8,7},{9,10},{10,... | collective-permute-start | bytes 368648 | tf_op jit(solution)/shard_map/ppermute | solution.py:649
  48.3 0.7 shard_map.150.coef
  49.0 4.5 %collective-permute-done.19.r4 = f32[240,128]{1,0:T(8,128)S(1)} collective-permute-done((f32[240,128]{1,0:T(8,128)S(1)}, f32[240,128]{1,0:T(8,128)S(1)}, u32[]{:S(2)}, u32[]{:S(2)}) %collective-permute-start.19) | collective-permute-done | bytes 122912 | tf_op jit(solution)/shard_map/ppermute | solution.py:649
  53.5 2.6 %shard_map.151 = (f32[1280,128]{1,0:T(8,128)S(1)}, f32[128,128]{1,0:T(8,128)S(1)}, f32[96,128]{1,0:T(8,128)S(1)}, f32[96,128]{1,0:T(8,128)S(1)}) custom-call(f32[128,128]{1,0:T(8,128)S(1)} %get-tuple-element.91.own, f32[96,128]{1,0:T(8,128)S(1)} %collective-permute-done.16.r1, f32[96,128]{1,0:T(8,128)S(1)} %collective-permute-done.17.r2, ...), custom_call_target="tpu_custom_call" | custom-call | tf_op jit(solution)/shard_map/pallas_call | solution.py:50
  56.1 0.1 collective-permute-start.20
  56.2 0.8 collective-permute-start.21
  57.0 3.3 %collective-permute-done.20.r1 = f32[96,128]{1,0:T(8,128)S(1)} collective-permute-done((f32[96,128]{1,0:T(8,128)S(1)}, f32[96,128]{1,0:T(8,128)S(1)}, u32[]{:S(2)}, u32[]{:S(2)}) %collective-permute-start.20) | collective-permute-done | bytes 49184 | tf_op jit(solution)/shard_map/ppermute | solution.py:649
  60.3 0.1 collective-permute-done.21.r2
  60.4 0.6 shard_map.152
  61.1 0.1 collective-permute-start.23
  61.2 1.2 %collective-permute-done.22.r3 = f32[240,128]{1,0:T(8,128)S(1)} collective-permute-done((f32[240,128]{1,0:T(8,128)S(1)}, f32[240,128]{1,0:T(8,128)S(1)}, u32[]{:S(2)}, u32[]{:S(2)}) %collective-permute-start.22) | collective-permute-done | bytes 122912 | tf_op jit(solution)/shard_map/ppermute | solution.py:649
  62.4 5.2 %collective-permute-done.23.r4 = f32[240,128]{1,0:T(8,128)S(1)} collective-permute-done((f32[240,128]{1,0:T(8,128)S(1)}, f32[240,128]{1,0:T(8,128)S(1)}, u32[]{:S(2)}, u32[]{:S(2)}) %collective-permute-start.23) | collective-permute-done | bytes 122912 | tf_op jit(solution)/shard_map/ppermute | solution.py:649
  67.6 3.2 %shard_map.153 = (f32[64,2048]{1,0:T(8,128)S(1)}, f32[16,512]{1,0:T(8,128)S(1)}, f32[16,512]{1,0:T(8,128)S(1)}, f32[32,512]{1,0:T(8,128)S(1)}, f32[32,512]{1,0:T(8,128)S(1)}) custom-call(f32[128,128]{1,0:T(8,128)S(1)} %get-tuple-element.96.own, f32[96,128]{1,0:T(8,128)S(1)} %collective-permute-done.20.r1, f32[96,128]{1,0:T(8,128)S(1)} %collective-permute-done.21.r2, ...), custom_call_target="tpu_custom_call" | custom-call | tf_op jit(solution)/shard_map/pallas_call | solution.py:50
  70.9 0.1 collective-permute-start.27
  71.0 0.2 collective-permute-start.24
  71.2 1.0 %collective-permute-start.25 = (f32[16,512]{1,0:T(8,128)S(1)}, f32[16,512]{1,0:T(8,128)S(1)}, u32[]{:S(2)}, u32[]{:S(2)}) collective-permute-start(f32[16,512]{1,0:T(8,128)S(1)} %get-tuple-element.105), channel_id=1, source_target_pairs={{0,1},{1,0},{2,3},{3,2},{4,5},{5,4},{6,7},{7,6},{8,9},{9,8},{10,11... | collective-permute-start | bytes 98312 | tf_op jit(solution)/shard_map/ppermute | solution.py:649
  72.2 0.5 shard_map.154.t_in
  72.8 2.2 %collective-permute-done.24.r1 = f32[16,512]{1,0:T(8,128)S(1)} collective-permute-done((f32[16,512]{1,0:T(8,128)S(1)}, f32[16,512]{1,0:T(8,128)S(1)}, u32[]{:S(2)}, u32[]{:S(2)}) %collective-permute-start.24) | collective-permute-done | bytes 32800 | tf_op jit(solution)/shard_map/ppermute | solution.py:649
  75.0 0.2 collective-permute-done.25.r2
  75.1 1.6 %collective-permute-done.27.r4 = f32[32,512]{1,0:T(8,128)S(1)} collective-permute-done((f32[32,512]{1,0:T(8,128)S(1)}, f32[32,512]{1,0:T(8,128)S(1)}, u32[]{:S(2)}, u32[]{:S(2)}) %collective-permute-start.27) | collective-permute-done | bytes 65568 | tf_op jit(solution)/shard_map/ppermute | solution.py:649
  76.8 1.0 %shard_map.155 = (f32[240,2048]{1,0:T(8,128)S(1)}, f32[40,512]{1,0:T(8,128)S(1)}, f32[40,512]{1,0:T(8,128)S(1)}, f32[48,512]{1,0:T(8,128)S(1)}, f32[48,512]{1,0:T(8,128)S(1)}) custom-call(f32[64,2048]{1,0:T(8,128)S(1)} %get-tuple-element.103.m_ref.m, f32[64,2048]{1,0:T(8,128)S(1)} %shard_map.154.t_in, f32[8,2048]{1,0:T(8,128)S(1)} %get-tuple-element.64.csr, ...), custom_call_target="tpu_custom_call" | custom-call | tf_op jit(solution)/shard_map/pallas_call | solution.py:50
  77.9 0.9 collective-permute-start.31
  78.8 0.3 collective-permute-start.28
  79.1 0.7 collective-permute-start.29
  79.9 1.6 %shard_map.156.t_in = f32[240,2048]{1,0:T(8,128)S(1)} custom-call(f32[240,2048]{1,0:T(8,128)S(1)} %get-tuple-element.109.u_ref.u, f32[240,2048]{1,0:T(8,128)S(1)} %get-tuple-element.63.g_ref, f32[8,2048]{1,0:T(8,128)S(1)} %get-tuple-element.64.csr, bf16[240,768]{1,0:T(8,128)(2,1)S(1)} %get-tuple-element.65.kf), custom_call_target="tpu_custom_call" | custom-call | tf_op jit(solution)/shard_map/pallas_call | solution.py:50
  81.4 1.9 %collective-permute-done.28.r1 = f32[40,512]{1,0:T(8,128)S(1)} collective-permute-done((f32[40,512]{1,0:T(8,128)S(1)}, f32[40,512]{1,0:T(8,128)S(1)}, u32[]{:S(2)}, u32[]{:S(2)}) %collective-permute-start.28) | collective-permute-done | bytes 81952 | tf_op jit(solution)/shard_map/ppermute | solution.py:649
  83.3 0.3 collective-permute-done.29.r2
  83.6 0.6 collective-permute-done.31.r4
  84.1 1.7 %shard_map.157 = (f32[240,2048]{1,0:T(8,128)S(1)}, f32[40,512]{1,0:T(8,128)S(1)}, f32[40,512]{1,0:T(8,128)S(1)}, f32[48,512]{1,0:T(8,128)S(1)}, f32[48,512]{1,0:T(8,128)S(1)}) custom-call(f32[240,2048]{1,0:T(8,128)S(1)} %get-tuple-element.109.u_ref.u, f32[240,2048]{1,0:T(8,128)S(1)} %shard_map.156.t_in, f32[8,2048]{1,0:T(8,128)S(1)} %get-tuple-element.64.csr, ...), custom_call_target="tpu_custom_call" | custom-call | tf_op jit(solution)/shard_map/pallas_call | solution.py:50
  86.0 1.1 %collective-permute-start.35 = (f32[48,512]{1,0:T(8,128)S(1)}, f32[48,512]{1,0:T(8,128)S(1)}, u32[]{:S(2)}, u32[]{:S(2)}) collective-permute-start(f32[48,512]{1,0:T(8,128)S(1)} %get-tuple-element.118), channel_id=1, source_target_pairs={{0,32},{1,2},{2,1},{3,4},{4,3},{5,6},{6,5},{7,8},{8,7},{9,10},{10,... | collective-permute-start | bytes 294920 | tf_op jit(solution)/shard_map/ppermute | solution.py:649
  87.1 0.5 collective-permute-start.32
  87.5 0.7 collective-permute-start.33
  88.3 1.5 %shard_map.158.t_in = f32[240,2048]{1,0:T(8,128)S(1)} custom-call(f32[240,2048]{1,0:T(8,128)S(1)} %get-tuple-element.114.u_ref.u, f32[240,2048]{1,0:T(8,128)S(1)} %get-tuple-element.63.g_ref, f32[8,2048]{1,0:T(8,128)S(1)} %get-tuple-element.64.csr, bf16[240,768]{1,0:T(8,128)(2,1)S(1)} %get-tuple-element.65.kf), custom_call_target="tpu_custom_call" | custom-call | tf_op jit(solution)/shard_map/pallas_call | solution.py:50
  89.8 1.7 %collective-permute-done.32.r1 = f32[40,512]{1,0:T(8,128)S(1)} collective-permute-done((f32[40,512]{1,0:T(8,128)S(1)}, f32[40,512]{1,0:T(8,128)S(1)}, u32[]{:S(2)}, u32[]{:S(2)}) %collective-permute-start.32) | collective-permute-done | bytes 81952 | tf_op jit(solution)/shard_map/ppermute | solution.py:649
  91.5 0.5 collective-permute-done.33.r2
  92.0 0.2 collective-permute-done.35.r4
  92.2 5.7 %shard_map.159 = (f32[3456,128]{1,0:T(8,128)}, f32[3456,128]{1,0:T(8,128)}) custom-call(f32[240,2048]{1,0:T(8,128)S(1)} %get-tuple-element.114.u_ref.u, f32[240,2048]{1,0:T(8,128)S(1)} %shard_map.158.t_in, f32[8,2048]{1,0:T(8,128)S(1)} %get-tuple-element.64.csr, s32[4]{0:T(128)S(1)} %pad_add_fusion.idx, f32[40,512]{1,0:T(8,128)S(1)} %collective-permute-done.32.r1, ...), custom_call_target="tpu_custom_call" | custom-call | tf_op jit(solution)/shard_map/pallas_call | solution.py:50
  (35 shorter events, 0.8 us)
Async XLA Ops:
  6.7 9.7 %collective-permute-start = (f32[56,512]{1,0:T(8,128)S(1)}, f32[56,512]{1,0:T(8,128)S(1)}, u32[]{:S(2)}, u32[]{:S(2)}) collective-permute-start(f32[56,512]{1,0:T(8,128)S(1)} %get-tuple-element.66), channel_id=1, source_target_pairs={{0,32},{1,33},{2,34},{3,35},{4,36},{5,37},{6,38},{7,39},{8,40},{9,... | collective-permute-start | bytes 344072 | tf_op jit(solution)/shard_map/ppermute | solution.py:649
  7.3 9.1 %collective-permute-start.1 = (f32[56,512]{1,0:T(8,128)S(1)}, f32[56,512]{1,0:T(8,128)S(1)}, u32[]{:S(2)}, u32[]{:S(2)}) collective-permute-start(f32[56,512]{1,0:T(8,128)S(1)} %get-tuple-element.67), channel_id=1, source_target_pairs={{0,1},{1,0},{2,3},{3,2},{4,5},{5,4},{6,7},{7,6},{8,9},{9,8},{10,11... | collective-permute-start | bytes 344072 | tf_op jit(solution)/shard_map/ppermute | solution.py:649
  9.7 6.0 %collective-permute-start.2 = (f32[48,512]{1,0:T(8,128)S(1)}, f32[48,512]{1,0:T(8,128)S(1)}, u32[]{:S(2)}, u32[]{:S(2)}) collective-permute-start(f32[48,512]{1,0:T(8,128)S(1)} %get-tuple-element.68), channel_id=1, source_target_pairs={{0,1},{1,0},{2,3},{3,2},{4,5},{5,4},{6,7},{7,6},{8,9},{9,8},{10,11... | collective-permute-start | bytes 294920 | tf_op jit(solution)/shard_map/ppermute | solution.py:649
  9.7 6.7 %collective-permute-start.3 = (f32[48,512]{1,0:T(8,128)S(1)}, f32[48,512]{1,0:T(8,128)S(1)}, u32[]{:S(2)}, u32[]{:S(2)}) collective-permute-start(f32[48,512]{1,0:T(8,128)S(1)} %get-tuple-element.69), channel_id=1, source_target_pairs={{0,32},{1,2},{2,1},{3,4},{4,3},{5,6},{6,5},{7,8},{8,7},{9,10},{10,... | collective-permute-start | bytes 294920 | tf_op jit(solution)/shard_map/ppermute | solution.py:649
  18.2 8.5 %collective-permute-start.6 = (f32[88,512]{1,0:T(8,128)S(1)}, f32[88,512]{1,0:T(8,128)S(1)}, u32[]{:S(2)}, u32[]{:S(2)}) collective-permute-start(f32[88,512]{1,0:T(8,128)S(1)} %get-tuple-element.75), channel_id=1, source_target_pairs={{0,1},{1,0},{2,3},{3,2},{4,5},{5,4},{6,7},{7,6},{8,9},{9,8},{10,11... | collective-permute-start | bytes 540680 | tf_op jit(solution)/shard_map/ppermute | solution.py:649
  18.3 8.4 %collective-permute-start.7 = (f32[88,512]{1,0:T(8,128)S(1)}, f32[88,512]{1,0:T(8,128)S(1)}, u32[]{:S(2)}, u32[]{:S(2)}) collective-permute-start(f32[88,512]{1,0:T(8,128)S(1)} %get-tuple-element.76), channel_id=1, source_target_pairs={{0,32},{1,2},{2,1},{3,4},{4,3},{5,6},{6,5},{7,8},{8,7},{9,10},{10,... | collective-permute-start | bytes 540680 | tf_op jit(solution)/shard_map/ppermute | solution.py:649
  22.2 4.4 %collective-permute-start.4 = (f32[40,512]{1,0:T(8,128)S(1)}, f32[40,512]{1,0:T(8,128)S(1)}, u32[]{:S(2)}, u32[]{:S(2)}) collective-permute-start(f32[40,512]{1,0:T(8,128)S(1)} %get-tuple-element.73), channel_id=1, source_target_pairs={{0,32},{1,33},{2,34},{3,35},{4,36},{5,37},{6,38},{7,39},{8,40},{9,... | collective-permute-start | bytes 245768 | tf_op jit(solution)/shard_map/ppermute | solution.py:649
  22.2 4.4 %collective-permute-start.5 = (f32[40,512]{1,0:T(8,128)S(1)}, f32[40,512]{1,0:T(8,128)S(1)}, u32[]{:S(2)}, u32[]{:S(2)}) collective-permute-start(f32[40,512]{1,0:T(8,128)S(1)} %get-tuple-element.74), channel_id=1, source_target_pairs={{0,1},{1,0},{2,3},{3,2},{4,5},{5,4},{6,7},{7,6},{8,9},{9,8},{10,11... | collective-permute-start | bytes 245768 | tf_op jit(solution)/shard_map/ppermute | solution.py:649
  28.0 6.7 %collective-permute-start.10 = (f32[32,512]{1,0:T(8,128)S(1)}, f32[32,512]{1,0:T(8,128)S(1)}, u32[]{:S(2)}, u32[]{:S(2)}) collective-permute-start(f32[32,512]{1,0:T(8,128)S(1)} %get-tuple-element.83), channel_id=1, source_target_pairs={{0,1},{1,0},{2,3},{3,2},{4,5},{5,4},{6,7},{7,6},{8,9},{9,8},{10,11... | collective-permute-start | bytes 196616 | tf_op jit(solution)/shard_map/ppermute | solution.py:649
  28.1 6.6 %collective-permute-start.11 = (f32[32,512]{1,0:T(8,128)S(1)}, f32[32,512]{1,0:T(8,128)S(1)}, u32[]{:S(2)}, u32[]{:S(2)}) collective-permute-start(f32[32,512]{1,0:T(8,128)S(1)} %get-tuple-element.84), channel_id=1, source_target_pairs={{0,32},{1,2},{2,1},{3,4},{4,3},{5,6},{6,5},{7,8},{8,7},{9,10},{10,... | collective-permute-start | bytes 196616 | tf_op jit(solution)/shard_map/ppermute | solution.py:649
  30.7 3.9 %collective-permute-start.8 = (f32[16,512]{1,0:T(8,128)S(1)}, f32[16,512]{1,0:T(8,128)S(1)}, u32[]{:S(2)}, u32[]{:S(2)}) collective-permute-start(f32[16,512]{1,0:T(8,128)S(1)} %get-tuple-element.81), channel_id=1, source_target_pairs={{0,32},{1,33},{2,34},{3,35},{4,36},{5,37},{6,38},{7,39},{8,40},{9,... | collective-permute-start | bytes 98312 | tf_op jit(solution)/shard_map/ppermute | solution.py:649
  30.7 3.9 %collective-permute-start.9 = (f32[16,512]{1,0:T(8,128)S(1)}, f32[16,512]{1,0:T(8,128)S(1)}, u32[]{:S(2)}, u32[]{:S(2)}) collective-permute-start(f32[16,512]{1,0:T(8,128)S(1)} %get-tuple-element.82), channel_id=1, source_target_pairs={{0,1},{1,0},{2,3},{3,2},{4,5},{5,4},{6,7},{7,6},{8,9},{9,8},{10,11... | collective-permute-start | bytes 98312 | tf_op jit(solution)/shard_map/ppermute | solution.py:649
  35.3 18.2 %copy-start.1 = (f32[8,8]{1,0:T(8,128)S(1)}, f32[8,8]{1,0:T(8,128)}, u32[]{:S(2)}) copy-start(f32[8,8]{1,0:T(8,128)} %kc.3) | copy-start | bytes 772
  35.3 6.0 %collective-permute-start.14 = (f32[32,512]{1,0:T(8,128)S(1)}, f32[32,512]{1,0:T(8,128)S(1)}, u32[]{:S(2)}, u32[]{:S(2)}) collective-permute-start(f32[32,512]{1,0:T(8,128)S(1)} %get-tuple-element.88), channel_id=1, source_target_pairs={{0,1},{1,0},{2,3},{3,2},{4,5},{5,4},{6,7},{7,6},{8,9},{9,8},{10,11... | collective-permute-start | bytes 196616 | tf_op jit(solution)/shard_map/ppermute | solution.py:649
  35.4 5.9 %collective-permute-start.15 = (f32[32,512]{1,0:T(8,128)S(1)}, f32[32,512]{1,0:T(8,128)S(1)}, u32[]{:S(2)}, u32[]{:S(2)}) collective-permute-start(f32[32,512]{1,0:T(8,128)S(1)} %get-tuple-element.89), channel_id=1, source_target_pairs={{0,32},{1,2},{2,1},{3,4},{4,3},{5,6},{6,5},{7,8},{8,7},{9,10},{10,... | collective-permute-start | bytes 196616 | tf_op jit(solution)/shard_map/ppermute | solution.py:649
  37.4 3.9 %collective-permute-start.12 = (f32[16,512]{1,0:T(8,128)S(1)}, f32[16,512]{1,0:T(8,128)S(1)}, u32[]{:S(2)}, u32[]{:S(2)}) collective-permute-start(f32[16,512]{1,0:T(8,128)S(1)} %get-tuple-element.86), channel_id=1, source_target_pairs={{0,32},{1,33},{2,34},{3,35},{4,36},{5,37},{6,38},{7,39},{8,40},{9,... | collective-permute-start | bytes 98312 | tf_op jit(solution)/shard_map/ppermute | solution.py:649
  37.4 3.9 %collective-permute-start.13 = (f32[16,512]{1,0:T(8,128)S(1)}, f32[16,512]{1,0:T(8,128)S(1)}, u32[]{:S(2)}, u32[]{:S(2)}) collective-permute-start(f32[16,512]{1,0:T(8,128)S(1)} %get-tuple-element.87), channel_id=1, source_target_pairs={{0,1},{1,0},{2,3},{3,2},{4,5},{5,4},{6,7},{7,6},{8,9},{9,8},{10,11... | collective-permute-start | bytes 98312 | tf_op jit(solution)/shard_map/ppermute | solution.py:649
  42.1 4.1 %collective-permute-start.16 = (f32[96,128]{1,0:T(8,128)S(1)}, f32[96,128]{1,0:T(8,128)S(1)}, u32[]{:S(2)}, u32[]{:S(2)}) collective-permute-start(f32[96,128]{1,0:T(8,128)S(1)} %get-tuple-element.92), channel_id=1, source_target_pairs={{0,32},{1,33},{2,34},{3,35},{4,36},{5,37},{6,38},{7,39},{8,40},{9,... | collective-permute-start | bytes 147464 | tf_op jit(solution)/shard_map/ppermute | solution.py:649
  42.2 4.2 %collective-permute-start.17 = (f32[96,128]{1,0:T(8,128)S(1)}, f32[96,128]{1,0:T(8,128)S(1)}, u32[]{:S(2)}, u32[]{:S(2)}) collective-permute-start(f32[96,128]{1,0:T(8,128)S(1)} %get-tuple-element.93), channel_id=1, source_target_pairs={{0,1},{1,0},{2,3},{3,2},{4,5},{5,4},{6,7},{7,6},{8,9},{9,8},{10,11... | collective-permute-start | bytes 147464 | tf_op jit(solution)/shard_map/ppermute | solution.py:649
  46.9 2.1 %collective-permute-start.18 = (f32[240,128]{1,0:T(8,128)S(1)}, f32[240,128]{1,0:T(8,128)S(1)}, u32[]{:S(2)}, u32[]{:S(2)}) collective-permute-start(f32[240,128]{1,0:T(8,128)S(1)} %get-tuple-element.94), channel_id=1, source_target_pairs={{0,1},{1,0},{2,3},{3,2},{4,5},{5,4},{6,7},{7,6},{8,9},{9,8},{10,11... | collective-permute-start | bytes 368648 | tf_op jit(solution)/shard_map/ppermute | solution.py:649
  47.0 6.5 %collective-permute-start.19 = (f32[240,128]{1,0:T(8,128)S(1)}, f32[240,128]{1,0:T(8,128)S(1)}, u32[]{:S(2)}, u32[]{:S(2)}) collective-permute-start(f32[240,128]{1,0:T(8,128)S(1)} %get-tuple-element.95), channel_id=1, source_target_pairs={{0,32},{1,2},{2,1},{3,4},{4,3},{5,6},{6,5},{7,8},{8,7},{9,10},{10,... | collective-permute-start | bytes 368648 | tf_op jit(solution)/shard_map/ppermute | solution.py:649
  56.1 4.2 %collective-permute-start.20 = (f32[96,128]{1,0:T(8,128)S(1)}, f32[96,128]{1,0:T(8,128)S(1)}, u32[]{:S(2)}, u32[]{:S(2)}) collective-permute-start(f32[96,128]{1,0:T(8,128)S(1)} %get-tuple-element.97), channel_id=1, source_target_pairs={{0,32},{1,33},{2,34},{3,35},{4,36},{5,37},{6,38},{7,39},{8,40},{9,... | collective-permute-start | bytes 147464 | tf_op jit(solution)/shard_map/ppermute | solution.py:649
  56.2 4.2 %collective-permute-start.21 = (f32[96,128]{1,0:T(8,128)S(1)}, f32[96,128]{1,0:T(8,128)S(1)}, u32[]{:S(2)}, u32[]{:S(2)}) collective-permute-start(f32[96,128]{1,0:T(8,128)S(1)} %get-tuple-element.98), channel_id=1, source_target_pairs={{0,1},{1,0},{2,3},{3,2},{4,5},{5,4},{6,7},{7,6},{8,9},{9,8},{10,11... | collective-permute-start | bytes 147464 | tf_op jit(solution)/shard_map/ppermute | solution.py:649
  61.0 1.4 %collective-permute-start.22 = (f32[240,128]{1,0:T(8,128)S(1)}, f32[240,128]{1,0:T(8,128)S(1)}, u32[]{:S(2)}, u32[]{:S(2)}) collective-permute-start(f32[240,128]{1,0:T(8,128)S(1)} %get-tuple-element.99), channel_id=1, source_target_pairs={{0,1},{1,0},{2,3},{3,2},{4,5},{5,4},{6,7},{7,6},{8,9},{9,8},{10,11... | collective-permute-start | bytes 368648 | tf_op jit(solution)/shard_map/ppermute | solution.py:649
  61.1 6.5 %collective-permute-start.23 = (f32[240,128]{1,0:T(8,128)S(1)}, f32[240,128]{1,0:T(8,128)S(1)}, u32[]{:S(2)}, u32[]{:S(2)}) collective-permute-start(f32[240,128]{1,0:T(8,128)S(1)} %get-tuple-element.100), channel_id=1, source_target_pairs={{0,32},{1,2},{2,1},{3,4},{4,3},{5,6},{6,5},{7,8},{8,7},{9,10},{10,... | collective-permute-start | bytes 368648 | tf_op jit(solution)/shard_map/ppermute | solution.py:649
  70.8 4.3 %collective-permute-start.26 = (f32[32,512]{1,0:T(8,128)S(1)}, f32[32,512]{1,0:T(8,128)S(1)}, u32[]{:S(2)}, u32[]{:S(2)}) collective-permute-start(f32[32,512]{1,0:T(8,128)S(1)} %get-tuple-element.106), channel_id=1, source_target_pairs={{0,1},{1,0},{2,3},{3,2},{4,5},{5,4},{6,7},{7,6},{8,9},{9,8},{10,11... | collective-permute-start | bytes 196616 | tf_op jit(solution)/shard_map/ppermute | solution.py:649
  70.9 5.9 %collective-permute-start.27 = (f32[32,512]{1,0:T(8,128)S(1)}, f32[32,512]{1,0:T(8,128)S(1)}, u32[]{:S(2)}, u32[]{:S(2)}) collective-permute-start(f32[32,512]{1,0:T(8,128)S(1)} %get-tuple-element.107), channel_id=1, source_target_pairs={{0,32},{1,2},{2,1},{3,4},{4,3},{5,6},{6,5},{7,8},{8,7},{9,10},{10,... | collective-permute-start | bytes 196616 | tf_op jit(solution)/shard_map/ppermute | solution.py:649
  71.0 4.0 %collective-permute-start.24 = (f32[16,512]{1,0:T(8,128)S(1)}, f32[16,512]{1,0:T(8,128)S(1)}, u32[]{:S(2)}, u32[]{:S(2)}) collective-permute-start(f32[16,512]{1,0:T(8,128)S(1)} %get-tuple-element.104), channel_id=1, source_target_pairs={{0,32},{1,33},{2,34},{3,35},{4,36},{5,37},{6,38},{7,39},{8,40},{9,... | collective-permute-start | bytes 98312 | tf_op jit(solution)/shard_map/ppermute | solution.py:649
  71.2 3.9 %collective-permute-start.25 = (f32[16,512]{1,0:T(8,128)S(1)}, f32[16,512]{1,0:T(8,128)S(1)}, u32[]{:S(2)}, u32[]{:S(2)}) collective-permute-start(f32[16,512]{1,0:T(8,128)S(1)} %get-tuple-element.105), channel_id=1, source_target_pairs={{0,1},{1,0},{2,3},{3,2},{4,5},{5,4},{6,7},{7,6},{8,9},{9,8},{10,11... | collective-permute-start | bytes 98312 | tf_op jit(solution)/shard_map/ppermute | solution.py:649
  77.8 5.7 %collective-permute-start.30 = (f32[48,512]{1,0:T(8,128)S(1)}, f32[48,512]{1,0:T(8,128)S(1)}, u32[]{:S(2)}, u32[]{:S(2)}) collective-permute-start(f32[48,512]{1,0:T(8,128)S(1)} %get-tuple-element.112), channel_id=1, source_target_pairs={{0,1},{1,0},{2,3},{3,2},{4,5},{5,4},{6,7},{7,6},{8,9},{9,8},{10,11... | collective-permute-start | bytes 294920 | tf_op jit(solution)/shard_map/ppermute | solution.py:649
  77.9 6.2 %collective-permute-start.31 = (f32[48,512]{1,0:T(8,128)S(1)}, f32[48,512]{1,0:T(8,128)S(1)}, u32[]{:S(2)}, u32[]{:S(2)}) collective-permute-start(f32[48,512]{1,0:T(8,128)S(1)} %get-tuple-element.113), channel_id=1, source_target_pairs={{0,32},{1,2},{2,1},{3,4},{4,3},{5,6},{6,5},{7,8},{8,7},{9,10},{10,... | collective-permute-start | bytes 294920 | tf_op jit(solution)/shard_map/ppermute | solution.py:649
  78.8 4.4 %collective-permute-start.28 = (f32[40,512]{1,0:T(8,128)S(1)}, f32[40,512]{1,0:T(8,128)S(1)}, u32[]{:S(2)}, u32[]{:S(2)}) collective-permute-start(f32[40,512]{1,0:T(8,128)S(1)} %get-tuple-element.110), channel_id=1, source_target_pairs={{0,32},{1,33},{2,34},{3,35},{4,36},{5,37},{6,38},{7,39},{8,40},{9,... | collective-permute-start | bytes 245768 | tf_op jit(solution)/shard_map/ppermute | solution.py:649
  79.1 4.4 %collective-permute-start.29 = (f32[40,512]{1,0:T(8,128)S(1)}, f32[40,512]{1,0:T(8,128)S(1)}, u32[]{:S(2)}, u32[]{:S(2)}) collective-permute-start(f32[40,512]{1,0:T(8,128)S(1)} %get-tuple-element.111), channel_id=1, source_target_pairs={{0,1},{1,0},{2,3},{3,2},{4,5},{5,4},{6,7},{7,6},{8,9},{9,8},{10,11... | collective-permute-start | bytes 245768 | tf_op jit(solution)/shard_map/ppermute | solution.py:649
  85.9 6.1 %collective-permute-start.34 = (f32[48,512]{1,0:T(8,128)S(1)}, f32[48,512]{1,0:T(8,128)S(1)}, u32[]{:S(2)}, u32[]{:S(2)}) collective-permute-start(f32[48,512]{1,0:T(8,128)S(1)} %get-tuple-element.117), channel_id=1, source_target_pairs={{0,1},{1,0},{2,3},{3,2},{4,5},{5,4},{6,7},{7,6},{8,9},{9,8},{10,11... | collective-permute-start | bytes 294920 | tf_op jit(solution)/shard_map/ppermute | solution.py:649
  86.0 6.2 %collective-permute-start.35 = (f32[48,512]{1,0:T(8,128)S(1)}, f32[48,512]{1,0:T(8,128)S(1)}, u32[]{:S(2)}, u32[]{:S(2)}) collective-permute-start(f32[48,512]{1,0:T(8,128)S(1)} %get-tuple-element.118), channel_id=1, source_target_pairs={{0,32},{1,2},{2,1},{3,4},{4,3},{5,6},{6,5},{7,8},{8,7},{9,10},{10,... | collective-permute-start | bytes 294920 | tf_op jit(solution)/shard_map/ppermute | solution.py:649
  87.1 4.4 %collective-permute-start.32 = (f32[40,512]{1,0:T(8,128)S(1)}, f32[40,512]{1,0:T(8,128)S(1)}, u32[]{:S(2)}, u32[]{:S(2)}) collective-permute-start(f32[40,512]{1,0:T(8,128)S(1)} %get-tuple-element.115), channel_id=1, source_target_pairs={{0,32},{1,33},{2,34},{3,35},{4,36},{5,37},{6,38},{7,39},{8,40},{9,... | collective-permute-start | bytes 245768 | tf_op jit(solution)/shard_map/ppermute | solution.py:649
  87.5 4.4 %collective-permute-start.33 = (f32[40,512]{1,0:T(8,128)S(1)}, f32[40,512]{1,0:T(8,128)S(1)}, u32[]{:S(2)}, u32[]{:S(2)}) collective-permute-start(f32[40,512]{1,0:T(8,128)S(1)} %get-tuple-element.116), channel_id=1, source_target_pairs={{0,1},{1,0},{2,3},{3,2},{4,5},{5,4},{6,7},{7,6},{8,9},{9,8},{10,11... | collective-permute-start | bytes 245768 | tf_op jit(solution)/shard_map/ppermute | solution.py:649
  88.3 3.9 %copy-start = (bf16[216,240]{1,0:T(8,128)(2,1)S(1)}, bf16[216,240]{1,0:T(8,128)(2,1)}, u32[]{:S(2)}) copy-start(bf16[216,240]{1,0:T(8,128)(2,1)} %constant.18.clone.from_slot) | copy-start | bytes 311044
  88.3 3.9 %copy-start.2 = (f32[4,4,128]{2,1,0:T(4,128)S(1)}, f32[4,4,128]{2,1,0:T(4,128)}, u32[]{:S(2)}) copy-start(f32[4,4,128]{2,1,0:T(4,128)} %param.23) | copy-start | bytes 24580

commit v4 on v3

--- a/solution.py
+++ b/solution.py
@@ -35,7 +35,7 @@
     return to_slot
 
 
-def call(kernel, outs, scratch=(), smem=(), hbm=(), cost=None):
+def call(kernel, outs, scratch=(), smem=(), hbm=(), hbm_outs=False):
     def run(*operands):
         specs = [
             pl.BlockSpec(
@@ -51,10 +51,11 @@
             kernel,
             out_shape=tuple(jax.ShapeDtypeStruct(s, d) for s, d in outs),
             in_specs=specs,
-            out_specs=tuple(pl.BlockSpec(memory_space=pltpu.VMEM) for _ in outs),
+            out_specs=tuple(
+                pl.BlockSpec(memory_space=pltpu.HBM if hbm_outs else pltpu.VMEM) for _ in outs
+            ),
             scratch_shapes=list(scratch),
             compiler_params=pltpu.CompilerParams(vmem_limit_bytes=20 * 1024 * 1024),
-            cost_estimate=cost,
         )(*operands)
 
     return run
@@ -115,43 +116,51 @@
     return idx_ref[axis] % 2 == 0
 
 
-def prepare(slot, fine, smooth, noise, mid, pmid_t, plow_t, kf, sf, nf, pmt, pm, km, plt, spread):
-    def grid(rows, columns):
-        return tuple(lax.broadcasted_iota(jnp.int32, (rows, columns), n) for n in range(2))
-
-    def one_hot(n):
-        row, col = grid(n, n)
-        return jnp.where(row == col, 1.0, 0.0).astype(BF16)
-
-    def wide(out, rows, high, low):
-        gap = jnp.zeros((rows, 16), BF16)
-        out[:, 0:256] = jnp.concatenate([high, gap], axis=1)
-        out[:, 256:512] = jnp.concatenate([high, gap], axis=1)
-        out[:, 512:768] = jnp.concatenate([low, gap], axis=1)
-
-    def narrow(out, high, low):
-        row, col = grid(64, 128)
-        twice = jnp.where((row == col) | (row == col - 64), 1.0, 0.0).astype(BF16)
-        once = jnp.where(row == col, 1.0, 0.0).astype(BF16)
-        out[:, 0:128] = dot(high, twice).astype(BF16)
-        out[:, 128:256] = dot(low, once).astype(BF16)
-
-    def moved(left, part, right):
-        return dot_nt(dot_nt(left, part).astype(BF16), right).astype(BF16)
-
-    wide(sf, SF, *[moved(slot, part, slot) for part in halves(smooth)])
-    wide(kf, SF, *[moved(slot, part, slot) for part in halves(fine)])
+def grid(rows, columns):
+    return tuple(lax.broadcasted_iota(jnp.int32, (rows, columns), n) for n in range(2))
+
+
+def one_hot(n):
+    row, col = grid(n, n)
+    return jnp.where(row == col, 1.0, 0.0).astype(BF16)
+
+
+def wide(out, rows, high, low):
+    gap = jnp.zeros((rows, 16), BF16)
+    out[:, 0:256] = jnp.concatenate([high, gap], axis=1)
+    out[:, 256:512] = jnp.concatenate([high, gap], axis=1)
+    out[:, 512:768] = jnp.concatenate([low, gap], axis=1)
+
+
+def narrow(out, high, low):
+    row, col = grid(64, 128)
+    twice = jnp.where((row == col) | (row == col - 64), 1.0, 0.0).astype(BF16)
+    once = jnp.where(row == col, 1.0, 0.0).astype(BF16)
+    out[:, 0:128] = dot(high, twice).astype(BF16)
+    out[:, 128:256] = dot(low, once).astype(BF16)
+
+
+def turned(left, part):
+    return dot_nt(left, part).astype(BF16)
+
+
+def prepare(slot, fine, mid, pmid_t, plow_t, kf, pmt, km, plt):
+    wide(kf, SF, *[turned(turned(slot, part), slot) for part in halves(fine)])
+    wide(pmt, QM, *[turned(part, slot) for part in halves(pmid_t)])
+    turn = one_hot(QM)
+    narrow(km, *[turned(turn, part) for part in halves(mid)])
+    gap = jnp.zeros((8, QM), BF16)
+    narrow(plt, *[jnp.concatenate([part, gap], axis=0) for part in halves(plow_t)])
+
+
+def late_kernel(slot, noise, pmid_t, plow_t, nf, pm, spread):
     turn = one_hot(QF)
-    wide(nf, QF, *[moved(turn, part, slot) for part in halves(noise)])
-    high, low = halves(pmid_t)
-    wide(pmt, QM, *[dot_nt(part, slot).astype(BF16) for part in (high, low)])
-    narrow(pm, *[dot_nt(slot, part).astype(BF16) for part in (high, low)])
+    wide(nf, QF, *[turned(turned(turn, part), slot[...]) for part in halves(noise[...])])
+    narrow(pm, *[turned(slot[...], part) for part in halves(pmid_t[...])])
     turn = one_hot(QM)
-    narrow(km, *[dot_nt(turn, part).astype(BF16) for part in halves(mid)])
-    high, low = halves(plow_t)
-    rest = (plow_t - high.astype(F32) - low.astype(F32)).astype(BF16)
-    gap = jnp.zeros((8, QM), BF16)
-    narrow(plt, *[jnp.concatenate([part, gap], axis=0) for part in (high, low)])
+    values = plow_t[...]
+    high, low = halves(values)
+    rest = (values - high.astype(F32) - low.astype(F32)).astype(BF16)
     columns = dot_nt(turn, high) + dot_nt(turn, low) + dot_nt(turn, rest)
     for d in range(QC):
         spread[d] = jnp.broadcast_to(columns[:, d : d + 1], (QM, 128))
@@ -166,6 +175,12 @@
 def clear_fine(x_ref):
     x_ref[SF:256, :] = jnp.zeros((256 - SF, LANES), BF16)
     x_ref[256 + SF : 512, :] = jnp.zeros((256 - SF, LANES), BF16)
+
+
+def split_product(w_ref, values):
+    high, low = halves(values)
+    w = w_ref[:, 0:SF]
+    return dot(w, high) + dot(w, low) + dot(w_ref[:, 512 : 512 + SF], high)
 
 
 def fine_product(w_ref, x_ref, lanes):
@@ -222,111 +237,116 @@
         t_ref[base + 16 : base + 24, :] += jnp.where(row < 4, lower, upper)
 
 
-def fine_edges(n, t_in, csr, idx, r1, r2, r3, r4, t_ref):
+def fine_edges(n, t_in, csr, idx, r1, r2, r3, r4):
     x_even, y_even = even(idx, 0), even(idx, 1)
-    lanes = chunk(n)
-    t_ref[:, lanes] = t_in[:, lanes]
-    if n == 0:
-        below = jnp.where(x_even, r2[0:40, :], r1[0:40, :])
-        t_ref[0:40, lanes] += csr[0:1, lanes] * below
-    if n == 3:
-        above = jnp.where(x_even, r1[0:40, :], r2[0:40, :])
-        t_ref[200:240, lanes] += csr[1:2, lanes] * above
-    edge = slice(n * 128, n * 128 + 128)
-    first, last = (slice(n * 512 + y * 128, n * 512 + y * 128 + 128) for y in (0, 3))
-    for i in range(6):
-        rows = slice(8 * i, 8 * i + 8)
-        below = jnp.where(y_even, r4[rows, edge], r3[rows, edge])
-        above = jnp.where(y_even, r3[rows, edge], r4[rows, edge])
-        t_ref[40 * i : 40 * i + 8, first] += csr[2:3, first] * below
-        t_ref[40 * i + 8 : 40 * i + 16, last] += csr[3:4, last] * above
-
-
-def fine_update(u_ref, t_in, csr, idx, received, out_ref, sf, x_ref, t_ref):
-    clear_fine(x_ref)
+    columns = []
+    for y in range(4):
+        lanes = slice(n * 512 + y * 128, n * 512 + y * 128 + 128)
+        side, edge = slice(y * 128, y * 128 + 128), slice(n * 128, n * 128 + 128)
+        tiles = []
+        for r in range(SF // 8):
+            tile = t_in[8 * r : 8 * r + 8, lanes]
+            if n == 0 and r < 5:
+                rows = slice(8 * r, 8 * r + 8)
+                tile = tile + csr[0:1, lanes] * jnp.where(x_even, r2[rows, side], r1[rows, side])
+            if n == 3 and r >= 25:
+                rows = slice(8 * r - 200, 8 * r - 192)
+                tile = tile + csr[1:2, lanes] * jnp.where(x_even, r1[rows, side], r2[rows, side])
+            rows = slice(r // 5 * 8, r // 5 * 8 + 8)
+            if y == 0 and r % 5 == 0:
+                tile = tile + csr[2:3, lanes] * jnp.where(y_even, r4[rows, edge], r3[rows, edge])
+            if y == 3 and r % 5 == 1:
+                tile = tile + csr[3:4, lanes] * jnp.where(y_even, r3[rows, edge], r4[rows, edge])
+            tiles.append(tile)
+        columns.append(jnp.concatenate(tiles, axis=0))
+    return jnp.concatenate(columns, axis=1)
+
+
+def fine_update(u_ref, t_in, csr, idx, received, out_ref, sf):
     for n in range(4):
-        fine_edges(n, t_in, csr, idx, *received, t_ref)
-        t = t_ref[:, chunk(n)]
-        split_fine(t, x_ref, chunk(n))
-        out_ref[:, chunk(n)] = u_ref[:, chunk(n)] + 0.25 * t + fine_product(sf, x_ref, chunk(n))
+        t = fine_edges(n, t_in, csr, idx, *received)
+        out_ref[:, chunk(n)] = u_ref[:, chunk(n)] + split_product(sf, t)
 
 
 def first_kernel(
-    seed_in, scale_in, coef_in, slot_in, smooth_in, fine_in, noise_in, mid_in, pmid_in, plow_in, idx,
-    g, u1, csx, csr, s1, s2, s3, s4, kf, sf, nf, pmt, pm, km, plt, spread,
-    x_ref, seed, scale, coef, slot, smooth, fine, noise, mid, pmid, plow, done,
+    seed_in, scale_in, coef_in, slot_in, smooth_in, fine_in, mid_in, pmid_in, plow_in, idx,
+    g, u1, csx, csr, s1, s2, s3, s4, kf, sf, pmt, km, plt,
+    seed, scale, coef, slot, smooth, fine, mid, pmid, plow, done,
 ):
     copies = {}
     for n, (name, source, target) in enumerate(
         (
+            ("scale", scale_in, scale),
+            ("coef", coef_in, coef),
             ("slot", slot_in, slot),
             ("smooth", smooth_in, smooth),
             ("fine", fine_in, fine),
-            ("noise", noise_in, noise),
             ("pmid", pmid_in, pmid),
             ("plow", plow_in, plow),
             ("mid", mid_in, mid),
-            ("scale", scale_in, scale),
-            ("coef", coef_in, coef),
             ("seed", seed_in, seed),
         )
     ):
         copies[name] = pltpu.make_async_copy(source, target, done.at[n])
         copies[name].start()
-    clear_fine(x_ref)
-    x_ref[QF:SF, :] = jnp.zeros((SF - QF, LANES), BF16)
-    x_ref[256 + QF : 256 + SF, :] = jnp.zeros((SF - QF, LANES), BF16)
-    csr[...] = jnp.zeros((8, LANES), F32)
+    csr[6:8, :] = jnp.zeros((2, LANES), F32)
     csx[...] = jnp.zeros((16, 512), F32)
-    for name in ("slot", "smooth", "fine", "noise", "pmid", "plow", "mid"):
-        copies[name].wait()
-    matrices = (ref[...] for ref in (slot, fine, smooth, noise, mid, pmid, plow))
-    prepare(*matrices, kf, sf, nf, pmt, pm, km, plt, spread)
     copies["scale"].wait()
     copies["coef"].wait()
     over = 1.0 / scale[...]
-    lane = lax.broadcasted_iota(jnp.int32, (1, 128), 1)
-    for c in range(COLS):
-        x, y = c // 4, c % 4
-        lanes = slice(c * 128, c * 128 + 128)
-        for d in range(3):
-            value = coef[16 * d + c : 16 * d + c + 1, :] * over[c : c + 1, :]
-            csx[4 * x + d : 4 * x + d + 1, y * 128 : y * 128 + 128] = value
-            low, high = 0.9 * value, 0.3 * value
-            if d == 0 and x == 0:
-                low = jnp.where(idx[0] == 0, 0.0, low)
-            if d == 0 and x == 3:
-                high = jnp.where(idx[0] == idx[2] - 1, 0.0, high)
-            if d == 1 and y == 0:
-                low = jnp.where(idx[1] == 0, 0.0, low)
-            if d == 1 and y == 3:
-                high = jnp.where(idx[1] == idx[3] - 1, 0.0, high)
-            if d == 2:
-                low = jnp.where(lane == 0, 0.0, low)
-                high = jnp.where(lane == 127, 0.0, high)
-            csr[2 * d : 2 * d + 1, lanes] = low
-            csr[2 * d + 1 : 2 * d + 2, lanes] = high
-    copies["seed"].wait()
-    for c in range(COLS):
-        lanes = slice(c * 128, c * 128 + 128)
-        values = seed[pl.ds(c, QF, stride=COLS), :] * over[c : c + 1, :]
-        high, low = halves(values)
-        rest = (values - high.astype(F32) - low.astype(F32)).astype(BF16)
-        g[:, lanes] = dot(slot[...], high) + dot(slot[...], low) + dot(slot[...], rest)
-    for n in range(4):
-        values = g[:, chunk(n)]
-        split_fine(values, x_ref, chunk(n))
-        u1[:, chunk(n)] = 0.25 * values + fine_product(sf, x_ref, chunk(n))
-    fine_sends(u1, idx, s1, s2, s3, s4)
+    lane = lax.broadcasted_iota(jnp.int32, (COLS, 128), 1)
+    column = lax.broadcasted_iota(jnp.int32, (COLS, 128), 0)
+    for d in range(3):
+        value = coef[16 * d : 16 * d + 16, :] * over
+        low, high = 0.9 * value, 0.3 * value
+        if d == 0:
+            low = jnp.where((column < 4) & (idx[0] == 0), 0.0, low)
+            high = jnp.where((column >= 12) & (idx[0] == idx[2] - 1), 0.0, high)
+        if d == 1:
+            low = jnp.where((column % 4 == 0) & (idx[1] == 0), 0.0, low)
+            high = jnp.where((column % 4 == 3) & (idx[1] == idx[3] - 1), 0.0, high)
+        if d == 2:
+            low = jnp.where(lane == 0, 0.0, low)
+            high = jnp.where(lane == 127, 0.0, high)
+        for c in range(COLS):
+            x, y = c // 4, c % 4
+            lanes = slice(c * 128, c * 128 + 128)
+            csx[4 * x + d : 4 * x + d + 1, y * 128 : y * 128 + 128] = value[c : c + 1, :]
+            csr[2 * d : 2 * d + 1, lanes] = low[c : c + 1, :]
+            csr[2 * d + 1 : 2 * d + 2, lanes] = high[c : c + 1, :]
     x_even = even(idx, 0)
     far, near = csx[4:16, :], csx[0:12, :]
     gap = jnp.zeros((4, 512), F32)
     s1[40:56, :] = jnp.concatenate([jnp.where(x_even, far, near), gap], axis=0)
     s2[40:56, :] = jnp.concatenate([jnp.where(x_even, near, far), gap], axis=0)
-
-
-def spread_kernel(u, t_in, csr, idx, r1, r2, r3, r4, sf, csx, out, s1, s2, s3, s4, x_ref, t_ref):
-    fine_update(u, t_in, csr, idx, (r1, r2, r3, r4), out, sf, x_ref, t_ref)
+    for name in ("slot", "smooth", "fine", "pmid", "plow", "mid"):
+        copies[name].wait()
+    row, col = grid(QF, QF)
+    first = [
+        turned(slot[...], part)
+        for part in halves(smooth[...] + jnp.where(row == col, 0.25, 0.0))
+    ]
+    wide(sf, SF, *[turned(part, slot[...]) for part in first])
+    prepare(slot[...], fine[...], mid[...], pmid[...], plow[...], kf, pmt, km, plt)
+    copies["seed"].wait()
+    both = jnp.concatenate([first[0], slot[...]], axis=0)
+    for n in range(4):
+        values = jnp.concatenate(
+            [
+                seed[pl.ds(c, QF, stride=COLS), :] * over[c : c + 1, :]
+                for c in range(4 * n, 4 * n + 4)
+            ],
+            axis=1,
+        )
+        high, low = halves(values)
+        result = dot(both, high) + dot(both, low)
+        g[:, chunk(n)] = result[SF:, :]
+        u1[:, chunk(n)] = result[:SF, :] + dot(first[1], high)
+    fine_sends(u1, idx, s1, s2, s3, s4)
+
+
+def spread_kernel(u, t_in, csr, idx, r1, r2, r3, r4, sf, csx, out, s1, s2, s3, s4):
+    fine_update(u, t_in, csr, idx, (r1, r2, r3, r4), out, sf)
     fine_sends(out, idx, s1, s2, s3, s4)
     x_even, y_even = even(idx, 0), even(idx, 1)
     left = jnp.where(x_even, r2[40:56, :], r1[40:56, :])
@@ -371,41 +391,44 @@
                 coef[2 * d + 1, row, :] = high
 
 
-def sweep_kernel(u, t_in, csr, idx, r1, r2, r3, r4, sf, out, s1, s2, s3, s4, x_ref, t_ref):
-    fine_update(u, t_in, csr, idx, (r1, r2, r3, r4), out, sf, x_ref, t_ref)
+def sweep_kernel(u, t_in, csr, idx, r1, r2, r3, r4, sf, out, s1, s2, s3, s4):
+    fine_update(u, t_in, csr, idx, (r1, r2, r3, r4), out, sf)
     fine_sends(out, idx, s1, s2, s3, s4)
 
 
-def restrict_kernel(t_in, csr, idx, r1, r2, r3, r4, pmt, gm, m1, s1, s2, s3, s4, x_ref, t_ref):
-    clear_fine(x_ref)
+def restrict_kernel(t_in, csr, idx, r1, r2, r3, r4, pmt, gm, m1, s1, s2, s3, s4):
     for n in range(4):
-        fine_edges(n, t_in, csr, idx, r1, r2, r3, r4, t_ref)
-        split_fine(t_ref[:, chunk(n)], x_ref, chunk(n))
-        value = fine_product(pmt, x_ref, chunk(n))
+        value = split_product(pmt, fine_edges(n, t_in, csr, idx, r1, r2, r3, r4))
         gm[:, chunk(n)] = value
         m1[:, chunk(n)] = 0.2 * value
     mid_sends(m1, idx, s1, s2, s3, s4)
 
 
 def last_kernel(
-    u, t_in, csr, idx, r1, r2, r3, r4, sf, nf, from_slot, inc, out, prev, x_ref, t_ref, w_ref
+    u, t_in, csr, idx, r1, r2, r3, r4, sf, nf, from_slot, inc, out, prev,
+    u_ref, natural, out_rows, prev_rows, done,
 ):
-    fine_update(u, t_in, csr, idx, (r1, r2, r3, r4), w_ref, sf, x_ref, t_ref)
+    fine_update(u, t_in, csr, idx, (r1, r2, r3, r4), u_ref, sf)
     slot = from_slot[...]
     for n in range(4):
-        values = w_ref[:, chunk(n)]
-        split_fine(values, x_ref, chunk(n))
-        high, low = halves(values)
-        rest = (values - high.astype(F32) - low.astype(F32)).astype(BF16)
-        natural = dot(slot, high) + dot(slot, low) + dot(slot, rest)
-        noise = fine_product(nf, x_ref, chunk(n))
+        high, low = halves(u_ref[:, chunk(n)])
+        natural[:, chunk(n)] = dot(slot, high) + dot(slot, low)
+        for c in range(4 * n, 4 * n + 4):
+            out_rows[pl.ds(c, QF, stride=COLS), :] = natural[:, c * 128 : c * 128 + 128]
+    first = pltpu.make_async_copy(out_rows, out, done.at[0])
+    first.start()
+    for n in range(4):
+        noise = split_product(nf, u_ref[:, chunk(n)])
         for y in range(4):
             c = 4 * n + y
-            lanes = slice(y * 128, y * 128 + 128)
-            out[pl.ds(c, QF, stride=COLS), :] = natural[:, lanes]
-            prev[pl.ds(c, QF, stride=COLS), :] = (
-                natural[:, lanes] + inc[c : c + 1, :] * noise[:, lanes]
+            prev_rows[pl.ds(c, QF, stride=COLS), :] = (
+                natural[:, c * 128 : c * 128 + 128]
+                + inc[c : c + 1, :] * noise[:, y * 128 : y * 128 + 128]
             )
+    second = pltpu.make_async_copy(prev_rows, prev, done.at[1])
+    second.start()
+    first.wait()
+    second.wait()
 
 
 def mid_sends(m_ref, idx, s1, s2, s3, s4):
@@ -554,11 +577,11 @@
 
 def coarse_sweep(c_ref, out_ref, g_ref, coef, kc, first, last):
     def rows(d, plane):
-        return pl.ds(pl.multiple_of(d * WROWS + plane * 16, 16), 16)
-
-    def step(plane, carry):
+        return pl.ds(d * WROWS + plane * 16, 16)
+
+    def step(plane):
         c = [c_ref[rows(d, plane), :] for d in range(QC)]
-        weights = [coef[n, pl.ds(pl.multiple_of(plane * 16, 16), 16), :] for n in range(6)]
+        weights = [coef[n, pl.ds(plane * 16, 16), :] for n in range(6)]
         for d in range(QC):
             t = g_ref[rows(d, plane), :] - 4.0 * c[d]
             for j in range(QC):
@@ -576,9 +599,9 @@
             else:
                 t = t + weights[4] * pltpu.roll(c[d + 1], 1, 1)
             out_ref[rows(d, plane), :] = c[d] + 0.2 * t
-        return carry
-
-    lax.fori_loop(first, last, step, 0)
+
+    for plane in range(first, last):
+        step(plane)
 
 
 def coarse_kernel(own, r1, r2, r3, r4, kc, idx, coef, g, pay, s1, s2, one, two):
@@ -678,7 +701,7 @@
     fine_faces = [((40, 512), F32)] * 2 + [((48, 512), F32)] * 2
     mid_field = ((QM, LANES), F32)
     mid_faces = [((16, 512), F32)] * 2 + [((32, 512), F32)] * 2
-    xf, tf = pltpu.VMEM((512, LANES), BF16), pltpu.VMEM((SF, LANES), F32)
+    xf = pltpu.VMEM((512, LANES), BF16)
     xm, tm = pltpu.VMEM((256, LANES), BF16), pltpu.VMEM((QM, LANES), F32)
     window = ((QC * WROWS, 128), F32)
     windows = [pltpu.VMEM((QC * WROWS, 128), F32)] * 2
@@ -691,12 +714,11 @@
         to_slot,
         smooth,
         fine,
-        noise,
         mid,
         pmid.T,
         plow.T,
     )
-    g, u, csx, csr, s1, s2, s3, s4, kf, sf, nf, pmt, pm, km, plt, spread = call(
+    g, u, csx, csr, s1, s2, s3, s4, kf, sf, pmt, km, plt = call(
         first_kernel,
         [fine_field, fine_field, ((16, 512), F32), ((8, LANES), F32)]
         + [((56, 512), F32)] * 2
@@ -704,19 +726,18 @@
         + [
             ((SF, 768), BF16),
             ((SF, 768), BF16),
-            ((QF, 768), BF16),
             ((QM, 768), BF16),
-            ((SF, 256), BF16),
             ((QM, 256), BF16),
             ((16, 256), BF16),
-            ((QC, QM, 128), F32),
         ],
-        [xf]
-        + [pltpu.VMEM(operand.shape, operand.dtype) for operand in operands]
+        [pltpu.VMEM(operand.shape, operand.dtype) for operand in operands]
         + [pltpu.SemaphoreType.DMA((len(operands),))],
-        (10,),
-        range(10),
+        (9,),
+        range(9),
     )(*operands, idx)
+    nf, pm, spread = call(
+        late_kernel, [((QF, 768), BF16), ((SF, 256), BF16), ((QC, QM, 128), F32)]
+    )(to_slot, noise, pmid.T, plow.T)
 
     def fine_local(u):
         (t,) = call(fine_local_kernel, [fine_field], [xf])(u, g, csr, kf)
@@ -730,14 +751,14 @@
     u, *sends = call(
         spread_kernel,
         [fine_field] + fine_faces[:2] + [((88, 512), F32)] * 2,
-        [xf, tf],
+        (),
         (3,),
     )(u, fine_local(u), csr, idx, *first, sf, csx)
     edges = exchange(sends)
     (coefw,) = call(coefficient_kernel, [((6, WROWS, 128), F32)], (), (0,))(
         idx, csx, first[0], first[1], edges[2], edges[3]
     )
-    gm, m, *sends = call(restrict_kernel, [mid_field, mid_field] + mid_faces, [xf, tf], (2,))(
+    gm, m, *sends = call(restrict_kernel, [mid_field, mid_field] + mid_faces, (), (2,))(
         fine_local(u), csr, idx, *edges, pmt
     )
     edges = exchange(sends)
@@ -760,15 +781,22 @@
         m, mid_local_part(m), csr, idx, *edges, pm, u
     )
     edges = exchange(sends)
-    u, *sends = call(sweep_kernel, [fine_field] + fine_faces, [xf, tf], (3,))(
+    u, *sends = call(sweep_kernel, [fine_field] + fine_faces, (), (3,))(
         u, fine_local(u), csr, idx, *edges, sf
     )
     edges = exchange(sends)
     out, prev = call(
         last_kernel,
         [((QF * COLS, 128), F32)] * 2,
-        [xf, tf, pltpu.VMEM((SF, LANES), F32)],
+        [
+            pltpu.VMEM((SF, LANES), F32),
+            pltpu.VMEM((QF, LANES), F32),
+            pltpu.VMEM((QF * COLS, 128), F32),
+            pltpu.VMEM((QF * COLS, 128), F32),
+            pltpu.SemaphoreType.DMA((2,)),
+        ],
         (3,),
+        hbm_outs=True,
     )(u, fine_local(u), csr, idx, *edges, sf, nf, from_slot, inc.reshape(COLS, 128))
     shape = seed.shape
     return out.reshape(shape), prev.reshape(shape)

time: 98 us -> 94.6 us (0.965)
  Pallas kernels: 34.4 us -> 31 us
    pallas_call x20 -> x21, Pallas kernels: 34.4 us -> 31 us  [run(): pl.pallas_call(kernel, out_shape=tuple((jax.ShapeDtypeStruct(s, d) for s,...]
where the time goes in v4:
time: 94.6 us; the launch traced here: 94.5 us
  waiting for transfers between devices  34.5 us (36%)
  Pallas kernels  31 us (33%)
  starting transfers between devices  27.8 us (29%)
  between operations  1.13 us (1%)
    ppermute x36, waiting for transfers between devices, swap(): return lax.ppermute(values, ('gx', 'yz'), partners(step))  34.5 us
    pallas_call x21, Pallas kernels, run(): pl.pallas_call(kernel, out_shape=tuple((jax.ShapeDtypeStruct(s, d) for s,...  31 us
    ppermute x36, starting transfers between devices, swap(): return lax.ppermute(values, ('gx', 'yz'), partners(step))  27.8 us
  transfers between devices with their start and end apart: 36, of which 20 were waited for; matrix products, arithmetic and copies ran while one was open for 0% of the time, Pallas kernels for 9%

profile of v4, /device:TPU:14, one launch (start us, length us, event | category | flops | bytes accessed | tf_op | source)
XLA Modules:
  0.0 94.5 jit_solution(1538023438944498123)
XLA Ops:
  0.7 4.2 %shard_map.140 = (f32[240,2048]{1,0:T(8,128)S(1)}, f32[240,2048]{1,0:T(8,128)S(1)}, f32[16,512]{1,0:T(8,128)S(1)}, f32[8,2048]{1,0:T(8,128)S(1)}, f32[56,512]{1,...) custom-call(f32[3456,128]{1,0:T(8,128)} %bitcast.15, ...), custom_call_target="tpu_custom_call" | custom-call | tf_op jit(solution)/shard_map/pallas_call | solution.py:50
  4.9 0.5 collective-permute-start
  5.4 2.4 %collective-permute-start.1 = (f32[56,512]{1,0:T(8,128)S(1)}, f32[56,512]{1,0:T(8,128)S(1)}, u32[]{:S(2)}, u32[]{:S(2)}) collective-permute-start(f32[56,512]{1,0:T(8,128)S(1)} %get-tuple-element.67), channel_id=1, source_target_pairs={{0,1},{1,0},{2,3},{3,2},{4,5},{5,4},{6,7},{7,6},{8,9},{9,8},{10,11... | collective-permute-start | bytes 344072 | tf_op jit(solution)/shard_map/ppermute | solution.py:672
  7.8 4.4 %collective-permute-start.3 = (f32[48,512]{1,0:T(8,128)S(1)}, f32[48,512]{1,0:T(8,128)S(1)}, u32[]{:S(2)}, u32[]{:S(2)}) collective-permute-start(f32[48,512]{1,0:T(8,128)S(1)} %get-tuple-element.69), channel_id=1, source_target_pairs={{0,32},{1,2},{2,1},{3,4},{4,3},{5,6},{6,5},{7,8},{8,7},{9,10},{10,... | collective-permute-start | bytes 294920 | tf_op jit(solution)/shard_map/ppermute | solution.py:672
  12.2 1.5 %shard_map.141.t_in = f32[240,2048]{1,0:T(8,128)S(1)} custom-call(f32[240,2048]{1,0:T(8,128)S(1)} %get-tuple-element.62.u_ref.u, f32[240,2048]{1,0:T(8,128)S(1)} %get-tuple-element.63.g_ref, f32[8,2048]{1,0:T(8,128)S(1)} %get-tuple-element.64.csr, bf16[240,768]{1,0:T(8,128)(2,1)S(1)} %get-tuple-element.65.kf), custom_call_target="tpu_custom_call" | custom-call | tf_op jit(solution)/shard_map/pallas_call | solution.py:50
  13.7 0.8 collective-permute-done.3.r4
  14.5 1.6 %shard_map.142 = (f32[240,2048]{1,0:T(8,128)S(1)}, f32[40,512]{1,0:T(8,128)S(1)}, f32[40,512]{1,0:T(8,128)S(1)}, f32[88,512]{1,0:T(8,128)S(1)}, f32[88,512]{1,0:T(8,128)S(1)}) custom-call(f32[240,2048]{1,0:T(8,128)S(1)} %get-tuple-element.62.u_ref.u, f32[240,2048]{1,0:T(8,128)S(1)} %shard_map.141.t_in, f32[8,2048]{1,0:T(8,128)S(1)} %get-tuple-element.64.csr, ...), custom_call_target="tpu_custom_call" | custom-call | tf_op jit(solution)/shard_map/pallas_call | solution.py:50
  16.2 3.9 %collective-permute-start.7 = (f32[88,512]{1,0:T(8,128)S(1)}, f32[88,512]{1,0:T(8,128)S(1)}, u32[]{:S(2)}, u32[]{:S(2)}) collective-permute-start(f32[88,512]{1,0:T(8,128)S(1)} %get-tuple-element.76), channel_id=1, source_target_pairs={{0,32},{1,2},{2,1},{3,4},{4,3},{5,6},{6,5},{7,8},{8,7},{9,10},{10,... | collective-permute-start | bytes 540680 | tf_op jit(solution)/shard_map/ppermute | solution.py:672
  20.1 0.7 collective-permute-start.5
  20.9 1.5 %shard_map.143.t_in = f32[240,2048]{1,0:T(8,128)S(1)} custom-call(f32[240,2048]{1,0:T(8,128)S(1)} %get-tuple-element.72.u_ref.u, f32[240,2048]{1,0:T(8,128)S(1)} %get-tuple-element.63.g_ref, f32[8,2048]{1,0:T(8,128)S(1)} %get-tuple-element.64.csr, bf16[240,768]{1,0:T(8,128)(2,1)S(1)} %get-tuple-element.65.kf), custom_call_target="tpu_custom_call" | custom-call | tf_op jit(solution)/shard_map/pallas_call | solution.py:50
  22.4 2.2 %collective-permute-done.4.r1 = f32[40,512]{1,0:T(8,128)S(1)} collective-permute-done((f32[40,512]{1,0:T(8,128)S(1)}, f32[40,512]{1,0:T(8,128)S(1)}, u32[]{:S(2)}, u32[]{:S(2)}) %collective-permute-start.4) | collective-permute-done | bytes 81952 | tf_op jit(solution)/shard_map/ppermute | solution.py:672
  24.6 1.3 %shard_map.144 = (f32[64,2048]{1,0:T(8,128)S(1)}, f32[64,2048]{1,0:T(8,128)S(1)}, f32[16,512]{1,0:T(8,128)S(1)}, f32[16,512]{1,0:T(8,128)S(1)}, f32[32,512]{1,0:T(8,128)S(1)}, /*index=5*/f32[32,512]{1,0:T(8,128)S(1)}) custom-call(f32[240,2048]{1,0:T(8,128)S(1)} %shard_map.143.t_in, f32[8,2048]{1,0:T(8,128)S(1)} %get-tuple-element.64.csr, ...), custom_call_target="tpu_custom_call" | custom-call | tf_op jit(solution)/shard_map/pallas_call | solution.py:50
  26.0 2.6 %collective-permute-start.11 = (f32[32,512]{1,0:T(8,128)S(1)}, f32[32,512]{1,0:T(8,128)S(1)}, u32[]{:S(2)}, u32[]{:S(2)}) collective-permute-start(f32[32,512]{1,0:T(8,128)S(1)} %get-tuple-element.84), channel_id=1, source_target_pairs={{0,32},{1,2},{2,1},{3,4},{4,3},{5,6},{6,5},{7,8},{8,7},{9,10},{10,... | collective-permute-start | bytes 196616 | tf_op jit(solution)/shard_map/ppermute | solution.py:672
  28.6 0.7 collective-permute-start.9
  29.4 0.5 shard_map.145.t_in
  29.9 2.6 %collective-permute-done.8.r1 = f32[16,512]{1,0:T(8,128)S(1)} collective-permute-done((f32[16,512]{1,0:T(8,128)S(1)}, f32[16,512]{1,0:T(8,128)S(1)}, u32[]{:S(2)}, u32[]{:S(2)}) %collective-permute-start.8) | collective-permute-done | bytes 32800 | tf_op jit(solution)/shard_map/ppermute | solution.py:672
  32.6 0.7 shard_map.146
  33.4 1.9 %collective-permute-start.15 = (f32[32,512]{1,0:T(8,128)S(1)}, f32[32,512]{1,0:T(8,128)S(1)}, u32[]{:S(2)}, u32[]{:S(2)}) collective-permute-start(f32[32,512]{1,0:T(8,128)S(1)} %get-tuple-element.89), channel_id=1, source_target_pairs={{0,32},{1,2},{2,1},{3,4},{4,3},{5,6},{6,5},{7,8},{8,7},{9,10},{10,... | collective-permute-start | bytes 196616 | tf_op jit(solution)/shard_map/ppermute | solution.py:672
  35.3 0.7 collective-permute-start.13
  36.1 0.5 shard_map.147.t_in
  36.6 2.6 %collective-permute-done.12.r1.q1 = f32[16,512]{1,0:T(8,128)S(1)} collective-permute-done((f32[16,512]{1,0:T(8,128)S(1)}, f32[16,512]{1,0:T(8,128)S(1)}, u32[]{:S(2)}, u32[]{:S(2)}) %collective-permute-start.12) | collective-permute-done | bytes 32800 | tf_op jit(solution)/shard_map/ppermute | solution.py:672
  39.2 0.8 shard_map.148
  40.1 0.2 collective-permute-start.16
  40.3 0.8 collective-permute-start.17
  41.1 3.3 %collective-permute-done.16.r1 = f32[96,128]{1,0:T(8,128)S(1)} collective-permute-done((f32[96,128]{1,0:T(8,128)S(1)}, f32[96,128]{1,0:T(8,128)S(1)}, u32[]{:S(2)}, u32[]{:S(2)}) %collective-permute-start.16) | collective-permute-done | bytes 49184 | tf_op jit(solution)/shard_map/ppermute | solution.py:672
  44.4 0.1 collective-permute-done.17.r2
  44.5 0.6 shard_map.149
  45.1 1.3 %collective-permute-start.19 = (f32[240,128]{1,0:T(8,128)S(1)}, f32[240,128]{1,0:T(8,128)S(1)}, u32[]{:S(2)}, u32[]{:S(2)}) collective-permute-start(f32[240,128]{1,0:T(8,128)S(1)} %get-tuple-element.95), channel_id=1, source_target_pairs={{0,32},{1,2},{2,1},{3,4},{4,3},{5,6},{6,5},{7,8},{8,7},{9,10},{10,... | collective-permute-start | bytes 368648 | tf_op jit(solution)/shard_map/ppermute | solution.py:672
  46.4 0.7 shard_map.150.coef
  47.1 4.5 %collective-permute-done.19.r4 = f32[240,128]{1,0:T(8,128)S(1)} collective-permute-done((f32[240,128]{1,0:T(8,128)S(1)}, f32[240,128]{1,0:T(8,128)S(1)}, u32[]{:S(2)}, u32[]{:S(2)}) %collective-permute-start.19) | collective-permute-done | bytes 122912 | tf_op jit(solution)/shard_map/ppermute | solution.py:672
  51.6 2.2 %shard_map.151 = (f32[1280,128]{1,0:T(8,128)S(1)}, f32[128,128]{1,0:T(8,128)S(1)}, f32[96,128]{1,0:T(8,128)S(1)}, f32[96,128]{1,0:T(8,128)S(1)}) custom-call(f32[128,128]{1,0:T(8,128)S(1)} %get-tuple-element.91.own, f32[96,128]{1,0:T(8,128)S(1)} %collective-permute-done.16.r1, f32[96,128]{1,0:T(8,128)S(1)} %collective-permute-done.17.r2, ...), custom_call_target="tpu_custom_call" | custom-call | tf_op jit(solution)/shard_map/pallas_call | solution.py:50
  53.9 0.8 collective-permute-start.21
  54.8 3.3 %collective-permute-done.20.r1 = f32[96,128]{1,0:T(8,128)S(1)} collective-permute-done((f32[96,128]{1,0:T(8,128)S(1)}, f32[96,128]{1,0:T(8,128)S(1)}, u32[]{:S(2)}, u32[]{:S(2)}) %collective-permute-start.20) | collective-permute-done | bytes 49184 | tf_op jit(solution)/shard_map/ppermute | solution.py:672
  58.0 0.1 collective-permute-done.21.r2
  58.1 0.6 shard_map.152
  58.8 0.1 collective-permute-start.23
  58.9 0.7 shard_map.153
  59.6 0.5 collective-permute-done.22.r3
  60.1 5.2 %collective-permute-done.23.r4 = f32[240,128]{1,0:T(8,128)S(1)} collective-permute-done((f32[240,128]{1,0:T(8,128)S(1)}, f32[240,128]{1,0:T(8,128)S(1)}, u32[]{:S(2)}, u32[]{:S(2)}) %collective-permute-start.23) | collective-permute-done | bytes 122912 | tf_op jit(solution)/shard_map/ppermute | solution.py:672
  65.3 2.8 %shard_map.154 = (f32[64,2048]{1,0:T(8,128)S(1)}, f32[16,512]{1,0:T(8,128)S(1)}, f32[16,512]{1,0:T(8,128)S(1)}, f32[32,512]{1,0:T(8,128)S(1)}, f32[32,512]{1,0:T(8,128)S(1)}) custom-call(f32[128,128]{1,0:T(8,128)S(1)} %get-tuple-element.96.own, f32[96,128]{1,0:T(8,128)S(1)} %collective-permute-done.20.r1, f32[96,128]{1,0:T(8,128)S(1)} %collective-permute-done.21.r2, ...), custom_call_target="tpu_custom_call" | custom-call | tf_op jit(solution)/shard_map/pallas_call | solution.py:50
  68.1 0.1 collective-permute-start.27
  68.3 0.2 collective-permute-start.24
  68.5 1.0 %collective-permute-start.25 = (f32[16,512]{1,0:T(8,128)S(1)}, f32[16,512]{1,0:T(8,128)S(1)}, u32[]{:S(2)}, u32[]{:S(2)}) collective-permute-start(f32[16,512]{1,0:T(8,128)S(1)} %get-tuple-element.105), channel_id=1, source_target_pairs={{0,1},{1,0},{2,3},{3,2},{4,5},{5,4},{6,7},{7,6},{8,9},{9,8},{10,11... | collective-permute-start | bytes 98312 | tf_op jit(solution)/shard_map/ppermute | solution.py:672
  69.5 0.5 shard_map.155.t_in
  70.0 2.2 %collective-permute-done.24.r1 = f32[16,512]{1,0:T(8,128)S(1)} collective-permute-done((f32[16,512]{1,0:T(8,128)S(1)}, f32[16,512]{1,0:T(8,128)S(1)}, u32[]{:S(2)}, u32[]{:S(2)}) %collective-permute-start.24) | collective-permute-done | bytes 32800 | tf_op jit(solution)/shard_map/ppermute | solution.py:672
  72.2 0.2 collective-permute-done.25.r2
  72.4 1.6 %collective-permute-done.27.r4 = f32[32,512]{1,0:T(8,128)S(1)} collective-permute-done((f32[32,512]{1,0:T(8,128)S(1)}, f32[32,512]{1,0:T(8,128)S(1)}, u32[]{:S(2)}, u32[]{:S(2)}) %collective-permute-start.27) | collective-permute-done | bytes 65568 | tf_op jit(solution)/shard_map/ppermute | solution.py:672
  74.0 1.0 %shard_map.156 = (f32[240,2048]{1,0:T(8,128)S(1)}, f32[40,512]{1,0:T(8,128)S(1)}, f32[40,512]{1,0:T(8,128)S(1)}, f32[48,512]{1,0:T(8,128)S(1)}, f32[48,512]{1,0:T(8,128)S(1)}) custom-call(f32[64,2048]{1,0:T(8,128)S(1)} %get-tuple-element.103.m_ref.m, f32[64,2048]{1,0:T(8,128)S(1)} %shard_map.155.t_in, f32[8,2048]{1,0:T(8,128)S(1)} %get-tuple-element.64.csr, ...), custom_call_target="tpu_custom_call" | custom-call | tf_op jit(solution)/shard_map/pallas_call | solution.py:50
  75.2 0.9 collective-permute-start.31
  76.1 0.3 collective-permute-start.28
  76.4 0.7 collective-permute-start.29
  77.1 1.5 %shard_map.157.t_in = f32[240,2048]{1,0:T(8,128)S(1)} custom-call(f32[240,2048]{1,0:T(8,128)S(1)} %get-tuple-element.109.u_ref.u, f32[240,2048]{1,0:T(8,128)S(1)} %get-tuple-element.63.g_ref, f32[8,2048]{1,0:T(8,128)S(1)} %get-tuple-element.64.csr, bf16[240,768]{1,0:T(8,128)(2,1)S(1)} %get-tuple-element.65.kf), custom_call_target="tpu_custom_call" | custom-call | tf_op jit(solution)/shard_map/pallas_call | solution.py:50
  78.6 1.9 %collective-permute-done.28.r1 = f32[40,512]{1,0:T(8,128)S(1)} collective-permute-done((f32[40,512]{1,0:T(8,128)S(1)}, f32[40,512]{1,0:T(8,128)S(1)}, u32[]{:S(2)}, u32[]{:S(2)}) %collective-permute-start.28) | collective-permute-done | bytes 81952 | tf_op jit(solution)/shard_map/ppermute | solution.py:672
  80.5 0.3 collective-permute-done.29.r2
  80.8 0.6 collective-permute-done.31.r4
  81.4 1.6 %shard_map.158 = (f32[240,2048]{1,0:T(8,128)S(1)}, f32[40,512]{1,0:T(8,128)S(1)}, f32[40,512]{1,0:T(8,128)S(1)}, f32[48,512]{1,0:T(8,128)S(1)}, f32[48,512]{1,0:T(8,128)S(1)}) custom-call(f32[240,2048]{1,0:T(8,128)S(1)} %get-tuple-element.109.u_ref.u, f32[240,2048]{1,0:T(8,128)S(1)} %shard_map.157.t_in, f32[8,2048]{1,0:T(8,128)S(1)} %get-tuple-element.64.csr, ...), custom_call_target="tpu_custom_call" | custom-call | tf_op jit(solution)/shard_map/pallas_call | solution.py:50
  83.1 1.3 %collective-permute-start.35 = (f32[48,512]{1,0:T(8,128)S(1)}, f32[48,512]{1,0:T(8,128)S(1)}, u32[]{:S(2)}, u32[]{:S(2)}) collective-permute-start(f32[48,512]{1,0:T(8,128)S(1)} %get-tuple-element.118), channel_id=1, source_target_pairs={{0,32},{1,2},{2,1},{3,4},{4,3},{5,6},{6,5},{7,8},{8,7},{9,10},{10,... | collective-permute-start | bytes 294920 | tf_op jit(solution)/shard_map/ppermute | solution.py:672
  84.4 0.3 collective-permute-start.32
  84.7 0.7 collective-permute-start.33
  85.4 1.5 %shard_map.159.t_in = f32[240,2048]{1,0:T(8,128)S(1)} custom-call(f32[240,2048]{1,0:T(8,128)S(1)} %get-tuple-element.114.u_ref.u, f32[240,2048]{1,0:T(8,128)S(1)} %get-tuple-element.63.g_ref, f32[8,2048]{1,0:T(8,128)S(1)} %get-tuple-element.64.csr, bf16[240,768]{1,0:T(8,128)(2,1)S(1)} %get-tuple-element.65.kf), custom_call_target="tpu_custom_call" | custom-call | tf_op jit(solution)/shard_map/pallas_call | solution.py:50
  86.9 1.9 %collective-permute-done.32.r1 = f32[40,512]{1,0:T(8,128)S(1)} collective-permute-done((f32[40,512]{1,0:T(8,128)S(1)}, f32[40,512]{1,0:T(8,128)S(1)}, u32[]{:S(2)}, u32[]{:S(2)}) %collective-permute-start.32) | collective-permute-done | bytes 81952 | tf_op jit(solution)/shard_map/ppermute | solution.py:672
  88.8 0.3 collective-permute-done.33.r2
  89.1 0.4 collective-permute-done.35.r4
  89.5 4.8 %shard_map.160 = (f32[3456,128]{1,0:T(8,128)}, f32[3456,128]{1,0:T(8,128)}) custom-call(f32[240,2048]{1,0:T(8,128)S(1)} %get-tuple-element.114.u_ref.u, f32[240,2048]{1,0:T(8,128)S(1)} %shard_map.159.t_in, f32[8,2048]{1,0:T(8,128)S(1)} %get-tuple-element.64.csr, s32[4]{0:T(128)S(1)} %pad_add_fusion.idx, f32[40,512]{1,0:T(8,128)S(1)} %collective-permute-done.32.r1, ...), custom_call_target="tpu_custom_call" | custom-call | tf_op jit(solution)/shard_map/pallas_call | solution.py:50
  (44 shorter events, 0.9 us)
Async XLA Ops:
  4.9 9.6 %collective-permute-start = (f32[56,512]{1,0:T(8,128)S(1)}, f32[56,512]{1,0:T(8,128)S(1)}, u32[]{:S(2)}, u32[]{:S(2)}) collective-permute-start(f32[56,512]{1,0:T(8,128)S(1)} %get-tuple-element.66), channel_id=1, source_target_pairs={{0,32},{1,33},{2,34},{3,35},{4,36},{5,37},{6,38},{7,39},{8,40},{9,... | collective-permute-start | bytes 344072 | tf_op jit(solution)/shard_map/ppermute | solution.py:672
  5.4 9.1 %collective-permute-start.1 = (f32[56,512]{1,0:T(8,128)S(1)}, f32[56,512]{1,0:T(8,128)S(1)}, u32[]{:S(2)}, u32[]{:S(2)}) collective-permute-start(f32[56,512]{1,0:T(8,128)S(1)} %get-tuple-element.67), channel_id=1, source_target_pairs={{0,1},{1,0},{2,3},{3,2},{4,5},{5,4},{6,7},{7,6},{8,9},{9,8},{10,11... | collective-permute-start | bytes 344072 | tf_op jit(solution)/shard_map/ppermute | solution.py:672
  7.8 5.9 %collective-permute-start.2 = (f32[48,512]{1,0:T(8,128)S(1)}, f32[48,512]{1,0:T(8,128)S(1)}, u32[]{:S(2)}, u32[]{:S(2)}) collective-permute-start(f32[48,512]{1,0:T(8,128)S(1)} %get-tuple-element.68), channel_id=1, source_target_pairs={{0,1},{1,0},{2,3},{3,2},{4,5},{5,4},{6,7},{7,6},{8,9},{9,8},{10,11... | collective-permute-start | bytes 294920 | tf_op jit(solution)/shard_map/ppermute | solution.py:672
  7.8 6.7 %collective-permute-start.3 = (f32[48,512]{1,0:T(8,128)S(1)}, f32[48,512]{1,0:T(8,128)S(1)}, u32[]{:S(2)}, u32[]{:S(2)}) collective-permute-start(f32[48,512]{1,0:T(8,128)S(1)} %get-tuple-element.69), channel_id=1, source_target_pairs={{0,32},{1,2},{2,1},{3,4},{4,3},{5,6},{6,5},{7,8},{8,7},{9,10},{10,... | collective-permute-start | bytes 294920 | tf_op jit(solution)/shard_map/ppermute | solution.py:672
  16.1 8.5 %collective-permute-start.6 = (f32[88,512]{1,0:T(8,128)S(1)}, f32[88,512]{1,0:T(8,128)S(1)}, u32[]{:S(2)}, u32[]{:S(2)}) collective-permute-start(f32[88,512]{1,0:T(8,128)S(1)} %get-tuple-element.75), channel_id=1, source_target_pairs={{0,1},{1,0},{2,3},{3,2},{4,5},{5,4},{6,7},{7,6},{8,9},{9,8},{10,11... | collective-permute-start | bytes 540680 | tf_op jit(solution)/shard_map/ppermute | solution.py:672
  16.2 8.4 %collective-permute-start.7 = (f32[88,512]{1,0:T(8,128)S(1)}, f32[88,512]{1,0:T(8,128)S(1)}, u32[]{:S(2)}, u32[]{:S(2)}) collective-permute-start(f32[88,512]{1,0:T(8,128)S(1)} %get-tuple-element.76), channel_id=1, source_target_pairs={{0,32},{1,2},{2,1},{3,4},{4,3},{5,6},{6,5},{7,8},{8,7},{9,10},{10,... | collective-permute-start | bytes 540680 | tf_op jit(solution)/shard_map/ppermute | solution.py:672
  20.1 4.4 %collective-permute-start.4 = (f32[40,512]{1,0:T(8,128)S(1)}, f32[40,512]{1,0:T(8,128)S(1)}, u32[]{:S(2)}, u32[]{:S(2)}) collective-permute-start(f32[40,512]{1,0:T(8,128)S(1)} %get-tuple-element.73), channel_id=1, source_target_pairs={{0,32},{1,33},{2,34},{3,35},{4,36},{5,37},{6,38},{7,39},{8,40},{9,... | collective-permute-start | bytes 245768 | tf_op jit(solution)/shard_map/ppermute | solution.py:672
  20.1 4.4 %collective-permute-start.5 = (f32[40,512]{1,0:T(8,128)S(1)}, f32[40,512]{1,0:T(8,128)S(1)}, u32[]{:S(2)}, u32[]{:S(2)}) collective-permute-start(f32[40,512]{1,0:T(8,128)S(1)} %get-tuple-element.74), channel_id=1, source_target_pairs={{0,1},{1,0},{2,3},{3,2},{4,5},{5,4},{6,7},{7,6},{8,9},{9,8},{10,11... | collective-permute-start | bytes 245768 | tf_op jit(solution)/shard_map/ppermute | solution.py:672
  25.9 6.7 %collective-permute-start.10 = (f32[32,512]{1,0:T(8,128)S(1)}, f32[32,512]{1,0:T(8,128)S(1)}, u32[]{:S(2)}, u32[]{:S(2)}) collective-permute-start(f32[32,512]{1,0:T(8,128)S(1)} %get-tuple-element.83), channel_id=1, source_target_pairs={{0,1},{1,0},{2,3},{3,2},{4,5},{5,4},{6,7},{7,6},{8,9},{9,8},{10,11... | collective-permute-start | bytes 196616 | tf_op jit(solution)/shard_map/ppermute | solution.py:672
  26.0 6.6 %collective-permute-start.11 = (f32[32,512]{1,0:T(8,128)S(1)}, f32[32,512]{1,0:T(8,128)S(1)}, u32[]{:S(2)}, u32[]{:S(2)}) collective-permute-start(f32[32,512]{1,0:T(8,128)S(1)} %get-tuple-element.84), channel_id=1, source_target_pairs={{0,32},{1,2},{2,1},{3,4},{4,3},{5,6},{6,5},{7,8},{8,7},{9,10},{10,... | collective-permute-start | bytes 196616 | tf_op jit(solution)/shard_map/ppermute | solution.py:672
  28.6 3.9 %collective-permute-start.8 = (f32[16,512]{1,0:T(8,128)S(1)}, f32[16,512]{1,0:T(8,128)S(1)}, u32[]{:S(2)}, u32[]{:S(2)}) collective-permute-start(f32[16,512]{1,0:T(8,128)S(1)} %get-tuple-element.81), channel_id=1, source_target_pairs={{0,32},{1,33},{2,34},{3,35},{4,36},{5,37},{6,38},{7,39},{8,40},{9,... | collective-permute-start | bytes 98312 | tf_op jit(solution)/shard_map/ppermute | solution.py:672
  28.6 3.9 %collective-permute-start.9 = (f32[16,512]{1,0:T(8,128)S(1)}, f32[16,512]{1,0:T(8,128)S(1)}, u32[]{:S(2)}, u32[]{:S(2)}) collective-permute-start(f32[16,512]{1,0:T(8,128)S(1)} %get-tuple-element.82), channel_id=1, source_target_pairs={{0,1},{1,0},{2,3},{3,2},{4,5},{5,4},{6,7},{7,6},{8,9},{9,8},{10,11... | collective-permute-start | bytes 98312 | tf_op jit(solution)/shard_map/ppermute | solution.py:672
  33.3 18.4 %copy-start.5 = (f32[8,8]{1,0:T(8,128)S(1)}, f32[8,8]{1,0:T(8,128)}, u32[]{:S(2)}) copy-start(f32[8,8]{1,0:T(8,128)} %kc.3) | copy-start | bytes 772
  33.3 6.0 %collective-permute-start.14 = (f32[32,512]{1,0:T(8,128)S(1)}, f32[32,512]{1,0:T(8,128)S(1)}, u32[]{:S(2)}, u32[]{:S(2)}) collective-permute-start(f32[32,512]{1,0:T(8,128)S(1)} %get-tuple-element.88), channel_id=1, source_target_pairs={{0,1},{1,0},{2,3},{3,2},{4,5},{5,4},{6,7},{7,6},{8,9},{9,8},{10,11... | collective-permute-start | bytes 196616 | tf_op jit(solution)/shard_map/ppermute | solution.py:672
  33.4 5.9 %collective-permute-start.15 = (f32[32,512]{1,0:T(8,128)S(1)}, f32[32,512]{1,0:T(8,128)S(1)}, u32[]{:S(2)}, u32[]{:S(2)}) collective-permute-start(f32[32,512]{1,0:T(8,128)S(1)} %get-tuple-element.89), channel_id=1, source_target_pairs={{0,32},{1,2},{2,1},{3,4},{4,3},{5,6},{6,5},{7,8},{8,7},{9,10},{10,... | collective-permute-start | bytes 196616 | tf_op jit(solution)/shard_map/ppermute | solution.py:672
  35.3 3.9 %collective-permute-start.12 = (f32[16,512]{1,0:T(8,128)S(1)}, f32[16,512]{1,0:T(8,128)S(1)}, u32[]{:S(2)}, u32[]{:S(2)}) collective-permute-start(f32[16,512]{1,0:T(8,128)S(1)} %get-tuple-element.86), channel_id=1, source_target_pairs={{0,32},{1,33},{2,34},{3,35},{4,36},{5,37},{6,38},{7,39},{8,40},{9,... | collective-permute-start | bytes 98312 | tf_op jit(solution)/shard_map/ppermute | solution.py:672
  35.3 3.9 %collective-permute-start.13 = (f32[16,512]{1,0:T(8,128)S(1)}, f32[16,512]{1,0:T(8,128)S(1)}, u32[]{:S(2)}, u32[]{:S(2)}) collective-permute-start(f32[16,512]{1,0:T(8,128)S(1)} %get-tuple-element.87), channel_id=1, source_target_pairs={{0,1},{1,0},{2,3},{3,2},{4,5},{5,4},{6,7},{7,6},{8,9},{9,8},{10,11... | collective-permute-start | bytes 98312 | tf_op jit(solution)/shard_map/ppermute | solution.py:672
  36.6 22.3 %copy-start = (bf16[240,216]{1,0:T(8,128)(2,1)S(1)}, bf16[240,216]{1,0:T(8,128)(2,1)}, u32[]{:S(2)}) copy-start(bf16[240,216]{1,0:T(8,128)(2,1)} %constant.17.clone.slot_in.slot) | copy-start | bytes 311044
  36.6 22.3 %copy-start.1 = (f32[216,64]{0,1:T(8,128)S(1)}, f32[216,64]{0,1:T(8,128)}, u32[]{:S(2)}) copy-start(f32[216,64]{0,1:T(8,128)} %param.20) | copy-start | bytes 165892
  36.6 22.3 %copy-start.2 = (f32[216,216]{1,0:T(8,128)S(1)}, f32[216,216]{1,0:T(8,128)}, u32[]{:S(2)}) copy-start(f32[216,216]{1,0:T(8,128)} %noise.1) | copy-start | bytes 559876
  36.6 22.3 %copy-start.4 = (f32[64,8]{0,1:T(8,128)S(1)}, f32[64,8]{0,1:T(8,128)}, u32[]{:S(2)}) copy-start(f32[64,8]{0,1:T(8,128)} %param.21) | copy-start | bytes 6148
  40.1 4.3 %collective-permute-start.16 = (f32[96,128]{1,0:T(8,128)S(1)}, f32[96,128]{1,0:T(8,128)S(1)}, u32[]{:S(2)}, u32[]{:S(2)}) collective-permute-start(f32[96,128]{1,0:T(8,128)S(1)} %get-tuple-element.92), channel_id=1, source_target_pairs={{0,32},{1,33},{2,34},{3,35},{4,36},{5,37},{6,38},{7,39},{8,40},{9,... | collective-permute-start | bytes 147464 | tf_op jit(solution)/shard_map/ppermute | solution.py:672
  40.3 4.2 %collective-permute-start.17 = (f32[96,128]{1,0:T(8,128)S(1)}, f32[96,128]{1,0:T(8,128)S(1)}, u32[]{:S(2)}, u32[]{:S(2)}) collective-permute-start(f32[96,128]{1,0:T(8,128)S(1)} %get-tuple-element.93), channel_id=1, source_target_pairs={{0,1},{1,0},{2,3},{3,2},{4,5},{5,4},{6,7},{7,6},{8,9},{9,8},{10,11... | collective-permute-start | bytes 147464 | tf_op jit(solution)/shard_map/ppermute | solution.py:672
  45.0 2.1 %collective-permute-start.18 = (f32[240,128]{1,0:T(8,128)S(1)}, f32[240,128]{1,0:T(8,128)S(1)}, u32[]{:S(2)}, u32[]{:S(2)}) collective-permute-start(f32[240,128]{1,0:T(8,128)S(1)} %get-tuple-element.94), channel_id=1, source_target_pairs={{0,1},{1,0},{2,3},{3,2},{4,5},{5,4},{6,7},{7,6},{8,9},{9,8},{10,11... | collective-permute-start | bytes 368648 | tf_op jit(solution)/shard_map/ppermute | solution.py:672
  45.1 6.5 %collective-permute-start.19 = (f32[240,128]{1,0:T(8,128)S(1)}, f32[240,128]{1,0:T(8,128)S(1)}, u32[]{:S(2)}, u32[]{:S(2)}) collective-permute-start(f32[240,128]{1,0:T(8,128)S(1)} %get-tuple-element.95), channel_id=1, source_target_pairs={{0,32},{1,2},{2,1},{3,4},{4,3},{5,6},{6,5},{7,8},{8,7},{9,10},{10,... | collective-permute-start | bytes 368648 | tf_op jit(solution)/shard_map/ppermute | solution.py:672
  53.8 4.2 %collective-permute-start.20 = (f32[96,128]{1,0:T(8,128)S(1)}, f32[96,128]{1,0:T(8,128)S(1)}, u32[]{:S(2)}, u32[]{:S(2)}) collective-permute-start(f32[96,128]{1,0:T(8,128)S(1)} %get-tuple-element.97), channel_id=1, source_target_pairs={{0,32},{1,33},{2,34},{3,35},{4,36},{5,37},{6,38},{7,39},{8,40},{9,... | collective-permute-start | bytes 147464 | tf_op jit(solution)/shard_map/ppermute | solution.py:672
  53.9 4.2 %collective-permute-start.21 = (f32[96,128]{1,0:T(8,128)S(1)}, f32[96,128]{1,0:T(8,128)S(1)}, u32[]{:S(2)}, u32[]{:S(2)}) collective-permute-start(f32[96,128]{1,0:T(8,128)S(1)} %get-tuple-element.98), channel_id=1, source_target_pairs={{0,1},{1,0},{2,3},{3,2},{4,5},{5,4},{6,7},{7,6},{8,9},{9,8},{10,11... | collective-permute-start | bytes 147464 | tf_op jit(solution)/shard_map/ppermute | solution.py:672
  58.7 1.4 %collective-permute-start.22 = (f32[240,128]{1,0:T(8,128)S(1)}, f32[240,128]{1,0:T(8,128)S(1)}, u32[]{:S(2)}, u32[]{:S(2)}) collective-permute-start(f32[240,128]{1,0:T(8,128)S(1)} %get-tuple-element.99), channel_id=1, source_target_pairs={{0,1},{1,0},{2,3},{3,2},{4,5},{5,4},{6,7},{7,6},{8,9},{9,8},{10,11... | collective-permute-start | bytes 368648 | tf_op jit(solution)/shard_map/ppermute | solution.py:672
  58.8 6.5 %collective-permute-start.23 = (f32[240,128]{1,0:T(8,128)S(1)}, f32[240,128]{1,0:T(8,128)S(1)}, u32[]{:S(2)}, u32[]{:S(2)}) collective-permute-start(f32[240,128]{1,0:T(8,128)S(1)} %get-tuple-element.100), channel_id=1, source_target_pairs={{0,32},{1,2},{2,1},{3,4},{4,3},{5,6},{6,5},{7,8},{8,7},{9,10},{10,... | collective-permute-start | bytes 368648 | tf_op jit(solution)/shard_map/ppermute | solution.py:672
  68.0 4.3 %collective-permute-start.26 = (f32[32,512]{1,0:T(8,128)S(1)}, f32[32,512]{1,0:T(8,128)S(1)}, u32[]{:S(2)}, u32[]{:S(2)}) collective-permute-start(f32[32,512]{1,0:T(8,128)S(1)} %get-tuple-element.106), channel_id=1, source_target_pairs={{0,1},{1,0},{2,3},{3,2},{4,5},{5,4},{6,7},{7,6},{8,9},{9,8},{10,11... | collective-permute-start | bytes 196616 | tf_op jit(solution)/shard_map/ppermute | solution.py:672
  68.1 5.9 %collective-permute-start.27 = (f32[32,512]{1,0:T(8,128)S(1)}, f32[32,512]{1,0:T(8,128)S(1)}, u32[]{:S(2)}, u32[]{:S(2)}) collective-permute-start(f32[32,512]{1,0:T(8,128)S(1)} %get-tuple-element.107), channel_id=1, source_target_pairs={{0,32},{1,2},{2,1},{3,4},{4,3},{5,6},{6,5},{7,8},{8,7},{9,10},{10,... | collective-permute-start | bytes 196616 | tf_op jit(solution)/shard_map/ppermute | solution.py:672
  68.3 4.0 %collective-permute-start.24 = (f32[16,512]{1,0:T(8,128)S(1)}, f32[16,512]{1,0:T(8,128)S(1)}, u32[]{:S(2)}, u32[]{:S(2)}) collective-permute-start(f32[16,512]{1,0:T(8,128)S(1)} %get-tuple-element.104), channel_id=1, source_target_pairs={{0,32},{1,33},{2,34},{3,35},{4,36},{5,37},{6,38},{7,39},{8,40},{9,... | collective-permute-start | bytes 98312 | tf_op jit(solution)/shard_map/ppermute | solution.py:672
  68.5 3.9 %collective-permute-start.25 = (f32[16,512]{1,0:T(8,128)S(1)}, f32[16,512]{1,0:T(8,128)S(1)}, u32[]{:S(2)}, u32[]{:S(2)}) collective-permute-start(f32[16,512]{1,0:T(8,128)S(1)} %get-tuple-element.105), channel_id=1, source_target_pairs={{0,1},{1,0},{2,3},{3,2},{4,5},{5,4},{6,7},{7,6},{8,9},{9,8},{10,11... | collective-permute-start | bytes 98312 | tf_op jit(solution)/shard_map/ppermute | solution.py:672
  75.1 5.7 %collective-permute-start.30 = (f32[48,512]{1,0:T(8,128)S(1)}, f32[48,512]{1,0:T(8,128)S(1)}, u32[]{:S(2)}, u32[]{:S(2)}) collective-permute-start(f32[48,512]{1,0:T(8,128)S(1)} %get-tuple-element.112), channel_id=1, source_target_pairs={{0,1},{1,0},{2,3},{3,2},{4,5},{5,4},{6,7},{7,6},{8,9},{9,8},{10,11... | collective-permute-start | bytes 294920 | tf_op jit(solution)/shard_map/ppermute | solution.py:672
  75.2 6.2 %collective-permute-start.31 = (f32[48,512]{1,0:T(8,128)S(1)}, f32[48,512]{1,0:T(8,128)S(1)}, u32[]{:S(2)}, u32[]{:S(2)}) collective-permute-start(f32[48,512]{1,0:T(8,128)S(1)} %get-tuple-element.113), channel_id=1, source_target_pairs={{0,32},{1,2},{2,1},{3,4},{4,3},{5,6},{6,5},{7,8},{8,7},{9,10},{10,... | collective-permute-start | bytes 294920 | tf_op jit(solution)/shard_map/ppermute | solution.py:672
  76.1 4.4 %collective-permute-start.28 = (f32[40,512]{1,0:T(8,128)S(1)}, f32[40,512]{1,0:T(8,128)S(1)}, u32[]{:S(2)}, u32[]{:S(2)}) collective-permute-start(f32[40,512]{1,0:T(8,128)S(1)} %get-tuple-element.110), channel_id=1, source_target_pairs={{0,32},{1,33},{2,34},{3,35},{4,36},{5,37},{6,38},{7,39},{8,40},{9,... | collective-permute-start | bytes 245768 | tf_op jit(solution)/shard_map/ppermute | solution.py:672
  76.4 4.4 %collective-permute-start.29 = (f32[40,512]{1,0:T(8,128)S(1)}, f32[40,512]{1,0:T(8,128)S(1)}, u32[]{:S(2)}, u32[]{:S(2)}) collective-permute-start(f32[40,512]{1,0:T(8,128)S(1)} %get-tuple-element.111), channel_id=1, source_target_pairs={{0,1},{1,0},{2,3},{3,2},{4,5},{5,4},{6,7},{7,6},{8,9},{9,8},{10,11... | collective-permute-start | bytes 245768 | tf_op jit(solution)/shard_map/ppermute | solution.py:672
  83.0 6.1 %collective-permute-start.34 = (f32[48,512]{1,0:T(8,128)S(1)}, f32[48,512]{1,0:T(8,128)S(1)}, u32[]{:S(2)}, u32[]{:S(2)}) collective-permute-start(f32[48,512]{1,0:T(8,128)S(1)} %get-tuple-element.117), channel_id=1, source_target_pairs={{0,1},{1,0},{2,3},{3,2},{4,5},{5,4},{6,7},{7,6},{8,9},{9,8},{10,11... | collective-permute-start | bytes 294920 | tf_op jit(solution)/shard_map/ppermute | solution.py:672
  83.1 6.5 %collective-permute-start.35 = (f32[48,512]{1,0:T(8,128)S(1)}, f32[48,512]{1,0:T(8,128)S(1)}, u32[]{:S(2)}, u32[]{:S(2)}) collective-permute-start(f32[48,512]{1,0:T(8,128)S(1)} %get-tuple-element.118), channel_id=1, source_target_pairs={{0,32},{1,2},{2,1},{3,4},{4,3},{5,6},{6,5},{7,8},{8,7},{9,10},{10,... | collective-permute-start | bytes 294920 | tf_op jit(solution)/shard_map/ppermute | solution.py:672
  84.4 4.4 %collective-permute-start.32 = (f32[40,512]{1,0:T(8,128)S(1)}, f32[40,512]{1,0:T(8,128)S(1)}, u32[]{:S(2)}, u32[]{:S(2)}) collective-permute-start(f32[40,512]{1,0:T(8,128)S(1)} %get-tuple-element.115), channel_id=1, source_target_pairs={{0,32},{1,33},{2,34},{3,35},{4,36},{5,37},{6,38},{7,39},{8,40},{9,... | collective-permute-start | bytes 245768 | tf_op jit(solution)/shard_map/ppermute | solution.py:672
  84.7 4.4 %collective-permute-start.33 = (f32[40,512]{1,0:T(8,128)S(1)}, f32[40,512]{1,0:T(8,128)S(1)}, u32[]{:S(2)}, u32[]{:S(2)}) collective-permute-start(f32[40,512]{1,0:T(8,128)S(1)} %get-tuple-element.116), channel_id=1, source_target_pairs={{0,1},{1,0},{2,3},{3,2},{4,5},{5,4},{6,7},{7,6},{8,9},{9,8},{10,11... | collective-permute-start | bytes 245768 | tf_op jit(solution)/shard_map/ppermute | solution.py:672
  85.4 4.1 %copy-start.3 = (bf16[216,240]{1,0:T(8,128)(2,1)S(1)}, bf16[216,240]{1,0:T(8,128)(2,1)}, u32[]{:S(2)}) copy-start(bf16[216,240]{1,0:T(8,128)(2,1)} %constant.18.clone.from_slot) | copy-start | bytes 311044
  85.4 4.1 %copy-start.6 = (f32[4,4,128]{2,1,0:T(4,128)S(1)}, f32[4,4,128]{2,1,0:T(4,128)}, u32[]{:S(2)}) copy-start(f32[4,4,128]{2,1,0:T(4,128)} %param.23) | copy-start | bytes 24580

commit v5 on v4

--- a/solution.py
+++ b/solution.py
@@ -144,13 +144,28 @@
     return dot_nt(left, part).astype(BF16)
 
 
-def prepare(slot, fine, mid, pmid_t, plow_t, kf, pmt, km, plt):
+def prepare(slot, fine, mid, pmid_t, plow_t, kf, pmt, km, plt, plv):
     wide(kf, SF, *[turned(turned(slot, part), slot) for part in halves(fine)])
     wide(pmt, QM, *[turned(part, slot) for part in halves(pmid_t)])
     turn = one_hot(QM)
     narrow(km, *[turned(turn, part) for part in halves(mid)])
     gap = jnp.zeros((8, QM), BF16)
     narrow(plt, *[jnp.concatenate([part, gap], axis=0) for part in halves(plow_t)])
+    row, col = grid(QM, QM)
+    moves = (
+        col == row + 48,
+        col == row - 48,
+        (col == row + 12) & (row // 4 % 4 == 0),
+        (col == row - 12) & (row // 4 % 4 == 3),
+    )
+    moves = [jnp.where(move, 1.0, 0.0).astype(BF16) for move in moves]
+    narrow(
+        plv,
+        *[
+            jnp.concatenate([dot(part, move).astype(BF16) for move in moves], axis=0)
+            for part in halves(plow_t)
+        ],
+    )
 
 
 def late_kernel(slot, noise, pmid_t, plow_t, nf, pm, spread):
@@ -270,7 +285,7 @@
 
 def first_kernel(
     seed_in, scale_in, coef_in, slot_in, smooth_in, fine_in, mid_in, pmid_in, plow_in, idx,
-    g, u1, csx, csr, s1, s2, s3, s4, kf, sf, pmt, km, plt,
+    g, u1, csx, csr, s1, s2, s3, s4, kf, sf, pmt, km, plt, plv,
     seed, scale, coef, slot, smooth, fine, mid, pmid, plow, done,
 ):
     copies = {}
@@ -327,7 +342,7 @@
         for part in halves(smooth[...] + jnp.where(row == col, 0.25, 0.0))
     ]
     wide(sf, SF, *[turned(part, slot[...]) for part in first])
-    prepare(slot[...], fine[...], mid[...], pmid[...], plow[...], kf, pmt, km, plt)
+    prepare(slot[...], fine[...], mid[...], pmid[...], plow[...], kf, pmt, km, plt, plv)
     copies["seed"].wait()
     both = jnp.concatenate([first[0], slot[...]], axis=0)
     for n in range(4):
@@ -495,45 +510,160 @@
     mid_local(m_ref, g_ref, csr, km, t_ref, x_ref)
 
 
-def mid_kernel(m, t_in, csr, idx, r1, r2, r3, r4, out, s1, s2, s3, s4, t_ref):
+def far_near(idx, far, near, s1, s2):
+    x_even = even(idx, 0)
+    s1[...] = jnp.where(x_even, far, near)
+    s2[...] = jnp.where(x_even, near, far)
+
+
+def smooth_kernel(
+    m, t_in, csr, idx, r1, r2, r3, r4, gm, km, plt, plv, out, own, s1, s2, x_ref, t_ref
+):
     t_ref[...] = t_in[...]
     mid_edge_terms(csr, mid_edges(idx, r1, r2, r3, r4), t_ref)
     out[...] = m[...] + 0.2 * t_ref[...]
-    mid_sends(out, idx, s1, s2, s3, s4)
-
-
-def block_sends(pay, idx, s1, s2):
-    x_even = even(idx, 0)
-    far, near = pay[32:128, :], pay[0:96, :]
-    s1[...] = jnp.where(x_even, far, near)
-    s2[...] = jnp.where(x_even, near, far)
-
-
-def row_kernel(idx, own, r1, r2, s3, s4):
-    x_even, y_even = even(idx, 0), even(idx, 1)
-    for plane in range(WX):
-        tiles = []
-        for y in range(4):
-            if 3 <= plane < 7:
-                at = QC * (4 * (plane - 3) + y)
-                tiles.append(own[at : at + QC, :])
-            else:
-                at = QC * (4 * (plane % 7) + y)
-                one, two = r1[at : at + QC, :], r2[at : at + QC, :]
-                tiles.append(jnp.where(x_even == (plane < 3), two, one))
-        for y in range(3):
-            rows = slice(QC * (3 * plane + y), QC * (3 * plane + y) + QC)
-            s3[rows, :] = jnp.where(y_even, tiles[y + 1], tiles[y])
-            s4[rows, :] = jnp.where(y_even, tiles[y], tiles[y + 1])
-
-
-def low_kernel(t_in, csr, idx, r1, r2, r3, r4, plt, pay, s1, s2, x_ref, t_ref):
-    t_ref[...] = t_in[...]
-    mid_edge_terms(csr, mid_edges(idx, r1, r2, r3, r4), t_ref)
+    mid_local(out, gm, csr, km, t_ref, x_ref)
+    faces = dot(plv[...], x_ref[...])
     value = mid_product(plt, t_ref[...], x_ref)
     for c in range(COLS):
-        pay[QC * c : QC * c + QC, :] = value[0:8, c * 128 : c * 128 + 128]
-    block_sends(pay, idx, s1, s2)
+        own[QC * c : QC * c + QC, :] = value[0:8, c * 128 : c * 128 + 128]
+    for n in range(4):
+        upper, lower = slice((12 + n) * 128, (13 + n) * 128), slice(n * 128, n * 128 + 128)
+        own[128 + 8 * n : 136 + 8 * n, :] = faces[0:8, upper]
+        own[160 + 8 * n : 168 + 8 * n, :] = faces[8:16, lower]
+        upper = slice((4 * n + 3) * 128, (4 * n + 4) * 128)
+        lower = slice(4 * n * 128, (4 * n + 1) * 128)
+        own[192 + 8 * n : 200 + 8 * n, :] = faces[16:24, upper]
+        own[224 + 8 * n : 232 + 8 * n, :] = faces[24:32, lower]
+    far = (own[32:128, :], own[128:160, :], own[200:224, :], own[232:256, :])
+    near = (own[0:96, :], own[160:192, :], own[192:216, :], own[224:248, :])
+    far_near(idx, jnp.concatenate(far, axis=0), jnp.concatenate(near, axis=0), s1, s2)
+
+
+WX = 10
+WROWS = WX * 16
+REACH = [(p, d) for p in range(WX) for d in range(1, 4 - max(0, 3 - p, p - 6))]
+
+
+def window_row(plane, y):
+    return plane * 16 + 4 + y
+
+
+def tile(ref, n):
+    return ref[QC * n : QC * n + QC, :]
+
+
+def window_tiles(idx, own, r1, r2):
+    x_even = even(idx, 0)
+    planes = []
+    for plane in range(WX):
+        if 3 <= plane < 7:
+            planes.append([tile(own, 4 * (plane - 3) + y) for y in range(4)])
+        else:
+            n = 4 * (plane % 7)
+            left = plane < 3
+            planes.append(
+                [
+                    jnp.where(x_even == left, tile(r2, n + y), tile(r1, n + y))
+                    for y in range(4)
+                ]
+            )
+    return planes
+
+
+def row_sends(idx, planes, s3, s4):
+    y_even = even(idx, 1)
+    for n, (p, d) in enumerate(REACH):
+        far, near = planes[p][4 - d], planes[p][d - 1]
+        s3[QC * n : QC * n + QC, :] = jnp.where(y_even, far, near)
+        s4[QC * n : QC * n + QC, :] = jnp.where(y_even, near, far)
+
+
+def row_kernel(idx, own, r1, r2, coef, s3, s4, whole):
+    x_even, y_even = even(idx, 0), even(idx, 1)
+    planes = window_tiles(idx, own, r1, r2)
+
+    def left(n):
+        return jnp.where(x_even, tile(r2, n), tile(r1, n))
+
+    def right(n):
+        return jnp.where(x_even, tile(r1, n), tile(r2, n))
+
+    def weight(n, plane, y):
+        row = window_row(plane, y)
+        return coef[n, row : row + 1, :]
+
+    for y in range(4):
+        planes[3][y] = planes[3][y] + weight(0, 3, y) * left(12 + y)
+        planes[6][y] = planes[6][y] + weight(1, 6, y) * right(12 + y)
+        planes[2][y] = planes[2][y] + weight(1, 2, y) * tile(own, 20 + y)
+        planes[7][y] = planes[7][y] + weight(0, 7, y) * tile(own, 16 + y)
+    row_sends(idx, planes, s3, s4)
+    for p in range(WX):
+        for y in range(4):
+            n = 4 * p + y
+            whole[QC * n : QC * n + QC, :] = planes[p][y]
+        if p < 3:
+            upper, lower = left(16 + p), left(19 + p)
+        elif p < 7:
+            upper, lower = tile(own, 24 + p - 3), tile(own, 28 + p - 3)
+        else:
+            upper, lower = right(16 + p - 7), right(19 + p - 7)
+        whole[320 + QC * p : 328 + QC * p, :] = upper
+        whole[400 + QC * p : 408 + QC * p, :] = lower
+        at = QC * (len(REACH) + p)
+        s3[at : at + QC, :] = jnp.where(y_even, upper, lower)
+        s4[at : at + QC, :] = jnp.where(y_even, lower, upper)
+
+
+def half_rows(first, second, upper):
+    low = sublane(first.shape) < 4
+    if upper:
+        return jnp.where(low, sub_roll(first, 4), second)
+    return jnp.where(low, first, sub_roll(second, 4))
+
+
+def second_row_kernel(idx, own, r1, r2, m, s3, s4):
+    y_even = even(idx, 1)
+    row_sends(idx, window_tiles(idx, own, r1, r2), s3, s4)
+    at = QC * len(REACH)
+    for x in range(4):
+        for pair in range(2):
+            base = 32 * pair
+            up, low = (
+                slice((4 * x + y) * 128, (4 * x + y) * 128 + 128) for y in (3, 0)
+            )
+            upper = half_rows(m[base + 8 : base + 16, up], m[base + 24 : base + 32, up], True)
+            lower = half_rows(m[base : base + 8, low], m[base + 16 : base + 24, low], False)
+            s3[at : at + 8, :] = jnp.where(y_even, upper, lower)
+            s4[at : at + 8, :] = jnp.where(y_even, lower, upper)
+            at += 8
+
+
+def second_edges(idx, r1, r2, r3, r4):
+    x_even, y_even = even(idx, 0), even(idx, 1)
+
+    def x_face(ref):
+        return jnp.concatenate([ref[96 + 16 * y : 112 + 16 * y, :] for y in range(4)], axis=1)
+
+    def y_face(ref, upper):
+        base = QC * len(REACH)
+        rows = []
+        for i in range(4):
+            parts = []
+            for x in range(4):
+                at = base + 16 * x + 8 * (i // 2)
+                part = ref[at : at + 8, :]
+                parts.append(sub_roll(part, 4) if (i % 2 == 0) == upper else part)
+            rows.append(jnp.concatenate(parts, axis=1))
+        return jnp.concatenate(rows, axis=0)
+
+    return (
+        jnp.where(x_even, x_face(r2), x_face(r1)),
+        jnp.where(x_even, x_face(r1), x_face(r2)),
+        jnp.where(y_even, y_face(r4, True), y_face(r3, True)),
+        jnp.where(y_even, y_face(r3, False), y_face(r4, False)),
+    )
 
 
 def lift_kernel(m, t_in, csr, idx, r1, r2, r3, r4, pm, u, out, s1, s2, s3, s4, x_ref, t_ref):
@@ -549,30 +679,55 @@
     fine_sends(out, idx, s1, s2, s3, s4)
 
 
-WX = 10
-WROWS = WX * 16
-
-
-def place(window, own, r1, r2, r3, r4, idx):
-    x_even, y_even = even(idx, 0), even(idx, 1)
+def place_first(window, whole, r3, r4, coef, idx):
+    y_even = even(idx, 1)
     window[...] = jnp.zeros((QC * WROWS, 128), F32)
 
-    def put(plane, y, tile):
-        window[pl.ds(plane * 16 + 4 + y, QC, stride=WROWS), :] = tile
-
-    for y in range(4):
-        for x in range(4):
-            c = 4 * x + y
-            put(3 + x, y, own[QC * c : QC * c + QC, :])
-        for x in range(3):
-            rows = slice(QC * (4 * x + y), QC * (4 * x + y) + QC)
-            put(x, y, jnp.where(x_even, r2[rows, :], r1[rows, :]))
-            put(7 + x, y, jnp.where(x_even, r1[rows, :], r2[rows, :]))
-    for plane in range(WX):
-        for y in range(3):
-            rows = slice(QC * (3 * plane + y), QC * (3 * plane + y) + QC)
-            put(plane, y - 3, jnp.where(y_even, r4[rows, :], r3[rows, :]))
-            put(plane, y + 4, jnp.where(y_even, r3[rows, :], r4[rows, :]))
+    def put(plane, y, value):
+        window[pl.ds(window_row(plane, y), QC, stride=WROWS), :] = value
+
+    def below(n):
+        return jnp.where(y_even, tile(r4, n), tile(r3, n))
+
+    def above(n):
+        return jnp.where(y_even, tile(r3, n), tile(r4, n))
+
+    def weight(n, plane, y):
+        row = window_row(plane, y)
+        return coef[n, row : row + 1, :]
+
+    count = len(REACH)
+    for p in range(WX):
+        for y in range(4):
+            value = tile(whole, 4 * p + y)
+            if y == 0:
+                value = value + weight(2, p, 0) * below(count + p)
+            if y == 3:
+                value = value + weight(3, p, 3) * above(count + p)
+            put(p, y, value)
+    for n, (p, d) in enumerate(REACH):
+        lower, upper = below(n), above(n)
+        if d == 1:
+            lower = lower + weight(3, p, -1) * tile(whole, 50 + p)
+            upper = upper + weight(2, p, 4) * tile(whole, 40 + p)
+        put(p, -d, lower)
+        put(p, 3 + d, upper)
+
+
+def place_second(window, own, r1, r2, r3, r4, idx):
+    y_even = even(idx, 1)
+    window[...] = jnp.zeros((QC * WROWS, 128), F32)
+
+    def put(plane, y, value):
+        window[pl.ds(window_row(plane, y), QC, stride=WROWS), :] = value
+
+    planes = window_tiles(idx, own, r1, r2)
+    for p in range(WX):
+        for y in range(4):
+            put(p, y, planes[p][y])
+    for n, (p, d) in enumerate(REACH):
+        put(p, -d, jnp.where(y_even, tile(r4, n), tile(r3, n)))
+        put(p, 3 + d, jnp.where(y_even, tile(r3, n), tile(r4, n)))
 
 
 def coarse_sweep(c_ref, out_ref, g_ref, coef, kc, first, last):
@@ -604,23 +759,27 @@
         step(plane)
 
 
-def coarse_kernel(own, r1, r2, r3, r4, kc, idx, coef, g, pay, s1, s2, one, two):
-    place(g, own, r1, r2, r3, r4, idx)
+def coarse_kernel(whole, r3, r4, kc, idx, coef, m, g, pay, s1, s2, one, two):
+    place_first(g, whole, r3, r4, coef, idx)
     one[...] = 0.2 * g[...]
     coarse_sweep(one, two, g, coef, kc, 1, 9)
     coarse_sweep(two, one, g, coef, kc, 2, 8)
     coarse_sweep(one, two, g, coef, kc, 3, 7)
     for c in range(COLS):
-        row = (3 + c // 4) * 16 + 4 + c % 4
+        row = window_row(3 + c // 4, c % 4)
         pay[QC * c : QC * c + QC, :] = two[pl.ds(row, QC, stride=WROWS), :]
-    block_sends(pay, idx, s1, s2)
+    far, near = [pay[32:128, :]], [pay[0:96, :]]
+    for y in range(4):
+        far.append(m[48:64, (12 + y) * 128 : (13 + y) * 128])
+        near.append(m[0:16, y * 128 : y * 128 + 128])
+    far_near(idx, jnp.concatenate(far, axis=0), jnp.concatenate(near, axis=0), s1, s2)
 
 
 def correct_kernel(
-    own, r1, r2, r3, r4, kc, idx, g, coef, spread, m, gm, csr, q1, q2, q3, q4, km,
+    own, r1, r2, r3, r4, kc, idx, g, coef, spread, m, gm, csr, km,
     out, s1, s2, s3, s4, one, two, x_ref, t_ref, m_ref,
 ):
-    place(one, own, r1, r2, r3, r4, idx)
+    place_second(one, own, r1, r2, r3, r4, idx)
     coarse_sweep(one, two, g, coef, kc, 1, 9)
     coarse_sweep(two, one, g, coef, kc, 2, 8)
 
@@ -636,7 +795,7 @@
     for c in range(COLS):
         lanes = slice(c * 128, c * 128 + 128)
         m_ref[:, lanes] = m[:, lanes] + lifted(c // 4, c % 4, whole)
-    below_x, above_x, below_y, above_y = mid_edges(idx, q1, q2, q3, q4)
+    below_x, above_x, below_y, above_y = second_edges(idx, r1, r2, r3, r4)
     below_x = below_x + jnp.concatenate([lifted(-1, y, slice(48, 64)) for y in range(4)], axis=1)
     above_x = above_x + jnp.concatenate([lifted(4, y, slice(0, 16)) for y in range(4)], axis=1)
     below_rows, above_rows = [], []
@@ -678,11 +837,13 @@
     return r1, r2, r3, r4
 
 
-def exchange_blocks(idx, own, s1, s2):
+def exchange_rows(kernel, rows, outs, idx, own, s1, s2, extra):
     r2, r1 = swap(s2, 1), swap(s1, 0)
-    s3, s4 = call(row_kernel, [((QC * 3 * WX, 128), F32)] * 2, (), (0,))(idx, own, r1, r2)
+    s3, s4, *rest = call(kernel, [((rows, 128), F32)] * 2 + outs, (), (0,))(
+        idx, own, r1, r2, extra
+    )
     r4, r3 = swap(s4, 3), swap(s3, 2)
-    return own, r1, r2, r3, r4
+    return r1, r2, r3, r4, rest
 
 
 def body(seed, scale, coef, fine, smooth, mid, coarse, pmid, plow, noise, inc):
@@ -705,7 +866,6 @@
     xm, tm = pltpu.VMEM((256, LANES), BF16), pltpu.VMEM((QM, LANES), F32)
     window = ((QC * WROWS, 128), F32)
     windows = [pltpu.VMEM((QC * WROWS, 128), F32)] * 2
-    blocks = [((QC * COLS, 128), F32)] + [((QC * 12, 128), F32)] * 2
 
     operands = (
         seed.reshape(QF * COLS, 128),
@@ -718,7 +878,7 @@
         pmid.T,
         plow.T,
     )
-    g, u, csx, csr, s1, s2, s3, s4, kf, sf, pmt, km, plt = call(
+    g, u, csx, csr, s1, s2, s3, s4, kf, sf, pmt, km, plt, plv = call(
         first_kernel,
         [fine_field, fine_field, ((16, 512), F32), ((8, LANES), F32)]
         + [((56, 512), F32)] * 2
@@ -729,6 +889,7 @@
             ((QM, 768), BF16),
             ((QM, 256), BF16),
             ((16, 256), BF16),
+            ((32, 256), BF16),
         ],
         [pltpu.VMEM(operand.shape, operand.dtype) for operand in operands]
         + [pltpu.SemaphoreType.DMA((len(operands),))],
@@ -762,20 +923,30 @@
         fine_local(u), csr, idx, *edges, pmt
     )
     edges = exchange(sends)
-    m, *sends = call(mid_kernel, [mid_field] + mid_faces, [tm], (3,))(
-        m, mid_local_part(m), csr, idx, *edges
-    )
-    edges = exchange(sends)
-    pay = call(low_kernel, blocks, [xm, tm], (2,))(mid_local_part(m), csr, idx, *edges, plt)
-    gw, *pay = call(coarse_kernel, [window] + blocks, windows, (5, 6))(
-        *exchange_blocks(idx, *pay), coarse, idx, coefw
+    m, own, s1, s2 = call(
+        smooth_kernel,
+        [mid_field, ((256, 128), F32)] + [((176, 128), F32)] * 2,
+        [xm, tm],
+        (3,),
+    )(m, mid_local_part(m), csr, idx, *edges, gm, km, plt, plv)
+    _, _, r3, r4, (whole,) = exchange_rows(
+        row_kernel, QC * (len(REACH) + WX), [((480, 128), F32)], idx, own, s1, s2, coefw
+    )
+    gw, own, s1, s2 = call(
+        coarse_kernel,
+        [window, ((QC * COLS, 128), F32)] + [((160, 128), F32)] * 2,
+        windows,
+        (3, 4),
+    )(whole, r3, r4, coarse, idx, coefw, m)
+    r1, r2, r3, r4, _ = exchange_rows(
+        second_row_kernel, QC * len(REACH) + 64, [], idx, own, s1, s2, m
     )
     m, *sends = call(
         correct_kernel,
         [mid_field] + mid_faces,
         windows + [xm, tm, pltpu.VMEM((QM, LANES), F32)],
         (5, 6),
-    )(*exchange_blocks(idx, *pay), coarse, idx, gw, coefw, spread, m, gm, csr, *edges, km)
+    )(own, r1, r2, r3, r4, coarse, idx, gw, coefw, spread, m, gm, csr, km)
     edges = exchange(sends)
     u, *sends = call(lift_kernel, [fine_field] + fine_faces, [xm, tm], (3,))(
         m, mid_local_part(m), csr, idx, *edges, pm, u

time: 94.6 us -> 89 us (0.941)
  starting transfers between devices: 27.8 us -> 24 us
  waiting for transfers between devices: 34.5 us -> 33.2 us
    ppermute x36 -> x32, starting transfers between devices: 27.8 us -> 24 us  [swap(): return lax.ppermute(values, ('gx', 'yz'), partners(step))]
    ppermute x36 -> x32, waiting for transfers between devices: 34.5 us -> 33.2 us  [swap(): return lax.ppermute(values, ('gx', 'yz'), partners(step))]
    pallas_call x21 -> x19, Pallas kernels: 31 us -> 30.5 us  [run(): pl.pallas_call(kernel, out_shape=tuple((jax.ShapeDtypeStruct(s, d) for s,...]
  transfers between devices with their start and end apart: 36 -> 32, of which waited for: 20 -> 20; matrix products, arithmetic and copies ran while one was open for 0% -> 0% of each run, Pallas kernels for 9% -> 9%
where the time goes in v5:
time: 89 us; the launch traced here: 88.9 us
  waiting for transfers between devices  33.2 us (37%)
  Pallas kernels  30.5 us (34%)
  starting transfers between devices  24 us (27%)
  between operations  1.14 us (1%)
    ppermute x32, waiting for transfers between devices, swap(): return lax.ppermute(values, ('gx', 'yz'), partners(step))  33.2 us
    pallas_call x19, Pallas kernels, run(): pl.pallas_call(kernel, out_shape=tuple((jax.ShapeDtypeStruct(s, d) for s,...  30.5 us
    ppermute x32, starting transfers between devices, swap(): return lax.ppermute(values, ('gx', 'yz'), partners(step))  24 us
  transfers between devices with their start and end apart: 32, of which 20 were waited for; matrix products, arithmetic and copies ran while one was open for 0% of the time, Pallas kernels for 9%

profile of v5, /device:TPU:14, one launch (start us, length us, event | category | flops | bytes accessed | tf_op | source)
XLA Modules:
  0.0 88.9 jit_solution(10260863336614469184)
XLA Ops:
  0.7 4.3 %shard_map.140 = (f32[240,2048]{1,0:T(8,128)S(1)}, f32[240,2048]{1,0:T(8,128)S(1)}, f32[16,512]{1,0:T(8,128)S(1)}, f32[8,2048]{1,0:T(8,128)S(1)}, f32[56,512]{1,...) custom-call(f32[3456,128]{1,0:T(8,128)} %bitcast.15, ...), custom_call_target="tpu_custom_call" | custom-call | tf_op jit(solution)/shard_map/pallas_call | solution.py:50
  5.0 0.5 collective-permute-start
  5.6 2.4 %collective-permute-start.1 = (f32[56,512]{1,0:T(8,128)S(1)}, f32[56,512]{1,0:T(8,128)S(1)}, u32[]{:S(2)}, u32[]{:S(2)}) collective-permute-start(f32[56,512]{1,0:T(8,128)S(1)} %get-tuple-element.65), channel_id=1, source_target_pairs={{0,1},{1,0},{2,3},{3,2},{4,5},{5,4},{6,7},{7,6},{8,9},{9,8},{10,11... | collective-permute-start | bytes 344072 | tf_op jit(solution)/shard_map/ppermute | solution.py:831
  8.0 4.4 %collective-permute-start.3 = (f32[48,512]{1,0:T(8,128)S(1)}, f32[48,512]{1,0:T(8,128)S(1)}, u32[]{:S(2)}, u32[]{:S(2)}) collective-permute-start(f32[48,512]{1,0:T(8,128)S(1)} %get-tuple-element.67), channel_id=1, source_target_pairs={{0,32},{1,2},{2,1},{3,4},{4,3},{5,6},{6,5},{7,8},{8,7},{9,10},{10,... | collective-permute-start | bytes 294920 | tf_op jit(solution)/shard_map/ppermute | solution.py:831
  12.4 1.5 %shard_map.141.t_in = f32[240,2048]{1,0:T(8,128)S(1)} custom-call(f32[240,2048]{1,0:T(8,128)S(1)} %get-tuple-element.60.u_ref.u, f32[240,2048]{1,0:T(8,128)S(1)} %get-tuple-element.61.g_ref, f32[8,2048]{1,0:T(8,128)S(1)} %get-tuple-element.62.csr, bf16[240,768]{1,0:T(8,128)(2,1)S(1)} %get-tuple-element.63.kf), custom_call_target="tpu_custom_call" | custom-call | tf_op jit(solution)/shard_map/pallas_call | solution.py:50
  13.9 0.8 collective-permute-done.3.r4
  14.7 1.6 %shard_map.142 = (f32[240,2048]{1,0:T(8,128)S(1)}, f32[40,512]{1,0:T(8,128)S(1)}, f32[40,512]{1,0:T(8,128)S(1)}, f32[88,512]{1,0:T(8,128)S(1)}, f32[88,512]{1,0:T(8,128)S(1)}) custom-call(f32[240,2048]{1,0:T(8,128)S(1)} %get-tuple-element.60.u_ref.u, f32[240,2048]{1,0:T(8,128)S(1)} %shard_map.141.t_in, f32[8,2048]{1,0:T(8,128)S(1)} %get-tuple-element.62.csr, ...), custom_call_target="tpu_custom_call" | custom-call | tf_op jit(solution)/shard_map/pallas_call | solution.py:50
  16.3 0.1 collective-permute-start.6
  16.4 3.9 %collective-permute-start.7 = (f32[88,512]{1,0:T(8,128)S(1)}, f32[88,512]{1,0:T(8,128)S(1)}, u32[]{:S(2)}, u32[]{:S(2)}) collective-permute-start(f32[88,512]{1,0:T(8,128)S(1)} %get-tuple-element.74), channel_id=1, source_target_pairs={{0,32},{1,2},{2,1},{3,4},{4,3},{5,6},{6,5},{7,8},{8,7},{9,10},{10,... | collective-permute-start | bytes 540680 | tf_op jit(solution)/shard_map/ppermute | solution.py:831
  20.3 0.7 collective-permute-start.5
  21.1 1.5 %shard_map.143.t_in = f32[240,2048]{1,0:T(8,128)S(1)} custom-call(f32[240,2048]{1,0:T(8,128)S(1)} %get-tuple-element.70.u_ref.u, f32[240,2048]{1,0:T(8,128)S(1)} %get-tuple-element.61.g_ref, f32[8,2048]{1,0:T(8,128)S(1)} %get-tuple-element.62.csr, bf16[240,768]{1,0:T(8,128)(2,1)S(1)} %get-tuple-element.63.kf), custom_call_target="tpu_custom_call" | custom-call | tf_op jit(solution)/shard_map/pallas_call | solution.py:50
  22.6 2.2 %collective-permute-done.4.r1 = f32[40,512]{1,0:T(8,128)S(1)} collective-permute-done((f32[40,512]{1,0:T(8,128)S(1)}, f32[40,512]{1,0:T(8,128)S(1)}, u32[]{:S(2)}, u32[]{:S(2)}) %collective-permute-start.4) | collective-permute-done | bytes 81952 | tf_op jit(solution)/shard_map/ppermute | solution.py:831
  24.8 1.3 %shard_map.144 = (f32[64,2048]{1,0:T(8,128)S(1)}, f32[64,2048]{1,0:T(8,128)S(1)}, f32[16,512]{1,0:T(8,128)S(1)}, f32[16,512]{1,0:T(8,128)S(1)}, f32[32,512]{1,0:T(8,128)S(1)}, /*index=5*/f32[32,512]{1,0:T(8,128)S(1)}) custom-call(f32[240,2048]{1,0:T(8,128)S(1)} %shard_map.143.t_in, f32[8,2048]{1,0:T(8,128)S(1)} %get-tuple-element.62.csr, ...), custom_call_target="tpu_custom_call" | custom-call | tf_op jit(solution)/shard_map/pallas_call | solution.py:50
  26.1 0.1 collective-permute-start.10
  26.2 2.7 %collective-permute-start.11 = (f32[32,512]{1,0:T(8,128)S(1)}, f32[32,512]{1,0:T(8,128)S(1)}, u32[]{:S(2)}, u32[]{:S(2)}) collective-permute-start(f32[32,512]{1,0:T(8,128)S(1)} %get-tuple-element.82), channel_id=1, source_target_pairs={{0,32},{1,2},{2,1},{3,4},{4,3},{5,6},{6,5},{7,8},{8,7},{9,10},{10,... | collective-permute-start | bytes 196616 | tf_op jit(solution)/shard_map/ppermute | solution.py:831
  28.8 0.7 collective-permute-start.9
  29.6 0.5 shard_map.145.t_in
  30.1 2.6 %collective-permute-done.8.r1 = f32[16,512]{1,0:T(8,128)S(1)} collective-permute-done((f32[16,512]{1,0:T(8,128)S(1)}, f32[16,512]{1,0:T(8,128)S(1)}, u32[]{:S(2)}, u32[]{:S(2)}) %collective-permute-start.8) | collective-permute-done | bytes 32800 | tf_op jit(solution)/shard_map/ppermute | solution.py:831
  32.7 1.4 %shard_map.146 = (f32[64,2048]{1,0:T(8,128)S(1)}, f32[256,128]{1,0:T(8,128)S(1)}, f32[176,128]{1,0:T(8,128)S(1)}, f32[176,128]{1,0:T(8,128)S(1)}) custom-call(f32[64,2048]{1,0:T(8,128)S(1)} %get-tuple-element.76.m_ref.m, f32[64,2048]{1,0:T(8,128)S(1)} %shard_map.145.t_in, f32[8,2048]{1,0:T(8,128)S(1)} %get-tuple-element.62.csr, s32[4]{0:T(128)S(1)} %pad_add_fusion.idx, ...), custom_call_target="tpu_custom_call" | custom-call | tf_op jit(solution)/shard_map/pallas_call | solution.py:50
  34.2 0.8 collective-permute-start.13
  35.0 0.7 shard_map.147.coef
  35.7 3.0 %collective-permute-done.12.r1 = f32[176,128]{1,0:T(8,128)S(1)} collective-permute-done((f32[176,128]{1,0:T(8,128)S(1)}, f32[176,128]{1,0:T(8,128)S(1)}, u32[]{:S(2)}, u32[]{:S(2)}) %collective-permute-start.12) | collective-permute-done | bytes 90144 | tf_op jit(solution)/shard_map/ppermute | solution.py:831
  38.7 0.1 collective-permute-done.13.r2
  38.8 0.6 shard_map.148
  39.4 0.1 collective-permute-start.14
  39.5 1.0 %collective-permute-start.15 = (f32[224,128]{1,0:T(8,128)S(1)}, f32[224,128]{1,0:T(8,128)S(1)}, u32[]{:S(2)}, u32[]{:S(2)}) collective-permute-start(f32[224,128]{1,0:T(8,128)S(1)} %get-tuple-element.90), channel_id=1, source_target_pairs={{0,32},{1,2},{2,1},{3,4},{4,3},{5,6},{6,5},{7,8},{8,7},{9,10},{10,... | collective-permute-start | bytes 344072 | tf_op jit(solution)/shard_map/ppermute | solution.py:831
  40.5 0.3 collective-permute-done.14.r3
  40.8 5.3 %collective-permute-done.15.r4 = f32[224,128]{1,0:T(8,128)S(1)} collective-permute-done((f32[224,128]{1,0:T(8,128)S(1)}, f32[224,128]{1,0:T(8,128)S(1)}, u32[]{:S(2)}, u32[]{:S(2)}) %collective-permute-start.15) | collective-permute-done | bytes 114720 | tf_op jit(solution)/shard_map/ppermute | solution.py:831
  46.1 2.2 %shard_map.149 = (f32[1280,128]{1,0:T(8,128)S(1)}, f32[128,128]{1,0:T(8,128)S(1)}, f32[160,128]{1,0:T(8,128)S(1)}, f32[160,128]{1,0:T(8,128)S(1)}) custom-call(f32[480,128]{1,0:T(8,128)S(1)} %get-tuple-element.88.whole, f32[224,128]{1,0:T(8,128)S(1)} %collective-permute-done.14.r3, f32[224,128]{1,0:T(8,128)S(1)} %collective-permute-done.15.r4, ...), custom_call_target="tpu_custom_call" | custom-call | tf_op jit(solution)/shard_map/pallas_call | solution.py:50
  48.3 0.1 collective-permute-start.16
  48.4 0.8 collective-permute-start.17
  49.2 3.6 %collective-permute-done.16.r1 = f32[160,128]{1,0:T(8,128)S(1)} collective-permute-done((f32[160,128]{1,0:T(8,128)S(1)}, f32[160,128]{1,0:T(8,128)S(1)}, u32[]{:S(2)}, u32[]{:S(2)}) %collective-permute-start.16) | collective-permute-done | bytes 81952 | tf_op jit(solution)/shard_map/ppermute | solution.py:831
  52.8 0.1 collective-permute-done.17.r2
  52.9 0.6 shard_map.150
  53.5 0.1 collective-permute-start.18
  53.6 0.1 collective-permute-start.19
  53.7 0.7 shard_map.151
  54.3 0.5 collective-permute-done.18.r3
  54.9 5.0 %collective-permute-done.19.r4 = f32[208,128]{1,0:T(8,128)S(1)} collective-permute-done((f32[208,128]{1,0:T(8,128)S(1)}, f32[208,128]{1,0:T(8,128)S(1)}, u32[]{:S(2)}, u32[]{:S(2)}) %collective-permute-start.19) | collective-permute-done | bytes 106528 | tf_op jit(solution)/shard_map/ppermute | solution.py:831
  59.9 2.8 %shard_map.152 = (f32[64,2048]{1,0:T(8,128)S(1)}, f32[16,512]{1,0:T(8,128)S(1)}, f32[16,512]{1,0:T(8,128)S(1)}, f32[32,512]{1,0:T(8,128)S(1)}, f32[32,512]{1,0:T(8,128)S(1)}) custom-call(f32[128,128]{1,0:T(8,128)S(1)} %get-tuple-element.92.own, f32[160,128]{1,0:T(8,128)S(1)} %collective-permute-done.16.r1, f32[160,128]{1,0:T(8,128)S(1)} %collective-permute-done.17.r2, ...), custom_call_target="tpu_custom_call" | custom-call | tf_op jit(solution)/shard_map/pallas_call | solution.py:50
  62.7 0.1 collective-permute-start.22
  62.7 0.1 collective-permute-start.23
  62.9 0.8 collective-permute-start.21
  63.8 0.5 shard_map.153.t_in
  64.3 2.5 %collective-permute-done.20.r1 = f32[16,512]{1,0:T(8,128)S(1)} collective-permute-done((f32[16,512]{1,0:T(8,128)S(1)}, f32[16,512]{1,0:T(8,128)S(1)}, u32[]{:S(2)}, u32[]{:S(2)}) %collective-permute-start.20) | collective-permute-done | bytes 32800 | tf_op jit(solution)/shard_map/ppermute | solution.py:831
  66.8 0.1 collective-permute-done.21.r2
  66.9 1.7 %collective-permute-done.23.r4 = f32[32,512]{1,0:T(8,128)S(1)} collective-permute-done((f32[32,512]{1,0:T(8,128)S(1)}, f32[32,512]{1,0:T(8,128)S(1)}, u32[]{:S(2)}, u32[]{:S(2)}) %collective-permute-start.23) | collective-permute-done | bytes 65568 | tf_op jit(solution)/shard_map/ppermute | solution.py:831
  68.6 1.0 %shard_map.154 = (f32[240,2048]{1,0:T(8,128)S(1)}, f32[40,512]{1,0:T(8,128)S(1)}, f32[40,512]{1,0:T(8,128)S(1)}, f32[48,512]{1,0:T(8,128)S(1)}, f32[48,512]{1,0:T(8,128)S(1)}) custom-call(f32[64,2048]{1,0:T(8,128)S(1)} %get-tuple-element.99.m_ref.m, f32[64,2048]{1,0:T(8,128)S(1)} %shard_map.153.t_in, f32[8,2048]{1,0:T(8,128)S(1)} %get-tuple-element.62.csr, ...), custom_call_target="tpu_custom_call" | custom-call | tf_op jit(solution)/shard_map/pallas_call | solution.py:50
  69.7 0.9 %collective-permute-start.27 = (f32[48,512]{1,0:T(8,128)S(1)}, f32[48,512]{1,0:T(8,128)S(1)}, u32[]{:S(2)}, u32[]{:S(2)}) collective-permute-start(f32[48,512]{1,0:T(8,128)S(1)} %get-tuple-element.109), channel_id=1, source_target_pairs={{0,32},{1,2},{2,1},{3,4},{4,3},{5,6},{6,5},{7,8},{8,7},{9,10},{10,... | collective-permute-start | bytes 294920 | tf_op jit(solution)/shard_map/ppermute | solution.py:831
  70.7 0.3 collective-permute-start.24
  70.9 0.7 collective-permute-start.25
  71.7 1.5 %shard_map.155.t_in = f32[240,2048]{1,0:T(8,128)S(1)} custom-call(f32[240,2048]{1,0:T(8,128)S(1)} %get-tuple-element.105.u_ref.u, f32[240,2048]{1,0:T(8,128)S(1)} %get-tuple-element.61.g_ref, f32[8,2048]{1,0:T(8,128)S(1)} %get-tuple-element.62.csr, bf16[240,768]{1,0:T(8,128)(2,1)S(1)} %get-tuple-element.63.kf), custom_call_target="tpu_custom_call" | custom-call | tf_op jit(solution)/shard_map/pallas_call | solution.py:50
  73.2 1.9 %collective-permute-done.24.r1 = f32[40,512]{1,0:T(8,128)S(1)} collective-permute-done((f32[40,512]{1,0:T(8,128)S(1)}, f32[40,512]{1,0:T(8,128)S(1)}, u32[]{:S(2)}, u32[]{:S(2)}) %collective-permute-start.24) | collective-permute-done | bytes 81952 | tf_op jit(solution)/shard_map/ppermute | solution.py:831
  75.1 0.3 collective-permute-done.25.r2
  75.4 0.6 collective-permute-done.27.r4
  76.0 1.6 %shard_map.156 = (f32[240,2048]{1,0:T(8,128)S(1)}, f32[40,512]{1,0:T(8,128)S(1)}, f32[40,512]{1,0:T(8,128)S(1)}, f32[48,512]{1,0:T(8,128)S(1)}, f32[48,512]{1,0:T(8,128)S(1)}) custom-call(f32[240,2048]{1,0:T(8,128)S(1)} %get-tuple-element.105.u_ref.u, f32[240,2048]{1,0:T(8,128)S(1)} %shard_map.155.t_in, f32[8,2048]{1,0:T(8,128)S(1)} %get-tuple-element.62.csr, ...), custom_call_target="tpu_custom_call" | custom-call | tf_op jit(solution)/shard_map/pallas_call | solution.py:50
  77.7 1.1 %collective-permute-start.31 = (f32[48,512]{1,0:T(8,128)S(1)}, f32[48,512]{1,0:T(8,128)S(1)}, u32[]{:S(2)}, u32[]{:S(2)}) collective-permute-start(f32[48,512]{1,0:T(8,128)S(1)} %get-tuple-element.114), channel_id=1, source_target_pairs={{0,32},{1,2},{2,1},{3,4},{4,3},{5,6},{6,5},{7,8},{8,7},{9,10},{10,... | collective-permute-start | bytes 294920 | tf_op jit(solution)/shard_map/ppermute | solution.py:831
  78.8 0.4 collective-permute-start.28
  79.2 0.7 collective-permute-start.29
  79.9 1.5 %shard_map.157.t_in = f32[240,2048]{1,0:T(8,128)S(1)} custom-call(f32[240,2048]{1,0:T(8,128)S(1)} %get-tuple-element.110.u_ref.u, f32[240,2048]{1,0:T(8,128)S(1)} %get-tuple-element.61.g_ref, f32[8,2048]{1,0:T(8,128)S(1)} %get-tuple-element.62.csr, bf16[240,768]{1,0:T(8,128)(2,1)S(1)} %get-tuple-element.63.kf), custom_call_target="tpu_custom_call" | custom-call | tf_op jit(solution)/shard_map/pallas_call | solution.py:50
  81.4 1.8 %collective-permute-done.28.r1 = f32[40,512]{1,0:T(8,128)S(1)} collective-permute-done((f32[40,512]{1,0:T(8,128)S(1)}, f32[40,512]{1,0:T(8,128)S(1)}, u32[]{:S(2)}, u32[]{:S(2)}) %collective-permute-start.28) | collective-permute-done | bytes 81952 | tf_op jit(solution)/shard_map/ppermute | solution.py:831
  83.2 0.4 collective-permute-done.29.r2
  83.6 0.3 collective-permute-done.31.r4
  83.9 4.8 %shard_map.158 = (f32[3456,128]{1,0:T(8,128)}, f32[3456,128]{1,0:T(8,128)}) custom-call(f32[240,2048]{1,0:T(8,128)S(1)} %get-tuple-element.110.u_ref.u, f32[240,2048]{1,0:T(8,128)S(1)} %shard_map.157.t_in, f32[8,2048]{1,0:T(8,128)S(1)} %get-tuple-element.62.csr, s32[4]{0:T(128)S(1)} %pad_add_fusion.idx, f32[40,512]{1,0:T(8,128)S(1)} %collective-permute-done.28.r1, ...), custom_call_target="tpu_custom_call" | custom-call | tf_op jit(solution)/shard_map/pallas_call | solution.py:50
  (34 shorter events, 0.5 us)
Async XLA Ops:
  5.0 9.6 %collective-permute-start = (f32[56,512]{1,0:T(8,128)S(1)}, f32[56,512]{1,0:T(8,128)S(1)}, u32[]{:S(2)}, u32[]{:S(2)}) collective-permute-start(f32[56,512]{1,0:T(8,128)S(1)} %get-tuple-element.64), channel_id=1, source_target_pairs={{0,32},{1,33},{2,34},{3,35},{4,36},{5,37},{6,38},{7,39},{8,40},{9,... | collective-permute-start | bytes 344072 | tf_op jit(solution)/shard_map/ppermute | solution.py:831
  5.6 9.1 %collective-permute-start.1 = (f32[56,512]{1,0:T(8,128)S(1)}, f32[56,512]{1,0:T(8,128)S(1)}, u32[]{:S(2)}, u32[]{:S(2)}) collective-permute-start(f32[56,512]{1,0:T(8,128)S(1)} %get-tuple-element.65), channel_id=1, source_target_pairs={{0,1},{1,0},{2,3},{3,2},{4,5},{5,4},{6,7},{7,6},{8,9},{9,8},{10,11... | collective-permute-start | bytes 344072 | tf_op jit(solution)/shard_map/ppermute | solution.py:831
  8.0 5.9 %collective-permute-start.2 = (f32[48,512]{1,0:T(8,128)S(1)}, f32[48,512]{1,0:T(8,128)S(1)}, u32[]{:S(2)}, u32[]{:S(2)}) collective-permute-start(f32[48,512]{1,0:T(8,128)S(1)} %get-tuple-element.66), channel_id=1, source_target_pairs={{0,1},{1,0},{2,3},{3,2},{4,5},{5,4},{6,7},{7,6},{8,9},{9,8},{10,11... | collective-permute-start | bytes 294920 | tf_op jit(solution)/shard_map/ppermute | solution.py:831
  8.0 6.7 %collective-permute-start.3 = (f32[48,512]{1,0:T(8,128)S(1)}, f32[48,512]{1,0:T(8,128)S(1)}, u32[]{:S(2)}, u32[]{:S(2)}) collective-permute-start(f32[48,512]{1,0:T(8,128)S(1)} %get-tuple-element.67), channel_id=1, source_target_pairs={{0,32},{1,2},{2,1},{3,4},{4,3},{5,6},{6,5},{7,8},{8,7},{9,10},{10,... | collective-permute-start | bytes 294920 | tf_op jit(solution)/shard_map/ppermute | solution.py:831
  16.3 8.5 %collective-permute-start.6 = (f32[88,512]{1,0:T(8,128)S(1)}, f32[88,512]{1,0:T(8,128)S(1)}, u32[]{:S(2)}, u32[]{:S(2)}) collective-permute-start(f32[88,512]{1,0:T(8,128)S(1)} %get-tuple-element.73), channel_id=1, source_target_pairs={{0,1},{1,0},{2,3},{3,2},{4,5},{5,4},{6,7},{7,6},{8,9},{9,8},{10,11... | collective-permute-start | bytes 540680 | tf_op jit(solution)/shard_map/ppermute | solution.py:831
  16.4 8.4 %collective-permute-start.7 = (f32[88,512]{1,0:T(8,128)S(1)}, f32[88,512]{1,0:T(8,128)S(1)}, u32[]{:S(2)}, u32[]{:S(2)}) collective-permute-start(f32[88,512]{1,0:T(8,128)S(1)} %get-tuple-element.74), channel_id=1, source_target_pairs={{0,32},{1,2},{2,1},{3,4},{4,3},{5,6},{6,5},{7,8},{8,7},{9,10},{10,... | collective-permute-start | bytes 540680 | tf_op jit(solution)/shard_map/ppermute | solution.py:831
  20.3 4.4 %collective-permute-start.4 = (f32[40,512]{1,0:T(8,128)S(1)}, f32[40,512]{1,0:T(8,128)S(1)}, u32[]{:S(2)}, u32[]{:S(2)}) collective-permute-start(f32[40,512]{1,0:T(8,128)S(1)} %get-tuple-element.71), channel_id=1, source_target_pairs={{0,32},{1,33},{2,34},{3,35},{4,36},{5,37},{6,38},{7,39},{8,40},{9,... | collective-permute-start | bytes 245768 | tf_op jit(solution)/shard_map/ppermute | solution.py:831
  20.3 4.4 %collective-permute-start.5 = (f32[40,512]{1,0:T(8,128)S(1)}, f32[40,512]{1,0:T(8,128)S(1)}, u32[]{:S(2)}, u32[]{:S(2)}) collective-permute-start(f32[40,512]{1,0:T(8,128)S(1)} %get-tuple-element.72), channel_id=1, source_target_pairs={{0,1},{1,0},{2,3},{3,2},{4,5},{5,4},{6,7},{7,6},{8,9},{9,8},{10,11... | collective-permute-start | bytes 245768 | tf_op jit(solution)/shard_map/ppermute | solution.py:831
  26.1 6.7 %collective-permute-start.10 = (f32[32,512]{1,0:T(8,128)S(1)}, f32[32,512]{1,0:T(8,128)S(1)}, u32[]{:S(2)}, u32[]{:S(2)}) collective-permute-start(f32[32,512]{1,0:T(8,128)S(1)} %get-tuple-element.81), channel_id=1, source_target_pairs={{0,1},{1,0},{2,3},{3,2},{4,5},{5,4},{6,7},{7,6},{8,9},{9,8},{10,11... | collective-permute-start | bytes 196616 | tf_op jit(solution)/shard_map/ppermute | solution.py:831
  26.2 6.6 %collective-permute-start.11 = (f32[32,512]{1,0:T(8,128)S(1)}, f32[32,512]{1,0:T(8,128)S(1)}, u32[]{:S(2)}, u32[]{:S(2)}) collective-permute-start(f32[32,512]{1,0:T(8,128)S(1)} %get-tuple-element.82), channel_id=1, source_target_pairs={{0,32},{1,2},{2,1},{3,4},{4,3},{5,6},{6,5},{7,8},{8,7},{9,10},{10,... | collective-permute-start | bytes 196616 | tf_op jit(solution)/shard_map/ppermute | solution.py:831
  28.8 3.9 %collective-permute-start.8 = (f32[16,512]{1,0:T(8,128)S(1)}, f32[16,512]{1,0:T(8,128)S(1)}, u32[]{:S(2)}, u32[]{:S(2)}) collective-permute-start(f32[16,512]{1,0:T(8,128)S(1)} %get-tuple-element.79), channel_id=1, source_target_pairs={{0,32},{1,33},{2,34},{3,35},{4,36},{5,37},{6,38},{7,39},{8,40},{9,... | collective-permute-start | bytes 98312 | tf_op jit(solution)/shard_map/ppermute | solution.py:831
  28.8 3.9 %collective-permute-start.9 = (f32[16,512]{1,0:T(8,128)S(1)}, f32[16,512]{1,0:T(8,128)S(1)}, u32[]{:S(2)}, u32[]{:S(2)}) collective-permute-start(f32[16,512]{1,0:T(8,128)S(1)} %get-tuple-element.80), channel_id=1, source_target_pairs={{0,1},{1,0},{2,3},{3,2},{4,5},{5,4},{6,7},{7,6},{8,9},{9,8},{10,11... | collective-permute-start | bytes 98312 | tf_op jit(solution)/shard_map/ppermute | solution.py:831
  30.1 16.0 %copy-start.5 = (f32[8,8]{1,0:T(8,128)S(1)}, f32[8,8]{1,0:T(8,128)}, u32[]{:S(2)}) copy-start(f32[8,8]{1,0:T(8,128)} %kc.3) | copy-start | bytes 772
  34.1 4.6 %collective-permute-start.12 = (f32[176,128]{1,0:T(8,128)S(1)}, f32[176,128]{1,0:T(8,128)S(1)}, u32[]{:S(2)}, u32[]{:S(2)}) collective-permute-start(f32[176,128]{1,0:T(8,128)S(1)} %get-tuple-element.86), channel_id=1, source_target_pairs={{0,32},{1,33},{2,34},{3,35},{4,36},{5,37},{6,38},{7,39},{8,40},{9,... | collective-permute-start | bytes 270344 | tf_op jit(solution)/shard_map/ppermute | solution.py:831
  34.2 19.5 %copy-start = (bf16[240,216]{1,0:T(8,128)(2,1)S(1)}, bf16[240,216]{1,0:T(8,128)(2,1)}, u32[]{:S(2)}) copy-start(bf16[240,216]{1,0:T(8,128)(2,1)} %constant.17.clone.slot_in.slot) | copy-start | bytes 311044
  34.2 19.5 %copy-start.1 = (f32[216,64]{0,1:T(8,128)S(1)}, f32[216,64]{0,1:T(8,128)}, u32[]{:S(2)}) copy-start(f32[216,64]{0,1:T(8,128)} %param.20) | copy-start | bytes 165892
  34.2 19.5 %copy-start.2 = (f32[216,216]{1,0:T(8,128)S(1)}, f32[216,216]{1,0:T(8,128)}, u32[]{:S(2)}) copy-start(f32[216,216]{1,0:T(8,128)} %noise.1) | copy-start | bytes 559876
  34.2 19.5 %copy-start.4 = (f32[64,8]{0,1:T(8,128)S(1)}, f32[64,8]{0,1:T(8,128)}, u32[]{:S(2)}) copy-start(f32[64,8]{0,1:T(8,128)} %param.21) | copy-start | bytes 6148
  34.2 4.6 %collective-permute-start.13 = (f32[176,128]{1,0:T(8,128)S(1)}, f32[176,128]{1,0:T(8,128)S(1)}, u32[]{:S(2)}, u32[]{:S(2)}) collective-permute-start(f32[176,128]{1,0:T(8,128)S(1)} %get-tuple-element.87), channel_id=1, source_target_pairs={{0,1},{1,0},{2,3},{3,2},{4,5},{5,4},{6,7},{7,6},{8,9},{9,8},{10,11... | collective-permute-start | bytes 270344 | tf_op jit(solution)/shard_map/ppermute | solution.py:831
  39.4 1.4 %collective-permute-start.14 = (f32[224,128]{1,0:T(8,128)S(1)}, f32[224,128]{1,0:T(8,128)S(1)}, u32[]{:S(2)}, u32[]{:S(2)}) collective-permute-start(f32[224,128]{1,0:T(8,128)S(1)} %get-tuple-element.89), channel_id=1, source_target_pairs={{0,1},{1,0},{2,3},{3,2},{4,5},{5,4},{6,7},{7,6},{8,9},{9,8},{10,11... | collective-permute-start | bytes 344072 | tf_op jit(solution)/shard_map/ppermute | solution.py:831
  39.5 6.6 %collective-permute-start.15 = (f32[224,128]{1,0:T(8,128)S(1)}, f32[224,128]{1,0:T(8,128)S(1)}, u32[]{:S(2)}, u32[]{:S(2)}) collective-permute-start(f32[224,128]{1,0:T(8,128)S(1)} %get-tuple-element.90), channel_id=1, source_target_pairs={{0,32},{1,2},{2,1},{3,4},{4,3},{5,6},{6,5},{7,8},{8,7},{9,10},{10,... | collective-permute-start | bytes 344072 | tf_op jit(solution)/shard_map/ppermute | solution.py:831
  48.3 4.5 %collective-permute-start.16 = (f32[160,128]{1,0:T(8,128)S(1)}, f32[160,128]{1,0:T(8,128)S(1)}, u32[]{:S(2)}, u32[]{:S(2)}) collective-permute-start(f32[160,128]{1,0:T(8,128)S(1)} %get-tuple-element.93), channel_id=1, source_target_pairs={{0,32},{1,33},{2,34},{3,35},{4,36},{5,37},{6,38},{7,39},{8,40},{9,... | collective-permute-start | bytes 245768 | tf_op jit(solution)/shard_map/ppermute | solution.py:831
  48.4 4.5 %collective-permute-start.17 = (f32[160,128]{1,0:T(8,128)S(1)}, f32[160,128]{1,0:T(8,128)S(1)}, u32[]{:S(2)}, u32[]{:S(2)}) collective-permute-start(f32[160,128]{1,0:T(8,128)S(1)} %get-tuple-element.94), channel_id=1, source_target_pairs={{0,1},{1,0},{2,3},{3,2},{4,5},{5,4},{6,7},{7,6},{8,9},{9,8},{10,11... | collective-permute-start | bytes 245768 | tf_op jit(solution)/shard_map/ppermute | solution.py:831
  53.5 1.4 %collective-permute-start.18 = (f32[208,128]{1,0:T(8,128)S(1)}, f32[208,128]{1,0:T(8,128)S(1)}, u32[]{:S(2)}, u32[]{:S(2)}) collective-permute-start(f32[208,128]{1,0:T(8,128)S(1)} %get-tuple-element.95), channel_id=1, source_target_pairs={{0,1},{1,0},{2,3},{3,2},{4,5},{5,4},{6,7},{7,6},{8,9},{9,8},{10,11... | collective-permute-start | bytes 319496 | tf_op jit(solution)/shard_map/ppermute | solution.py:831
  53.6 6.3 %collective-permute-start.19 = (f32[208,128]{1,0:T(8,128)S(1)}, f32[208,128]{1,0:T(8,128)S(1)}, u32[]{:S(2)}, u32[]{:S(2)}) collective-permute-start(f32[208,128]{1,0:T(8,128)S(1)} %get-tuple-element.96), channel_id=1, source_target_pairs={{0,32},{1,2},{2,1},{3,4},{4,3},{5,6},{6,5},{7,8},{8,7},{9,10},{10,... | collective-permute-start | bytes 319496 | tf_op jit(solution)/shard_map/ppermute | solution.py:831
  62.7 4.3 %collective-permute-start.22 = (f32[32,512]{1,0:T(8,128)S(1)}, f32[32,512]{1,0:T(8,128)S(1)}, u32[]{:S(2)}, u32[]{:S(2)}) collective-permute-start(f32[32,512]{1,0:T(8,128)S(1)} %get-tuple-element.102), channel_id=1, source_target_pairs={{0,1},{1,0},{2,3},{3,2},{4,5},{5,4},{6,7},{7,6},{8,9},{9,8},{10,11... | collective-permute-start | bytes 196616 | tf_op jit(solution)/shard_map/ppermute | solution.py:831
  62.7 5.9 %collective-permute-start.23 = (f32[32,512]{1,0:T(8,128)S(1)}, f32[32,512]{1,0:T(8,128)S(1)}, u32[]{:S(2)}, u32[]{:S(2)}) collective-permute-start(f32[32,512]{1,0:T(8,128)S(1)} %get-tuple-element.103), channel_id=1, source_target_pairs={{0,32},{1,2},{2,1},{3,4},{4,3},{5,6},{6,5},{7,8},{8,7},{9,10},{10,... | collective-permute-start | bytes 196616 | tf_op jit(solution)/shard_map/ppermute | solution.py:831
  62.8 4.0 %collective-permute-start.20 = (f32[16,512]{1,0:T(8,128)S(1)}, f32[16,512]{1,0:T(8,128)S(1)}, u32[]{:S(2)}, u32[]{:S(2)}) collective-permute-start(f32[16,512]{1,0:T(8,128)S(1)} %get-tuple-element.100), channel_id=1, source_target_pairs={{0,32},{1,33},{2,34},{3,35},{4,36},{5,37},{6,38},{7,39},{8,40},{9,... | collective-permute-start | bytes 98312 | tf_op jit(solution)/shard_map/ppermute | solution.py:831
  62.9 4.0 %collective-permute-start.21 = (f32[16,512]{1,0:T(8,128)S(1)}, f32[16,512]{1,0:T(8,128)S(1)}, u32[]{:S(2)}, u32[]{:S(2)}) collective-permute-start(f32[16,512]{1,0:T(8,128)S(1)} %get-tuple-element.101), channel_id=1, source_target_pairs={{0,1},{1,0},{2,3},{3,2},{4,5},{5,4},{6,7},{7,6},{8,9},{9,8},{10,11... | collective-permute-start | bytes 98312 | tf_op jit(solution)/shard_map/ppermute | solution.py:831
  69.7 5.7 %collective-permute-start.26 = (f32[48,512]{1,0:T(8,128)S(1)}, f32[48,512]{1,0:T(8,128)S(1)}, u32[]{:S(2)}, u32[]{:S(2)}) collective-permute-start(f32[48,512]{1,0:T(8,128)S(1)} %get-tuple-element.108), channel_id=1, source_target_pairs={{0,1},{1,0},{2,3},{3,2},{4,5},{5,4},{6,7},{7,6},{8,9},{9,8},{10,11... | collective-permute-start | bytes 294920 | tf_op jit(solution)/shard_map/ppermute | solution.py:831
  69.7 6.2 %collective-permute-start.27 = (f32[48,512]{1,0:T(8,128)S(1)}, f32[48,512]{1,0:T(8,128)S(1)}, u32[]{:S(2)}, u32[]{:S(2)}) collective-permute-start(f32[48,512]{1,0:T(8,128)S(1)} %get-tuple-element.109), channel_id=1, source_target_pairs={{0,32},{1,2},{2,1},{3,4},{4,3},{5,6},{6,5},{7,8},{8,7},{9,10},{10,... | collective-permute-start | bytes 294920 | tf_op jit(solution)/shard_map/ppermute | solution.py:831
  70.7 4.4 %collective-permute-start.24 = (f32[40,512]{1,0:T(8,128)S(1)}, f32[40,512]{1,0:T(8,128)S(1)}, u32[]{:S(2)}, u32[]{:S(2)}) collective-permute-start(f32[40,512]{1,0:T(8,128)S(1)} %get-tuple-element.106), channel_id=1, source_target_pairs={{0,32},{1,33},{2,34},{3,35},{4,36},{5,37},{6,38},{7,39},{8,40},{9,... | collective-permute-start | bytes 245768 | tf_op jit(solution)/shard_map/ppermute | solution.py:831
  70.9 4.4 %collective-permute-start.25 = (f32[40,512]{1,0:T(8,128)S(1)}, f32[40,512]{1,0:T(8,128)S(1)}, u32[]{:S(2)}, u32[]{:S(2)}) collective-permute-start(f32[40,512]{1,0:T(8,128)S(1)} %get-tuple-element.107), channel_id=1, source_target_pairs={{0,1},{1,0},{2,3},{3,2},{4,5},{5,4},{6,7},{7,6},{8,9},{9,8},{10,11... | collective-permute-start | bytes 245768 | tf_op jit(solution)/shard_map/ppermute | solution.py:831
  77.6 6.0 %collective-permute-start.30 = (f32[48,512]{1,0:T(8,128)S(1)}, f32[48,512]{1,0:T(8,128)S(1)}, u32[]{:S(2)}, u32[]{:S(2)}) collective-permute-start(f32[48,512]{1,0:T(8,128)S(1)} %get-tuple-element.113), channel_id=1, source_target_pairs={{0,1},{1,0},{2,3},{3,2},{4,5},{5,4},{6,7},{7,6},{8,9},{9,8},{10,11... | collective-permute-start | bytes 294920 | tf_op jit(solution)/shard_map/ppermute | solution.py:831
  77.7 6.2 %collective-permute-start.31 = (f32[48,512]{1,0:T(8,128)S(1)}, f32[48,512]{1,0:T(8,128)S(1)}, u32[]{:S(2)}, u32[]{:S(2)}) collective-permute-start(f32[48,512]{1,0:T(8,128)S(1)} %get-tuple-element.114), channel_id=1, source_target_pairs={{0,32},{1,2},{2,1},{3,4},{4,3},{5,6},{6,5},{7,8},{8,7},{9,10},{10,... | collective-permute-start | bytes 294920 | tf_op jit(solution)/shard_map/ppermute | solution.py:831
  78.8 4.4 %collective-permute-start.28 = (f32[40,512]{1,0:T(8,128)S(1)}, f32[40,512]{1,0:T(8,128)S(1)}, u32[]{:S(2)}, u32[]{:S(2)}) collective-permute-start(f32[40,512]{1,0:T(8,128)S(1)} %get-tuple-element.111), channel_id=1, source_target_pairs={{0,32},{1,33},{2,34},{3,35},{4,36},{5,37},{6,38},{7,39},{8,40},{9,... | collective-permute-start | bytes 245768 | tf_op jit(solution)/shard_map/ppermute | solution.py:831
  79.2 4.4 %collective-permute-start.29 = (f32[40,512]{1,0:T(8,128)S(1)}, f32[40,512]{1,0:T(8,128)S(1)}, u32[]{:S(2)}, u32[]{:S(2)}) collective-permute-start(f32[40,512]{1,0:T(8,128)S(1)} %get-tuple-element.112), channel_id=1, source_target_pairs={{0,1},{1,0},{2,3},{3,2},{4,5},{5,4},{6,7},{7,6},{8,9},{9,8},{10,11... | collective-permute-start | bytes 245768 | tf_op jit(solution)/shard_map/ppermute | solution.py:831
  79.9 4.0 %copy-start.3 = (bf16[216,240]{1,0:T(8,128)(2,1)S(1)}, bf16[216,240]{1,0:T(8,128)(2,1)}, u32[]{:S(2)}) copy-start(bf16[216,240]{1,0:T(8,128)(2,1)} %constant.18.clone.from_slot) | copy-start | bytes 311044
  79.9 4.0 %copy-start.6 = (f32[4,4,128]{2,1,0:T(4,128)S(1)}, f32[4,4,128]{2,1,0:T(4,128)}, u32[]{:S(2)}) copy-start(f32[4,4,128]{2,1,0:T(4,128)} %param.23) | copy-start | bytes 24580

commit v6 on v5

--- a/solution.py
+++ b/solution.py
@@ -144,7 +144,9 @@
     return dot_nt(left, part).astype(BF16)
 
 
-def prepare(slot, fine, mid, pmid_t, plow_t, kf, pmt, km, plt, plv):
+def prepare_kernel(slot_in, fine_in, mid_in, pmid_in, plow_in, kf, pmt, km, plt, plv):
+    slot, fine, mid = slot_in[...], fine_in[...], mid_in[...]
+    pmid_t, plow_t = pmid_in[...], plow_in[...]
     wide(kf, SF, *[turned(turned(slot, part), slot) for part in halves(fine)])
     wide(pmt, QM, *[turned(part, slot) for part in halves(pmid_t)])
     turn = one_hot(QM)
@@ -215,11 +217,30 @@
     return slice(n * 512, n * 512 + 512)
 
 
+FACE_ROWS = [slice(8 * r, min(8 * r + 8, 36)) for r in range(5)]
+
+
+def x_face(u_ref, base, lanes):
+    parts = [u_ref[base + 8 * r : base + 8 * r + 8, lanes] for r in range(5)]
+    row = sublane(parts[0].shape)
+    parts[0] = jnp.where(row < 6, parts[0], sub_roll(parts[4], 2))
+    parts[1] = jnp.where(row < 6, parts[1], parts[4])
+    parts[4] = parts[4][0:4]
+    return parts
+
+
+def x_face_tile(ref, r, lanes):
+    if r < 4:
+        return ref[8 * r : 8 * r + 8, lanes]
+    return jnp.concatenate([ref[32:36, lanes], ref[6:8, lanes], ref[14:16, lanes]], axis=0)
+
+
 def fine_sends(u_ref, idx, s1, s2, s3, s4):
     x_even, y_even = even(idx, 0), even(idx, 1)
-    upper, lower = u_ref[200:240, 1536:2048], u_ref[0:40, 0:512]
-    s1[0:40, :] = jnp.where(x_even, upper, lower)
-    s2[0:40, :] = jnp.where(x_even, lower, upper)
+    upper, lower = x_face(u_ref, 200, slice(1536, 2048)), x_face(u_ref, 0, slice(0, 512))
+    for rows, up, low in zip(FACE_ROWS, upper, lower):
+        s1[rows, :] = jnp.where(x_even, up, low)
+        s2[rows, :] = jnp.where(x_even, low, up)
     for i in range(6):
         upper = y_column(u_ref[40 * i + 8 : 40 * i + 16, :], 3)
         lower = y_column(u_ref[40 * i : 40 * i + 8, :], 0)
@@ -262,11 +283,11 @@
         for r in range(SF // 8):
             tile = t_in[8 * r : 8 * r + 8, lanes]
             if n == 0 and r < 5:
-                rows = slice(8 * r, 8 * r + 8)
-                tile = tile + csr[0:1, lanes] * jnp.where(x_even, r2[rows, side], r1[rows, side])
+                one, two = x_face_tile(r1, r, side), x_face_tile(r2, r, side)
+                tile = tile + csr[0:1, lanes] * jnp.where(x_even, two, one)
             if n == 3 and r >= 25:
-                rows = slice(8 * r - 200, 8 * r - 192)
-                tile = tile + csr[1:2, lanes] * jnp.where(x_even, r1[rows, side], r2[rows, side])
+                one, two = x_face_tile(r1, r - 25, side), x_face_tile(r2, r - 25, side)
+                tile = tile + csr[1:2, lanes] * jnp.where(x_even, one, two)
             rows = slice(r // 5 * 8, r // 5 * 8 + 8)
             if y == 0 and r % 5 == 0:
                 tile = tile + csr[2:3, lanes] * jnp.where(y_even, r4[rows, edge], r3[rows, edge])
@@ -285,8 +306,8 @@
 
 def first_kernel(
     seed_in, scale_in, coef_in, slot_in, smooth_in, fine_in, mid_in, pmid_in, plow_in, idx,
-    g, u1, csx, csr, s1, s2, s3, s4, kf, sf, pmt, km, plt, plv,
-    seed, scale, coef, slot, smooth, fine, mid, pmid, plow, done,
+    g, u1, csx, csr, s1, s2, s3, s4, sf, slot, fine, mid, pmid, plow,
+    seed, scale, coef, smooth, done,
 ):
     copies = {}
     for n, (name, source, target) in enumerate(
@@ -295,11 +316,11 @@
             ("coef", coef_in, coef),
             ("slot", slot_in, slot),
             ("smooth", smooth_in, smooth),
+            ("seed", seed_in, seed),
             ("fine", fine_in, fine),
             ("pmid", pmid_in, pmid),
             ("plow", plow_in, plow),
             ("mid", mid_in, mid),
-            ("seed", seed_in, seed),
         )
     ):
         copies[name] = pltpu.make_async_copy(source, target, done.at[n])
@@ -331,18 +352,16 @@
             csr[2 * d + 1 : 2 * d + 2, lanes] = high[c : c + 1, :]
     x_even = even(idx, 0)
     far, near = csx[4:16, :], csx[0:12, :]
-    gap = jnp.zeros((4, 512), F32)
-    s1[40:56, :] = jnp.concatenate([jnp.where(x_even, far, near), gap], axis=0)
-    s2[40:56, :] = jnp.concatenate([jnp.where(x_even, near, far), gap], axis=0)
-    for name in ("slot", "smooth", "fine", "pmid", "plow", "mid"):
-        copies[name].wait()
+    s1[36:48, :] = jnp.where(x_even, far, near)
+    s2[36:48, :] = jnp.where(x_even, near, far)
+    copies["slot"].wait()
+    copies["smooth"].wait()
     row, col = grid(QF, QF)
     first = [
         turned(slot[...], part)
         for part in halves(smooth[...] + jnp.where(row == col, 0.25, 0.0))
     ]
     wide(sf, SF, *[turned(part, slot[...]) for part in first])
-    prepare(slot[...], fine[...], mid[...], pmid[...], plow[...], kf, pmt, km, plt, plv)
     copies["seed"].wait()
     both = jnp.concatenate([first[0], slot[...]], axis=0)
     for n in range(4):
@@ -358,15 +377,17 @@
         g[:, chunk(n)] = result[SF:, :]
         u1[:, chunk(n)] = result[:SF, :] + dot(first[1], high)
     fine_sends(u1, idx, s1, s2, s3, s4)
+    for name in ("fine", "pmid", "plow", "mid"):
+        copies[name].wait()
 
 
 def spread_kernel(u, t_in, csr, idx, r1, r2, r3, r4, sf, csx, out, s1, s2, s3, s4):
     fine_update(u, t_in, csr, idx, (r1, r2, r3, r4), out, sf)
     fine_sends(out, idx, s1, s2, s3, s4)
     x_even, y_even = even(idx, 0), even(idx, 1)
-    left = jnp.where(x_even, r2[40:56, :], r1[40:56, :])
-    right = jnp.where(x_even, r1[40:56, :], r2[40:56, :])
-    planes = jnp.concatenate([left[0:12], csx[...], right[0:12]], axis=0)
+    left = jnp.where(x_even, r2[36:48, :], r1[36:48, :])
+    right = jnp.where(x_even, r1[36:48, :], r2[36:48, :])
+    planes = jnp.concatenate([left, csx[...], right], axis=0)
     gap = jnp.zeros((40, 128), F32)
     far, near = planes[:, 128:512], planes[:, 0:384]
     s3[48:88, :] = jnp.concatenate([jnp.where(y_even, far, near), gap], axis=1)
@@ -375,9 +396,9 @@
 
 def coefficient_kernel(idx, csx, r1, r2, r3, r4, coef):
     x_even, y_even = even(idx, 0), even(idx, 1)
-    left = jnp.where(x_even, r2[40:56, :], r1[40:56, :])
-    right = jnp.where(x_even, r1[40:56, :], r2[40:56, :])
-    planes = jnp.concatenate([left[0:12], csx[...], right[0:12]], axis=0)
+    left = jnp.where(x_even, r2[36:48, :], r1[36:48, :])
+    right = jnp.where(x_even, r1[36:48, :], r2[36:48, :])
+    planes = jnp.concatenate([left, csx[...], right], axis=0)
     below = jnp.where(y_even, r4[48:88, :], r3[48:88, :])
     above = jnp.where(y_even, r3[48:88, :], r4[48:88, :])
     first_x, last_x = idx[0] == 0, idx[0] == idx[2] - 1
@@ -679,12 +700,20 @@
     fine_sends(out, idx, s1, s2, s3, s4)
 
 
+def spot(x, y):
+    n = QC * (WX * (x + 3) + y + 3)
+    return slice(n, n + QC)
+
+
+def within(steps):
+    for x in range(-3, 7):
+        for y in range(-3, 7):
+            if max(0, -x, x - 3) + max(0, -y, y - 3) <= steps:
+                yield x, y
+
+
 def place_first(window, whole, r3, r4, coef, idx):
     y_even = even(idx, 1)
-    window[...] = jnp.zeros((QC * WROWS, 128), F32)
-
-    def put(plane, y, value):
-        window[pl.ds(window_row(plane, y), QC, stride=WROWS), :] = value
 
     def below(n):
         return jnp.where(y_even, tile(r4, n), tile(r3, n))
@@ -704,70 +733,71 @@
                 value = value + weight(2, p, 0) * below(count + p)
             if y == 3:
                 value = value + weight(3, p, 3) * above(count + p)
-            put(p, y, value)
+            window[spot(p - 3, y), :] = 0.2 * value
     for n, (p, d) in enumerate(REACH):
         lower, upper = below(n), above(n)
         if d == 1:
             lower = lower + weight(3, p, -1) * tile(whole, 50 + p)
             upper = upper + weight(2, p, 4) * tile(whole, 40 + p)
-        put(p, -d, lower)
-        put(p, 3 + d, upper)
+        window[spot(p - 3, -d), :] = 0.2 * lower
+        window[spot(p - 3, 3 + d), :] = 0.2 * upper
 
 
 def place_second(window, own, r1, r2, r3, r4, idx):
     y_even = even(idx, 1)
-    window[...] = jnp.zeros((QC * WROWS, 128), F32)
-
-    def put(plane, y, value):
-        window[pl.ds(window_row(plane, y), QC, stride=WROWS), :] = value
-
     planes = window_tiles(idx, own, r1, r2)
     for p in range(WX):
         for y in range(4):
-            put(p, y, planes[p][y])
+            window[spot(p - 3, y), :] = planes[p][y]
     for n, (p, d) in enumerate(REACH):
-        put(p, -d, jnp.where(y_even, tile(r4, n), tile(r3, n)))
-        put(p, 3 + d, jnp.where(y_even, tile(r3, n), tile(r4, n)))
-
-
-def coarse_sweep(c_ref, out_ref, g_ref, coef, kc, first, last):
-    def rows(d, plane):
-        return pl.ds(d * WROWS + plane * 16, 16)
-
-    def step(plane):
-        c = [c_ref[rows(d, plane), :] for d in range(QC)]
-        weights = [coef[n, pl.ds(plane * 16, 16), :] for n in range(6)]
+        window[spot(p - 3, -d), :] = jnp.where(y_even, tile(r4, n), tile(r3, n))
+        window[spot(p - 3, 3 + d), :] = jnp.where(y_even, tile(r3, n), tile(r4, n))
+
+
+def coarse_columns(kc):
+    row = sublane((QC, 128))
+    columns = []
+    for j in range(QC):
+        column = jnp.zeros((QC, 128), F32)
         for d in range(QC):
-            t = g_ref[rows(d, plane), :] - 4.0 * c[d]
-            for j in range(QC):
-                t = t - kc[j, d] * c[j]
-            if d & 4:
-                t = t + weights[1] * c_ref[rows(d - 4, plane + 1), :]
-            else:
-                t = t + weights[0] * c_ref[rows(d + 4, plane - 1), :]
-            if d & 2:
-                t = t + weights[3] * sub_roll(c[d - 2], -1)
-            else:
-                t = t + weights[2] * sub_roll(c[d + 2], 1)
-            if d & 1:
-                t = t + weights[5] * pltpu.roll(c[d - 1], 127, 1)
-            else:
-                t = t + weights[4] * pltpu.roll(c[d + 1], 1, 1)
-            out_ref[rows(d, plane), :] = c[d] + 0.2 * t
-
-    for plane in range(first, last):
-        step(plane)
+            entry = (0.2 if j == d else 0.0) - 0.2 * kc[j, d]
+            column = jnp.where(row == d, entry, column)
+        columns.append(column)
+    return columns
+
+
+def coarse_sweep(c_ref, out_ref, g_ref, coef, columns, steps):
+    row = sublane((QC, 128))
+    x_low, y_low, z_low = row < 4, row % 4 < 2, row % 2 == 0
+    for x, y in within(steps):
+        at = spot(x, y)
+        c = c_ref[at, :]
+        value = g_ref[at, :]
+        for j in range(QC):
+            value = value + columns[j] * c_ref[at.start + j : at.start + j + 1, :]
+        place = window_row(x + 3, y)
+        w = [coef[n, place : place + 1, :] for n in range(6)]
+        along_x = jnp.where(x_low, c_ref[spot(x + 1, y), :], c_ref[spot(x - 1, y), :])
+        along_y = jnp.where(y_low, c_ref[spot(x, y + 1), :], c_ref[spot(x, y - 1), :])
+        along_z = jnp.where(z_low, pltpu.roll(c, 127, 1), pltpu.roll(c, 1, 1))
+        faces = jnp.where(x_low, w[0], w[1]) * sub_roll(along_x, 4)
+        faces = faces + jnp.where(y_low, w[2], w[3]) * jnp.where(
+            y_low, sub_roll(along_y, 6), sub_roll(along_y, 2)
+        )
+        faces = faces + jnp.where(z_low, w[4], w[5]) * jnp.where(
+            z_low, sub_roll(along_z, 7), sub_roll(along_z, 1)
+        )
+        out_ref[at, :] = value + 0.2 * faces
 
 
 def coarse_kernel(whole, r3, r4, kc, idx, coef, m, g, pay, s1, s2, one, two):
     place_first(g, whole, r3, r4, coef, idx)
-    one[...] = 0.2 * g[...]
-    coarse_sweep(one, two, g, coef, kc, 1, 9)
-    coarse_sweep(two, one, g, coef, kc, 2, 8)
-    coarse_sweep(one, two, g, coef, kc, 3, 7)
+    columns = coarse_columns(kc)
+    coarse_sweep(g, one, g, coef, columns, 2)
+    coarse_sweep(one, two, g, coef, columns, 1)
+    coarse_sweep(two, one, g, coef, columns, 0)
     for c in range(COLS):
-        row = window_row(3 + c // 4, c % 4)
-        pay[QC * c : QC * c + QC, :] = two[pl.ds(row, QC, stride=WROWS), :]
+        pay[QC * c : QC * c + QC, :] = one[spot(c // 4, c % 4), :]
     far, near = [pay[32:128, :]], [pay[0:96, :]]
     for y in range(4):
         far.append(m[48:64, (12 + y) * 128 : (13 + y) * 128])
@@ -780,13 +810,14 @@
     out, s1, s2, s3, s4, one, two, x_ref, t_ref, m_ref,
 ):
     place_second(one, own, r1, r2, r3, r4, idx)
-    coarse_sweep(one, two, g, coef, kc, 1, 9)
-    coarse_sweep(two, one, g, coef, kc, 2, 8)
+    columns = coarse_columns(kc)
+    coarse_sweep(one, two, g, coef, columns, 2)
+    coarse_sweep(two, one, g, coef, columns, 1)
 
     def lifted(x, y, rows):
         total = None
         for d in range(QC):
-            row = d * WROWS + (3 + x) * 16 + 4 + y
+            row = spot(x, y).start + d
             part = spread[d, rows, :] * one[row : row + 1, :]
             total = part if total is None else total + part
         return total
@@ -859,13 +890,13 @@
     to_slot, from_slot = jnp.asarray(slots, BF16), jnp.asarray(slots.T, BF16)
 
     fine_field = ((SF, LANES), F32)
-    fine_faces = [((40, 512), F32)] * 2 + [((48, 512), F32)] * 2
+    fine_faces = [((36, 512), F32)] * 2 + [((48, 512), F32)] * 2
     mid_field = ((QM, LANES), F32)
     mid_faces = [((16, 512), F32)] * 2 + [((32, 512), F32)] * 2
     xf = pltpu.VMEM((512, LANES), BF16)
     xm, tm = pltpu.VMEM((256, LANES), BF16), pltpu.VMEM((QM, LANES), F32)
-    window = ((QC * WROWS, 128), F32)
-    windows = [pltpu.VMEM((QC * WROWS, 128), F32)] * 2
+    window = ((QC * WX * WX, 128), F32)
+    windows = [pltpu.VMEM((QC * WX * WX, 128), F32)] * 2
 
     operands = (
         seed.reshape(QF * COLS, 128),
@@ -878,27 +909,37 @@
         pmid.T,
         plow.T,
     )
-    g, u, csx, csr, s1, s2, s3, s4, kf, sf, pmt, km, plt, plv = call(
+    g, u, csx, csr, s1, s2, s3, s4, sf, *matrices = call(
         first_kernel,
         [fine_field, fine_field, ((16, 512), F32), ((8, LANES), F32)]
-        + [((56, 512), F32)] * 2
+        + [((48, 512), F32)] * 2
         + [((48, 512), F32)] * 2
         + [
             ((SF, 768), BF16),
+            ((SF, QF), BF16),
+            ((QF, QF), F32),
+            ((QM, QM), F32),
+            ((QM, QF), F32),
+            ((QC, QM), F32),
+        ],
+        [pltpu.VMEM(operands[n].shape, F32) for n in (0, 1, 2, 4)]
+        + [pltpu.SemaphoreType.DMA((len(operands),))],
+        (9,),
+        range(9),
+    )(*operands, idx)
+    kf, pmt, km, plt, plv = call(
+        prepare_kernel,
+        [
             ((SF, 768), BF16),
             ((QM, 768), BF16),
             ((QM, 256), BF16),
             ((16, 256), BF16),
             ((32, 256), BF16),
         ],
-        [pltpu.VMEM(operand.shape, operand.dtype) for operand in operands]
-        + [pltpu.SemaphoreType.DMA((len(operands),))],
-        (9,),
-        range(9),
-    )(*operands, idx)
+    )(*matrices)
     nf, pm, spread = call(
         late_kernel, [((QF, 768), BF16), ((SF, 256), BF16), ((QC, QM, 128), F32)]
-    )(to_slot, noise, pmid.T, plow.T)
+    )(matrices[0], noise, matrices[3], matrices[4])
 
     def fine_local(u):
         (t,) = call(fine_local_kernel, [fine_field], [xf])(u, g, csr, kf)

time: 89 us -> 87.3 us (0.981)
  Pallas kernels: 30.5 us -> 29.5 us
    pallas_call x19 -> x20, Pallas kernels: 30.5 us -> 29.5 us  [run(): pl.pallas_call(kernel, out_shape=tuple((jax.ShapeDtypeStruct(s, d) for s,...]
  transfers between devices with their start and end apart: 32 -> 32, of which waited for: 20 -> 19; matrix products, arithmetic and copies ran while one was open for 0% -> 0% of each run, Pallas kernels for 9% -> 10%
where the time goes in v6:
time: 87.3 us; the launch traced here: 87.2 us
  waiting for transfers between devices  32.5 us (37%)
  Pallas kernels  29.5 us (34%)
  starting transfers between devices  24 us (27%)
  between operations  1.1 us (1%)
    ppermute x32, waiting for transfers between devices, swap(): return lax.ppermute(values, ('gx', 'yz'), partners(step))  32.5 us
    pallas_call x20, Pallas kernels, run(): pl.pallas_call(kernel, out_shape=tuple((jax.ShapeDtypeStruct(s, d) for s,...  29.5 us
    ppermute x32, starting transfers between devices, swap(): return lax.ppermute(values, ('gx', 'yz'), partners(step))  24 us
  transfers between devices with their start and end apart: 32, of which 19 were waited for; matrix products, arithmetic and copies ran while one was open for 0% of the time, Pallas kernels for 10%

profile of v6, /device:TPU:14, one launch (start us, length us, event | category | flops | bytes accessed | tf_op | source)
XLA Modules:
  0.0 87.2 jit_solution(17468100733759053010)
XLA Ops:
  0.7 3.9 %shard_map.140 = (f32[240,2048]{1,0:T(8,128)S(1)}, f32[240,2048]{1,0:T(8,128)S(1)}, f32[16,512]{1,0:T(8,128)S(1)}, f32[8,2048]{1,0:T(8,128)S(1)}, f32[48,512]{1,...) custom-call(f32[3456,128]{1,0:T(8,128)} %bitcast.11, ...), custom_call_target="tpu_custom_call" | custom-call | tf_op jit(solution)/shard_map/pallas_call | solution.py:50
  4.7 0.5 collective-permute-start
  5.2 2.4 %collective-permute-start.1 = (f32[48,512]{1,0:T(8,128)S(1)}, f32[48,512]{1,0:T(8,128)S(1)}, u32[]{:S(2)}, u32[]{:S(2)}) collective-permute-start(f32[48,512]{1,0:T(8,128)S(1)} %get-tuple-element.75), channel_id=1, source_target_pairs={{0,1},{1,0},{2,3},{3,2},{4,5},{5,4},{6,7},{7,6},{8,9},{9,8},{10,11... | collective-permute-start | bytes 294920 | tf_op jit(solution)/shard_map/ppermute | solution.py:862
  7.6 4.4 %collective-permute-start.3 = (f32[48,512]{1,0:T(8,128)S(1)}, f32[48,512]{1,0:T(8,128)S(1)}, u32[]{:S(2)}, u32[]{:S(2)}) collective-permute-start(f32[48,512]{1,0:T(8,128)S(1)} %get-tuple-element.77), channel_id=1, source_target_pairs={{0,32},{1,2},{2,1},{3,4},{4,3},{5,6},{6,5},{7,8},{8,7},{9,10},{10,... | collective-permute-start | bytes 294920 | tf_op jit(solution)/shard_map/ppermute | solution.py:862
  12.0 0.7 shard_map.141
  12.7 1.5 %shard_map.142.t_in = f32[240,2048]{1,0:T(8,128)S(1)} custom-call(f32[240,2048]{1,0:T(8,128)S(1)} %get-tuple-element.65.u_ref.u, f32[240,2048]{1,0:T(8,128)S(1)} %get-tuple-element.66.g_ref, f32[8,2048]{1,0:T(8,128)S(1)} %get-tuple-element.67.csr, bf16[240,768]{1,0:T(8,128)(2,1)S(1)} %get-tuple-element.73.kf), custom_call_target="tpu_custom_call" | custom-call | tf_op jit(solution)/shard_map/pallas_call | solution.py:50
  14.3 1.6 %shard_map.143 = (f32[240,2048]{1,0:T(8,128)S(1)}, f32[36,512]{1,0:T(8,128)S(1)}, f32[36,512]{1,0:T(8,128)S(1)}, f32[88,512]{1,0:T(8,128)S(1)}, f32[88,512]{1,0:T(8,128)S(1)}) custom-call(f32[240,2048]{1,0:T(8,128)S(1)} %get-tuple-element.65.u_ref.u, f32[240,2048]{1,0:T(8,128)S(1)} %shard_map.142.t_in, f32[8,2048]{1,0:T(8,128)S(1)} %get-tuple-element.67.csr, ...), custom_call_target="tpu_custom_call" | custom-call | tf_op jit(solution)/shard_map/pallas_call | solution.py:50
  15.9 0.1 collective-permute-start.6
  16.0 3.9 %collective-permute-start.7 = (f32[88,512]{1,0:T(8,128)S(1)}, f32[88,512]{1,0:T(8,128)S(1)}, u32[]{:S(2)}, u32[]{:S(2)}) collective-permute-start(f32[88,512]{1,0:T(8,128)S(1)} %get-tuple-element.84), channel_id=1, source_target_pairs={{0,32},{1,2},{2,1},{3,4},{4,3},{5,6},{6,5},{7,8},{8,7},{9,10},{10,... | collective-permute-start | bytes 540680 | tf_op jit(solution)/shard_map/ppermute | solution.py:862
  20.0 0.7 collective-permute-start.5
  20.7 1.5 %shard_map.144.t_in = f32[240,2048]{1,0:T(8,128)S(1)} custom-call(f32[240,2048]{1,0:T(8,128)S(1)} %get-tuple-element.80.u_ref.u, f32[240,2048]{1,0:T(8,128)S(1)} %get-tuple-element.66.g_ref, f32[8,2048]{1,0:T(8,128)S(1)} %get-tuple-element.67.csr, bf16[240,768]{1,0:T(8,128)(2,1)S(1)} %get-tuple-element.73.kf), custom_call_target="tpu_custom_call" | custom-call | tf_op jit(solution)/shard_map/pallas_call | solution.py:50
  22.2 2.2 %collective-permute-done.4.r1 = f32[36,512]{1,0:T(8,128)S(1)} collective-permute-done((f32[36,512]{1,0:T(8,128)S(1)}, f32[36,512]{1,0:T(8,128)S(1)}, u32[]{:S(2)}, u32[]{:S(2)}) %collective-permute-start.4) | collective-permute-done | bytes 73760 | tf_op jit(solution)/shard_map/ppermute | solution.py:862
  24.4 1.3 %shard_map.145 = (f32[64,2048]{1,0:T(8,128)S(1)}, f32[64,2048]{1,0:T(8,128)S(1)}, f32[16,512]{1,0:T(8,128)S(1)}, f32[16,512]{1,0:T(8,128)S(1)}, f32[32,512]{1,0:T(8,128)S(1)}, /*index=5*/f32[32,512]{1,0:T(8,128)S(1)}) custom-call(f32[240,2048]{1,0:T(8,128)S(1)} %shard_map.144.t_in, f32[8,2048]{1,0:T(8,128)S(1)} %get-tuple-element.67.csr, ...), custom_call_target="tpu_custom_call" | custom-call | tf_op jit(solution)/shard_map/pallas_call | solution.py:50
  25.7 0.1 collective-permute-start.10
  25.8 2.7 %collective-permute-start.11 = (f32[32,512]{1,0:T(8,128)S(1)}, f32[32,512]{1,0:T(8,128)S(1)}, u32[]{:S(2)}, u32[]{:S(2)}) collective-permute-start(f32[32,512]{1,0:T(8,128)S(1)} %get-tuple-element.92), channel_id=1, source_target_pairs={{0,32},{1,2},{2,1},{3,4},{4,3},{5,6},{6,5},{7,8},{8,7},{9,10},{10,... | collective-permute-start | bytes 196616 | tf_op jit(solution)/shard_map/ppermute | solution.py:862
  28.5 0.7 collective-permute-start.9
  29.2 0.5 shard_map.146.t_in
  29.8 2.6 %collective-permute-done.8.r1 = f32[16,512]{1,0:T(8,128)S(1)} collective-permute-done((f32[16,512]{1,0:T(8,128)S(1)}, f32[16,512]{1,0:T(8,128)S(1)}, u32[]{:S(2)}, u32[]{:S(2)}) %collective-permute-start.8) | collective-permute-done | bytes 32800 | tf_op jit(solution)/shard_map/ppermute | solution.py:862
  32.4 1.4 %shard_map.147 = (f32[64,2048]{1,0:T(8,128)S(1)}, f32[256,128]{1,0:T(8,128)S(1)}, f32[176,128]{1,0:T(8,128)S(1)}, f32[176,128]{1,0:T(8,128)S(1)}) custom-call(f32[64,2048]{1,0:T(8,128)S(1)} %get-tuple-element.86.m_ref.m, f32[64,2048]{1,0:T(8,128)S(1)} %shard_map.146.t_in, f32[8,2048]{1,0:T(8,128)S(1)} %get-tuple-element.67.csr, s32[4]{0:T(128)S(1)} %pad_add_fusion.idx, ...), custom_call_target="tpu_custom_call" | custom-call | tf_op jit(solution)/shard_map/pallas_call | solution.py:50
  33.9 0.8 collective-permute-start.13
  34.7 0.7 shard_map.148.coef
  35.4 3.0 %collective-permute-done.12.r1 = f32[176,128]{1,0:T(8,128)S(1)} collective-permute-done((f32[176,128]{1,0:T(8,128)S(1)}, f32[176,128]{1,0:T(8,128)S(1)}, u32[]{:S(2)}, u32[]{:S(2)}) %collective-permute-start.12) | collective-permute-done | bytes 90144 | tf_op jit(solution)/shard_map/ppermute | solution.py:862
  38.4 0.1 collective-permute-done.13.r2
  38.5 0.6 shard_map.149
  39.1 0.1 collective-permute-start.14
  39.1 1.0 %collective-permute-start.15 = (f32[224,128]{1,0:T(8,128)S(1)}, f32[224,128]{1,0:T(8,128)S(1)}, u32[]{:S(2)}, u32[]{:S(2)}) collective-permute-start(f32[224,128]{1,0:T(8,128)S(1)} %get-tuple-element.100), channel_id=1, source_target_pairs={{0,32},{1,2},{2,1},{3,4},{4,3},{5,6},{6,5},{7,8},{8,7},{9,10},{10,... | collective-permute-start | bytes 344072 | tf_op jit(solution)/shard_map/ppermute | solution.py:862
  40.1 0.3 collective-permute-done.14.r3
  40.5 5.3 %collective-permute-done.15.r4 = f32[224,128]{1,0:T(8,128)S(1)} collective-permute-done((f32[224,128]{1,0:T(8,128)S(1)}, f32[224,128]{1,0:T(8,128)S(1)}, u32[]{:S(2)}, u32[]{:S(2)}) %collective-permute-start.15) | collective-permute-done | bytes 114720 | tf_op jit(solution)/shard_map/ppermute | solution.py:862
  45.7 1.2 %shard_map.150 = (f32[800,128]{1,0:T(8,128)S(1)}, f32[128,128]{1,0:T(8,128)S(1)}, f32[160,128]{1,0:T(8,128)S(1)}, f32[160,128]{1,0:T(8,128)S(1)}) custom-call(f32[480,128]{1,0:T(8,128)S(1)} %get-tuple-element.98.whole, f32[224,128]{1,0:T(8,128)S(1)} %collective-permute-done.14.r3, f32[224,128]{1,0:T(8,128)S(1)} %collective-permute-done.15.r4, ...), custom_call_target="tpu_custom_call" | custom-call | tf_op jit(solution)/shard_map/pallas_call | solution.py:50
  47.0 0.1 collective-permute-start.16
  47.1 0.8 collective-permute-start.17
  47.9 3.6 %collective-permute-done.16.r1 = f32[160,128]{1,0:T(8,128)S(1)} collective-permute-done((f32[160,128]{1,0:T(8,128)S(1)}, f32[160,128]{1,0:T(8,128)S(1)}, u32[]{:S(2)}, u32[]{:S(2)}) %collective-permute-start.16) | collective-permute-done | bytes 81952 | tf_op jit(solution)/shard_map/ppermute | solution.py:862
  51.5 0.1 collective-permute-done.17.r2
  51.6 0.6 shard_map.151
  52.2 0.1 collective-permute-start.18
  52.3 0.1 collective-permute-start.19
  52.4 0.7 shard_map.152
  53.0 0.5 collective-permute-done.18.r3
  53.6 5.0 %collective-permute-done.19.r4 = f32[208,128]{1,0:T(8,128)S(1)} collective-permute-done((f32[208,128]{1,0:T(8,128)S(1)}, f32[208,128]{1,0:T(8,128)S(1)}, u32[]{:S(2)}, u32[]{:S(2)}) %collective-permute-start.19) | collective-permute-done | bytes 106528 | tf_op jit(solution)/shard_map/ppermute | solution.py:862
  58.6 2.2 %shard_map.153 = (f32[64,2048]{1,0:T(8,128)S(1)}, f32[16,512]{1,0:T(8,128)S(1)}, f32[16,512]{1,0:T(8,128)S(1)}, f32[32,512]{1,0:T(8,128)S(1)}, f32[32,512]{1,0:T(8,128)S(1)}) custom-call(f32[128,128]{1,0:T(8,128)S(1)} %get-tuple-element.102.own, f32[160,128]{1,0:T(8,128)S(1)} %collective-permute-done.16.r1, f32[160,128]{1,0:T(8,128)S(1)} %collective-permute-done.17.r2, ...), custom_call_target="tpu_custom_call" | custom-call | tf_op jit(solution)/shard_map/pallas_call | solution.py:50
  60.9 0.1 collective-permute-start.23
  60.9 0.1 collective-permute-start.20
  61.0 0.8 collective-permute-start.21
  61.9 0.5 shard_map.154.t_in
  62.4 2.5 %collective-permute-done.20.r1 = f32[16,512]{1,0:T(8,128)S(1)} collective-permute-done((f32[16,512]{1,0:T(8,128)S(1)}, f32[16,512]{1,0:T(8,128)S(1)}, u32[]{:S(2)}, u32[]{:S(2)}) %collective-permute-start.20) | collective-permute-done | bytes 32800 | tf_op jit(solution)/shard_map/ppermute | solution.py:862
  64.9 0.1 collective-permute-done.21.r2
  65.0 1.7 %collective-permute-done.23.r4 = f32[32,512]{1,0:T(8,128)S(1)} collective-permute-done((f32[32,512]{1,0:T(8,128)S(1)}, f32[32,512]{1,0:T(8,128)S(1)}, u32[]{:S(2)}, u32[]{:S(2)}) %collective-permute-start.23) | collective-permute-done | bytes 65568 | tf_op jit(solution)/shard_map/ppermute | solution.py:862
  66.7 1.0 %shard_map.155 = (f32[240,2048]{1,0:T(8,128)S(1)}, f32[36,512]{1,0:T(8,128)S(1)}, f32[36,512]{1,0:T(8,128)S(1)}, f32[48,512]{1,0:T(8,128)S(1)}, f32[48,512]{1,0:T(8,128)S(1)}) custom-call(f32[64,2048]{1,0:T(8,128)S(1)} %get-tuple-element.109.m_ref.m, f32[64,2048]{1,0:T(8,128)S(1)} %shard_map.154.t_in, f32[8,2048]{1,0:T(8,128)S(1)} %get-tuple-element.67.csr, ...), custom_call_target="tpu_custom_call" | custom-call | tf_op jit(solution)/shard_map/pallas_call | solution.py:50
  67.9 0.9 %collective-permute-start.27 = (f32[48,512]{1,0:T(8,128)S(1)}, f32[48,512]{1,0:T(8,128)S(1)}, u32[]{:S(2)}, u32[]{:S(2)}) collective-permute-start(f32[48,512]{1,0:T(8,128)S(1)} %get-tuple-element.119), channel_id=1, source_target_pairs={{0,32},{1,2},{2,1},{3,4},{4,3},{5,6},{6,5},{7,8},{8,7},{9,10},{10,... | collective-permute-start | bytes 294920 | tf_op jit(solution)/shard_map/ppermute | solution.py:862
  68.8 0.3 collective-permute-start.24
  69.1 0.7 collective-permute-start.25
  69.8 1.5 %shard_map.156.t_in = f32[240,2048]{1,0:T(8,128)S(1)} custom-call(f32[240,2048]{1,0:T(8,128)S(1)} %get-tuple-element.115.u_ref.u, f32[240,2048]{1,0:T(8,128)S(1)} %get-tuple-element.66.g_ref, f32[8,2048]{1,0:T(8,128)S(1)} %get-tuple-element.67.csr, bf16[240,768]{1,0:T(8,128)(2,1)S(1)} %get-tuple-element.73.kf), custom_call_target="tpu_custom_call" | custom-call | tf_op jit(solution)/shard_map/pallas_call | solution.py:50
  71.3 1.9 %collective-permute-done.24.r1 = f32[36,512]{1,0:T(8,128)S(1)} collective-permute-done((f32[36,512]{1,0:T(8,128)S(1)}, f32[36,512]{1,0:T(8,128)S(1)}, u32[]{:S(2)}, u32[]{:S(2)}) %collective-permute-start.24) | collective-permute-done | bytes 73760 | tf_op jit(solution)/shard_map/ppermute | solution.py:862
  73.2 0.3 collective-permute-done.25.r2
  73.5 0.6 collective-permute-done.27.r4
  74.1 1.6 %shard_map.157 = (f32[240,2048]{1,0:T(8,128)S(1)}, f32[36,512]{1,0:T(8,128)S(1)}, f32[36,512]{1,0:T(8,128)S(1)}, f32[48,512]{1,0:T(8,128)S(1)}, f32[48,512]{1,0:T(8,128)S(1)}) custom-call(f32[240,2048]{1,0:T(8,128)S(1)} %get-tuple-element.115.u_ref.u, f32[240,2048]{1,0:T(8,128)S(1)} %shard_map.156.t_in, f32[8,2048]{1,0:T(8,128)S(1)} %get-tuple-element.67.csr, ...), custom_call_target="tpu_custom_call" | custom-call | tf_op jit(solution)/shard_map/pallas_call | solution.py:50
  75.8 1.1 %collective-permute-start.31 = (f32[48,512]{1,0:T(8,128)S(1)}, f32[48,512]{1,0:T(8,128)S(1)}, u32[]{:S(2)}, u32[]{:S(2)}) collective-permute-start(f32[48,512]{1,0:T(8,128)S(1)} %get-tuple-element.124), channel_id=1, source_target_pairs={{0,32},{1,2},{2,1},{3,4},{4,3},{5,6},{6,5},{7,8},{8,7},{9,10},{10,... | collective-permute-start | bytes 294920 | tf_op jit(solution)/shard_map/ppermute | solution.py:862
  76.9 0.4 collective-permute-start.28
  77.3 0.7 collective-permute-start.29
  78.0 1.5 %shard_map.158.t_in = f32[240,2048]{1,0:T(8,128)S(1)} custom-call(f32[240,2048]{1,0:T(8,128)S(1)} %get-tuple-element.120.u_ref.u, f32[240,2048]{1,0:T(8,128)S(1)} %get-tuple-element.66.g_ref, f32[8,2048]{1,0:T(8,128)S(1)} %get-tuple-element.67.csr, bf16[240,768]{1,0:T(8,128)(2,1)S(1)} %get-tuple-element.73.kf), custom_call_target="tpu_custom_call" | custom-call | tf_op jit(solution)/shard_map/pallas_call | solution.py:50
  79.5 1.8 %collective-permute-done.28.r1 = f32[36,512]{1,0:T(8,128)S(1)} collective-permute-done((f32[36,512]{1,0:T(8,128)S(1)}, f32[36,512]{1,0:T(8,128)S(1)}, u32[]{:S(2)}, u32[]{:S(2)}) %collective-permute-start.28) | collective-permute-done | bytes 73760 | tf_op jit(solution)/shard_map/ppermute | solution.py:862
  81.3 0.4 collective-permute-done.29.r2
  81.7 0.3 collective-permute-done.31.r4
  82.0 5.0 %shard_map.159 = (f32[3456,128]{1,0:T(8,128)}, f32[3456,128]{1,0:T(8,128)}) custom-call(f32[240,2048]{1,0:T(8,128)S(1)} %get-tuple-element.120.u_ref.u, f32[240,2048]{1,0:T(8,128)S(1)} %shard_map.158.t_in, f32[8,2048]{1,0:T(8,128)S(1)} %get-tuple-element.67.csr, s32[4]{0:T(128)S(1)} %pad_add_fusion.idx, f32[36,512]{1,0:T(8,128)S(1)} %collective-permute-done.28.r1, ...), custom_call_target="tpu_custom_call" | custom-call | tf_op jit(solution)/shard_map/pallas_call | solution.py:50
  (29 shorter events, 0.5 us)
Async XLA Ops:
  4.7 9.6 %collective-permute-start = (f32[48,512]{1,0:T(8,128)S(1)}, f32[48,512]{1,0:T(8,128)S(1)}, u32[]{:S(2)}, u32[]{:S(2)}) collective-permute-start(f32[48,512]{1,0:T(8,128)S(1)} %get-tuple-element.74), channel_id=1, source_target_pairs={{0,32},{1,33},{2,34},{3,35},{4,36},{5,37},{6,38},{7,39},{8,40},{9,... | collective-permute-start | bytes 294920 | tf_op jit(solution)/shard_map/ppermute | solution.py:862
  5.2 9.1 %collective-permute-start.1 = (f32[48,512]{1,0:T(8,128)S(1)}, f32[48,512]{1,0:T(8,128)S(1)}, u32[]{:S(2)}, u32[]{:S(2)}) collective-permute-start(f32[48,512]{1,0:T(8,128)S(1)} %get-tuple-element.75), channel_id=1, source_target_pairs={{0,1},{1,0},{2,3},{3,2},{4,5},{5,4},{6,7},{7,6},{8,9},{9,8},{10,11... | collective-permute-start | bytes 294920 | tf_op jit(solution)/shard_map/ppermute | solution.py:862
  7.6 6.7 %collective-permute-start.2 = (f32[48,512]{1,0:T(8,128)S(1)}, f32[48,512]{1,0:T(8,128)S(1)}, u32[]{:S(2)}, u32[]{:S(2)}) collective-permute-start(f32[48,512]{1,0:T(8,128)S(1)} %get-tuple-element.76), channel_id=1, source_target_pairs={{0,1},{1,0},{2,3},{3,2},{4,5},{5,4},{6,7},{7,6},{8,9},{9,8},{10,11... | collective-permute-start | bytes 294920 | tf_op jit(solution)/shard_map/ppermute | solution.py:862
  7.6 6.7 %collective-permute-start.3 = (f32[48,512]{1,0:T(8,128)S(1)}, f32[48,512]{1,0:T(8,128)S(1)}, u32[]{:S(2)}, u32[]{:S(2)}) collective-permute-start(f32[48,512]{1,0:T(8,128)S(1)} %get-tuple-element.77), channel_id=1, source_target_pairs={{0,32},{1,2},{2,1},{3,4},{4,3},{5,6},{6,5},{7,8},{8,7},{9,10},{10,... | collective-permute-start | bytes 294920 | tf_op jit(solution)/shard_map/ppermute | solution.py:862
  15.9 8.5 %collective-permute-start.6 = (f32[88,512]{1,0:T(8,128)S(1)}, f32[88,512]{1,0:T(8,128)S(1)}, u32[]{:S(2)}, u32[]{:S(2)}) collective-permute-start(f32[88,512]{1,0:T(8,128)S(1)} %get-tuple-element.83), channel_id=1, source_target_pairs={{0,1},{1,0},{2,3},{3,2},{4,5},{5,4},{6,7},{7,6},{8,9},{9,8},{10,11... | collective-permute-start | bytes 540680 | tf_op jit(solution)/shard_map/ppermute | solution.py:862
  16.0 8.4 %collective-permute-start.7 = (f32[88,512]{1,0:T(8,128)S(1)}, f32[88,512]{1,0:T(8,128)S(1)}, u32[]{:S(2)}, u32[]{:S(2)}) collective-permute-start(f32[88,512]{1,0:T(8,128)S(1)} %get-tuple-element.84), channel_id=1, source_target_pairs={{0,32},{1,2},{2,1},{3,4},{4,3},{5,6},{6,5},{7,8},{8,7},{9,10},{10,... | collective-permute-start | bytes 540680 | tf_op jit(solution)/shard_map/ppermute | solution.py:862
  20.0 4.4 %collective-permute-start.4 = (f32[36,512]{1,0:T(8,128)S(1)}, f32[36,512]{1,0:T(8,128)S(1)}, u32[]{:S(2)}, u32[]{:S(2)}) collective-permute-start(f32[36,512]{1,0:T(8,128)S(1)} %get-tuple-element.81), channel_id=1, source_target_pairs={{0,32},{1,33},{2,34},{3,35},{4,36},{5,37},{6,38},{7,39},{8,40},{9,... | collective-permute-start | bytes 221192 | tf_op jit(solution)/shard_map/ppermute | solution.py:862
  20.0 4.4 %collective-permute-start.5 = (f32[36,512]{1,0:T(8,128)S(1)}, f32[36,512]{1,0:T(8,128)S(1)}, u32[]{:S(2)}, u32[]{:S(2)}) collective-permute-start(f32[36,512]{1,0:T(8,128)S(1)} %get-tuple-element.82), channel_id=1, source_target_pairs={{0,1},{1,0},{2,3},{3,2},{4,5},{5,4},{6,7},{7,6},{8,9},{9,8},{10,11... | collective-permute-start | bytes 221192 | tf_op jit(solution)/shard_map/ppermute | solution.py:862
  25.7 6.7 %collective-permute-start.10 = (f32[32,512]{1,0:T(8,128)S(1)}, f32[32,512]{1,0:T(8,128)S(1)}, u32[]{:S(2)}, u32[]{:S(2)}) collective-permute-start(f32[32,512]{1,0:T(8,128)S(1)} %get-tuple-element.91), channel_id=1, source_target_pairs={{0,1},{1,0},{2,3},{3,2},{4,5},{5,4},{6,7},{7,6},{8,9},{9,8},{10,11... | collective-permute-start | bytes 196616 | tf_op jit(solution)/shard_map/ppermute | solution.py:862
  25.8 6.6 %collective-permute-start.11 = (f32[32,512]{1,0:T(8,128)S(1)}, f32[32,512]{1,0:T(8,128)S(1)}, u32[]{:S(2)}, u32[]{:S(2)}) collective-permute-start(f32[32,512]{1,0:T(8,128)S(1)} %get-tuple-element.92), channel_id=1, source_target_pairs={{0,32},{1,2},{2,1},{3,4},{4,3},{5,6},{6,5},{7,8},{8,7},{9,10},{10,... | collective-permute-start | bytes 196616 | tf_op jit(solution)/shard_map/ppermute | solution.py:862
  28.5 3.9 %collective-permute-start.8 = (f32[16,512]{1,0:T(8,128)S(1)}, f32[16,512]{1,0:T(8,128)S(1)}, u32[]{:S(2)}, u32[]{:S(2)}) collective-permute-start(f32[16,512]{1,0:T(8,128)S(1)} %get-tuple-element.89), channel_id=1, source_target_pairs={{0,32},{1,33},{2,34},{3,35},{4,36},{5,37},{6,38},{7,39},{8,40},{9,... | collective-permute-start | bytes 98312 | tf_op jit(solution)/shard_map/ppermute | solution.py:862
  28.5 3.9 %collective-permute-start.9 = (f32[16,512]{1,0:T(8,128)S(1)}, f32[16,512]{1,0:T(8,128)S(1)}, u32[]{:S(2)}, u32[]{:S(2)}) collective-permute-start(f32[16,512]{1,0:T(8,128)S(1)} %get-tuple-element.90), channel_id=1, source_target_pairs={{0,1},{1,0},{2,3},{3,2},{4,5},{5,4},{6,7},{7,6},{8,9},{9,8},{10,11... | collective-permute-start | bytes 98312 | tf_op jit(solution)/shard_map/ppermute | solution.py:862
  29.8 16.0 %copy-start.2 = (f32[8,8]{1,0:T(8,128)S(1)}, f32[8,8]{1,0:T(8,128)}, u32[]{:S(2)}) copy-start(f32[8,8]{1,0:T(8,128)} %kc.3) | copy-start | bytes 772
  33.8 4.6 %collective-permute-start.12 = (f32[176,128]{1,0:T(8,128)S(1)}, f32[176,128]{1,0:T(8,128)S(1)}, u32[]{:S(2)}, u32[]{:S(2)}) collective-permute-start(f32[176,128]{1,0:T(8,128)S(1)} %get-tuple-element.96), channel_id=1, source_target_pairs={{0,32},{1,33},{2,34},{3,35},{4,36},{5,37},{6,38},{7,39},{8,40},{9,... | collective-permute-start | bytes 270344 | tf_op jit(solution)/shard_map/ppermute | solution.py:862
  33.8 18.5 %copy-start = (f32[216,216]{1,0:T(8,128)S(1)}, f32[216,216]{1,0:T(8,128)}, u32[]{:S(2)}) copy-start(f32[216,216]{1,0:T(8,128)} %noise.1) | copy-start | bytes 559876
  33.9 4.6 %collective-permute-start.13 = (f32[176,128]{1,0:T(8,128)S(1)}, f32[176,128]{1,0:T(8,128)S(1)}, u32[]{:S(2)}, u32[]{:S(2)}) collective-permute-start(f32[176,128]{1,0:T(8,128)S(1)} %get-tuple-element.97), channel_id=1, source_target_pairs={{0,1},{1,0},{2,3},{3,2},{4,5},{5,4},{6,7},{7,6},{8,9},{9,8},{10,11... | collective-permute-start | bytes 270344 | tf_op jit(solution)/shard_map/ppermute | solution.py:862
  39.1 1.4 %collective-permute-start.14 = (f32[224,128]{1,0:T(8,128)S(1)}, f32[224,128]{1,0:T(8,128)S(1)}, u32[]{:S(2)}, u32[]{:S(2)}) collective-permute-start(f32[224,128]{1,0:T(8,128)S(1)} %get-tuple-element.99), channel_id=1, source_target_pairs={{0,1},{1,0},{2,3},{3,2},{4,5},{5,4},{6,7},{7,6},{8,9},{9,8},{10,11... | collective-permute-start | bytes 344072 | tf_op jit(solution)/shard_map/ppermute | solution.py:862
  39.1 6.6 %collective-permute-start.15 = (f32[224,128]{1,0:T(8,128)S(1)}, f32[224,128]{1,0:T(8,128)S(1)}, u32[]{:S(2)}, u32[]{:S(2)}) collective-permute-start(f32[224,128]{1,0:T(8,128)S(1)} %get-tuple-element.100), channel_id=1, source_target_pairs={{0,32},{1,2},{2,1},{3,4},{4,3},{5,6},{6,5},{7,8},{8,7},{9,10},{10,... | collective-permute-start | bytes 344072 | tf_op jit(solution)/shard_map/ppermute | solution.py:862
  47.0 4.5 %collective-permute-start.16 = (f32[160,128]{1,0:T(8,128)S(1)}, f32[160,128]{1,0:T(8,128)S(1)}, u32[]{:S(2)}, u32[]{:S(2)}) collective-permute-start(f32[160,128]{1,0:T(8,128)S(1)} %get-tuple-element.103), channel_id=1, source_target_pairs={{0,32},{1,33},{2,34},{3,35},{4,36},{5,37},{6,38},{7,39},{8,40},{9,... | collective-permute-start | bytes 245768 | tf_op jit(solution)/shard_map/ppermute | solution.py:862
  47.1 4.5 %collective-permute-start.17 = (f32[160,128]{1,0:T(8,128)S(1)}, f32[160,128]{1,0:T(8,128)S(1)}, u32[]{:S(2)}, u32[]{:S(2)}) collective-permute-start(f32[160,128]{1,0:T(8,128)S(1)} %get-tuple-element.104), channel_id=1, source_target_pairs={{0,1},{1,0},{2,3},{3,2},{4,5},{5,4},{6,7},{7,6},{8,9},{9,8},{10,11... | collective-permute-start | bytes 245768 | tf_op jit(solution)/shard_map/ppermute | solution.py:862
  52.2 1.4 %collective-permute-start.18 = (f32[208,128]{1,0:T(8,128)S(1)}, f32[208,128]{1,0:T(8,128)S(1)}, u32[]{:S(2)}, u32[]{:S(2)}) collective-permute-start(f32[208,128]{1,0:T(8,128)S(1)} %get-tuple-element.105), channel_id=1, source_target_pairs={{0,1},{1,0},{2,3},{3,2},{4,5},{5,4},{6,7},{7,6},{8,9},{9,8},{10,11... | collective-permute-start | bytes 319496 | tf_op jit(solution)/shard_map/ppermute | solution.py:862
  52.3 6.3 %collective-permute-start.19 = (f32[208,128]{1,0:T(8,128)S(1)}, f32[208,128]{1,0:T(8,128)S(1)}, u32[]{:S(2)}, u32[]{:S(2)}) collective-permute-start(f32[208,128]{1,0:T(8,128)S(1)} %get-tuple-element.106), channel_id=1, source_target_pairs={{0,32},{1,2},{2,1},{3,4},{4,3},{5,6},{6,5},{7,8},{8,7},{9,10},{10,... | collective-permute-start | bytes 319496 | tf_op jit(solution)/shard_map/ppermute | solution.py:862
  60.8 4.3 %collective-permute-start.22 = (f32[32,512]{1,0:T(8,128)S(1)}, f32[32,512]{1,0:T(8,128)S(1)}, u32[]{:S(2)}, u32[]{:S(2)}) collective-permute-start(f32[32,512]{1,0:T(8,128)S(1)} %get-tuple-element.112), channel_id=1, source_target_pairs={{0,1},{1,0},{2,3},{3,2},{4,5},{5,4},{6,7},{7,6},{8,9},{9,8},{10,11... | collective-permute-start | bytes 196616 | tf_op jit(solution)/shard_map/ppermute | solution.py:862
  60.9 5.9 %collective-permute-start.23 = (f32[32,512]{1,0:T(8,128)S(1)}, f32[32,512]{1,0:T(8,128)S(1)}, u32[]{:S(2)}, u32[]{:S(2)}) collective-permute-start(f32[32,512]{1,0:T(8,128)S(1)} %get-tuple-element.113), channel_id=1, source_target_pairs={{0,32},{1,2},{2,1},{3,4},{4,3},{5,6},{6,5},{7,8},{8,7},{9,10},{10,... | collective-permute-start | bytes 196616 | tf_op jit(solution)/shard_map/ppermute | solution.py:862
  60.9 4.0 %collective-permute-start.20 = (f32[16,512]{1,0:T(8,128)S(1)}, f32[16,512]{1,0:T(8,128)S(1)}, u32[]{:S(2)}, u32[]{:S(2)}) collective-permute-start(f32[16,512]{1,0:T(8,128)S(1)} %get-tuple-element.110), channel_id=1, source_target_pairs={{0,32},{1,33},{2,34},{3,35},{4,36},{5,37},{6,38},{7,39},{8,40},{9,... | collective-permute-start | bytes 98312 | tf_op jit(solution)/shard_map/ppermute | solution.py:862
  61.0 4.0 %collective-permute-start.21 = (f32[16,512]{1,0:T(8,128)S(1)}, f32[16,512]{1,0:T(8,128)S(1)}, u32[]{:S(2)}, u32[]{:S(2)}) collective-permute-start(f32[16,512]{1,0:T(8,128)S(1)} %get-tuple-element.111), channel_id=1, source_target_pairs={{0,1},{1,0},{2,3},{3,2},{4,5},{5,4},{6,7},{7,6},{8,9},{9,8},{10,11... | collective-permute-start | bytes 98312 | tf_op jit(solution)/shard_map/ppermute | solution.py:862
  67.8 5.7 %collective-permute-start.26 = (f32[48,512]{1,0:T(8,128)S(1)}, f32[48,512]{1,0:T(8,128)S(1)}, u32[]{:S(2)}, u32[]{:S(2)}) collective-permute-start(f32[48,512]{1,0:T(8,128)S(1)} %get-tuple-element.118), channel_id=1, source_target_pairs={{0,1},{1,0},{2,3},{3,2},{4,5},{5,4},{6,7},{7,6},{8,9},{9,8},{10,11... | collective-permute-start | bytes 294920 | tf_op jit(solution)/shard_map/ppermute | solution.py:862
  67.9 6.2 %collective-permute-start.27 = (f32[48,512]{1,0:T(8,128)S(1)}, f32[48,512]{1,0:T(8,128)S(1)}, u32[]{:S(2)}, u32[]{:S(2)}) collective-permute-start(f32[48,512]{1,0:T(8,128)S(1)} %get-tuple-element.119), channel_id=1, source_target_pairs={{0,32},{1,2},{2,1},{3,4},{4,3},{5,6},{6,5},{7,8},{8,7},{9,10},{10,... | collective-permute-start | bytes 294920 | tf_op jit(solution)/shard_map/ppermute | solution.py:862
  68.8 4.4 %collective-permute-start.24 = (f32[36,512]{1,0:T(8,128)S(1)}, f32[36,512]{1,0:T(8,128)S(1)}, u32[]{:S(2)}, u32[]{:S(2)}) collective-permute-start(f32[36,512]{1,0:T(8,128)S(1)} %get-tuple-element.116), channel_id=1, source_target_pairs={{0,32},{1,33},{2,34},{3,35},{4,36},{5,37},{6,38},{7,39},{8,40},{9,... | collective-permute-start | bytes 221192 | tf_op jit(solution)/shard_map/ppermute | solution.py:862
  69.1 4.4 %collective-permute-start.25 = (f32[36,512]{1,0:T(8,128)S(1)}, f32[36,512]{1,0:T(8,128)S(1)}, u32[]{:S(2)}, u32[]{:S(2)}) collective-permute-start(f32[36,512]{1,0:T(8,128)S(1)} %get-tuple-element.117), channel_id=1, source_target_pairs={{0,1},{1,0},{2,3},{3,2},{4,5},{5,4},{6,7},{7,6},{8,9},{9,8},{10,11... | collective-permute-start | bytes 221192 | tf_op jit(solution)/shard_map/ppermute | solution.py:862
  75.7 6.0 %collective-permute-start.30 = (f32[48,512]{1,0:T(8,128)S(1)}, f32[48,512]{1,0:T(8,128)S(1)}, u32[]{:S(2)}, u32[]{:S(2)}) collective-permute-start(f32[48,512]{1,0:T(8,128)S(1)} %get-tuple-element.123), channel_id=1, source_target_pairs={{0,1},{1,0},{2,3},{3,2},{4,5},{5,4},{6,7},{7,6},{8,9},{9,8},{10,11... | collective-permute-start | bytes 294920 | tf_op jit(solution)/shard_map/ppermute | solution.py:862
  75.8 6.2 %collective-permute-start.31 = (f32[48,512]{1,0:T(8,128)S(1)}, f32[48,512]{1,0:T(8,128)S(1)}, u32[]{:S(2)}, u32[]{:S(2)}) collective-permute-start(f32[48,512]{1,0:T(8,128)S(1)} %get-tuple-element.124), channel_id=1, source_target_pairs={{0,32},{1,2},{2,1},{3,4},{4,3},{5,6},{6,5},{7,8},{8,7},{9,10},{10,... | collective-permute-start | bytes 294920 | tf_op jit(solution)/shard_map/ppermute | solution.py:862
  76.9 4.4 %collective-permute-start.28 = (f32[36,512]{1,0:T(8,128)S(1)}, f32[36,512]{1,0:T(8,128)S(1)}, u32[]{:S(2)}, u32[]{:S(2)}) collective-permute-start(f32[36,512]{1,0:T(8,128)S(1)} %get-tuple-element.121), channel_id=1, source_target_pairs={{0,32},{1,33},{2,34},{3,35},{4,36},{5,37},{6,38},{7,39},{8,40},{9,... | collective-permute-start | bytes 221192 | tf_op jit(solution)/shard_map/ppermute | solution.py:862
  77.3 4.4 %collective-permute-start.29 = (f32[36,512]{1,0:T(8,128)S(1)}, f32[36,512]{1,0:T(8,128)S(1)}, u32[]{:S(2)}, u32[]{:S(2)}) collective-permute-start(f32[36,512]{1,0:T(8,128)S(1)} %get-tuple-element.122), channel_id=1, source_target_pairs={{0,1},{1,0},{2,3},{3,2},{4,5},{5,4},{6,7},{7,6},{8,9},{9,8},{10,11... | collective-permute-start | bytes 221192 | tf_op jit(solution)/shard_map/ppermute | solution.py:862
  78.0 4.0 %copy-start.1 = (bf16[216,240]{1,0:T(8,128)(2,1)S(1)}, bf16[216,240]{1,0:T(8,128)(2,1)}, u32[]{:S(2)}) copy-start(bf16[216,240]{1,0:T(8,128)(2,1)} %constant.18.clone.from_slot) | copy-start | bytes 311044
  78.0 4.0 %copy-start.3 = (f32[4,4,128]{2,1,0:T(4,128)S(1)}, f32[4,4,128]{2,1,0:T(4,128)}, u32[]{:S(2)}) copy-start(f32[4,4,128]{2,1,0:T(4,128)} %param.23) | copy-start | bytes 24580

commit v7 on v6

--- a/solution.py
+++ b/solution.py
@@ -453,18 +453,23 @@
             out_rows[pl.ds(c, QF, stride=COLS), :] = natural[:, c * 128 : c * 128 + 128]
     first = pltpu.make_async_copy(out_rows, out, done.at[0])
     first.start()
-    for n in range(4):
-        noise = split_product(nf, u_ref[:, chunk(n)])
-        for y in range(4):
-            c = 4 * n + y
-            prev_rows[pl.ds(c, QF, stride=COLS), :] = (
-                natural[:, c * 128 : c * 128 + 128]
-                + inc[c : c + 1, :] * noise[:, y * 128 : y * 128 + 128]
-            )
-    second = pltpu.make_async_copy(prev_rows, prev, done.at[1])
-    second.start()
-    first.wait()
-    second.wait()
+    copies = [first]
+    for low, high in ((0, 112), (112, QF)):
+        for n in range(4):
+            noise = split_product(nf.at[low:high], u_ref[:, chunk(n)])
+            for y in range(4):
+                c = 4 * n + y
+                prev_rows[pl.ds(low * COLS + c, high - low, stride=COLS), :] = (
+                    natural[low:high, c * 128 : c * 128 + 128]
+                    + inc[c : c + 1, :] * noise[:, y * 128 : y * 128 + 128]
+                )
+        rows = slice(low * COLS, high * COLS)
+        copies.append(
+            pltpu.make_async_copy(prev_rows.at[rows], prev.at[rows], done.at[len(copies)])
+        )
+        copies[-1].start()
+    for copy in copies:
+        copy.wait()
 
 
 def mid_sends(m_ref, idx, s1, s2, s3, s4):
@@ -594,6 +599,7 @@
 
 def row_sends(idx, planes, s3, s4):
     y_even = even(idx, 1)
+    s4[s3.shape[0] :, :] = jnp.zeros((8, 128), F32)
     for n, (p, d) in enumerate(REACH):
         far, near = planes[p][4 - d], planes[p][d - 1]
         s3[QC * n : QC * n + QC, :] = jnp.where(y_even, far, near)
@@ -870,10 +876,11 @@
 
 def exchange_rows(kernel, rows, outs, idx, own, s1, s2, extra):
     r2, r1 = swap(s2, 1), swap(s1, 0)
-    s3, s4, *rest = call(kernel, [((rows, 128), F32)] * 2 + outs, (), (0,))(
+    faces = [((rows, 128), F32), ((rows + 8, 128), F32)]
+    s3, s4, *rest = call(kernel, faces + outs, (), (0,))(
         idx, own, r1, r2, extra
     )
-    r4, r3 = swap(s4, 3), swap(s3, 2)
+    r3, r4 = swap(s3, 2), swap(s4, 3)
     return r1, r2, r3, r4, rest
 
 
@@ -1005,7 +1012,7 @@
             pltpu.VMEM((QF, LANES), F32),
             pltpu.VMEM((QF * COLS, 128), F32),
             pltpu.VMEM((QF * COLS, 128), F32),
-            pltpu.SemaphoreType.DMA((2,)),
+            pltpu.SemaphoreType.DMA((3,)),
         ],
         (3,),
         hbm_outs=True,

time: 87.3 us -> 86.7 us (level)
  no operation moved by 1% of the time
where the time goes in v7:
time: 86.7 us; the launch traced here: 86.6 us
  waiting for transfers between devices  32.4 us (37%)
  Pallas kernels  29.2 us (34%)
  starting transfers between devices  23.8 us (27%)
  between operations  1.1 us (1%)
    ppermute x32, waiting for transfers between devices, swap(): return lax.ppermute(values, ('gx', 'yz'), partners(step))  32.4 us
    pallas_call x20, Pallas kernels, run(): pl.pallas_call(kernel, out_shape=tuple((jax.ShapeDtypeStruct(s, d) for s,...  29.2 us
    ppermute x32, starting transfers between devices, swap(): return lax.ppermute(values, ('gx', 'yz'), partners(step))  23.8 us
  transfers between devices with their start and end apart: 32, of which 19 were waited for; matrix products, arithmetic and copies ran while one was open for 0% of the time, Pallas kernels for 10%

profile of v7, /device:TPU:14, one launch (start us, length us, event | category | flops | bytes accessed | tf_op | source)
XLA Modules:
  0.0 86.6 jit_solution(6377587395545526443)
XLA Ops:
  0.7 3.9 %shard_map.140 = (f32[240,2048]{1,0:T(8,128)S(1)}, f32[240,2048]{1,0:T(8,128)S(1)}, f32[16,512]{1,0:T(8,128)S(1)}, f32[8,2048]{1,0:T(8,128)S(1)}, f32[48,512]{1,...) custom-call(f32[3456,128]{1,0:T(8,128)} %bitcast.11, ...), custom_call_target="tpu_custom_call" | custom-call | tf_op jit(solution)/shard_map/pallas_call | solution.py:50
  4.7 0.5 collective-permute-start
  5.2 2.4 %collective-permute-start.1 = (f32[48,512]{1,0:T(8,128)S(1)}, f32[48,512]{1,0:T(8,128)S(1)}, u32[]{:S(2)}, u32[]{:S(2)}) collective-permute-start(f32[48,512]{1,0:T(8,128)S(1)} %get-tuple-element.75), channel_id=1, source_target_pairs={{0,1},{1,0},{2,3},{3,2},{4,5},{5,4},{6,7},{7,6},{8,9},{9,8},{10,11... | collective-permute-start | bytes 294920 | tf_op jit(solution)/shard_map/ppermute | solution.py:868
  7.6 4.4 %collective-permute-start.3 = (f32[48,512]{1,0:T(8,128)S(1)}, f32[48,512]{1,0:T(8,128)S(1)}, u32[]{:S(2)}, u32[]{:S(2)}) collective-permute-start(f32[48,512]{1,0:T(8,128)S(1)} %get-tuple-element.77), channel_id=1, source_target_pairs={{0,32},{1,2},{2,1},{3,4},{4,3},{5,6},{6,5},{7,8},{8,7},{9,10},{10,... | collective-permute-start | bytes 294920 | tf_op jit(solution)/shard_map/ppermute | solution.py:868
  12.0 0.7 shard_map.141
  12.7 1.5 %shard_map.142.t_in = f32[240,2048]{1,0:T(8,128)S(1)} custom-call(f32[240,2048]{1,0:T(8,128)S(1)} %get-tuple-element.65.u_ref.u, f32[240,2048]{1,0:T(8,128)S(1)} %get-tuple-element.66.g_ref, f32[8,2048]{1,0:T(8,128)S(1)} %get-tuple-element.67.csr, bf16[240,768]{1,0:T(8,128)(2,1)S(1)} %get-tuple-element.73.kf), custom_call_target="tpu_custom_call" | custom-call | tf_op jit(solution)/shard_map/pallas_call | solution.py:50
  14.3 1.6 %shard_map.143 = (f32[240,2048]{1,0:T(8,128)S(1)}, f32[36,512]{1,0:T(8,128)S(1)}, f32[36,512]{1,0:T(8,128)S(1)}, f32[88,512]{1,0:T(8,128)S(1)}, f32[88,512]{1,0:T(8,128)S(1)}) custom-call(f32[240,2048]{1,0:T(8,128)S(1)} %get-tuple-element.65.u_ref.u, f32[240,2048]{1,0:T(8,128)S(1)} %shard_map.142.t_in, f32[8,2048]{1,0:T(8,128)S(1)} %get-tuple-element.67.csr, ...), custom_call_target="tpu_custom_call" | custom-call | tf_op jit(solution)/shard_map/pallas_call | solution.py:50
  15.9 0.1 collective-permute-start.6
  16.0 3.9 %collective-permute-start.7 = (f32[88,512]{1,0:T(8,128)S(1)}, f32[88,512]{1,0:T(8,128)S(1)}, u32[]{:S(2)}, u32[]{:S(2)}) collective-permute-start(f32[88,512]{1,0:T(8,128)S(1)} %get-tuple-element.84), channel_id=1, source_target_pairs={{0,32},{1,2},{2,1},{3,4},{4,3},{5,6},{6,5},{7,8},{8,7},{9,10},{10,... | collective-permute-start | bytes 540680 | tf_op jit(solution)/shard_map/ppermute | solution.py:868
  20.0 0.7 collective-permute-start.5
  20.7 1.5 %shard_map.144.t_in = f32[240,2048]{1,0:T(8,128)S(1)} custom-call(f32[240,2048]{1,0:T(8,128)S(1)} %get-tuple-element.80.u_ref.u, f32[240,2048]{1,0:T(8,128)S(1)} %get-tuple-element.66.g_ref, f32[8,2048]{1,0:T(8,128)S(1)} %get-tuple-element.67.csr, bf16[240,768]{1,0:T(8,128)(2,1)S(1)} %get-tuple-element.73.kf), custom_call_target="tpu_custom_call" | custom-call | tf_op jit(solution)/shard_map/pallas_call | solution.py:50
  22.2 2.2 %collective-permute-done.4.r1 = f32[36,512]{1,0:T(8,128)S(1)} collective-permute-done((f32[36,512]{1,0:T(8,128)S(1)}, f32[36,512]{1,0:T(8,128)S(1)}, u32[]{:S(2)}, u32[]{:S(2)}) %collective-permute-start.4) | collective-permute-done | bytes 73760 | tf_op jit(solution)/shard_map/ppermute | solution.py:868
  24.4 1.3 %shard_map.145 = (f32[64,2048]{1,0:T(8,128)S(1)}, f32[64,2048]{1,0:T(8,128)S(1)}, f32[16,512]{1,0:T(8,128)S(1)}, f32[16,512]{1,0:T(8,128)S(1)}, f32[32,512]{1,0:T(8,128)S(1)}, /*index=5*/f32[32,512]{1,0:T(8,128)S(1)}) custom-call(f32[240,2048]{1,0:T(8,128)S(1)} %shard_map.144.t_in, f32[8,2048]{1,0:T(8,128)S(1)} %get-tuple-element.67.csr, ...), custom_call_target="tpu_custom_call" | custom-call | tf_op jit(solution)/shard_map/pallas_call | solution.py:50
  25.7 0.1 collective-permute-start.10
  25.8 2.7 %collective-permute-start.11 = (f32[32,512]{1,0:T(8,128)S(1)}, f32[32,512]{1,0:T(8,128)S(1)}, u32[]{:S(2)}, u32[]{:S(2)}) collective-permute-start(f32[32,512]{1,0:T(8,128)S(1)} %get-tuple-element.92), channel_id=1, source_target_pairs={{0,32},{1,2},{2,1},{3,4},{4,3},{5,6},{6,5},{7,8},{8,7},{9,10},{10,... | collective-permute-start | bytes 196616 | tf_op jit(solution)/shard_map/ppermute | solution.py:868
  28.5 0.7 collective-permute-start.9
  29.2 0.5 shard_map.146.t_in
  29.8 2.6 %collective-permute-done.8.r1 = f32[16,512]{1,0:T(8,128)S(1)} collective-permute-done((f32[16,512]{1,0:T(8,128)S(1)}, f32[16,512]{1,0:T(8,128)S(1)}, u32[]{:S(2)}, u32[]{:S(2)}) %collective-permute-start.8) | collective-permute-done | bytes 32800 | tf_op jit(solution)/shard_map/ppermute | solution.py:868
  32.4 1.4 %shard_map.147 = (f32[64,2048]{1,0:T(8,128)S(1)}, f32[256,128]{1,0:T(8,128)S(1)}, f32[176,128]{1,0:T(8,128)S(1)}, f32[176,128]{1,0:T(8,128)S(1)}) custom-call(f32[64,2048]{1,0:T(8,128)S(1)} %get-tuple-element.86.m_ref.m, f32[64,2048]{1,0:T(8,128)S(1)} %shard_map.146.t_in, f32[8,2048]{1,0:T(8,128)S(1)} %get-tuple-element.67.csr, s32[4]{0:T(128)S(1)} %pad_add_fusion.idx, ...), custom_call_target="tpu_custom_call" | custom-call | tf_op jit(solution)/shard_map/pallas_call | solution.py:50
  33.9 0.8 collective-permute-start.13
  34.7 0.7 shard_map.148.coef
  35.4 3.0 %collective-permute-done.12.r1 = f32[176,128]{1,0:T(8,128)S(1)} collective-permute-done((f32[176,128]{1,0:T(8,128)S(1)}, f32[176,128]{1,0:T(8,128)S(1)}, u32[]{:S(2)}, u32[]{:S(2)}) %collective-permute-start.12) | collective-permute-done | bytes 90144 | tf_op jit(solution)/shard_map/ppermute | solution.py:868
  38.4 0.1 collective-permute-done.13.r2
  38.5 0.6 shard_map.149
  39.1 0.8 collective-permute-start.15
  39.9 1.3 %collective-permute-done.14.r3 = f32[224,128]{1,0:T(8,128)S(1)} collective-permute-done((f32[224,128]{1,0:T(8,128)S(1)}, f32[224,128]{1,0:T(8,128)S(1)}, u32[]{:S(2)}, u32[]{:S(2)}) %collective-permute-start.14) | collective-permute-done | bytes 114720 | tf_op jit(solution)/shard_map/ppermute | solution.py:868
  41.2 4.3 %collective-permute-done.15.r4 = f32[232,128]{1,0:T(8,128)S(1)} collective-permute-done((f32[232,128]{1,0:T(8,128)S(1)}, f32[232,128]{1,0:T(8,128)S(1)}, u32[]{:S(2)}, u32[]{:S(2)}) %collective-permute-start.15) | collective-permute-done | bytes 118816 | tf_op jit(solution)/shard_map/ppermute | solution.py:868
  45.5 1.2 %shard_map.150 = (f32[800,128]{1,0:T(8,128)S(1)}, f32[128,128]{1,0:T(8,128)S(1)}, f32[160,128]{1,0:T(8,128)S(1)}, f32[160,128]{1,0:T(8,128)S(1)}) custom-call(f32[480,128]{1,0:T(8,128)S(1)} %get-tuple-element.98.whole, f32[224,128]{1,0:T(8,128)S(1)} %collective-permute-done.14.r3, f32[232,128]{1,0:T(8,128)S(1)} %collective-permute-done.15.r4, ...), custom_call_target="tpu_custom_call" | custom-call | tf_op jit(solution)/shard_map/pallas_call | solution.py:50
  46.7 0.1 collective-permute-start.16
  46.8 0.8 collective-permute-start.17
  47.6 3.6 %collective-permute-done.16.r1 = f32[160,128]{1,0:T(8,128)S(1)} collective-permute-done((f32[160,128]{1,0:T(8,128)S(1)}, f32[160,128]{1,0:T(8,128)S(1)}, u32[]{:S(2)}, u32[]{:S(2)}) %collective-permute-start.16) | collective-permute-done | bytes 81952 | tf_op jit(solution)/shard_map/ppermute | solution.py:868
  51.2 0.1 collective-permute-done.17.r2
  51.3 0.6 shard_map.151
  51.9 0.1 collective-permute-start.19
  52.0 0.1 collective-permute-start.18
  52.1 0.7 shard_map.152
  52.8 0.6 collective-permute-done.18.r3
  53.4 4.9 %collective-permute-done.19.r4 = f32[216,128]{1,0:T(8,128)S(1)} collective-permute-done((f32[216,128]{1,0:T(8,128)S(1)}, f32[216,128]{1,0:T(8,128)S(1)}, u32[]{:S(2)}, u32[]{:S(2)}) %collective-permute-start.19) | collective-permute-done | bytes 110624 | tf_op jit(solution)/shard_map/ppermute | solution.py:868
  58.3 2.2 %shard_map.153 = (f32[64,2048]{1,0:T(8,128)S(1)}, f32[16,512]{1,0:T(8,128)S(1)}, f32[16,512]{1,0:T(8,128)S(1)}, f32[32,512]{1,0:T(8,128)S(1)}, f32[32,512]{1,0:T(8,128)S(1)}) custom-call(f32[128,128]{1,0:T(8,128)S(1)} %get-tuple-element.102.own, f32[160,128]{1,0:T(8,128)S(1)} %collective-permute-done.16.r1, f32[160,128]{1,0:T(8,128)S(1)} %collective-permute-done.17.r2, ...), custom_call_target="tpu_custom_call" | custom-call | tf_op jit(solution)/shard_map/pallas_call | solution.py:50
  60.4 0.1 collective-permute-start.22
  60.5 0.1 collective-permute-start.23
  60.6 0.1 collective-permute-start.20
  60.7 0.8 collective-permute-start.21
  61.5 0.5 shard_map.154.t_in
  62.1 2.5 %collective-permute-done.20.r1 = f32[16,512]{1,0:T(8,128)S(1)} collective-permute-done((f32[16,512]{1,0:T(8,128)S(1)}, f32[16,512]{1,0:T(8,128)S(1)}, u32[]{:S(2)}, u32[]{:S(2)}) %collective-permute-start.20) | collective-permute-done | bytes 32800 | tf_op jit(solution)/shard_map/ppermute | solution.py:868
  64.6 0.1 collective-permute-done.21.r2
  64.7 1.7 %collective-permute-done.23.r4 = f32[32,512]{1,0:T(8,128)S(1)} collective-permute-done((f32[32,512]{1,0:T(8,128)S(1)}, f32[32,512]{1,0:T(8,128)S(1)}, u32[]{:S(2)}, u32[]{:S(2)}) %collective-permute-start.23) | collective-permute-done | bytes 65568 | tf_op jit(solution)/shard_map/ppermute | solution.py:868
  66.4 1.0 %shard_map.155 = (f32[240,2048]{1,0:T(8,128)S(1)}, f32[36,512]{1,0:T(8,128)S(1)}, f32[36,512]{1,0:T(8,128)S(1)}, f32[48,512]{1,0:T(8,128)S(1)}, f32[48,512]{1,0:T(8,128)S(1)}) custom-call(f32[64,2048]{1,0:T(8,128)S(1)} %get-tuple-element.109.m_ref.m, f32[64,2048]{1,0:T(8,128)S(1)} %shard_map.154.t_in, f32[8,2048]{1,0:T(8,128)S(1)} %get-tuple-element.67.csr, ...), custom_call_target="tpu_custom_call" | custom-call | tf_op jit(solution)/shard_map/pallas_call | solution.py:50
  67.5 0.9 %collective-permute-start.27 = (f32[48,512]{1,0:T(8,128)S(1)}, f32[48,512]{1,0:T(8,128)S(1)}, u32[]{:S(2)}, u32[]{:S(2)}) collective-permute-start(f32[48,512]{1,0:T(8,128)S(1)} %get-tuple-element.119), channel_id=1, source_target_pairs={{0,32},{1,2},{2,1},{3,4},{4,3},{5,6},{6,5},{7,8},{8,7},{9,10},{10,... | collective-permute-start | bytes 294920 | tf_op jit(solution)/shard_map/ppermute | solution.py:868
  68.5 0.3 collective-permute-start.24
  68.7 0.7 collective-permute-start.25
  69.5 1.5 %shard_map.156.t_in = f32[240,2048]{1,0:T(8,128)S(1)} custom-call(f32[240,2048]{1,0:T(8,128)S(1)} %get-tuple-element.115.u_ref.u, f32[240,2048]{1,0:T(8,128)S(1)} %get-tuple-element.66.g_ref, f32[8,2048]{1,0:T(8,128)S(1)} %get-tuple-element.67.csr, bf16[240,768]{1,0:T(8,128)(2,1)S(1)} %get-tuple-element.73.kf), custom_call_target="tpu_custom_call" | custom-call | tf_op jit(solution)/shard_map/pallas_call | solution.py:50
  71.0 1.9 %collective-permute-done.24.r1 = f32[36,512]{1,0:T(8,128)S(1)} collective-permute-done((f32[36,512]{1,0:T(8,128)S(1)}, f32[36,512]{1,0:T(8,128)S(1)}, u32[]{:S(2)}, u32[]{:S(2)}) %collective-permute-start.24) | collective-permute-done | bytes 73760 | tf_op jit(solution)/shard_map/ppermute | solution.py:868
  72.9 0.3 collective-permute-done.25.r2
  73.2 0.6 collective-permute-done.27.r4
  73.8 1.6 %shard_map.157 = (f32[240,2048]{1,0:T(8,128)S(1)}, f32[36,512]{1,0:T(8,128)S(1)}, f32[36,512]{1,0:T(8,128)S(1)}, f32[48,512]{1,0:T(8,128)S(1)}, f32[48,512]{1,0:T(8,128)S(1)}) custom-call(f32[240,2048]{1,0:T(8,128)S(1)} %get-tuple-element.115.u_ref.u, f32[240,2048]{1,0:T(8,128)S(1)} %shard_map.156.t_in, f32[8,2048]{1,0:T(8,128)S(1)} %get-tuple-element.67.csr, ...), custom_call_target="tpu_custom_call" | custom-call | tf_op jit(solution)/shard_map/pallas_call | solution.py:50
  75.5 1.1 %collective-permute-start.31 = (f32[48,512]{1,0:T(8,128)S(1)}, f32[48,512]{1,0:T(8,128)S(1)}, u32[]{:S(2)}, u32[]{:S(2)}) collective-permute-start(f32[48,512]{1,0:T(8,128)S(1)} %get-tuple-element.124), channel_id=1, source_target_pairs={{0,32},{1,2},{2,1},{3,4},{4,3},{5,6},{6,5},{7,8},{8,7},{9,10},{10,... | collective-permute-start | bytes 294920 | tf_op jit(solution)/shard_map/ppermute | solution.py:868
  76.6 0.4 collective-permute-start.28
  77.0 0.7 collective-permute-start.29
  77.7 1.5 %shard_map.158.t_in = f32[240,2048]{1,0:T(8,128)S(1)} custom-call(f32[240,2048]{1,0:T(8,128)S(1)} %get-tuple-element.120.u_ref.u, f32[240,2048]{1,0:T(8,128)S(1)} %get-tuple-element.66.g_ref, f32[8,2048]{1,0:T(8,128)S(1)} %get-tuple-element.67.csr, bf16[240,768]{1,0:T(8,128)(2,1)S(1)} %get-tuple-element.73.kf), custom_call_target="tpu_custom_call" | custom-call | tf_op jit(solution)/shard_map/pallas_call | solution.py:50
  79.2 1.8 %collective-permute-done.28.r1 = f32[36,512]{1,0:T(8,128)S(1)} collective-permute-done((f32[36,512]{1,0:T(8,128)S(1)}, f32[36,512]{1,0:T(8,128)S(1)}, u32[]{:S(2)}, u32[]{:S(2)}) %collective-permute-start.28) | collective-permute-done | bytes 73760 | tf_op jit(solution)/shard_map/ppermute | solution.py:868
  81.0 0.4 collective-permute-done.29.r2
  81.4 0.3 collective-permute-done.31.r4
  81.7 4.7 %shard_map.159 = (f32[3456,128]{1,0:T(8,128)}, f32[3456,128]{1,0:T(8,128)}) custom-call(f32[240,2048]{1,0:T(8,128)S(1)} %get-tuple-element.120.u_ref.u, f32[240,2048]{1,0:T(8,128)S(1)} %shard_map.158.t_in, f32[8,2048]{1,0:T(8,128)S(1)} %get-tuple-element.67.csr, s32[4]{0:T(128)S(1)} %pad_add_fusion.idx, f32[36,512]{1,0:T(8,128)S(1)} %collective-permute-done.28.r1, ...), custom_call_target="tpu_custom_call" | custom-call | tf_op jit(solution)/shard_map/pallas_call | solution.py:50
  (29 shorter events, 0.4 us)
Async XLA Ops:
  4.7 9.6 %collective-permute-start = (f32[48,512]{1,0:T(8,128)S(1)}, f32[48,512]{1,0:T(8,128)S(1)}, u32[]{:S(2)}, u32[]{:S(2)}) collective-permute-start(f32[48,512]{1,0:T(8,128)S(1)} %get-tuple-element.74), channel_id=1, source_target_pairs={{0,32},{1,33},{2,34},{3,35},{4,36},{5,37},{6,38},{7,39},{8,40},{9,... | collective-permute-start | bytes 294920 | tf_op jit(solution)/shard_map/ppermute | solution.py:868
  5.2 9.1 %collective-permute-start.1 = (f32[48,512]{1,0:T(8,128)S(1)}, f32[48,512]{1,0:T(8,128)S(1)}, u32[]{:S(2)}, u32[]{:S(2)}) collective-permute-start(f32[48,512]{1,0:T(8,128)S(1)} %get-tuple-element.75), channel_id=1, source_target_pairs={{0,1},{1,0},{2,3},{3,2},{4,5},{5,4},{6,7},{7,6},{8,9},{9,8},{10,11... | collective-permute-start | bytes 294920 | tf_op jit(solution)/shard_map/ppermute | solution.py:868
  7.6 6.7 %collective-permute-start.2 = (f32[48,512]{1,0:T(8,128)S(1)}, f32[48,512]{1,0:T(8,128)S(1)}, u32[]{:S(2)}, u32[]{:S(2)}) collective-permute-start(f32[48,512]{1,0:T(8,128)S(1)} %get-tuple-element.76), channel_id=1, source_target_pairs={{0,1},{1,0},{2,3},{3,2},{4,5},{5,4},{6,7},{7,6},{8,9},{9,8},{10,11... | collective-permute-start | bytes 294920 | tf_op jit(solution)/shard_map/ppermute | solution.py:868
  7.6 6.7 %collective-permute-start.3 = (f32[48,512]{1,0:T(8,128)S(1)}, f32[48,512]{1,0:T(8,128)S(1)}, u32[]{:S(2)}, u32[]{:S(2)}) collective-permute-start(f32[48,512]{1,0:T(8,128)S(1)} %get-tuple-element.77), channel_id=1, source_target_pairs={{0,32},{1,2},{2,1},{3,4},{4,3},{5,6},{6,5},{7,8},{8,7},{9,10},{10,... | collective-permute-start | bytes 294920 | tf_op jit(solution)/shard_map/ppermute | solution.py:868
  15.9 8.5 %collective-permute-start.6 = (f32[88,512]{1,0:T(8,128)S(1)}, f32[88,512]{1,0:T(8,128)S(1)}, u32[]{:S(2)}, u32[]{:S(2)}) collective-permute-start(f32[88,512]{1,0:T(8,128)S(1)} %get-tuple-element.83), channel_id=1, source_target_pairs={{0,1},{1,0},{2,3},{3,2},{4,5},{5,4},{6,7},{7,6},{8,9},{9,8},{10,11... | collective-permute-start | bytes 540680 | tf_op jit(solution)/shard_map/ppermute | solution.py:868
  16.0 8.4 %collective-permute-start.7 = (f32[88,512]{1,0:T(8,128)S(1)}, f32[88,512]{1,0:T(8,128)S(1)}, u32[]{:S(2)}, u32[]{:S(2)}) collective-permute-start(f32[88,512]{1,0:T(8,128)S(1)} %get-tuple-element.84), channel_id=1, source_target_pairs={{0,32},{1,2},{2,1},{3,4},{4,3},{5,6},{6,5},{7,8},{8,7},{9,10},{10,... | collective-permute-start | bytes 540680 | tf_op jit(solution)/shard_map/ppermute | solution.py:868
  20.0 4.4 %collective-permute-start.4 = (f32[36,512]{1,0:T(8,128)S(1)}, f32[36,512]{1,0:T(8,128)S(1)}, u32[]{:S(2)}, u32[]{:S(2)}) collective-permute-start(f32[36,512]{1,0:T(8,128)S(1)} %get-tuple-element.81), channel_id=1, source_target_pairs={{0,32},{1,33},{2,34},{3,35},{4,36},{5,37},{6,38},{7,39},{8,40},{9,... | collective-permute-start | bytes 221192 | tf_op jit(solution)/shard_map/ppermute | solution.py:868
  20.0 4.4 %collective-permute-start.5 = (f32[36,512]{1,0:T(8,128)S(1)}, f32[36,512]{1,0:T(8,128)S(1)}, u32[]{:S(2)}, u32[]{:S(2)}) collective-permute-start(f32[36,512]{1,0:T(8,128)S(1)} %get-tuple-element.82), channel_id=1, source_target_pairs={{0,1},{1,0},{2,3},{3,2},{4,5},{5,4},{6,7},{7,6},{8,9},{9,8},{10,11... | collective-permute-start | bytes 221192 | tf_op jit(solution)/shard_map/ppermute | solution.py:868
  25.7 6.7 %collective-permute-start.10 = (f32[32,512]{1,0:T(8,128)S(1)}, f32[32,512]{1,0:T(8,128)S(1)}, u32[]{:S(2)}, u32[]{:S(2)}) collective-permute-start(f32[32,512]{1,0:T(8,128)S(1)} %get-tuple-element.91), channel_id=1, source_target_pairs={{0,1},{1,0},{2,3},{3,2},{4,5},{5,4},{6,7},{7,6},{8,9},{9,8},{10,11... | collective-permute-start | bytes 196616 | tf_op jit(solution)/shard_map/ppermute | solution.py:868
  25.8 6.6 %collective-permute-start.11 = (f32[32,512]{1,0:T(8,128)S(1)}, f32[32,512]{1,0:T(8,128)S(1)}, u32[]{:S(2)}, u32[]{:S(2)}) collective-permute-start(f32[32,512]{1,0:T(8,128)S(1)} %get-tuple-element.92), channel_id=1, source_target_pairs={{0,32},{1,2},{2,1},{3,4},{4,3},{5,6},{6,5},{7,8},{8,7},{9,10},{10,... | collective-permute-start | bytes 196616 | tf_op jit(solution)/shard_map/ppermute | solution.py:868
  28.5 3.9 %collective-permute-start.8 = (f32[16,512]{1,0:T(8,128)S(1)}, f32[16,512]{1,0:T(8,128)S(1)}, u32[]{:S(2)}, u32[]{:S(2)}) collective-permute-start(f32[16,512]{1,0:T(8,128)S(1)} %get-tuple-element.89), channel_id=1, source_target_pairs={{0,32},{1,33},{2,34},{3,35},{4,36},{5,37},{6,38},{7,39},{8,40},{9,... | collective-permute-start | bytes 98312 | tf_op jit(solution)/shard_map/ppermute | solution.py:868
  28.5 3.9 %collective-permute-start.9 = (f32[16,512]{1,0:T(8,128)S(1)}, f32[16,512]{1,0:T(8,128)S(1)}, u32[]{:S(2)}, u32[]{:S(2)}) collective-permute-start(f32[16,512]{1,0:T(8,128)S(1)} %get-tuple-element.90), channel_id=1, source_target_pairs={{0,1},{1,0},{2,3},{3,2},{4,5},{5,4},{6,7},{7,6},{8,9},{9,8},{10,11... | collective-permute-start | bytes 98312 | tf_op jit(solution)/shard_map/ppermute | solution.py:868
  29.8 15.8 %copy-start.2 = (f32[8,8]{1,0:T(8,128)S(1)}, f32[8,8]{1,0:T(8,128)}, u32[]{:S(2)}) copy-start(f32[8,8]{1,0:T(8,128)} %kc.3) | copy-start | bytes 772
  33.8 4.6 %collective-permute-start.12 = (f32[176,128]{1,0:T(8,128)S(1)}, f32[176,128]{1,0:T(8,128)S(1)}, u32[]{:S(2)}, u32[]{:S(2)}) collective-permute-start(f32[176,128]{1,0:T(8,128)S(1)} %get-tuple-element.96), channel_id=1, source_target_pairs={{0,32},{1,33},{2,34},{3,35},{4,36},{5,37},{6,38},{7,39},{8,40},{9,... | collective-permute-start | bytes 270344 | tf_op jit(solution)/shard_map/ppermute | solution.py:868
  33.8 18.3 %copy-start = (f32[216,216]{1,0:T(8,128)S(1)}, f32[216,216]{1,0:T(8,128)}, u32[]{:S(2)}) copy-start(f32[216,216]{1,0:T(8,128)} %noise.1) | copy-start | bytes 559876
  33.9 4.6 %collective-permute-start.13 = (f32[176,128]{1,0:T(8,128)S(1)}, f32[176,128]{1,0:T(8,128)S(1)}, u32[]{:S(2)}, u32[]{:S(2)}) collective-permute-start(f32[176,128]{1,0:T(8,128)S(1)} %get-tuple-element.97), channel_id=1, source_target_pairs={{0,1},{1,0},{2,3},{3,2},{4,5},{5,4},{6,7},{7,6},{8,9},{9,8},{10,11... | collective-permute-start | bytes 270344 | tf_op jit(solution)/shard_map/ppermute | solution.py:868
  39.1 6.5 %collective-permute-start.15 = (f32[232,128]{1,0:T(8,128)S(1)}, f32[232,128]{1,0:T(8,128)S(1)}, u32[]{:S(2)}, u32[]{:S(2)}) collective-permute-start(f32[232,128]{1,0:T(8,128)S(1)} %get-tuple-element.100), channel_id=1, source_target_pairs={{0,32},{1,2},{2,1},{3,4},{4,3},{5,6},{6,5},{7,8},{8,7},{9,10},{10,... | collective-permute-start | bytes 356360 | tf_op jit(solution)/shard_map/ppermute | solution.py:868
  39.9 1.3 %collective-permute-start.14 = (f32[224,128]{1,0:T(8,128)S(1)}, f32[224,128]{1,0:T(8,128)S(1)}, u32[]{:S(2)}, u32[]{:S(2)}) collective-permute-start(f32[224,128]{1,0:T(8,128)S(1)} %get-tuple-element.99), channel_id=1, source_target_pairs={{0,1},{1,0},{2,3},{3,2},{4,5},{5,4},{6,7},{7,6},{8,9},{9,8},{10,11... | collective-permute-start | bytes 344072 | tf_op jit(solution)/shard_map/ppermute | solution.py:868
  46.7 4.5 %collective-permute-start.16 = (f32[160,128]{1,0:T(8,128)S(1)}, f32[160,128]{1,0:T(8,128)S(1)}, u32[]{:S(2)}, u32[]{:S(2)}) collective-permute-start(f32[160,128]{1,0:T(8,128)S(1)} %get-tuple-element.103), channel_id=1, source_target_pairs={{0,32},{1,33},{2,34},{3,35},{4,36},{5,37},{6,38},{7,39},{8,40},{9,... | collective-permute-start | bytes 245768 | tf_op jit(solution)/shard_map/ppermute | solution.py:868
  46.8 4.5 %collective-permute-start.17 = (f32[160,128]{1,0:T(8,128)S(1)}, f32[160,128]{1,0:T(8,128)S(1)}, u32[]{:S(2)}, u32[]{:S(2)}) collective-permute-start(f32[160,128]{1,0:T(8,128)S(1)} %get-tuple-element.104), channel_id=1, source_target_pairs={{0,1},{1,0},{2,3},{3,2},{4,5},{5,4},{6,7},{7,6},{8,9},{9,8},{10,11... | collective-permute-start | bytes 245768 | tf_op jit(solution)/shard_map/ppermute | solution.py:868
  51.9 6.4 %collective-permute-start.19 = (f32[216,128]{1,0:T(8,128)S(1)}, f32[216,128]{1,0:T(8,128)S(1)}, u32[]{:S(2)}, u32[]{:S(2)}) collective-permute-start(f32[216,128]{1,0:T(8,128)S(1)} %get-tuple-element.106), channel_id=1, source_target_pairs={{0,32},{1,2},{2,1},{3,4},{4,3},{5,6},{6,5},{7,8},{8,7},{9,10},{10,... | collective-permute-start | bytes 331784 | tf_op jit(solution)/shard_map/ppermute | solution.py:868
  52.0 1.4 %collective-permute-start.18 = (f32[208,128]{1,0:T(8,128)S(1)}, f32[208,128]{1,0:T(8,128)S(1)}, u32[]{:S(2)}, u32[]{:S(2)}) collective-permute-start(f32[208,128]{1,0:T(8,128)S(1)} %get-tuple-element.105), channel_id=1, source_target_pairs={{0,1},{1,0},{2,3},{3,2},{4,5},{5,4},{6,7},{7,6},{8,9},{9,8},{10,11... | collective-permute-start | bytes 319496 | tf_op jit(solution)/shard_map/ppermute | solution.py:868
  60.4 4.3 %collective-permute-start.22 = (f32[32,512]{1,0:T(8,128)S(1)}, f32[32,512]{1,0:T(8,128)S(1)}, u32[]{:S(2)}, u32[]{:S(2)}) collective-permute-start(f32[32,512]{1,0:T(8,128)S(1)} %get-tuple-element.112), channel_id=1, source_target_pairs={{0,1},{1,0},{2,3},{3,2},{4,5},{5,4},{6,7},{7,6},{8,9},{9,8},{10,11... | collective-permute-start | bytes 196616 | tf_op jit(solution)/shard_map/ppermute | solution.py:868
  60.5 5.9 %collective-permute-start.23 = (f32[32,512]{1,0:T(8,128)S(1)}, f32[32,512]{1,0:T(8,128)S(1)}, u32[]{:S(2)}, u32[]{:S(2)}) collective-permute-start(f32[32,512]{1,0:T(8,128)S(1)} %get-tuple-element.113), channel_id=1, source_target_pairs={{0,32},{1,2},{2,1},{3,4},{4,3},{5,6},{6,5},{7,8},{8,7},{9,10},{10,... | collective-permute-start | bytes 196616 | tf_op jit(solution)/shard_map/ppermute | solution.py:868
  60.6 4.0 %collective-permute-start.20 = (f32[16,512]{1,0:T(8,128)S(1)}, f32[16,512]{1,0:T(8,128)S(1)}, u32[]{:S(2)}, u32[]{:S(2)}) collective-permute-start(f32[16,512]{1,0:T(8,128)S(1)} %get-tuple-element.110), channel_id=1, source_target_pairs={{0,32},{1,33},{2,34},{3,35},{4,36},{5,37},{6,38},{7,39},{8,40},{9,... | collective-permute-start | bytes 98312 | tf_op jit(solution)/shard_map/ppermute | solution.py:868
  60.7 4.0 %collective-permute-start.21 = (f32[16,512]{1,0:T(8,128)S(1)}, f32[16,512]{1,0:T(8,128)S(1)}, u32[]{:S(2)}, u32[]{:S(2)}) collective-permute-start(f32[16,512]{1,0:T(8,128)S(1)} %get-tuple-element.111), channel_id=1, source_target_pairs={{0,1},{1,0},{2,3},{3,2},{4,5},{5,4},{6,7},{7,6},{8,9},{9,8},{10,11... | collective-permute-start | bytes 98312 | tf_op jit(solution)/shard_map/ppermute | solution.py:868
  67.4 5.7 %collective-permute-start.26 = (f32[48,512]{1,0:T(8,128)S(1)}, f32[48,512]{1,0:T(8,128)S(1)}, u32[]{:S(2)}, u32[]{:S(2)}) collective-permute-start(f32[48,512]{1,0:T(8,128)S(1)} %get-tuple-element.118), channel_id=1, source_target_pairs={{0,1},{1,0},{2,3},{3,2},{4,5},{5,4},{6,7},{7,6},{8,9},{9,8},{10,11... | collective-permute-start | bytes 294920 | tf_op jit(solution)/shard_map/ppermute | solution.py:868
  67.5 6.2 %collective-permute-start.27 = (f32[48,512]{1,0:T(8,128)S(1)}, f32[48,512]{1,0:T(8,128)S(1)}, u32[]{:S(2)}, u32[]{:S(2)}) collective-permute-start(f32[48,512]{1,0:T(8,128)S(1)} %get-tuple-element.119), channel_id=1, source_target_pairs={{0,32},{1,2},{2,1},{3,4},{4,3},{5,6},{6,5},{7,8},{8,7},{9,10},{10,... | collective-permute-start | bytes 294920 | tf_op jit(solution)/shard_map/ppermute | solution.py:868
  68.5 4.4 %collective-permute-start.24 = (f32[36,512]{1,0:T(8,128)S(1)}, f32[36,512]{1,0:T(8,128)S(1)}, u32[]{:S(2)}, u32[]{:S(2)}) collective-permute-start(f32[36,512]{1,0:T(8,128)S(1)} %get-tuple-element.116), channel_id=1, source_target_pairs={{0,32},{1,33},{2,34},{3,35},{4,36},{5,37},{6,38},{7,39},{8,40},{9,... | collective-permute-start | bytes 221192 | tf_op jit(solution)/shard_map/ppermute | solution.py:868
  68.7 4.4 %collective-permute-start.25 = (f32[36,512]{1,0:T(8,128)S(1)}, f32[36,512]{1,0:T(8,128)S(1)}, u32[]{:S(2)}, u32[]{:S(2)}) collective-permute-start(f32[36,512]{1,0:T(8,128)S(1)} %get-tuple-element.117), channel_id=1, source_target_pairs={{0,1},{1,0},{2,3},{3,2},{4,5},{5,4},{6,7},{7,6},{8,9},{9,8},{10,11... | collective-permute-start | bytes 221192 | tf_op jit(solution)/shard_map/ppermute | solution.py:868
  75.4 6.0 %collective-permute-start.30 = (f32[48,512]{1,0:T(8,128)S(1)}, f32[48,512]{1,0:T(8,128)S(1)}, u32[]{:S(2)}, u32[]{:S(2)}) collective-permute-start(f32[48,512]{1,0:T(8,128)S(1)} %get-tuple-element.123), channel_id=1, source_target_pairs={{0,1},{1,0},{2,3},{3,2},{4,5},{5,4},{6,7},{7,6},{8,9},{9,8},{10,11... | collective-permute-start | bytes 294920 | tf_op jit(solution)/shard_map/ppermute | solution.py:868
  75.5 6.2 %collective-permute-start.31 = (f32[48,512]{1,0:T(8,128)S(1)}, f32[48,512]{1,0:T(8,128)S(1)}, u32[]{:S(2)}, u32[]{:S(2)}) collective-permute-start(f32[48,512]{1,0:T(8,128)S(1)} %get-tuple-element.124), channel_id=1, source_target_pairs={{0,32},{1,2},{2,1},{3,4},{4,3},{5,6},{6,5},{7,8},{8,7},{9,10},{10,... | collective-permute-start | bytes 294920 | tf_op jit(solution)/shard_map/ppermute | solution.py:868
  76.6 4.4 %collective-permute-start.28 = (f32[36,512]{1,0:T(8,128)S(1)}, f32[36,512]{1,0:T(8,128)S(1)}, u32[]{:S(2)}, u32[]{:S(2)}) collective-permute-start(f32[36,512]{1,0:T(8,128)S(1)} %get-tuple-element.121), channel_id=1, source_target_pairs={{0,32},{1,33},{2,34},{3,35},{4,36},{5,37},{6,38},{7,39},{8,40},{9,... | collective-permute-start | bytes 221192 | tf_op jit(solution)/shard_map/ppermute | solution.py:868
  77.0 4.4 %collective-permute-start.29 = (f32[36,512]{1,0:T(8,128)S(1)}, f32[36,512]{1,0:T(8,128)S(1)}, u32[]{:S(2)}, u32[]{:S(2)}) collective-permute-start(f32[36,512]{1,0:T(8,128)S(1)} %get-tuple-element.122), channel_id=1, source_target_pairs={{0,1},{1,0},{2,3},{3,2},{4,5},{5,4},{6,7},{7,6},{8,9},{9,8},{10,11... | collective-permute-start | bytes 221192 | tf_op jit(solution)/shard_map/ppermute | solution.py:868
  77.7 4.0 %copy-start.1 = (bf16[216,240]{1,0:T(8,128)(2,1)S(1)}, bf16[216,240]{1,0:T(8,128)(2,1)}, u32[]{:S(2)}) copy-start(bf16[216,240]{1,0:T(8,128)(2,1)} %constant.18.clone.from_slot) | copy-start | bytes 311044
  77.7 4.0 %copy-start.3 = (f32[4,4,128]{2,1,0:T(4,128)S(1)}, f32[4,4,128]{2,1,0:T(4,128)}, u32[]{:S(2)}) copy-start(f32[4,4,128]{2,1,0:T(4,128)} %param.23) | copy-start | bytes 24580

commit v8 on v7

--- a/solution.py
+++ b/solution.py
@@ -241,6 +241,8 @@
     for rows, up, low in zip(FACE_ROWS, upper, lower):
         s1[rows, :] = jnp.where(x_even, up, low)
         s2[rows, :] = jnp.where(x_even, low, up)
+    if s4.shape[0] == 56:
+        s4[48:56, :] = jnp.zeros((8, 512), F32)
     for i in range(6):
         upper = y_column(u_ref[40 * i + 8 : 40 * i + 16, :], 3)
         lower = y_column(u_ref[40 * i : 40 * i + 8, :], 0)
@@ -477,6 +479,7 @@
     upper, lower = m_ref[48:64, 1536:2048], m_ref[0:16, 0:512]
     s1[...] = jnp.where(x_even, upper, lower)
     s2[...] = jnp.where(x_even, lower, upper)
+    s4[32:40, :] = jnp.zeros((8, 512), F32)
     for i in range(4):
         upper = y_column(m_ref[16 * i + 8 : 16 * i + 16, :], 3)
         lower = y_column(m_ref[16 * i : 16 * i + 8, :], 0)
@@ -489,8 +492,8 @@
     return (
         jnp.where(x_even, r2[...], r1[...]),
         jnp.where(x_even, r1[...], r2[...]),
-        jnp.where(y_even, r4[...], r3[...]),
-        jnp.where(y_even, r3[...], r4[...]),
+        jnp.where(y_even, r4[0:32, :], r3[0:32, :]),
+        jnp.where(y_even, r3[0:32, :], r4[0:32, :]),
     )
 
 
@@ -897,9 +900,9 @@
     to_slot, from_slot = jnp.asarray(slots, BF16), jnp.asarray(slots.T, BF16)
 
     fine_field = ((SF, LANES), F32)
-    fine_faces = [((36, 512), F32)] * 2 + [((48, 512), F32)] * 2
+    fine_faces = [((36, 512), F32)] * 2 + [((48, 512), F32), ((56, 512), F32)]
     mid_field = ((QM, LANES), F32)
-    mid_faces = [((16, 512), F32)] * 2 + [((32, 512), F32)] * 2
+    mid_faces = [((16, 512), F32)] * 2 + [((32, 512), F32), ((40, 512), F32)]
     xf = pltpu.VMEM((512, LANES), BF16)
     xm, tm = pltpu.VMEM((256, LANES), BF16), pltpu.VMEM((QM, LANES), F32)
     window = ((QC * WX * WX, 128), F32)

time: 86.7 us -> 87 us (level)
  starting transfers between devices: 23.8 us -> 25.8 us
  waiting for transfers between devices: 32.4 us -> 30.7 us
    ppermute x32, starting transfers between devices: 23.8 us -> 25.8 us  [swap(): return lax.ppermute(values, ('gx', 'yz'), partners(step))]
    ppermute x32, waiting for transfers between devices: 32.4 us -> 30.7 us  [swap(): return lax.ppermute(values, ('gx', 'yz'), partners(step))]
where the time goes in v8:
time: 87 us; the launch traced here: 86.8 us
  waiting for transfers between devices  30.7 us (35%)
  Pallas kernels  29.2 us (34%)
  starting transfers between devices  25.8 us (30%)
  between operations  1.02 us (1%)
    ppermute x32, waiting for transfers between devices, swap(): return lax.ppermute(values, ('gx', 'yz'), partners(step))  30.7 us
    pallas_call x20, Pallas kernels, run(): pl.pallas_call(kernel, out_shape=tuple((jax.ShapeDtypeStruct(s, d) for s,...  29.2 us
    ppermute x32, starting transfers between devices, swap(): return lax.ppermute(values, ('gx', 'yz'), partners(step))  25.8 us
  transfers between devices with their start and end apart: 32, of which 19 were waited for; matrix products, arithmetic and copies ran while one was open for 0% of the time, Pallas kernels for 10%

profile of v8, /device:TPU:14, one launch (start us, length us, event | category | flops | bytes accessed | tf_op | source)
XLA Modules:
  0.0 86.8 jit_solution(409942900900745467)
XLA Ops:
  0.6 0.1 pad_add_fusion.idx
  0.7 3.9 %shard_map.140 = (f32[240,2048]{1,0:T(8,128)S(1)}, f32[240,2048]{1,0:T(8,128)S(1)}, f32[16,512]{1,0:T(8,128)S(1)}, f32[8,2048]{1,0:T(8,128)S(1)}, f32[48,512]{1,...) custom-call(f32[3456,128]{1,0:T(8,128)} %bitcast.11, ...), custom_call_target="tpu_custom_call" | custom-call | tf_op jit(solution)/shard_map/pallas_call | solution.py:50
  4.7 0.5 collective-permute-start
  5.2 2.4 %collective-permute-start.1 = (f32[48,512]{1,0:T(8,128)S(1)}, f32[48,512]{1,0:T(8,128)S(1)}, u32[]{:S(2)}, u32[]{:S(2)}) collective-permute-start(f32[48,512]{1,0:T(8,128)S(1)} %get-tuple-element.75), channel_id=1, source_target_pairs={{0,1},{1,0},{2,3},{3,2},{4,5},{5,4},{6,7},{7,6},{8,9},{9,8},{10,11... | collective-permute-start | bytes 294920 | tf_op jit(solution)/shard_map/ppermute | solution.py:871
  7.6 4.4 %collective-permute-start.3 = (f32[48,512]{1,0:T(8,128)S(1)}, f32[48,512]{1,0:T(8,128)S(1)}, u32[]{:S(2)}, u32[]{:S(2)}) collective-permute-start(f32[48,512]{1,0:T(8,128)S(1)} %get-tuple-element.77), channel_id=1, source_target_pairs={{0,32},{1,2},{2,1},{3,4},{4,3},{5,6},{6,5},{7,8},{8,7},{9,10},{10,... | collective-permute-start | bytes 294920 | tf_op jit(solution)/shard_map/ppermute | solution.py:871
  12.0 0.7 shard_map.141
  12.7 1.5 %shard_map.142.t_in = f32[240,2048]{1,0:T(8,128)S(1)} custom-call(f32[240,2048]{1,0:T(8,128)S(1)} %get-tuple-element.65.u_ref.u, f32[240,2048]{1,0:T(8,128)S(1)} %get-tuple-element.66.g_ref, f32[8,2048]{1,0:T(8,128)S(1)} %get-tuple-element.67.csr, bf16[240,768]{1,0:T(8,128)(2,1)S(1)} %get-tuple-element.73.kf), custom_call_target="tpu_custom_call" | custom-call | tf_op jit(solution)/shard_map/pallas_call | solution.py:50
  14.3 0.0 collective-permute-done.3.r4
  14.3 1.6 %shard_map.143 = (f32[240,2048]{1,0:T(8,128)S(1)}, f32[36,512]{1,0:T(8,128)S(1)}, f32[36,512]{1,0:T(8,128)S(1)}, f32[88,512]{1,0:T(8,128)S(1)}, f32[88,512]{1,0:T(8,128)S(1)}) custom-call(f32[240,2048]{1,0:T(8,128)S(1)} %get-tuple-element.65.u_ref.u, f32[240,2048]{1,0:T(8,128)S(1)} %shard_map.142.t_in, f32[8,2048]{1,0:T(8,128)S(1)} %get-tuple-element.67.csr, ...), custom_call_target="tpu_custom_call" | custom-call | tf_op jit(solution)/shard_map/pallas_call | solution.py:50
  15.9 0.1 collective-permute-start.6
  16.0 3.9 %collective-permute-start.7 = (f32[88,512]{1,0:T(8,128)S(1)}, f32[88,512]{1,0:T(8,128)S(1)}, u32[]{:S(2)}, u32[]{:S(2)}) collective-permute-start(f32[88,512]{1,0:T(8,128)S(1)} %get-tuple-element.84), channel_id=1, source_target_pairs={{0,32},{1,2},{2,1},{3,4},{4,3},{5,6},{6,5},{7,8},{8,7},{9,10},{10,... | collective-permute-start | bytes 540680 | tf_op jit(solution)/shard_map/ppermute | solution.py:871
  20.0 0.7 collective-permute-start.5
  20.7 1.5 %shard_map.144.t_in = f32[240,2048]{1,0:T(8,128)S(1)} custom-call(f32[240,2048]{1,0:T(8,128)S(1)} %get-tuple-element.80.u_ref.u, f32[240,2048]{1,0:T(8,128)S(1)} %get-tuple-element.66.g_ref, f32[8,2048]{1,0:T(8,128)S(1)} %get-tuple-element.67.csr, bf16[240,768]{1,0:T(8,128)(2,1)S(1)} %get-tuple-element.73.kf), custom_call_target="tpu_custom_call" | custom-call | tf_op jit(solution)/shard_map/pallas_call | solution.py:50
  22.2 2.2 %collective-permute-done.4.r1 = f32[36,512]{1,0:T(8,128)S(1)} collective-permute-done((f32[36,512]{1,0:T(8,128)S(1)}, f32[36,512]{1,0:T(8,128)S(1)}, u32[]{:S(2)}, u32[]{:S(2)}) %collective-permute-start.4) | collective-permute-done | bytes 73760 | tf_op jit(solution)/shard_map/ppermute | solution.py:871
  24.4 1.3 %shard_map.145 = (f32[64,2048]{1,0:T(8,128)S(1)}, f32[64,2048]{1,0:T(8,128)S(1)}, f32[16,512]{1,0:T(8,128)S(1)}, f32[16,512]{1,0:T(8,128)S(1)}, f32[32,512]{1,0:T(8,128)S(1)}, /*index=5*/f32[40,512]{1,0:T(8,128)S(1)}) custom-call(f32[240,2048]{1,0:T(8,128)S(1)} %shard_map.144.t_in, f32[8,2048]{1,0:T(8,128)S(1)} %get-tuple-element.67.csr, ...), custom_call_target="tpu_custom_call" | custom-call | tf_op jit(solution)/shard_map/pallas_call | solution.py:50
  25.7 2.7 %collective-permute-start.11 = (f32[40,512]{1,0:T(8,128)S(1)}, f32[40,512]{1,0:T(8,128)S(1)}, u32[]{:S(2)}, u32[]{:S(2)}) collective-permute-start(f32[40,512]{1,0:T(8,128)S(1)} %get-tuple-element.92), channel_id=1, source_target_pairs={{0,32},{1,2},{2,1},{3,4},{4,3},{5,6},{6,5},{7,8},{8,7},{9,10},{10,... | collective-permute-start | bytes 245768 | tf_op jit(solution)/shard_map/ppermute | solution.py:871
  28.4 0.7 collective-permute-start.9
  29.1 0.5 shard_map.146.t_in
  29.7 2.6 %collective-permute-done.8.r1 = f32[16,512]{1,0:T(8,128)S(1)} collective-permute-done((f32[16,512]{1,0:T(8,128)S(1)}, f32[16,512]{1,0:T(8,128)S(1)}, u32[]{:S(2)}, u32[]{:S(2)}) %collective-permute-start.8) | collective-permute-done | bytes 32800 | tf_op jit(solution)/shard_map/ppermute | solution.py:871
  32.3 1.4 %shard_map.147 = (f32[64,2048]{1,0:T(8,128)S(1)}, f32[256,128]{1,0:T(8,128)S(1)}, f32[176,128]{1,0:T(8,128)S(1)}, f32[176,128]{1,0:T(8,128)S(1)}) custom-call(f32[64,2048]{1,0:T(8,128)S(1)} %get-tuple-element.86.m_ref.m, f32[64,2048]{1,0:T(8,128)S(1)} %shard_map.146.t_in, f32[8,2048]{1,0:T(8,128)S(1)} %get-tuple-element.67.csr, s32[4]{0:T(128)S(1)} %pad_add_fusion.idx, ...), custom_call_target="tpu_custom_call" | custom-call | tf_op jit(solution)/shard_map/pallas_call | solution.py:50
  33.7 0.2 collective-permute-start.12
  33.9 0.7 collective-permute-start.13
  34.6 0.7 shard_map.148.coef
  35.3 3.0 %collective-permute-done.12.r1 = f32[176,128]{1,0:T(8,128)S(1)} collective-permute-done((f32[176,128]{1,0:T(8,128)S(1)}, f32[176,128]{1,0:T(8,128)S(1)}, u32[]{:S(2)}, u32[]{:S(2)}) %collective-permute-start.12) | collective-permute-done | bytes 90144 | tf_op jit(solution)/shard_map/ppermute | solution.py:871
  38.3 0.2 collective-permute-done.13.r2
  38.4 0.6 shard_map.149
  39.0 1.9 %collective-permute-start.15 = (f32[232,128]{1,0:T(8,128)S(1)}, f32[232,128]{1,0:T(8,128)S(1)}, u32[]{:S(2)}, u32[]{:S(2)}) collective-permute-start(f32[232,128]{1,0:T(8,128)S(1)} %get-tuple-element.100), channel_id=1, source_target_pairs={{0,32},{1,2},{2,1},{3,4},{4,3},{5,6},{6,5},{7,8},{8,7},{9,10},{10,... | collective-permute-start | bytes 356360 | tf_op jit(solution)/shard_map/ppermute | solution.py:871
  41.0 1.3 %collective-permute-done.14.r3 = f32[224,128]{1,0:T(8,128)S(1)} collective-permute-done((f32[224,128]{1,0:T(8,128)S(1)}, f32[224,128]{1,0:T(8,128)S(1)}, u32[]{:S(2)}, u32[]{:S(2)}) %collective-permute-start.14) | collective-permute-done | bytes 114720 | tf_op jit(solution)/shard_map/ppermute | solution.py:871
  42.3 3.2 %collective-permute-done.15.r4 = f32[232,128]{1,0:T(8,128)S(1)} collective-permute-done((f32[232,128]{1,0:T(8,128)S(1)}, f32[232,128]{1,0:T(8,128)S(1)}, u32[]{:S(2)}, u32[]{:S(2)}) %collective-permute-start.15) | collective-permute-done | bytes 118816 | tf_op jit(solution)/shard_map/ppermute | solution.py:871
  45.5 1.2 %shard_map.150 = (f32[800,128]{1,0:T(8,128)S(1)}, f32[128,128]{1,0:T(8,128)S(1)}, f32[160,128]{1,0:T(8,128)S(1)}, f32[160,128]{1,0:T(8,128)S(1)}) custom-call(f32[480,128]{1,0:T(8,128)S(1)} %get-tuple-element.98.whole, f32[224,128]{1,0:T(8,128)S(1)} %collective-permute-done.14.r3, f32[232,128]{1,0:T(8,128)S(1)} %collective-permute-done.15.r4, ...), custom_call_target="tpu_custom_call" | custom-call | tf_op jit(solution)/shard_map/pallas_call | solution.py:50
  46.7 0.1 collective-permute-start.16
  46.8 0.7 collective-permute-start.17
  47.5 3.7 %collective-permute-done.16.r1 = f32[160,128]{1,0:T(8,128)S(1)} collective-permute-done((f32[160,128]{1,0:T(8,128)S(1)}, f32[160,128]{1,0:T(8,128)S(1)}, u32[]{:S(2)}, u32[]{:S(2)}) %collective-permute-start.16) | collective-permute-done | bytes 81952 | tf_op jit(solution)/shard_map/ppermute | solution.py:871
  51.2 0.1 collective-permute-done.17.r2
  51.3 0.6 shard_map.151
  51.9 0.8 collective-permute-start.19
  52.7 0.7 shard_map.152
  53.3 0.7 collective-permute-done.18.r3
  54.0 4.2 %collective-permute-done.19.r4 = f32[216,128]{1,0:T(8,128)S(1)} collective-permute-done((f32[216,128]{1,0:T(8,128)S(1)}, f32[216,128]{1,0:T(8,128)S(1)}, u32[]{:S(2)}, u32[]{:S(2)}) %collective-permute-start.19) | collective-permute-done | bytes 110624 | tf_op jit(solution)/shard_map/ppermute | solution.py:871
  58.2 2.2 %shard_map.153 = (f32[64,2048]{1,0:T(8,128)S(1)}, f32[16,512]{1,0:T(8,128)S(1)}, f32[16,512]{1,0:T(8,128)S(1)}, f32[32,512]{1,0:T(8,128)S(1)}, f32[40,512]{1,0:T(8,128)S(1)}) custom-call(f32[128,128]{1,0:T(8,128)S(1)} %get-tuple-element.102.own, f32[160,128]{1,0:T(8,128)S(1)} %collective-permute-done.16.r1, f32[160,128]{1,0:T(8,128)S(1)} %collective-permute-done.17.r2, ...), custom_call_target="tpu_custom_call" | custom-call | tf_op jit(solution)/shard_map/pallas_call | solution.py:50
  60.4 0.8 collective-permute-start.23
  61.2 0.2 collective-permute-start.20
  61.4 0.4 collective-permute-start.21
  61.8 0.5 shard_map.154.t_in
  62.3 2.8 %collective-permute-done.20.r1 = f32[16,512]{1,0:T(8,128)S(1)} collective-permute-done((f32[16,512]{1,0:T(8,128)S(1)}, f32[16,512]{1,0:T(8,128)S(1)}, u32[]{:S(2)}, u32[]{:S(2)}) %collective-permute-start.20) | collective-permute-done | bytes 32800 | tf_op jit(solution)/shard_map/ppermute | solution.py:871
  65.1 0.2 collective-permute-done.21.r2
  65.3 1.1 %collective-permute-done.23.r4 = f32[40,512]{1,0:T(8,128)S(1)} collective-permute-done((f32[40,512]{1,0:T(8,128)S(1)}, f32[40,512]{1,0:T(8,128)S(1)}, u32[]{:S(2)}, u32[]{:S(2)}) %collective-permute-start.23) | collective-permute-done | bytes 81952 | tf_op jit(solution)/shard_map/ppermute | solution.py:871
  66.5 1.0 %shard_map.155 = (f32[240,2048]{1,0:T(8,128)S(1)}, f32[36,512]{1,0:T(8,128)S(1)}, f32[36,512]{1,0:T(8,128)S(1)}, f32[48,512]{1,0:T(8,128)S(1)}, f32[56,512]{1,0:T(8,128)S(1)}) custom-call(f32[64,2048]{1,0:T(8,128)S(1)} %get-tuple-element.109.m_ref.m, f32[64,2048]{1,0:T(8,128)S(1)} %shard_map.154.t_in, f32[8,2048]{1,0:T(8,128)S(1)} %get-tuple-element.67.csr, ...), custom_call_target="tpu_custom_call" | custom-call | tf_op jit(solution)/shard_map/pallas_call | solution.py:50
  67.5 0.8 collective-permute-start.27
  68.3 0.6 collective-permute-start.24
  68.9 0.7 collective-permute-start.25
  69.5 1.5 %shard_map.156.t_in = f32[240,2048]{1,0:T(8,128)S(1)} custom-call(f32[240,2048]{1,0:T(8,128)S(1)} %get-tuple-element.115.u_ref.u, f32[240,2048]{1,0:T(8,128)S(1)} %get-tuple-element.66.g_ref, f32[8,2048]{1,0:T(8,128)S(1)} %get-tuple-element.67.csr, bf16[240,768]{1,0:T(8,128)(2,1)S(1)} %get-tuple-element.73.kf), custom_call_target="tpu_custom_call" | custom-call | tf_op jit(solution)/shard_map/pallas_call | solution.py:50
  71.0 2.1 %collective-permute-done.24.r1 = f32[36,512]{1,0:T(8,128)S(1)} collective-permute-done((f32[36,512]{1,0:T(8,128)S(1)}, f32[36,512]{1,0:T(8,128)S(1)}, u32[]{:S(2)}, u32[]{:S(2)}) %collective-permute-start.24) | collective-permute-done | bytes 73760 | tf_op jit(solution)/shard_map/ppermute | solution.py:871
  73.2 0.3 collective-permute-done.25.r2
  73.5 0.5 collective-permute-done.27.r4
  73.9 1.6 %shard_map.157 = (f32[240,2048]{1,0:T(8,128)S(1)}, f32[36,512]{1,0:T(8,128)S(1)}, f32[36,512]{1,0:T(8,128)S(1)}, f32[48,512]{1,0:T(8,128)S(1)}, f32[56,512]{1,0:T(8,128)S(1)}) custom-call(f32[240,2048]{1,0:T(8,128)S(1)} %get-tuple-element.115.u_ref.u, f32[240,2048]{1,0:T(8,128)S(1)} %shard_map.156.t_in, f32[8,2048]{1,0:T(8,128)S(1)} %get-tuple-element.67.csr, ...), custom_call_target="tpu_custom_call" | custom-call | tf_op jit(solution)/shard_map/pallas_call | solution.py:50
  75.5 0.9 %collective-permute-start.31 = (f32[56,512]{1,0:T(8,128)S(1)}, f32[56,512]{1,0:T(8,128)S(1)}, u32[]{:S(2)}, u32[]{:S(2)}) collective-permute-start(f32[56,512]{1,0:T(8,128)S(1)} %get-tuple-element.124), channel_id=1, source_target_pairs={{0,32},{1,2},{2,1},{3,4},{4,3},{5,6},{6,5},{7,8},{8,7},{9,10},{10,... | collective-permute-start | bytes 344072 | tf_op jit(solution)/shard_map/ppermute | solution.py:871
  76.4 0.8 collective-permute-start.28
  77.3 0.7 collective-permute-start.29
  77.9 1.5 %shard_map.158.t_in = f32[240,2048]{1,0:T(8,128)S(1)} custom-call(f32[240,2048]{1,0:T(8,128)S(1)} %get-tuple-element.120.u_ref.u, f32[240,2048]{1,0:T(8,128)S(1)} %get-tuple-element.66.g_ref, f32[8,2048]{1,0:T(8,128)S(1)} %get-tuple-element.67.csr, bf16[240,768]{1,0:T(8,128)(2,1)S(1)} %get-tuple-element.73.kf), custom_call_target="tpu_custom_call" | custom-call | tf_op jit(solution)/shard_map/pallas_call | solution.py:50
  79.4 1.9 %collective-permute-done.28.r1 = f32[36,512]{1,0:T(8,128)S(1)} collective-permute-done((f32[36,512]{1,0:T(8,128)S(1)}, f32[36,512]{1,0:T(8,128)S(1)}, u32[]{:S(2)}, u32[]{:S(2)}) %collective-permute-start.28) | collective-permute-done | bytes 73760 | tf_op jit(solution)/shard_map/ppermute | solution.py:871
  81.3 0.5 collective-permute-done.29.r2
  81.8 0.1 collective-permute-done.31.r4
  81.9 4.7 %shard_map.159 = (f32[3456,128]{1,0:T(8,128)}, f32[3456,128]{1,0:T(8,128)}) custom-call(f32[240,2048]{1,0:T(8,128)S(1)} %get-tuple-element.120.u_ref.u, f32[240,2048]{1,0:T(8,128)S(1)} %shard_map.158.t_in, f32[8,2048]{1,0:T(8,128)S(1)} %get-tuple-element.67.csr, s32[4]{0:T(128)S(1)} %pad_add_fusion.idx, f32[36,512]{1,0:T(8,128)S(1)} %collective-permute-done.28.r1, ...), custom_call_target="tpu_custom_call" | custom-call | tf_op jit(solution)/shard_map/pallas_call | solution.py:50
  (29 shorter events, 0.1 us)
Async XLA Ops:
  4.7 9.6 %collective-permute-start = (f32[48,512]{1,0:T(8,128)S(1)}, f32[48,512]{1,0:T(8,128)S(1)}, u32[]{:S(2)}, u32[]{:S(2)}) collective-permute-start(f32[48,512]{1,0:T(8,128)S(1)} %get-tuple-element.74), channel_id=1, source_target_pairs={{0,32},{1,33},{2,34},{3,35},{4,36},{5,37},{6,38},{7,39},{8,40},{9,... | collective-permute-start | bytes 294920 | tf_op jit(solution)/shard_map/ppermute | solution.py:871
  5.2 9.1 %collective-permute-start.1 = (f32[48,512]{1,0:T(8,128)S(1)}, f32[48,512]{1,0:T(8,128)S(1)}, u32[]{:S(2)}, u32[]{:S(2)}) collective-permute-start(f32[48,512]{1,0:T(8,128)S(1)} %get-tuple-element.75), channel_id=1, source_target_pairs={{0,1},{1,0},{2,3},{3,2},{4,5},{5,4},{6,7},{7,6},{8,9},{9,8},{10,11... | collective-permute-start | bytes 294920 | tf_op jit(solution)/shard_map/ppermute | solution.py:871
  7.6 6.7 %collective-permute-start.2 = (f32[48,512]{1,0:T(8,128)S(1)}, f32[48,512]{1,0:T(8,128)S(1)}, u32[]{:S(2)}, u32[]{:S(2)}) collective-permute-start(f32[48,512]{1,0:T(8,128)S(1)} %get-tuple-element.76), channel_id=1, source_target_pairs={{0,1},{1,0},{2,3},{3,2},{4,5},{5,4},{6,7},{7,6},{8,9},{9,8},{10,11... | collective-permute-start | bytes 294920 | tf_op jit(solution)/shard_map/ppermute | solution.py:871
  7.6 6.7 %collective-permute-start.3 = (f32[48,512]{1,0:T(8,128)S(1)}, f32[48,512]{1,0:T(8,128)S(1)}, u32[]{:S(2)}, u32[]{:S(2)}) collective-permute-start(f32[48,512]{1,0:T(8,128)S(1)} %get-tuple-element.77), channel_id=1, source_target_pairs={{0,32},{1,2},{2,1},{3,4},{4,3},{5,6},{6,5},{7,8},{8,7},{9,10},{10,... | collective-permute-start | bytes 294920 | tf_op jit(solution)/shard_map/ppermute | solution.py:871
  15.9 8.5 %collective-permute-start.6 = (f32[88,512]{1,0:T(8,128)S(1)}, f32[88,512]{1,0:T(8,128)S(1)}, u32[]{:S(2)}, u32[]{:S(2)}) collective-permute-start(f32[88,512]{1,0:T(8,128)S(1)} %get-tuple-element.83), channel_id=1, source_target_pairs={{0,1},{1,0},{2,3},{3,2},{4,5},{5,4},{6,7},{7,6},{8,9},{9,8},{10,11... | collective-permute-start | bytes 540680 | tf_op jit(solution)/shard_map/ppermute | solution.py:871
  16.0 8.4 %collective-permute-start.7 = (f32[88,512]{1,0:T(8,128)S(1)}, f32[88,512]{1,0:T(8,128)S(1)}, u32[]{:S(2)}, u32[]{:S(2)}) collective-permute-start(f32[88,512]{1,0:T(8,128)S(1)} %get-tuple-element.84), channel_id=1, source_target_pairs={{0,32},{1,2},{2,1},{3,4},{4,3},{5,6},{6,5},{7,8},{8,7},{9,10},{10,... | collective-permute-start | bytes 540680 | tf_op jit(solution)/shard_map/ppermute | solution.py:871
  20.0 4.4 %collective-permute-start.4 = (f32[36,512]{1,0:T(8,128)S(1)}, f32[36,512]{1,0:T(8,128)S(1)}, u32[]{:S(2)}, u32[]{:S(2)}) collective-permute-start(f32[36,512]{1,0:T(8,128)S(1)} %get-tuple-element.81), channel_id=1, source_target_pairs={{0,32},{1,33},{2,34},{3,35},{4,36},{5,37},{6,38},{7,39},{8,40},{9,... | collective-permute-start | bytes 221192 | tf_op jit(solution)/shard_map/ppermute | solution.py:871
  20.0 4.4 %collective-permute-start.5 = (f32[36,512]{1,0:T(8,128)S(1)}, f32[36,512]{1,0:T(8,128)S(1)}, u32[]{:S(2)}, u32[]{:S(2)}) collective-permute-start(f32[36,512]{1,0:T(8,128)S(1)} %get-tuple-element.82), channel_id=1, source_target_pairs={{0,1},{1,0},{2,3},{3,2},{4,5},{5,4},{6,7},{7,6},{8,9},{9,8},{10,11... | collective-permute-start | bytes 221192 | tf_op jit(solution)/shard_map/ppermute | solution.py:871
  25.7 6.6 %collective-permute-start.11 = (f32[40,512]{1,0:T(8,128)S(1)}, f32[40,512]{1,0:T(8,128)S(1)}, u32[]{:S(2)}, u32[]{:S(2)}) collective-permute-start(f32[40,512]{1,0:T(8,128)S(1)} %get-tuple-element.92), channel_id=1, source_target_pairs={{0,32},{1,2},{2,1},{3,4},{4,3},{5,6},{6,5},{7,8},{8,7},{9,10},{10,... | collective-permute-start | bytes 245768 | tf_op jit(solution)/shard_map/ppermute | solution.py:871
  28.4 3.9 %collective-permute-start.10 = (f32[32,512]{1,0:T(8,128)S(1)}, f32[32,512]{1,0:T(8,128)S(1)}, u32[]{:S(2)}, u32[]{:S(2)}) collective-permute-start(f32[32,512]{1,0:T(8,128)S(1)} %get-tuple-element.91), channel_id=1, source_target_pairs={{0,1},{1,0},{2,3},{3,2},{4,5},{5,4},{6,7},{7,6},{8,9},{9,8},{10,11... | collective-permute-start | bytes 196616 | tf_op jit(solution)/shard_map/ppermute | solution.py:871
  28.4 3.9 %collective-permute-start.8 = (f32[16,512]{1,0:T(8,128)S(1)}, f32[16,512]{1,0:T(8,128)S(1)}, u32[]{:S(2)}, u32[]{:S(2)}) collective-permute-start(f32[16,512]{1,0:T(8,128)S(1)} %get-tuple-element.89), channel_id=1, source_target_pairs={{0,32},{1,33},{2,34},{3,35},{4,36},{5,37},{6,38},{7,39},{8,40},{9,... | collective-permute-start | bytes 98312 | tf_op jit(solution)/shard_map/ppermute | solution.py:871
  28.4 3.9 %collective-permute-start.9 = (f32[16,512]{1,0:T(8,128)S(1)}, f32[16,512]{1,0:T(8,128)S(1)}, u32[]{:S(2)}, u32[]{:S(2)}) collective-permute-start(f32[16,512]{1,0:T(8,128)S(1)} %get-tuple-element.90), channel_id=1, source_target_pairs={{0,1},{1,0},{2,3},{3,2},{4,5},{5,4},{6,7},{7,6},{8,9},{9,8},{10,11... | collective-permute-start | bytes 98312 | tf_op jit(solution)/shard_map/ppermute | solution.py:871
  29.7 15.8 %copy-start.2 = (f32[8,8]{1,0:T(8,128)S(1)}, f32[8,8]{1,0:T(8,128)}, u32[]{:S(2)}) copy-start(f32[8,8]{1,0:T(8,128)} %kc.3) | copy-start | bytes 772
  33.7 4.6 %collective-permute-start.12 = (f32[176,128]{1,0:T(8,128)S(1)}, f32[176,128]{1,0:T(8,128)S(1)}, u32[]{:S(2)}, u32[]{:S(2)}) collective-permute-start(f32[176,128]{1,0:T(8,128)S(1)} %get-tuple-element.96), channel_id=1, source_target_pairs={{0,32},{1,33},{2,34},{3,35},{4,36},{5,37},{6,38},{7,39},{8,40},{9,... | collective-permute-start | bytes 270344 | tf_op jit(solution)/shard_map/ppermute | solution.py:871
  33.9 18.8 %copy-start = (f32[216,216]{1,0:T(8,128)S(1)}, f32[216,216]{1,0:T(8,128)}, u32[]{:S(2)}) copy-start(f32[216,216]{1,0:T(8,128)} %noise.1) | copy-start | bytes 559876
  33.9 4.5 %collective-permute-start.13 = (f32[176,128]{1,0:T(8,128)S(1)}, f32[176,128]{1,0:T(8,128)S(1)}, u32[]{:S(2)}, u32[]{:S(2)}) collective-permute-start(f32[176,128]{1,0:T(8,128)S(1)} %get-tuple-element.97), channel_id=1, source_target_pairs={{0,1},{1,0},{2,3},{3,2},{4,5},{5,4},{6,7},{7,6},{8,9},{9,8},{10,11... | collective-permute-start | bytes 270344 | tf_op jit(solution)/shard_map/ppermute | solution.py:871
  39.0 6.5 %collective-permute-start.15 = (f32[232,128]{1,0:T(8,128)S(1)}, f32[232,128]{1,0:T(8,128)S(1)}, u32[]{:S(2)}, u32[]{:S(2)}) collective-permute-start(f32[232,128]{1,0:T(8,128)S(1)} %get-tuple-element.100), channel_id=1, source_target_pairs={{0,32},{1,2},{2,1},{3,4},{4,3},{5,6},{6,5},{7,8},{8,7},{9,10},{10,... | collective-permute-start | bytes 356360 | tf_op jit(solution)/shard_map/ppermute | solution.py:871
  41.0 1.3 %collective-permute-start.14 = (f32[224,128]{1,0:T(8,128)S(1)}, f32[224,128]{1,0:T(8,128)S(1)}, u32[]{:S(2)}, u32[]{:S(2)}) collective-permute-start(f32[224,128]{1,0:T(8,128)S(1)} %get-tuple-element.99), channel_id=1, source_target_pairs={{0,1},{1,0},{2,3},{3,2},{4,5},{5,4},{6,7},{7,6},{8,9},{9,8},{10,11... | collective-permute-start | bytes 344072 | tf_op jit(solution)/shard_map/ppermute | solution.py:871
  46.7 4.5 %collective-permute-start.16 = (f32[160,128]{1,0:T(8,128)S(1)}, f32[160,128]{1,0:T(8,128)S(1)}, u32[]{:S(2)}, u32[]{:S(2)}) collective-permute-start(f32[160,128]{1,0:T(8,128)S(1)} %get-tuple-element.103), channel_id=1, source_target_pairs={{0,32},{1,33},{2,34},{3,35},{4,36},{5,37},{6,38},{7,39},{8,40},{9,... | collective-permute-start | bytes 245768 | tf_op jit(solution)/shard_map/ppermute | solution.py:871
  46.8 4.5 %collective-permute-start.17 = (f32[160,128]{1,0:T(8,128)S(1)}, f32[160,128]{1,0:T(8,128)S(1)}, u32[]{:S(2)}, u32[]{:S(2)}) collective-permute-start(f32[160,128]{1,0:T(8,128)S(1)} %get-tuple-element.104), channel_id=1, source_target_pairs={{0,1},{1,0},{2,3},{3,2},{4,5},{5,4},{6,7},{7,6},{8,9},{9,8},{10,11... | collective-permute-start | bytes 245768 | tf_op jit(solution)/shard_map/ppermute | solution.py:871
  51.9 6.4 %collective-permute-start.19 = (f32[216,128]{1,0:T(8,128)S(1)}, f32[216,128]{1,0:T(8,128)S(1)}, u32[]{:S(2)}, u32[]{:S(2)}) collective-permute-start(f32[216,128]{1,0:T(8,128)S(1)} %get-tuple-element.106), channel_id=1, source_target_pairs={{0,32},{1,2},{2,1},{3,4},{4,3},{5,6},{6,5},{7,8},{8,7},{9,10},{10,... | collective-permute-start | bytes 331784 | tf_op jit(solution)/shard_map/ppermute | solution.py:871
  52.7 1.3 %collective-permute-start.18 = (f32[208,128]{1,0:T(8,128)S(1)}, f32[208,128]{1,0:T(8,128)S(1)}, u32[]{:S(2)}, u32[]{:S(2)}) collective-permute-start(f32[208,128]{1,0:T(8,128)S(1)} %get-tuple-element.105), channel_id=1, source_target_pairs={{0,1},{1,0},{2,3},{3,2},{4,5},{5,4},{6,7},{7,6},{8,9},{9,8},{10,11... | collective-permute-start | bytes 319496 | tf_op jit(solution)/shard_map/ppermute | solution.py:871
  60.4 6.1 %collective-permute-start.23 = (f32[40,512]{1,0:T(8,128)S(1)}, f32[40,512]{1,0:T(8,128)S(1)}, u32[]{:S(2)}, u32[]{:S(2)}) collective-permute-start(f32[40,512]{1,0:T(8,128)S(1)} %get-tuple-element.113), channel_id=1, source_target_pairs={{0,32},{1,2},{2,1},{3,4},{4,3},{5,6},{6,5},{7,8},{8,7},{9,10},{10,... | collective-permute-start | bytes 245768 | tf_op jit(solution)/shard_map/ppermute | solution.py:871
  61.2 4.1 %collective-permute-start.22 = (f32[32,512]{1,0:T(8,128)S(1)}, f32[32,512]{1,0:T(8,128)S(1)}, u32[]{:S(2)}, u32[]{:S(2)}) collective-permute-start(f32[32,512]{1,0:T(8,128)S(1)} %get-tuple-element.112), channel_id=1, source_target_pairs={{0,1},{1,0},{2,3},{3,2},{4,5},{5,4},{6,7},{7,6},{8,9},{9,8},{10,11... | collective-permute-start | bytes 196616 | tf_op jit(solution)/shard_map/ppermute | solution.py:871
  61.2 3.9 %collective-permute-start.20 = (f32[16,512]{1,0:T(8,128)S(1)}, f32[16,512]{1,0:T(8,128)S(1)}, u32[]{:S(2)}, u32[]{:S(2)}) collective-permute-start(f32[16,512]{1,0:T(8,128)S(1)} %get-tuple-element.110), channel_id=1, source_target_pairs={{0,32},{1,33},{2,34},{3,35},{4,36},{5,37},{6,38},{7,39},{8,40},{9,... | collective-permute-start | bytes 98312 | tf_op jit(solution)/shard_map/ppermute | solution.py:871
  61.4 3.9 %collective-permute-start.21 = (f32[16,512]{1,0:T(8,128)S(1)}, f32[16,512]{1,0:T(8,128)S(1)}, u32[]{:S(2)}, u32[]{:S(2)}) collective-permute-start(f32[16,512]{1,0:T(8,128)S(1)} %get-tuple-element.111), channel_id=1, source_target_pairs={{0,1},{1,0},{2,3},{3,2},{4,5},{5,4},{6,7},{7,6},{8,9},{9,8},{10,11... | collective-permute-start | bytes 98312 | tf_op jit(solution)/shard_map/ppermute | solution.py:871
  67.5 6.4 %collective-permute-start.27 = (f32[56,512]{1,0:T(8,128)S(1)}, f32[56,512]{1,0:T(8,128)S(1)}, u32[]{:S(2)}, u32[]{:S(2)}) collective-permute-start(f32[56,512]{1,0:T(8,128)S(1)} %get-tuple-element.119), channel_id=1, source_target_pairs={{0,32},{1,2},{2,1},{3,4},{4,3},{5,6},{6,5},{7,8},{8,7},{9,10},{10,... | collective-permute-start | bytes 344072 | tf_op jit(solution)/shard_map/ppermute | solution.py:871
  68.3 5.2 %collective-permute-start.26 = (f32[48,512]{1,0:T(8,128)S(1)}, f32[48,512]{1,0:T(8,128)S(1)}, u32[]{:S(2)}, u32[]{:S(2)}) collective-permute-start(f32[48,512]{1,0:T(8,128)S(1)} %get-tuple-element.118), channel_id=1, source_target_pairs={{0,1},{1,0},{2,3},{3,2},{4,5},{5,4},{6,7},{7,6},{8,9},{9,8},{10,11... | collective-permute-start | bytes 294920 | tf_op jit(solution)/shard_map/ppermute | solution.py:871
  68.3 4.9 %collective-permute-start.24 = (f32[36,512]{1,0:T(8,128)S(1)}, f32[36,512]{1,0:T(8,128)S(1)}, u32[]{:S(2)}, u32[]{:S(2)}) collective-permute-start(f32[36,512]{1,0:T(8,128)S(1)} %get-tuple-element.116), channel_id=1, source_target_pairs={{0,32},{1,33},{2,34},{3,35},{4,36},{5,37},{6,38},{7,39},{8,40},{9,... | collective-permute-start | bytes 221192 | tf_op jit(solution)/shard_map/ppermute | solution.py:871
  68.9 4.6 %collective-permute-start.25 = (f32[36,512]{1,0:T(8,128)S(1)}, f32[36,512]{1,0:T(8,128)S(1)}, u32[]{:S(2)}, u32[]{:S(2)}) collective-permute-start(f32[36,512]{1,0:T(8,128)S(1)} %get-tuple-element.117), channel_id=1, source_target_pairs={{0,1},{1,0},{2,3},{3,2},{4,5},{5,4},{6,7},{7,6},{8,9},{9,8},{10,11... | collective-permute-start | bytes 221192 | tf_op jit(solution)/shard_map/ppermute | solution.py:871
  75.5 6.4 %collective-permute-start.31 = (f32[56,512]{1,0:T(8,128)S(1)}, f32[56,512]{1,0:T(8,128)S(1)}, u32[]{:S(2)}, u32[]{:S(2)}) collective-permute-start(f32[56,512]{1,0:T(8,128)S(1)} %get-tuple-element.124), channel_id=1, source_target_pairs={{0,32},{1,2},{2,1},{3,4},{4,3},{5,6},{6,5},{7,8},{8,7},{9,10},{10,... | collective-permute-start | bytes 344072 | tf_op jit(solution)/shard_map/ppermute | solution.py:871
  76.4 5.4 %collective-permute-start.30 = (f32[48,512]{1,0:T(8,128)S(1)}, f32[48,512]{1,0:T(8,128)S(1)}, u32[]{:S(2)}, u32[]{:S(2)}) collective-permute-start(f32[48,512]{1,0:T(8,128)S(1)} %get-tuple-element.123), channel_id=1, source_target_pairs={{0,1},{1,0},{2,3},{3,2},{4,5},{5,4},{6,7},{7,6},{8,9},{9,8},{10,11... | collective-permute-start | bytes 294920 | tf_op jit(solution)/shard_map/ppermute | solution.py:871
  76.4 4.9 %collective-permute-start.28 = (f32[36,512]{1,0:T(8,128)S(1)}, f32[36,512]{1,0:T(8,128)S(1)}, u32[]{:S(2)}, u32[]{:S(2)}) collective-permute-start(f32[36,512]{1,0:T(8,128)S(1)} %get-tuple-element.121), channel_id=1, source_target_pairs={{0,32},{1,33},{2,34},{3,35},{4,36},{5,37},{6,38},{7,39},{8,40},{9,... | collective-permute-start | bytes 221192 | tf_op jit(solution)/shard_map/ppermute | solution.py:871
  77.3 4.6 %collective-permute-start.29 = (f32[36,512]{1,0:T(8,128)S(1)}, f32[36,512]{1,0:T(8,128)S(1)}, u32[]{:S(2)}, u32[]{:S(2)}) collective-permute-start(f32[36,512]{1,0:T(8,128)S(1)} %get-tuple-element.122), channel_id=1, source_target_pairs={{0,1},{1,0},{2,3},{3,2},{4,5},{5,4},{6,7},{7,6},{8,9},{9,8},{10,11... | collective-permute-start | bytes 221192 | tf_op jit(solution)/shard_map/ppermute | solution.py:871
  77.9 4.0 %copy-start.1 = (bf16[216,240]{1,0:T(8,128)(2,1)S(1)}, bf16[216,240]{1,0:T(8,128)(2,1)}, u32[]{:S(2)}) copy-start(bf16[216,240]{1,0:T(8,128)(2,1)} %constant.18.clone.from_slot) | copy-start | bytes 311044
  77.9 4.0 %copy-start.3 = (f32[4,4,128]{2,1,0:T(4,128)S(1)}, f32[4,4,128]{2,1,0:T(4,128)}, u32[]{:S(2)}) copy-start(f32[4,4,128]{2,1,0:T(4,128)} %param.23) | copy-start | bytes 24580
